TPU v7x, 32 devices: a whole 2x2x4 slice. The times are simulated.
32 devices in a mesh: inst: 16 (over z, y, x), tp: 2 (over core).
Axes of the slice: x: 2, y: 2, z: 4, core: 2. Of those that a mesh axis runs over, the one named last changes fastest.
Arguments:
- query_one: bfloat16 [256, 16, 128], P('inst', 'tp'), may hold values from -32 to 32
- key_one: bfloat16 [256, 2, 128], P('inst', 'tp'), may hold values from -6 to 6
- value_one: bfloat16 [256, 2, 128], P('inst', 'tp'), may hold values from -6 to 6
- key_pages: bfloat16 [1024, 2, 64, 128], P('inst', 'tp'), may hold values from -32 to 32
- value_pages: bfloat16 [1024, 2, 64, 128], P('inst', 'tp'), may hold values from -6 to 6
- page_table: int32 [256, 4], P('inst'), may hold values from 0 to 63, as said below
- lengths: int32 [256], P('inst'), may hold values from 8 to 254, as said below
- dest_instance: int32 [256], P('inst'), may hold values from 0 to 15, as said below
- dest_slot: int32 [256], P('inst'), may hold values from 0 to 15, as said below
- query_two: bfloat16 [256, 16, 128], P('inst', 'tp'), may hold values from -32 to 32
- key_two: bfloat16 [256, 2, 128], P('inst', 'tp'), may hold values from -6 to 6
- value_two: bfloat16 [256, 2, 128], P('inst', 'tp'), may hold values from -6 to 6
- out_weight: bfloat16 [2048, 4096], P('tp'), may hold values from -0.1875 to 0.1875
Outputs:
- out_one: bfloat16 [256, 4096], P('inst')
- out_two: bfloat16 [256, 4096], P('inst')
- key_cache: bfloat16 [1024, 2, 64, 128], P('inst', 'tp')
- value_cache: bfloat16 [1024, 2, 64, 128], P('inst', 'tp')
Inputs may be any that keep to these rules, and one draw needn't show every extreme that they name: `page_table`: the rows of one instance name each of its 64 pages exactly once. `lengths`: some request has exactly 254. `dest_instance`: the 16 requests of one instance go to 16 different instances, and every instance receives exactly 16 requests. `dest_slot`: the requests that reach one instance take its slots once each.
All inputs are finite; a program needn't handle non-finite values.
Results may differ from a plain program's by a relative error of at most 0.022.
Values may be sent and summed in bfloat16 or wider, within the bound.
No kernel may reach another device: no remote copies, remote signals or barrier semaphores. Data moves between devices by JAX's collectives and lax.ppermute only.
A program may use at most 64 MiB of HBM per device.

v0:
```python
import jax
import jax.numpy as jnp
from jax import lax
from jax.sharding import PartitionSpec as P

NEG = -1e30


def put_token(pages, token, position):
    rows = jnp.arange(pages.shape[0], dtype=jnp.int32)
    size = pages.shape[3]
    return pages.at[rows, position // size, :, position % size, :].set(token)


def attend(query, pages_k, pages_v, count):
    slots, heads, width = query.shape
    kv_heads = pages_k.shape[2]
    group = heads // kv_heads
    span = pages_k.shape[1] * pages_k.shape[3]
    grouped = query.reshape(slots, kv_heads, group, width)
    scores = jnp.einsum("skgd,spktd->skgpt", grouped, pages_k, preferred_element_type=jnp.float32)
    scores = scores.reshape(slots, kv_heads, group, span) * width ** (-0.5)
    live = jnp.arange(span, dtype=jnp.int32)[None, :] < count[:, None]
    live = live[:, None, None, :]
    scores = jnp.where(live, scores, NEG)
    top = jnp.max(scores, axis=-1, keepdims=True)
    expo = jnp.where(live, jnp.exp(scores - top), 0.0)
    weights = (expo / jnp.sum(expo, axis=-1, keepdims=True)).astype(jnp.bfloat16)
    weights = weights.reshape(slots, kv_heads, group, pages_k.shape[1], pages_k.shape[3])
    mixed = jnp.einsum("skgpt,spktd->skgd", weights, pages_v, preferred_element_type=jnp.float32)
    return mixed.astype(jnp.bfloat16).reshape(slots, heads * width)


def shards(
    query_one,
    key_one,
    value_one,
    key_pages,
    value_pages,
    page_table,
    lengths,
    dest_instance,
    dest_slot,
    query_two,
    key_two,
    value_two,
    out_weight,
):
    slots = lengths.shape[0]
    rows = jnp.arange(slots, dtype=jnp.int32)
    request_k = key_pages[page_table]
    request_v = value_pages[page_table]
    written_k = put_token(request_k, key_one, lengths)
    written_v = put_token(request_v, value_one, lengths)
    first = attend(query_one, written_k, written_v, lengths + 1)
    partial_one = jnp.dot(first, out_weight, preferred_element_type=jnp.float32)
    summed_one = lax.psum(partial_one.astype(jnp.bfloat16), "tp")
    count = lax.axis_size("inst")
    targets = jnp.arange(count, dtype=jnp.int32)
    chosen = dest_instance[None, :] == targets[:, None]
    source_row = jnp.sum(jnp.where(chosen, rows[None, :], 0), axis=1)
    present = jnp.any(chosen, axis=1)
    header = jnp.stack([jnp.where(present, dest_slot[source_row], -1), lengths[source_row]], axis=1)
    arrived_k, arrived_v, info = (
        lax.all_to_all(written_k[source_row], "inst", split_axis=0, concat_axis=0, tiled=True),
        lax.all_to_all(written_v[source_row], "inst", split_axis=0, concat_axis=0, tiled=True),
        lax.all_to_all(header, "inst", split_axis=0, concat_axis=0, tiled=True),
    )
    owner = jnp.sum(jnp.where(info[None, :, 0] == rows[:, None], targets[None, :], 0), axis=1)
    moved_k = arrived_k[owner]
    moved_v = arrived_v[owner]
    moved_lengths = info[owner, 1]
    moved_k = put_token(moved_k, key_two, moved_lengths + 1)
    moved_v = put_token(moved_v, value_two, moved_lengths + 1)
    second = attend(query_two, moved_k, moved_v, moved_lengths + 2)
    partial_two = jnp.dot(second, out_weight, preferred_element_type=jnp.float32)
    summed_two = lax.psum(partial_two.astype(jnp.bfloat16), "tp")
    pages_per = moved_k.shape[1]
    key_cache = moved_k.reshape(
        slots * pages_per, moved_k.shape[2], moved_k.shape[3], moved_k.shape[4]
    )
    value_cache = moved_v.reshape(
        slots * pages_per, moved_v.shape[2], moved_v.shape[3], moved_v.shape[4]
    )
    return (summed_one, summed_two, key_cache, value_cache)


def solution(mesh):
    return jax.shard_map(
        shards,
        mesh=mesh,
        in_specs=(
            P("inst", "tp", None),
            P("inst", "tp", None),
            P("inst", "tp", None),
            P("inst", "tp", None, None),
            P("inst", "tp", None, None),
            P("inst", None),
            P("inst"),
            P("inst"),
            P("inst"),
            P("inst", "tp", None),
            P("inst", "tp", None),
            P("inst", "tp", None),
            P("tp", None),
        ),
        out_specs=(
            P("inst", None),
            P("inst", None),
            P("inst", "tp", None, None),
            P("inst", "tp", None, None),
        ),
        check_vma=False,
    )
```

profile of v0, /device:TPU:0, one launch (start us, length us, event | category | flops | bytes accessed | tf_op | source)
XLA Modules:
  0.0 129.3 jit_solution(9580042641090715734)
XLA Ops:
  7.2 0.0 copy-start
  7.2 0.0 copy-start.1
  7.2 0.9 select_reduce_fusion.1
  8.1 0.8 fusion.22
  8.9 1.3 %gather_fusion.3 = s32[16]{0:T(128)S(1)} fusion(s32[16]{0:T(128)} %param.19, s32[1024]{0:T(1024)S(1)} %pad_clamp_fusion.1), kind=kCustom, calls=%fused_computation.3 | custom fusion | bytes 192 | tf_op jit(solution)/shard_map/gather | solution.py:63
  10.2 1.3 %gather_fusion.2 = s32[16]{0:T(128)S(1)} fusion(s32[16]{0:T(128)} %param.21, s32[1024]{0:T(1024)S(1)} %pad_clamp_fusion.1), kind=kCustom, calls=%fused_computation.2 | custom fusion | bytes 192 | tf_op jit(solution)/shard_map/gather | solution.py:63
  11.5 0.7 copy.25
  12.2 8.3 %all-to-all-start = ((s32[16,1,2]{2,1,0:T(1,128)}), s32[16,1,2]{2,1,0:T(1,128)S(1)}, u32[]{:S(2)}, u32[]{:S(2)}) async-start(s32[16,1,2]{2,1,0:T(1,128)} %copy.25), calls=%async_computation | async-start | bytes 16384 | tf_op jit(solution)/shard_map/all_to_all | solution.py:67
  20.5 0.7 fusion.31
  21.2 0.7 compare_select_fusion
  21.9 0.1 copy.24
  22.0 0.1 reshape.309
  22.1 0.0 copy-start.7
  22.1 0.0 copy-start.5
  22.1 0.7 gather_fusion
  22.9 1.6 %scatter_fusion = bf16[16,4,64,128]{3,2,1,0:T(8,128)(2,1)S(1)} fusion(bf16[16,4,64,128]{3,2,1,0:T(8,128)(2,1)S(1)} %bitcast.120, s32[16]{0:T(128)S(1)} %fusion.31, bf16[16,128]{1,0:T(8,128)(2,1)} %bitcast.128), kind=kCustom, calls=%fused_computation.9 | custom fusion | bytes 12480 | tf_op jit(solution)/shard_map/scatter | solution.py:12
  24.5 1.7 %gather_fusion.5 = bf16[16,4,64,128]{3,2,1,0:T(8,128)(2,1)} fusion(bf16[16,4,64,128]{3,2,1,0:T(8,128)(2,1)S(1)} %scatter_fusion, s32[1024]{0:T(1024)S(1)} %pad_clamp_fusion.1), kind=kCustom, calls=%fused_computation.5 | custom fusion | bytes 2097216 | tf_op jit(solution)/shard_map/gather | solution.py:65
  26.1 1.6 %all-to-all-done = s32[16,1,2]{2,1,0:T(1,128)S(1)} async-done(((s32[16,1,2]{2,1,0:T(1,128)}), s32[16,1,2]{2,1,0:T(1,128)S(1)}, u32[]{:S(2)}, u32[]{:S(2)}) %all-to-all-start) | async-done | bytes 160 | tf_op jit(solution)/shard_map/all_to_all | solution.py:67
  27.7 5.3 %all-to-all-start.1 = ((bf16[16,4,1,64,128]{4,3,1,2,0:T(8,128)(2,1)}), bf16[16,4,1,64,128]{4,3,1,2,0:T(8,128)(2,1)}, u32[]{:S(2)}, u32[]{:S(2)}) async-start(bf16[16,4,1,64,128]{4,3,1,2,0:T(8,128)(2,1)} %bitcast.23), calls=%async_computation.1 | async-start | bytes 2097152 | tf_op jit(solution)/shard_map/all_to_all | solution.py:65
  33.1 0.0 copy-start.8
  33.1 2.0 %gather_fusion.1 = bf16[64,64,128]{2,1,0:T(8,128)(2,1)S(1)} fusion(bf16[64,64,128]{2,1,0:T(8,128)(2,1)} %bitcast.125, s32[1024]{0:T(1024)S(1)} %pad_clamp_fusion.2), kind=kCustom, calls=%fused_computation.1 | custom fusion | bytes 2097408 | tf_op jit(solution)/shard_map/gather | solution.py:52
  35.1 1.5 %scatter_fusion.1 = bf16[16,4,64,128]{3,2,1,0:T(8,128)(2,1)S(1)} fusion(bf16[16,4,64,128]{3,2,1,0:T(8,128)(2,1)S(1)} %bitcast.121, s32[16]{0:T(128)S(1)} %fusion.31, bf16[16,128]{1,0:T(8,128)(2,1)S(1)} %bitcast.129), kind=kCustom, calls=%fused_computation.10 | custom fusion | bytes 12480 | tf_op jit(solution)/shard_map/scatter | solution.py:12
  36.6 1.7 %gather_fusion.7 = bf16[16,4,64,128]{3,2,1,0:T(8,128)(2,1)} fusion(bf16[16,4,64,128]{3,2,1,0:T(8,128)(2,1)S(1)} %scatter_fusion.1, s32[1024]{0:T(1024)S(1)} %pad_clamp_fusion.1), kind=kCustom, calls=%fused_computation.7 | custom fusion | bytes 2097216 | tf_op jit(solution)/shard_map/gather | solution.py:66
  38.3 0.1 copy.26
  38.4 18.6 %all-to-all-done.1 = bf16[16,4,1,64,128]{4,3,1,2,0:T(8,128)(2,1)} async-done(((bf16[16,4,1,64,128]{4,3,1,2,0:T(8,128)(2,1)}), bf16[16,4,1,64,128]{4,3,1,2,0:T(8,128)(2,1)}, u32[]{:S(2)}, u32[]{:S(2)}) %all-to-all-start.1) | async-done | bytes 1048608 | tf_op jit(solution)/shard_map/all_to_all | solution.py:65
  57.0 5.9 %all-to-all-start.2 = ((bf16[16,4,1,64,128]{4,3,1,2,0:T(8,128)(2,1)}), bf16[16,4,1,64,128]{4,3,1,2,0:T(8,128)(2,1)}, u32[]{:S(2)}, u32[]{:S(2)}) async-start(bf16[16,4,1,64,128]{4,3,1,2,0:T(8,128)(2,1)} %bitcast.123), calls=%async_computation.2 | async-start | bytes 2097152 | tf_op jit(solution)/shard_map/all_to_all | solution.py:66
  62.9 0.0 all-reduce.4.cloned.1.call-start
  62.9 0.1 select_reduce_fusion
  63.1 0.7 gather_fusion.4
  63.8 0.1 broadcast_compare_fusion
  63.9 1.6 %fusion.36 = (f32[16,8]{1,0:T(8,128)S(1)}, f32[16,8,4,64]{3,1,2,0:T(8,128)}) fusion(bf16[16,4,64,128]{3,2,1,0:T(8,128)(2,1)S(1)} %scatter_fusion, bf16[16,8,128]{2,1,0:T(8,128)(2,1)S(1)} %copy-done.4, pred[16,4,64]{2,1,0:T(4,128)(4,1)S(1)} %get-tuple-element.15), kind=kOutput, calls=%fused_computation.101 | convolution fusion | flops 8486784 | bytes 1217024 | tf_op jit(solution)/shard_map/skgd,spktd->skgpt/dot_general | solution.py:21
  65.5 2.0 %gather_fusion.6 = bf16[16,4,64,128]{3,2,1,0:T(8,128)(2,1)S(1)} fusion(bf16[16,4,64,128]{3,2,1,0:T(8,128)(2,1)} %bitcast.24, s32[1024]{0:T(1024)S(1)} %pad_clamp_fusion), kind=kCustom, calls=%fused_computation.6 | custom fusion | bytes 2097216 | tf_op jit(solution)/shard_map/gather | solution.py:70
  67.5 1.5 %scatter_fusion.2 = bf16[16,4,64,128]{3,2,1,0:T(8,128)(2,1)S(1)} fusion(bf16[16,4,64,128]{3,2,1,0:T(8,128)(2,1)S(1)} %gather_fusion.6, s32[16]{0:T(128)S(1)} %fusion.32, bf16[16,128]{1,0:T(8,128)(2,1)S(1)} %bitcast.130), kind=kCustom, calls=%fused_computation.11 | custom fusion | bytes 12480 | tf_op jit(solution)/shard_map/scatter | solution.py:12
  69.1 0.0 copy-start.2
  69.1 1.0 fusion.37
  70.1 1.2 fusion.6
  71.3 1.4 %fusion.4 = bf16[16,8,128]{2,1,0:T(8,128)(2,1)S(1)} fusion(bf16[16,4,64,128]{3,2,1,0:T(8,128)(2,1)S(1)} %scatter_fusion.1, f32[16,8,4,64]{3,1,2,0:T(8,128)} %get-tuple-element.19, f32[16,8]{1,0:T(8,128)S(1)} %get-tuple-element.22, f32[16,8]{1,0:T(8,128)S(1)} %get-tuple-element.18, pred[16,4,64]{2,1,0:T(4,128)(4,1)S(1)} %get-tuple-element.15), kind=kOutput, calls=%fused_computation.23 | convolution fusion | flops 8536064 | bytes 1217536 | tf_op jit(solution)/shard_map/skgpt,spktd->skgd/dot_general | solution.py:30
  72.7 13.2 %all-to-all-done.2 = bf16[16,4,1,64,128]{4,3,1,2,0:T(8,128)(2,1)} async-done(((bf16[16,4,1,64,128]{4,3,1,2,0:T(8,128)(2,1)}), bf16[16,4,1,64,128]{4,3,1,2,0:T(8,128)(2,1)}, u32[]{:S(2)}, u32[]{:S(2)}) %all-to-all-start.2) | async-done | bytes 1048608 | tf_op jit(solution)/shard_map/all_to_all | solution.py:66
  85.9 2.0 %gather_fusion.8 = bf16[16,4,64,128]{3,2,1,0:T(8,128)(2,1)S(1)} fusion(bf16[16,4,64,128]{3,2,1,0:T(8,128)(2,1)} %bitcast.33, s32[1024]{0:T(1024)S(1)} %pad_clamp_fusion), kind=kCustom, calls=%fused_computation.8 | custom fusion | bytes 2097216 | tf_op jit(solution)/shard_map/gather | solution.py:71
  87.9 1.5 %scatter_fusion.3 = bf16[16,4,64,128]{3,2,1,0:T(8,128)(2,1)S(1)} fusion(bf16[16,4,64,128]{3,2,1,0:T(8,128)(2,1)S(1)} %gather_fusion.8, s32[16]{0:T(128)S(1)} %fusion.32, bf16[16,128]{1,0:T(8,128)(2,1)S(1)} %bitcast.131), kind=kCustom, calls=%fused_computation.12 | custom fusion | bytes 12480 | tf_op jit(solution)/shard_map/scatter | solution.py:12
  89.4 0.0 copy-start.3
  89.5 0.4 fusion.5
  89.9 5.3 %convolution_convert_fusion = bf16[16,4096]{1,0:T(8,128)(2,1)} fusion(bf16[1024,4096]{1,0:T(8,128)(2,1)} %param.25, bf16[2,8,8,128]{3,2,1,0:T(8,128)(2,1)S(1)} %bitcast.127), kind=kOutput, calls=%fused_computation.13 | convolution fusion | flops 134283264 | bytes 8552448 | tf_op jit(solution)/shard_map/dot_general | solution.py:76
  95.2 5.2 %convolution_convert_fusion.1 = bf16[16,4096]{1,0:T(8,128)(2,1)} fusion(bf16[1024,4096]{1,0:T(8,128)(2,1)} %param.25, bf16[2,8,8,128]{3,2,1,0:T(8,128)(2,1)S(1)} %bitcast.126), kind=kOutput, calls=%fused_computation.14 | convolution fusion | flops 134283264 | bytes 8552448 | tf_op jit(solution)/shard_map/dot_general | solution.py:56
  100.4 0.0 all-reduce.4.cloned.1.call-update
  100.4 18.9 %all-reduce.4.cloned.1.call-done = (bf16[16,4096]{1,0:T(8,128)(2,1)}, bf16[16,4096]{1,0:T(8,128)(2,1)}) async-done(((bf16[16,4096]{1,0:T(8,128)(2,1)}, bf16[16,4096]{1,0:T(8,128)(2,1)}), (bf16[16,4096]{1,0:T(8,128)(2,1)}, bf16[16,4096]{1,0:T(8,128)(2,1)})) %all-reduce.4.cloned.1.call-update) | async-done | bytes 262160 | tf_op jit(solution)/shard_map/psum | solution.py:57
  119.3 1.6 %copy.49 = bf16[16,4096]{1,0:T(8,128)(2,1)} copy(bf16[16,4096]{1,0:T(8,128)(2,1)} %get-tuple-element.24) | data formatting | bytes 262144
  120.9 1.6 %copy.50 = bf16[16,4096]{1,0:T(8,128)(2,1)} copy(bf16[16,4096]{1,0:T(8,128)(2,1)} %get-tuple-element.25) | data formatting | bytes 262144
  (23 shorter events, 0.1 us)
Async XLA Ops:
  7.2 14.9 %copy-start = (bf16[64,1,64,128]{3,2,1,0:T(8,128)(2,1)S(1)}, bf16[64,1,64,128]{3,2,1,0:T(8,128)(2,1)}, u32[]{:S(2)}) copy-start(bf16[64,1,64,128]{3,2,1,0:T(8,128)(2,1)} %param.16) | copy-start | bytes 3145732
  7.2 31.1 %copy-start.1 = (s32[16]{0:T(128)S(1)}, s32[16]{0:T(128)}, u32[]{:S(2)}) copy-start(s32[16]{0:T(128)} %param.19) | copy-start | bytes 196
  7.2 27.9 %copy-start.6 = (bf16[16,1,128]{2,0,1:T(8,128)(2,1)S(1)}, bf16[16,1,128]{2,0,1:T(8,128)(2,1)}, u32[]{:S(2)}) copy-start(bf16[16,1,128]{2,0,1:T(8,128)(2,1)} %param.15) | copy-start | bytes 12292
  7.2 56.7 %copy-start.4 = (bf16[16,8,128]{2,1,0:T(8,128)(2,1)S(1)}, bf16[16,8,128]{2,1,0:T(8,128)(2,1)}, u32[]{:S(2)}) copy-start(bf16[16,8,128]{2,1,0:T(8,128)(2,1)} %param.13) | copy-start | bytes 98308
  12.2 15.5 %all-to-all-start = ((s32[16,1,2]{2,1,0:T(1,128)}), s32[16,1,2]{2,1,0:T(1,128)S(1)}, u32[]{:S(2)}, u32[]{:S(2)}) async-start(s32[16,1,2]{2,1,0:T(1,128)} %copy.25), calls=%async_computation | async-start | bytes 16384 | tf_op jit(solution)/shard_map/all_to_all | solution.py:67
  22.1 45.4 %copy-start.7 = (bf16[16,1,128]{2,0,1:T(8,128)(2,1)S(1)}, bf16[16,1,128]{2,0,1:T(8,128)(2,1)}, u32[]{:S(2)}) copy-start(bf16[16,1,128]{2,0,1:T(8,128)(2,1)} %param.23) | copy-start | bytes 12292
  22.1 47.0 %copy-start.5 = (bf16[16,8,128]{2,1,0:T(8,128)(2,1)S(1)}, bf16[16,8,128]{2,1,0:T(8,128)(2,1)}, u32[]{:S(2)}) copy-start(bf16[16,8,128]{2,1,0:T(8,128)(2,1)} %param.22) | copy-start | bytes 98308
  27.7 29.3 %all-to-all-start.1 = ((bf16[16,4,1,64,128]{4,3,1,2,0:T(8,128)(2,1)}), bf16[16,4,1,64,128]{4,3,1,2,0:T(8,128)(2,1)}, u32[]{:S(2)}, u32[]{:S(2)}) async-start(bf16[16,4,1,64,128]{4,3,1,2,0:T(8,128)(2,1)} %bitcast.23), calls=%async_computation.1 | async-start | bytes 2097152 | tf_op jit(solution)/shard_map/all_to_all | solution.py:65
  33.1 54.8 %copy-start.8 = (bf16[16,1,128]{2,0,1:T(8,128)(2,1)S(1)}, bf16[16,1,128]{2,0,1:T(8,128)(2,1)}, u32[]{:S(2)}) copy-start(bf16[16,1,128]{2,0,1:T(8,128)(2,1)} %param.24) | copy-start | bytes 12292
  57.0 28.9 %all-to-all-start.2 = ((bf16[16,4,1,64,128]{4,3,1,2,0:T(8,128)(2,1)}), bf16[16,4,1,64,128]{4,3,1,2,0:T(8,128)(2,1)}, u32[]{:S(2)}, u32[]{:S(2)}) async-start(bf16[16,4,1,64,128]{4,3,1,2,0:T(8,128)(2,1)} %bitcast.123), calls=%async_computation.2 | async-start | bytes 2097152 | tf_op jit(solution)/shard_map/all_to_all | solution.py:66
  62.9 56.4 %all-reduce.4.cloned.1.call-start = ((), (), s32[]{:S(2)}) async-start(), calls=%async_computation.3 | async-start | bytes 524288 | tf_op jit(solution)/shard_map/psum | solution.py:57
  69.1 26.1 %copy-start.2 = (bf16[16,4,64,128]{3,2,1,0:T(8,128)(2,1)}, bf16[16,4,64,128]{3,2,1,0:T(8,128)(2,1)S(1)}, u32[]{:S(2)}) copy-start(bf16[16,4,64,128]{3,2,1,0:T(8,128)(2,1)S(1)} %scatter_fusion.2) | copy-start | bytes 3145732
  89.4 11.0 %copy-start.3 = (bf16[16,4,64,128]{3,2,1,0:T(8,128)(2,1)}, bf16[16,4,64,128]{3,2,1,0:T(8,128)(2,1)S(1)}, u32[]{:S(2)}) copy-start(bf16[16,4,64,128]{3,2,1,0:T(8,128)(2,1)S(1)} %scatter_fusion.3) | copy-start | bytes 3145732
Sparse Core Ops, SparseCore 0:
  100.6 18.6 all-reduce.3
where the time goes:
time: 130 us; the launch traced here: 129 us
  waiting for transfers between devices  52.3 us (40%)
  local copies, waits for them, and re-layouts  23.6 us (18%)
  starting transfers between devices  19.6 us (15%)
  matrix products  15 us (12%)
  between operations  14.3 us (11%)
  other arithmetic  4.52 us (3%)
    psum x1, waiting for transfers between devices, shards(): summed_one = lax.psum(partial_one.astype(jnp.bfloat16), 'tp')  18.9 us
    all_to_all x1, waiting for transfers between devices, shards(): lax.all_to_all(written_k[source_row], 'inst', split_axis=0, concat_axis=0...  18.6 us
    all_to_all x1, waiting for transfers between devices, shards(): lax.all_to_all(written_v[source_row], 'inst', split_axis=0, concat_axis=0...  13.2 us
    all_to_all x1, starting transfers between devices, shards(): lax.all_to_all(header, 'inst', split_axis=0, concat_axis=0, tiled=True)  8.31 us
    scatter x4, local copies, waits for them, and re-layouts, put_token(): return pages.at[rows, position // size, :, position % size, :].set(token)  6.15 us
    all_to_all x1, starting transfers between devices, shards(): lax.all_to_all(written_v[source_row], 'inst', split_axis=0, concat_axis=0...  5.9 us
    all_to_all x1, starting transfers between devices, shards(): lax.all_to_all(written_k[source_row], 'inst', split_axis=0, concat_axis=0...  5.34 us
    dot_general x1, matrix products, shards(): jnp.dot(second, out_weight, preferred_element_type=jnp.float32)  5.26 us
  transfers between devices with their start and end apart: 4, of which 4 were waited for; matrix products, arithmetic and copies ran while one was open for 16% of the time, Pallas kernels for 0%

commit v1 on v0

v1 whole, which is shorter than its diff:
```python
import functools

import jax
import jax.numpy as jnp
from jax import lax
from jax.experimental import pallas as pl
from jax.experimental.pallas import tpu as pltpu
from jax.sharding import PartitionSpec as P

NEG = -1e30
TAIL = 16
CHUNK = 512
VMEM_BYTES = 32 * 1024 * 1024


def row_of(block, at):
    rows = lax.broadcasted_iota(jnp.int32, block.shape, 0)
    return jnp.sum(jnp.where(rows == at, block, 0.0), axis=0, keepdims=True)


def pack_kernel(n, pages, *refs):
    table, lengths, dest, slot, key_one, value_one, key_pages, value_pages = refs[:8]
    outs = refs[8 : 8 + n]
    source, tails, sems = refs[8 + n :]
    me = lax.axis_index("inst")
    size = key_pages.shape[1]
    span = pages * size

    def note(r, carry):
        source[dest[r]] = r
        return carry

    lax.fori_loop(0, n, note, 0)
    for s in range(n):
        r = source[me ^ s]
        for p in range(pages):
            page = table[r, p]
            pltpu.make_async_copy(
                key_pages.at[page], outs[s].at[pl.ds(p * size, size)], sems.at[s]
            ).start()
            pltpu.make_async_copy(
                value_pages.at[page], outs[s].at[pl.ds(span + p * size, size)], sems.at[s]
            ).start()
    keys = key_one[...].astype(jnp.float32)
    values = value_one[...].astype(jnp.float32)
    at = lax.broadcasted_iota(jnp.int32, (TAIL, keys.shape[1]), 0)
    for s in range(n):
        r = source[me ^ s]
        tail = jnp.where(at == 0, row_of(keys, r), row_of(values, r))
        tail = jnp.where(at == 2, slot[r].astype(jnp.float32), tail)
        tail = jnp.where(at == 3, lengths[r].astype(jnp.float32), tail)
        tails[s] = tail.astype(jnp.bfloat16)
        pltpu.make_async_copy(
            tails.at[s], outs[s].at[pl.ds(2 * span, TAIL)], sems.at[s]
        ).start()
    for s in range(n):
        pltpu.make_async_copy(outs[s], outs[s], sems.at[s]).wait()


def put_row(cache, index, row, position):
    size = cache.shape[2]
    page = position // size
    base = pl.multiple_of((position % size) // TAIL * TAIL, TAIL)
    block = cache[index, page, pl.ds(base, TAIL), :]
    at = lax.broadcasted_iota(jnp.int32, block.shape, 0)
    mixed = jnp.where(at == position % TAIL, row, block.astype(jnp.float32))
    cache[index, page, pl.ds(base, TAIL), :] = mixed.astype(jnp.bfloat16)


def attend(queries, keys, values, counts):
    width = queries[0].shape[1]
    scores = []
    for q, k, count in zip(queries, keys, counts):
        s = lax.dot_general(q, k, (((1,), (1,)), ((), ())), preferred_element_type=jnp.float32)
        live = lax.broadcasted_iota(jnp.int32, s.shape, 1) < count
        scores.append(jnp.where(live, s * width ** (-0.5), NEG))
    group = scores[0].shape[0]
    score = jnp.concatenate(scores, axis=0)
    top = jnp.max(score, axis=-1, keepdims=True)
    expo = jnp.where(score > 0.5 * NEG, jnp.exp(score - top), 0.0)
    weights = (expo / jnp.sum(expo, axis=-1, keepdims=True)).astype(jnp.bfloat16)
    return [
        jnp.dot(weights[i * group : (i + 1) * group], v, preferred_element_type=jnp.float32)
        for i, v in enumerate(values)
    ]


def weight_copies(weight, held, sems):
    width = weight.shape[1] // sems.shape[0]
    return [
        pltpu.make_async_copy(
            weight.at[:, pl.ds(c * width, width)], held.at[:, pl.ds(c * width, width)], sems.at[c]
        )
        for c in range(sems.shape[0])
    ]


def project(mixed, held, out, copies):
    heads = mixed.shape[1]
    rows = jnp.concatenate([mixed[:, h, :] for h in range(heads)], axis=1).astype(jnp.bfloat16)
    width = held.shape[1] // len(copies)
    for c, copy in enumerate(copies):
        copy.wait()
        part = jnp.dot(
            rows, held[:, c * width : (c + 1) * width], preferred_element_type=jnp.float32
        )
        out[:, c * width : (c + 1) * width] = part.astype(jnp.bfloat16)


def first_kernel(slots, pages, *refs):
    table, lengths, query, key_one, value_one, key_pages, value_pages, weight, out = refs[:9]
    keys, values, new_k, new_v, mixed, held, sems, wsems = refs[9:]
    copies = weight_copies(weight, held, wsems)
    for r in range(slots):
        for p in range(pages):
            page = table[r, p]
            pltpu.make_async_copy(key_pages.at[page], keys.at[r, p], sems.at[0, r]).start()
            pltpu.make_async_copy(value_pages.at[page], values.at[r, p], sems.at[1, r]).start()
    for copy in copies:
        copy.start()
    new_k[...] = key_one[...].astype(jnp.float32)
    new_v[...] = value_one[...].astype(jnp.float32)
    for r in range(slots):
        pltpu.make_async_copy(keys.at[r], keys.at[r], sems.at[0, r]).wait()
        pltpu.make_async_copy(values.at[r], values.at[r], sems.at[1, r]).wait()
        put_row(keys, r, new_k[r : r + 1, :], lengths[r])
        put_row(values, r, new_v[r : r + 1, :], lengths[r])
    span = pages * keys.shape[2]
    width = keys.shape[3]
    results = attend(
        [query[r] for r in range(slots)],
        [keys[r].reshape(span, width) for r in range(slots)],
        [values[r].reshape(span, width) for r in range(slots)],
        [lengths[r] + 1 for r in range(slots)],
    )
    for r in range(slots):
        mixed[r] = results[r]
    project(mixed, held, out, copies)


def second_kernel(n, pages, *refs):
    arrived = refs[:n]
    query, key_two, value_two, weight, out, key_cache, value_cache = refs[n : n + 7]
    keys, values, tails, new_k, new_v, mixed, held, sems, osems, wsems = refs[n + 7 :]
    size = keys.shape[2]
    span = pages * size
    width = keys.shape[3]
    copies = weight_copies(weight, held, wsems)
    for s in range(n):
        pltpu.make_async_copy(arrived[s].at[pl.ds(2 * span, TAIL)], tails.at[s], sems.at[2, s]).start()
        for p in range(pages):
            pltpu.make_async_copy(
                arrived[s].at[pl.ds(p * size, size)], keys.at[s, p], sems.at[0, s]
            ).start()
            pltpu.make_async_copy(
                arrived[s].at[pl.ds(span + p * size, size)], values.at[s, p], sems.at[1, s]
            ).start()
    for copy in copies:
        copy.start()
    new_k[...] = key_two[...].astype(jnp.float32)
    new_v[...] = value_two[...].astype(jnp.float32)
    slots = []
    lengths = []
    outgoing = []
    for s in range(n):
        pltpu.make_async_copy(tails.at[s], tails.at[s], sems.at[2, s]).wait()
        tail = tails[s].astype(jnp.float32)
        slots.append(jnp.max(tail[2:3, :]).astype(jnp.int32))
        lengths.append(jnp.max(tail[3:4, :]).astype(jnp.int32))
    for s in range(n):
        tail = tails[s].astype(jnp.float32)
        pltpu.make_async_copy(keys.at[s], keys.at[s], sems.at[0, s]).wait()
        pltpu.make_async_copy(values.at[s], values.at[s], sems.at[1, s]).wait()
        put_row(keys, s, tail[0:1, :], lengths[s])
        put_row(values, s, tail[1:2, :], lengths[s])
        put_row(keys, s, new_k[pl.ds(slots[s], 1), :], lengths[s] + 1)
        put_row(values, s, new_v[pl.ds(slots[s], 1), :], lengths[s] + 1)
        for ref, cache, at in ((keys, key_cache, 0), (values, value_cache, 1)):
            copy = pltpu.make_async_copy(
                ref.at[s], cache.at[pl.ds(slots[s] * pages, pages)], osems.at[at, s]
            )
            copy.start()
            outgoing.append(copy)
    results = attend(
        [query[slots[s]] for s in range(n)],
        [keys[s].reshape(span, width) for s in range(n)],
        [values[s].reshape(span, width) for s in range(n)],
        [lengths[s] + 2 for s in range(n)],
    )
    for s in range(n):
        mixed[slots[s]] = results[s]
    project(mixed, held, out, copies)
    for copy in outgoing:
        copy.wait()


def total(partial, size):
    if size == 2:
        other = lax.ppermute(partial, "tp", [(0, 1), (1, 0)])
        return (partial.astype(jnp.float32) + other.astype(jnp.float32)).astype(jnp.bfloat16)
    return lax.psum(partial, "tp")


def shards(
    n,
    tp,
    query_one,
    key_one,
    value_one,
    key_pages,
    value_pages,
    page_table,
    lengths,
    dest_instance,
    dest_slot,
    query_two,
    key_two,
    value_two,
    out_weight,
):
    slots, pages = page_table.shape
    pool, kv_heads, size, width = key_pages.shape
    heads = query_one.shape[1]
    depth, columns = out_weight.shape
    span = pages * size
    assert kv_heads == 1 and slots == n and n & (n - 1) == 0 and span <= 256
    key_pages = key_pages.reshape(pool, size, width)
    value_pages = value_pages.reshape(pool, size, width)
    key_one = key_one.reshape(slots, width)
    value_one = value_one.reshape(slots, width)
    key_two = key_two.reshape(slots, width)
    value_two = value_two.reshape(slots, width)

    smem = pl.BlockSpec(memory_space=pltpu.SMEM)
    vmem = pl.BlockSpec(memory_space=pltpu.VMEM)
    far = pl.BlockSpec(memory_space=pl.ANY)
    params = pltpu.CompilerParams(vmem_limit_bytes=VMEM_BYTES)
    bf16 = jnp.bfloat16
    parcel = jax.ShapeDtypeStruct((2 * span + TAIL, width), bf16)
    parcel_bytes = (2 * span + TAIL) * width * 2

    packed = pl.pallas_call(
        functools.partial(pack_kernel, n, pages),
        out_shape=[parcel] * n,
        in_specs=[smem] * 4 + [vmem] * 2 + [far] * 2,
        out_specs=[far] * n,
        scratch_shapes=[
            pltpu.SMEM((n,), jnp.int32),
            pltpu.VMEM((n, TAIL, width), bf16),
            pltpu.SemaphoreType.DMA((n,)),
        ],
        compiler_params=params,
        cost_estimate=pl.CostEstimate(flops=0, bytes_accessed=2 * n * parcel_bytes, transcendentals=0),
        name="pack",
    )(page_table, lengths, dest_instance, dest_slot, key_one, value_one, key_pages, value_pages)

    arrived = [packed[0]] + [None] * (n - 1)
    for s in reversed(range(1, n)):
        arrived[s] = lax.ppermute(packed[s], "inst", [(i, i ^ s) for i in range(n)])

    chunks = max(1, columns // CHUNK)
    attend_scratch = [
        pltpu.VMEM((slots, pages, size, width), bf16),
        pltpu.VMEM((slots, pages, size, width), bf16),
    ]
    flops = 4 * slots * heads * span * width + 2 * slots * depth * columns
    moved = 2 * depth * columns + 4 * slots * span * width
    partial_one = pl.pallas_call(
        functools.partial(first_kernel, slots, pages),
        out_shape=jax.ShapeDtypeStruct((slots, columns), bf16),
        in_specs=[smem] * 2 + [vmem] * 3 + [far] * 3,
        out_specs=vmem,
        scratch_shapes=attend_scratch
        + [
            pltpu.VMEM((slots, width), jnp.float32),
            pltpu.VMEM((slots, width), jnp.float32),
            pltpu.VMEM((slots, heads, width), jnp.float32),
            pltpu.VMEM((depth, columns), bf16),
            pltpu.SemaphoreType.DMA((2, slots)),
            pltpu.SemaphoreType.DMA((chunks,)),
        ],
        compiler_params=params,
        cost_estimate=pl.CostEstimate(flops=flops, bytes_accessed=moved, transcendentals=slots * heads * span),
        name="first",
    )(page_table, lengths, query_one, key_one, value_one, key_pages, value_pages, out_weight)
    out_one = total(partial_one, tp)

    cache = jax.ShapeDtypeStruct((slots * pages, size, width), bf16)
    partial_two, key_cache, value_cache = pl.pallas_call(
        functools.partial(second_kernel, n, pages),
        out_shape=[jax.ShapeDtypeStruct((slots, columns), bf16), cache, cache],
        in_specs=[far] * n + [vmem] * 3 + [far],
        out_specs=[vmem, far, far],
        scratch_shapes=attend_scratch
        + [
            pltpu.VMEM((n, TAIL, width), bf16),
            pltpu.VMEM((slots, width), jnp.float32),
            pltpu.VMEM((slots, width), jnp.float32),
            pltpu.VMEM((slots, heads, width), jnp.float32),
            pltpu.VMEM((depth, columns), bf16),
            pltpu.SemaphoreType.DMA((3, n)),
            pltpu.SemaphoreType.DMA((2, n)),
            pltpu.SemaphoreType.DMA((chunks,)),
        ],
        compiler_params=params,
        cost_estimate=pl.CostEstimate(
            flops=flops, bytes_accessed=moved + 4 * slots * span * width, transcendentals=slots * heads * span
        ),
        name="second",
    )(*arrived, query_two, key_two, value_two, out_weight)
    out_two = total(partial_two, tp)
    shape = (slots * pages, kv_heads, size, width)
    return (out_one, out_two, key_cache.reshape(shape), value_cache.reshape(shape))


def solution(mesh):
    sizes = dict(mesh.shape)
    return jax.shard_map(
        functools.partial(shards, sizes["inst"], sizes["tp"]),
        mesh=mesh,
        in_specs=(
            P("inst", "tp", None),
            P("inst", "tp", None),
            P("inst", "tp", None),
            P("inst", "tp", None, None),
            P("inst", "tp", None, None),
            P("inst", None),
            P("inst"),
            P("inst"),
            P("inst"),
            P("inst", "tp", None),
            P("inst", "tp", None),
            P("inst", "tp", None),
            P("tp", None),
        ),
        out_specs=(
            P("inst", None),
            P("inst", None),
            P("inst", "tp", None, None),
            P("inst", "tp", None, None),
        ),
        check_vma=False,
    )
```

time: 130 us -> 91.7 us (0.71)
  waiting for transfers between devices: 52.3 us -> 9.75 us
  Pallas kernels: 0 us -> 23.3 us
  starting transfers between devices: 19.6 us -> 41.4 us
  matrix products: 15 us -> 0 us
  between operations: 14.3 us -> 0.78 us
  local copies, waits for them, and re-layouts: 23.6 us -> 14.5 us
  other arithmetic: 4.52 us -> 1.38 us
    ppermute x0 -> x17, starting transfers between devices: none -> 41.4 us  [the longest x15 40.8 us: shards(): arrived[s] = lax.ppermute(packed[s], 'inst', [(i, i ^ s) for i in range(n)])]
    all_to_all x3 -> x0, waiting for transfers between devices: 33.4 us -> none  [the longest x1 18.6 us: shards(): lax.all_to_all(written_k[source_row], 'inst', split_axis=0, concat_axis=0...]
    pallas_call x0 -> x3, Pallas kernels: none -> 23.3 us  [the longest x1 10.4 us: shards(): pl.pallas_call(functools.partial(second_kernel, n, pages), out_shape=[jax...]
    all_to_all x3 -> x0, starting transfers between devices: 19.5 us -> none  [the longest x1 8.31 us: shards(): lax.all_to_all(header, 'inst', split_axis=0, concat_axis=0, tiled=True)]
    psum x1 -> x0, waiting for transfers between devices: 18.9 us -> none  [shards(): summed_one = lax.psum(partial_one.astype(jnp.bfloat16), 'tp')]
    dot_general x6 -> x0, matrix products: 15 us -> none  [the longest x1 5.26 us: shards(): jnp.dot(second, out_weight, preferred_element_type=jnp.float32)]
    gather x9 -> x0, local copies, waits for them, and re-layouts: 13.3 us -> none  [the longest x1 1.98 us: shards(): request_v = value_pages[page_table]]
    unnamed x20 -> x35, local copies, waits for them, and re-layouts: 3.19 us -> 14.5 us
  transfers between devices with their start and end apart: 4 -> 17, of which waited for: 4 -> 2; matrix products, arithmetic and copies ran while one was open for 16% -> 1% of each run, Pallas kernels for 0% -> 20%
where the time goes in v1:
time: 91.7 us; the launch traced here: 91.2 us
  starting transfers between devices  41.4 us (45%)
  Pallas kernels  23.3 us (25%)
  local copies, waits for them, and re-layouts  14.5 us (16%)
  waiting for transfers between devices  9.75 us (11%)
  other arithmetic  1.38 us (2%)
    ppermute x15, starting transfers between devices, shards(): arrived[s] = lax.ppermute(packed[s], 'inst', [(i, i ^ s) for i in range(n)])  40.8 us
    unnamed x35, local copies, waits for them, and re-layouts  14.5 us
    pallas_call x1, Pallas kernels, shards(): pl.pallas_call(functools.partial(second_kernel, n, pages), out_shape=[jax...  10.4 us
    ppermute x15, waiting for transfers between devices, shards(): arrived[s] = lax.ppermute(packed[s], 'inst', [(i, i ^ s) for i in range(n)])  9.45 us
    pallas_call x1, Pallas kernels, shards(): pl.pallas_call(functools.partial(first_kernel, slots, pages), out_shape=j...  8.18 us
    pallas_call x1, Pallas kernels, shards(): pl.pallas_call(functools.partial(pack_kernel, n, pages), out_shape=[parce...  4.67 us
  transfers between devices with their start and end apart: 17, of which 2 were waited for; matrix products, arithmetic and copies ran while one was open for 1% of the time, Pallas kernels for 20%

profile of v1, /device:TPU:0, one launch (start us, length us, event | category | flops | bytes accessed | tf_op | source)
XLA Modules:
  0.0 91.2 jit_solution(10032788219222278532)
XLA Ops:
  0.7 0.8 copy.17.refs_0_
  1.4 1.2 %copy-done.2 = bf16[64,1,64,128]{3,2,1,0:T(8,128)(2,1)S(1)} copy-done((bf16[64,1,64,128]{3,2,1,0:T(8,128)(2,1)S(1)}, bf16[64,1,64,128]{3,2,1,0:T(8,128)(2,1)}, u32[]{:S(2)}) %copy-start.2) | copy-done | bytes 1048600
  2.6 1.2 %copy-done.4 = bf16[64,1,64,128]{3,2,1,0:T(8,128)(2,1)S(1)} copy-done((bf16[64,1,64,128]{3,2,1,0:T(8,128)(2,1)S(1)}, bf16[64,1,64,128]{3,2,1,0:T(8,128)(2,1)}, u32[]{:S(2)}) %copy-start.4) | copy-done | bytes 1048600
  3.9 0.7 copy-done.8
  4.6 0.7 copy-done.10
  5.2 0.7 copy-done.14
  5.9 0.7 copy-done.15
  6.6 0.7 copy-done.16
  7.2 4.7 %pack.1 = (bf16[528,128]{1,0:T(8,128)(2,1)S(1)}, bf16[528,128]{1,0:T(8,128)(2,1)S(1)}, bf16[528,128]{1,0:T(8,128)(2,1)S(1)}, bf16[528,128]{1,0:T(8,128)(2,1)S(1)...) custom-call(s32[16,4]{1,0:T(8,128)S(1)} %copy.17.refs_0_, ...), custom_call_target="tpu_custom_call" | custom-call | bytes 4325376 | tf_op jit(solution)/shard_map/pack/pallas_call | solution.py:242
  11.9 3.0 %collective-permute-start.1 = (bf16[528,128]{1,0:T(8,128)(2,1)S(1)}, bf16[528,128]{1,0:T(8,128)(2,1)S(1)}, u32[]{:S(2)}, u32[]{:S(2)}) collective-permute-start(bf16[528,128]{1,0:T(8,128)(2,1)S(1)} %get-tuple-element.24), channel_id=1, source_target_pairs={{0,2},{2,0},{4,6},{6,4},{8,10},{10,8},{12,14},{14,12},{16,18},{18,... | collective-permute-start | bytes 405512 | tf_op jit(solution)/shard_map/ppermute | solution.py:259
  14.9 3.5 %collective-permute-start.10 = (bf16[528,128]{1,0:T(8,128)(2,1)S(1)}, bf16[528,128]{1,0:T(8,128)(2,1)S(1)}, u32[]{:S(2)}, u32[]{:S(2)}) collective-permute-start(bf16[528,128]{1,0:T(8,128)(2,1)S(1)} %get-tuple-element.33), channel_id=1, source_target_pairs={{0,20},{2,22},{4,16},{6,18},{8,28},{10,30},{12,24},{14,26},{16,4},... | collective-permute-start | bytes 405512 | tf_op jit(solution)/shard_map/ppermute | solution.py:259
  18.4 0.0 collective-permute-start.11
  18.5 3.8 %collective-permute-start.12 = (bf16[528,128]{1,0:T(8,128)(2,1)S(1)}, bf16[528,128]{1,0:T(8,128)(2,1)S(1)}, u32[]{:S(2)}, u32[]{:S(2)}) collective-permute-start(bf16[528,128]{1,0:T(8,128)(2,1)S(1)} %get-tuple-element.35), channel_id=1, source_target_pairs={{0,24},{2,26},{4,28},{6,30},{8,16},{10,18},{12,20},{14,22},{16,8},... | collective-permute-start | bytes 405512 | tf_op jit(solution)/shard_map/ppermute | solution.py:259
  22.3 1.1 %collective-permute-start.13 = (bf16[528,128]{1,0:T(8,128)(2,1)S(1)}, bf16[528,128]{1,0:T(8,128)(2,1)S(1)}, u32[]{:S(2)}, u32[]{:S(2)}) collective-permute-start(bf16[528,128]{1,0:T(8,128)(2,1)S(1)} %get-tuple-element.36), channel_id=1, source_target_pairs={{0,26},{2,24},{4,30},{6,28},{8,18},{10,16},{12,22},{14,20},{16,10}... | collective-permute-start | bytes 405512 | tf_op jit(solution)/shard_map/ppermute | solution.py:259
  23.5 0.0 collective-permute-done.1.refs_1_
  23.5 4.6 %collective-permute-start.14 = (bf16[528,128]{1,0:T(8,128)(2,1)S(1)}, bf16[528,128]{1,0:T(8,128)(2,1)S(1)}, u32[]{:S(2)}, u32[]{:S(2)}) collective-permute-start(bf16[528,128]{1,0:T(8,128)(2,1)S(1)} %get-tuple-element.37), channel_id=1, source_target_pairs={{0,28},{2,30},{4,24},{6,26},{8,20},{10,22},{12,16},{14,18},{16,12}... | collective-permute-start | bytes 405512 | tf_op jit(solution)/shard_map/ppermute | solution.py:259
  28.0 9.4 %collective-permute-done.10.refs_10_ = bf16[528,128]{1,0:T(8,128)(2,1)S(1)} collective-permute-done((bf16[528,128]{1,0:T(8,128)(2,1)S(1)}, bf16[528,128]{1,0:T(8,128)(2,1)S(1)}, u32[]{:S(2)}, u32[]{:S(2)}) %collective-permute-start.10) | collective-permute-done | bytes 135200 | tf_op jit(solution)/shard_map/ppermute | solution.py:259
  37.4 3.3 %collective-permute-start.15 = (bf16[528,128]{1,0:T(8,128)(2,1)S(1)}, bf16[528,128]{1,0:T(8,128)(2,1)S(1)}, u32[]{:S(2)}, u32[]{:S(2)}) collective-permute-start(bf16[528,128]{1,0:T(8,128)(2,1)S(1)} %get-tuple-element.38), channel_id=1, source_target_pairs={{0,30},{2,28},{4,26},{6,24},{8,22},{10,20},{12,18},{14,16},{16,14}... | collective-permute-start | bytes 405512 | tf_op jit(solution)/shard_map/ppermute | solution.py:259
  40.7 0.0 collective-permute-done.11.refs_11_
  40.7 1.0 %collective-permute-start.2 = (bf16[528,128]{1,0:T(8,128)(2,1)S(1)}, bf16[528,128]{1,0:T(8,128)(2,1)S(1)}, u32[]{:S(2)}, u32[]{:S(2)}) collective-permute-start(bf16[528,128]{1,0:T(8,128)(2,1)S(1)} %get-tuple-element.25), channel_id=1, source_target_pairs={{0,4},{2,6},{4,0},{6,2},{8,12},{10,14},{12,8},{14,10},{16,20},{18,... | collective-permute-start | bytes 405512 | tf_op jit(solution)/shard_map/ppermute | solution.py:259
  41.8 0.0 collective-permute-done.12.refs_12_
  41.8 1.9 %collective-permute-start.3 = (bf16[528,128]{1,0:T(8,128)(2,1)S(1)}, bf16[528,128]{1,0:T(8,128)(2,1)S(1)}, u32[]{:S(2)}, u32[]{:S(2)}) collective-permute-start(bf16[528,128]{1,0:T(8,128)(2,1)S(1)} %get-tuple-element.26), channel_id=1, source_target_pairs={{0,6},{2,4},{4,2},{6,0},{8,14},{10,12},{12,10},{14,8},{16,22},{18,... | collective-permute-start | bytes 405512 | tf_op jit(solution)/shard_map/ppermute | solution.py:259
  43.7 0.0 collective-permute-done.13.refs_13_
  43.7 5.8 %collective-permute-start.4 = (bf16[528,128]{1,0:T(8,128)(2,1)S(1)}, bf16[528,128]{1,0:T(8,128)(2,1)S(1)}, u32[]{:S(2)}, u32[]{:S(2)}) collective-permute-start(bf16[528,128]{1,0:T(8,128)(2,1)S(1)} %get-tuple-element.27), channel_id=1, source_target_pairs={{0,8},{2,10},{4,12},{6,14},{8,0},{10,2},{12,4},{14,6},{16,24},{18,... | collective-permute-start | bytes 405512 | tf_op jit(solution)/shard_map/ppermute | solution.py:259
  49.6 0.0 collective-permute-done.14.refs_14_
  49.6 3.6 %collective-permute-start.5 = (bf16[528,128]{1,0:T(8,128)(2,1)S(1)}, bf16[528,128]{1,0:T(8,128)(2,1)S(1)}, u32[]{:S(2)}, u32[]{:S(2)}) collective-permute-start(bf16[528,128]{1,0:T(8,128)(2,1)S(1)} %get-tuple-element.28), channel_id=1, source_target_pairs={{0,10},{2,8},{4,14},{6,12},{8,2},{10,0},{12,6},{14,4},{16,26},{18,... | collective-permute-start | bytes 405512 | tf_op jit(solution)/shard_map/ppermute | solution.py:259
  53.1 0.0 collective-permute-done.15.refs_15_
  53.1 2.7 %collective-permute-start.6 = (bf16[528,128]{1,0:T(8,128)(2,1)S(1)}, bf16[528,128]{1,0:T(8,128)(2,1)S(1)}, u32[]{:S(2)}, u32[]{:S(2)}) collective-permute-start(bf16[528,128]{1,0:T(8,128)(2,1)S(1)} %get-tuple-element.29), channel_id=1, source_target_pairs={{0,12},{2,14},{4,8},{6,10},{8,4},{10,6},{12,0},{14,2},{16,28},{18,... | collective-permute-start | bytes 405512 | tf_op jit(solution)/shard_map/ppermute | solution.py:259
  55.9 1.2 %collective-permute-start.7 = (bf16[528,128]{1,0:T(8,128)(2,1)S(1)}, bf16[528,128]{1,0:T(8,128)(2,1)S(1)}, u32[]{:S(2)}, u32[]{:S(2)}) collective-permute-start(bf16[528,128]{1,0:T(8,128)(2,1)S(1)} %get-tuple-element.30), channel_id=1, source_target_pairs={{0,14},{2,12},{4,10},{6,8},{8,6},{10,4},{12,2},{14,0},{16,30},{18,... | collective-permute-start | bytes 405512 | tf_op jit(solution)/shard_map/ppermute | solution.py:259
  57.1 4.6 %collective-permute-start.8 = (bf16[528,128]{1,0:T(8,128)(2,1)S(1)}, bf16[528,128]{1,0:T(8,128)(2,1)S(1)}, u32[]{:S(2)}, u32[]{:S(2)}) collective-permute-start(bf16[528,128]{1,0:T(8,128)(2,1)S(1)} %get-tuple-element.31), channel_id=1, source_target_pairs={{0,16},{2,18},{4,20},{6,22},{8,24},{10,26},{12,28},{14,30},{16,0},... | collective-permute-start | bytes 405512 | tf_op jit(solution)/shard_map/ppermute | solution.py:259
  61.6 0.5 collective-permute-start.9
  62.2 3.4 %copy-done = bf16[1024,4096]{1,0:T(8,128)(2,1)S(1)} copy-done((bf16[1024,4096]{1,0:T(8,128)(2,1)S(1)}, bf16[1024,4096]{1,0:T(8,128)(2,1)}, u32[]{:S(2)}) %copy-start) | copy-done | bytes 8388632
  65.5 1.2 %copy-done.3 = bf16[64,1,64,128]{3,2,1,0:T(8,128)(2,1)S(1)} copy-done((bf16[64,1,64,128]{3,2,1,0:T(8,128)(2,1)S(1)}, bf16[64,1,64,128]{3,2,1,0:T(8,128)(2,1)}, u32[]{:S(2)}) %copy-start.3) | copy-done | bytes 1048600
  66.8 1.2 %copy-done.5 = bf16[64,1,64,128]{3,2,1,0:T(8,128)(2,1)S(1)} copy-done((bf16[64,1,64,128]{3,2,1,0:T(8,128)(2,1)S(1)}, bf16[64,1,64,128]{3,2,1,0:T(8,128)(2,1)}, u32[]{:S(2)}) %copy-start.5) | copy-done | bytes 1048600
  68.0 0.8 copy-done.6
  68.8 0.7 copy-done.9
  69.4 0.7 copy-done.11
  70.1 8.2 %first.1 = bf16[16,4096]{1,0:T(8,128)(2,1)S(1)} custom-call(s32[16,4]{1,0:T(8,128)S(1)} %copy.17.refs_0_, s32[16]{0:T(128)S(1)} %copy-done.14, bf16[16,8,128]{2,1,0:T(8,128)(2,1)S(1)} %copy-done.6, bf16[16,128]{1,0:T(8,128)(2,1)S(1)} %bitcast.17, bf16[16,128]{1,0:T(8,128)(2,1)S(1)} %bitcast.19, bf16[64,64,128]{2,1,0:T(8,128)(2,1)S(1)} %bitcast.13, ...), custom_call_target="tpu_custom_call" | custom-call | flops 150994944 | bytes 10485760 | tf_op jit(solution)/shard_map/first/pallas_call | solution.py:268
  78.3 0.0 collective-permute-done.5.refs_5_
  78.3 0.1 collective-permute-start
  78.4 0.0 collective-permute-done.6.refs_6_
  78.4 0.0 collective-permute-done.7.refs_7_
  78.4 0.0 collective-permute-done.9.refs_9_
  78.5 10.4 %second.1 = (bf16[16,4096]{1,0:T(8,128)(2,1)S(1)}, bf16[64,64,128]{2,1,0:T(8,128)(2,1)}, bf16[64,64,128]{2,1,0:T(8,128)(2,1)}) custom-call(bf16[528,128]{1,0:T(8,128)(2,1)S(1)} %get-tuple-element.23.refs_0_, bf16[528,128]{1,0:T(8,128)(2,1)S(1)} %collective-permute-done.1.refs_1_, bf16[528,128]{1,0:T(8,128)(2,1)S(1)} %collective-permute-done.2.refs_2_, ...), custom_call_target="tpu_custom_call" | custom-call | flops 150994944 | bytes 12582912 | tf_op jit(solution)/shard_map/second/pallas_call | solution.py:289
  88.9 0.5 collective-permute-start.16
  89.5 0.7 add_convert_fusion.1
  90.2 0.3 collective-permute-done.16
  90.5 0.7 add_convert_fusion
  (26 shorter events, 0.0 us)
Async XLA Ops:
  0.6 77.8 %copy-start.12 = (bf16[16,1,128]{2,0,1:T(8,128)(2,1)S(1)}, bf16[16,1,128]{2,0,1:T(8,128)(2,1)}, u32[]{:S(2)}) copy-start(bf16[16,1,128]{2,0,1:T(8,128)(2,1)} %param.23) | copy-start | bytes 12292
  0.6 77.8 %copy-start.13 = (bf16[16,1,128]{2,0,1:T(8,128)(2,1)S(1)}, bf16[16,1,128]{2,0,1:T(8,128)(2,1)}, u32[]{:S(2)}) copy-start(bf16[16,1,128]{2,0,1:T(8,128)(2,1)} %param.24) | copy-start | bytes 12292
  1.4 1.2 %copy-start.2 = (bf16[64,1,64,128]{3,2,1,0:T(8,128)(2,1)S(1)}, bf16[64,1,64,128]{3,2,1,0:T(8,128)(2,1)}, u32[]{:S(2)}) copy-start(bf16[64,1,64,128]{3,2,1,0:T(8,128)(2,1)} %param.16) | copy-start | bytes 3145732
  2.6 1.2 %copy-start.4 = (bf16[64,1,64,128]{3,2,1,0:T(8,128)(2,1)S(1)}, bf16[64,1,64,128]{3,2,1,0:T(8,128)(2,1)}, u32[]{:S(2)}) copy-start(bf16[64,1,64,128]{3,2,1,0:T(8,128)(2,1)} %param.17) | copy-start | bytes 3145732
  3.9 0.7 copy-start.8
  4.6 0.7 copy-start.10
  5.2 0.7 copy-start.14
  5.9 0.7 copy-start.15
  6.6 0.7 copy-start.16
  7.2 71.3 %copy-start.7 = (bf16[16,8,128]{2,1,0:T(8,128)(2,1)S(1)}, bf16[16,8,128]{2,1,0:T(8,128)(2,1)}, u32[]{:S(2)}) copy-start(bf16[16,8,128]{2,1,0:T(8,128)(2,1)} %refs_16_.1) | copy-start | bytes 98308
  11.9 11.6 %collective-permute-start.1 = (bf16[528,128]{1,0:T(8,128)(2,1)S(1)}, bf16[528,128]{1,0:T(8,128)(2,1)S(1)}, u32[]{:S(2)}, u32[]{:S(2)}) collective-permute-start(bf16[528,128]{1,0:T(8,128)(2,1)S(1)} %get-tuple-element.24), channel_id=1, source_target_pairs={{0,2},{2,0},{4,6},{6,4},{8,10},{10,8},{12,14},{14,12},{16,18},{18,... | collective-permute-start | bytes 405512 | tf_op jit(solution)/shard_map/ppermute | solution.py:259
  14.9 22.5 %collective-permute-start.10 = (bf16[528,128]{1,0:T(8,128)(2,1)S(1)}, bf16[528,128]{1,0:T(8,128)(2,1)S(1)}, u32[]{:S(2)}, u32[]{:S(2)}) collective-permute-start(bf16[528,128]{1,0:T(8,128)(2,1)S(1)} %get-tuple-element.33), channel_id=1, source_target_pairs={{0,20},{2,22},{4,16},{6,18},{8,28},{10,30},{12,24},{14,26},{16,4},... | collective-permute-start | bytes 405512 | tf_op jit(solution)/shard_map/ppermute | solution.py:259
  18.4 22.3 %collective-permute-start.11 = (bf16[528,128]{1,0:T(8,128)(2,1)S(1)}, bf16[528,128]{1,0:T(8,128)(2,1)S(1)}, u32[]{:S(2)}, u32[]{:S(2)}) collective-permute-start(bf16[528,128]{1,0:T(8,128)(2,1)S(1)} %get-tuple-element.34), channel_id=1, source_target_pairs={{0,22},{2,20},{4,18},{6,16},{8,30},{10,28},{12,26},{14,24},{16,6},... | collective-permute-start | bytes 405512 | tf_op jit(solution)/shard_map/ppermute | solution.py:259
  18.5 23.3 %collective-permute-start.12 = (bf16[528,128]{1,0:T(8,128)(2,1)S(1)}, bf16[528,128]{1,0:T(8,128)(2,1)S(1)}, u32[]{:S(2)}, u32[]{:S(2)}) collective-permute-start(bf16[528,128]{1,0:T(8,128)(2,1)S(1)} %get-tuple-element.35), channel_id=1, source_target_pairs={{0,24},{2,26},{4,28},{6,30},{8,16},{10,18},{12,20},{14,22},{16,8},... | collective-permute-start | bytes 405512 | tf_op jit(solution)/shard_map/ppermute | solution.py:259
  22.3 21.4 %collective-permute-start.13 = (bf16[528,128]{1,0:T(8,128)(2,1)S(1)}, bf16[528,128]{1,0:T(8,128)(2,1)S(1)}, u32[]{:S(2)}, u32[]{:S(2)}) collective-permute-start(bf16[528,128]{1,0:T(8,128)(2,1)S(1)} %get-tuple-element.36), channel_id=1, source_target_pairs={{0,26},{2,24},{4,30},{6,28},{8,18},{10,16},{12,22},{14,20},{16,10}... | collective-permute-start | bytes 405512 | tf_op jit(solution)/shard_map/ppermute | solution.py:259
  23.5 26.1 %collective-permute-start.14 = (bf16[528,128]{1,0:T(8,128)(2,1)S(1)}, bf16[528,128]{1,0:T(8,128)(2,1)S(1)}, u32[]{:S(2)}, u32[]{:S(2)}) collective-permute-start(bf16[528,128]{1,0:T(8,128)(2,1)S(1)} %get-tuple-element.37), channel_id=1, source_target_pairs={{0,28},{2,30},{4,24},{6,26},{8,20},{10,22},{12,16},{14,18},{16,12}... | collective-permute-start | bytes 405512 | tf_op jit(solution)/shard_map/ppermute | solution.py:259
  37.4 15.7 %collective-permute-start.15 = (bf16[528,128]{1,0:T(8,128)(2,1)S(1)}, bf16[528,128]{1,0:T(8,128)(2,1)S(1)}, u32[]{:S(2)}, u32[]{:S(2)}) collective-permute-start(bf16[528,128]{1,0:T(8,128)(2,1)S(1)} %get-tuple-element.38), channel_id=1, source_target_pairs={{0,30},{2,28},{4,26},{6,24},{8,22},{10,20},{12,18},{14,16},{16,14}... | collective-permute-start | bytes 405512 | tf_op jit(solution)/shard_map/ppermute | solution.py:259
  40.7 15.1 %collective-permute-start.2 = (bf16[528,128]{1,0:T(8,128)(2,1)S(1)}, bf16[528,128]{1,0:T(8,128)(2,1)S(1)}, u32[]{:S(2)}, u32[]{:S(2)}) collective-permute-start(bf16[528,128]{1,0:T(8,128)(2,1)S(1)} %get-tuple-element.25), channel_id=1, source_target_pairs={{0,4},{2,6},{4,0},{6,2},{8,12},{10,14},{12,8},{14,10},{16,20},{18,... | collective-permute-start | bytes 405512 | tf_op jit(solution)/shard_map/ppermute | solution.py:259
  41.8 15.3 %collective-permute-start.3 = (bf16[528,128]{1,0:T(8,128)(2,1)S(1)}, bf16[528,128]{1,0:T(8,128)(2,1)S(1)}, u32[]{:S(2)}, u32[]{:S(2)}) collective-permute-start(bf16[528,128]{1,0:T(8,128)(2,1)S(1)} %get-tuple-element.26), channel_id=1, source_target_pairs={{0,6},{2,4},{4,2},{6,0},{8,14},{10,12},{12,10},{14,8},{16,22},{18,... | collective-permute-start | bytes 405512 | tf_op jit(solution)/shard_map/ppermute | solution.py:259
  43.7 17.9 %collective-permute-start.4 = (bf16[528,128]{1,0:T(8,128)(2,1)S(1)}, bf16[528,128]{1,0:T(8,128)(2,1)S(1)}, u32[]{:S(2)}, u32[]{:S(2)}) collective-permute-start(bf16[528,128]{1,0:T(8,128)(2,1)S(1)} %get-tuple-element.27), channel_id=1, source_target_pairs={{0,8},{2,10},{4,12},{6,14},{8,0},{10,2},{12,4},{14,6},{16,24},{18,... | collective-permute-start | bytes 405512 | tf_op jit(solution)/shard_map/ppermute | solution.py:259
  49.6 28.7 %collective-permute-start.5 = (bf16[528,128]{1,0:T(8,128)(2,1)S(1)}, bf16[528,128]{1,0:T(8,128)(2,1)S(1)}, u32[]{:S(2)}, u32[]{:S(2)}) collective-permute-start(bf16[528,128]{1,0:T(8,128)(2,1)S(1)} %get-tuple-element.28), channel_id=1, source_target_pairs={{0,10},{2,8},{4,14},{6,12},{8,2},{10,0},{12,6},{14,4},{16,26},{18,... | collective-permute-start | bytes 405512 | tf_op jit(solution)/shard_map/ppermute | solution.py:259
  53.1 25.3 %collective-permute-start.6 = (bf16[528,128]{1,0:T(8,128)(2,1)S(1)}, bf16[528,128]{1,0:T(8,128)(2,1)S(1)}, u32[]{:S(2)}, u32[]{:S(2)}) collective-permute-start(bf16[528,128]{1,0:T(8,128)(2,1)S(1)} %get-tuple-element.29), channel_id=1, source_target_pairs={{0,12},{2,14},{4,8},{6,10},{8,4},{10,6},{12,0},{14,2},{16,28},{18,... | collective-permute-start | bytes 405512 | tf_op jit(solution)/shard_map/ppermute | solution.py:259
  55.9 22.6 %collective-permute-start.7 = (bf16[528,128]{1,0:T(8,128)(2,1)S(1)}, bf16[528,128]{1,0:T(8,128)(2,1)S(1)}, u32[]{:S(2)}, u32[]{:S(2)}) collective-permute-start(bf16[528,128]{1,0:T(8,128)(2,1)S(1)} %get-tuple-element.30), channel_id=1, source_target_pairs={{0,14},{2,12},{4,10},{6,8},{8,6},{10,4},{12,2},{14,0},{16,30},{18,... | collective-permute-start | bytes 405512 | tf_op jit(solution)/shard_map/ppermute | solution.py:259
  57.1 21.3 %collective-permute-start.8 = (bf16[528,128]{1,0:T(8,128)(2,1)S(1)}, bf16[528,128]{1,0:T(8,128)(2,1)S(1)}, u32[]{:S(2)}, u32[]{:S(2)}) collective-permute-start(bf16[528,128]{1,0:T(8,128)(2,1)S(1)} %get-tuple-element.31), channel_id=1, source_target_pairs={{0,16},{2,18},{4,20},{6,22},{8,24},{10,26},{12,28},{14,30},{16,0},... | collective-permute-start | bytes 405512 | tf_op jit(solution)/shard_map/ppermute | solution.py:259
  61.6 16.8 %collective-permute-start.9 = (bf16[528,128]{1,0:T(8,128)(2,1)S(1)}, bf16[528,128]{1,0:T(8,128)(2,1)S(1)}, u32[]{:S(2)}, u32[]{:S(2)}) collective-permute-start(bf16[528,128]{1,0:T(8,128)(2,1)S(1)} %get-tuple-element.32), channel_id=1, source_target_pairs={{0,18},{2,16},{4,22},{6,20},{8,26},{10,24},{12,30},{14,28},{16,2},... | collective-permute-start | bytes 405512 | tf_op jit(solution)/shard_map/ppermute | solution.py:259
  62.2 3.4 %copy-start = (bf16[1024,4096]{1,0:T(8,128)(2,1)S(1)}, bf16[1024,4096]{1,0:T(8,128)(2,1)}, u32[]{:S(2)}) copy-start(bf16[1024,4096]{1,0:T(8,128)(2,1)} %refs_19_.1) | copy-start | bytes 25165828
  65.5 1.2 %copy-start.3 = (bf16[64,1,64,128]{3,2,1,0:T(8,128)(2,1)S(1)}, bf16[64,1,64,128]{3,2,1,0:T(8,128)(2,1)}, u32[]{:S(2)}) copy-start(bf16[64,1,64,128]{3,2,1,0:T(8,128)(2,1)} %param.16) | copy-start | bytes 3145732
  66.8 1.2 %copy-start.5 = (bf16[64,1,64,128]{3,2,1,0:T(8,128)(2,1)S(1)}, bf16[64,1,64,128]{3,2,1,0:T(8,128)(2,1)}, u32[]{:S(2)}) copy-start(bf16[64,1,64,128]{3,2,1,0:T(8,128)(2,1)} %param.17) | copy-start | bytes 3145732
  68.0 0.8 copy-start.6
  68.8 0.7 copy-start.9
  69.4 0.7 copy-start.11
  70.1 8.4 %copy-start.1 = (bf16[1024,4096]{1,0:T(8,128)(2,1)S(1)}, bf16[1024,4096]{1,0:T(8,128)(2,1)}, u32[]{:S(2)}) copy-start(bf16[1024,4096]{1,0:T(8,128)(2,1)} %refs_19_.1) | copy-start | bytes 25165828
  78.3 11.2 %collective-permute-start = (bf16[16,4096]{1,0:T(8,128)(2,1)S(1)}, bf16[16,4096]{1,0:T(8,128)(2,1)S(1)}, u32[]{:S(2)}, u32[]{:S(2)}) collective-permute-start(bf16[16,4096]{1,0:T(8,128)(2,1)S(1)} %first.1), channel_id=1, source_target_pairs={{0,1},{1,0},{2,3},{3,2},{4,5},{5,4},{6,7},{7,6},{8,9},{9,8},{10,11... | collective-permute-start | bytes 393224 | tf_op jit(solution)/shard_map/ppermute | solution.py:199
  88.9 1.5 %collective-permute-start.16 = (bf16[16,4096]{1,0:T(8,128)(2,1)S(1)}, bf16[16,4096]{1,0:T(8,128)(2,1)S(1)}, u32[]{:S(2)}, u32[]{:S(2)}) collective-permute-start(bf16[16,4096]{1,0:T(8,128)(2,1)S(1)} %get-tuple-element.39), channel_id=1, source_target_pairs={{0,1},{1,0},{2,3},{3,2},{4,5},{5,4},{6,7},{7,6},{8,9},{9,8},{10,11... | collective-permute-start | bytes 393224 | tf_op jit(solution)/shard_map/ppermute | solution.py:199

commit v2 on v1

v2 whole, which is shorter than its diff:
```python
import functools

import jax
import jax.numpy as jnp
from jax import lax
from jax.experimental import pallas as pl
from jax.experimental.pallas import tpu as pltpu
from jax.sharding import PartitionSpec as P

NEG = -1e30
TAIL = 16
GROUPS = 4
CHUNKS = 8
VMEM_BYTES = 24 * 1024 * 1024


def row_of(block, at):
    rows = lax.broadcasted_iota(jnp.int32, block.shape, 0)
    return jnp.sum(jnp.where(rows == at, block, 0.0), axis=0, keepdims=True)


def put_row(parcels, index, offset, row, position):
    base = pl.multiple_of(offset + position // TAIL * TAIL, TAIL)
    block = parcels[index, pl.ds(base, TAIL), :]
    at = lax.broadcasted_iota(jnp.int32, block.shape, 0)
    mixed = jnp.where(at == position % TAIL, row, block.astype(jnp.float32))
    parcels[index, pl.ds(base, TAIL), :] = mixed.astype(jnp.bfloat16)


def invert(dest, source, n):
    def note(r, carry):
        source[dest[r]] = r
        return carry

    lax.fori_loop(0, n, note, 0)


def begin(pairs, sem):
    copies = [pltpu.make_async_copy(a, b, sem.at[i]) for i, (a, b) in enumerate(pairs)]
    for copy in copies:
        copy.start()
    return copies


def finish(copies):
    for copy in copies:
        copy.wait()


def pack_kernel(n, pages, *refs):
    far, out = refs[:8], refs[8]
    table, lengths, dest, slot, key_one, value_one, key_pool, value_pool = refs[9:17]
    source, parcels, sems, osems = refs[17:]
    copies = begin(list(zip(far, (table, lengths, dest, slot, key_one, value_one, key_pool, value_pool))), sems)
    size = key_pool.shape[1]
    span = pages * size
    finish(copies[:6])
    invert(dest, source, n)
    keys = key_one[...].astype(jnp.float32)
    values = value_one[...].astype(jnp.float32)
    at = lax.broadcasted_iota(jnp.int32, (TAIL, keys.shape[1]), 0)
    copies[6].wait()
    for d in range(n):
        r = source[d]
        for p in range(pages):
            parcels[d, p * size : (p + 1) * size, :] = key_pool[table[p, r]]
    for d in range(n):
        r = source[d]
        put_row(parcels, d, 0, row_of(keys, r), lengths[r])
        tail = jnp.where(at == 0, slot[r].astype(jnp.float32), lengths[r].astype(jnp.float32))
        parcels[d, 2 * span : 2 * span + TAIL, :] = tail.astype(jnp.bfloat16)
    copies[7].wait()
    outgoing = []
    for d in range(n):
        r = source[d]
        for p in range(pages):
            parcels[d, span + p * size : span + (p + 1) * size, :] = value_pool[table[p, r]]
        put_row(parcels, d, span, row_of(values, r), lengths[r])
        copy = pltpu.make_async_copy(parcels.at[d], out.at[d], osems.at[d])
        copy.start()
        outgoing.append(copy)
    finish(outgoing)


def attend(queries, keys, values, counts):
    width = queries[0].shape[1]
    scores = []
    for q, k, count in zip(queries, keys, counts):
        s = lax.dot_general(q, k, (((1,), (1,)), ((), ())), preferred_element_type=jnp.float32)
        live = lax.broadcasted_iota(jnp.int32, s.shape, 1) < count
        scores.append(jnp.where(live, s * width ** (-0.5), NEG))
    group = scores[0].shape[0]
    score = jnp.concatenate(scores, axis=0)
    top = jnp.max(score, axis=-1, keepdims=True)
    expo = jnp.exp(score - top)
    weights = (expo / jnp.sum(expo, axis=-1, keepdims=True)).astype(jnp.bfloat16)
    return [
        jnp.dot(weights[i * group : (i + 1) * group], v, preferred_element_type=jnp.float32)
        for i, v in enumerate(values)
    ]


def project(mixed, weight, out):
    heads = mixed.shape[1]
    rows = jnp.concatenate([mixed[:, h, :] for h in range(heads)], axis=1).astype(jnp.bfloat16)
    width = weight.shape[1] // CHUNKS
    for c in range(CHUNKS):
        part = jnp.dot(
            rows, weight[:, c * width : (c + 1) * width], preferred_element_type=jnp.float32
        )
        out[:, c * width : (c + 1) * width] = part.astype(jnp.bfloat16)


def load_groups(source, parcels, sems):
    step = source.shape[0] // GROUPS
    return begin(
        [(source.at[pl.ds(g * step, step)], parcels.at[pl.ds(g * step, step)]) for g in range(GROUPS)],
        sems,
    )


def first_kernel(n, span, *refs):
    far, weight, out = refs[:4], refs[4], refs[5]
    lengths, dest, query, parcels, source, mixed, sems, psems = refs[6:]
    copies = begin(list(zip(far[:3], (lengths, dest, query))), sems)
    loads = load_groups(far[3], parcels, psems)
    finish(copies)
    invert(dest, source, n)
    finish(loads)
    at = [source[d] for d in range(n)]
    results = attend(
        [query[r] for r in at],
        [parcels[d, :span, :] for d in range(n)],
        [parcels[d, span : 2 * span, :] for d in range(n)],
        [lengths[r] + 1 for r in at],
    )
    for r, result in zip(at, results):
        mixed[r] = result
    project(mixed, weight, out)


def second_kernel(n, pages, *refs):
    far, weight, out, key_cache, value_cache = refs[:4], refs[4], refs[5], refs[6], refs[7]
    query, key_two, value_two, parcels, new_k, new_v, mixed, sems, psems, osems = refs[8:]
    span = (parcels.shape[1] - TAIL) // 2
    loads = load_groups(far[0], parcels, psems)
    copies = begin(list(zip(far[1:], (query, key_two, value_two))), sems)
    finish(copies)
    new_k[...] = key_two[...].astype(jnp.float32)
    new_v[...] = value_two[...].astype(jnp.float32)
    finish(loads)
    slots = []
    lengths = []
    for s in range(n):
        tail = parcels[s, 2 * span : 2 * span + TAIL, :].astype(jnp.float32)
        slots.append(jnp.max(tail[0:1, :]).astype(jnp.int32))
        lengths.append(jnp.max(tail[1:2, :]).astype(jnp.int32))
    outgoing = []
    for s in range(n):
        put_row(parcels, s, 0, new_k[pl.ds(slots[s], 1), :], lengths[s] + 1)
        put_row(parcels, s, span, new_v[pl.ds(slots[s], 1), :], lengths[s] + 1)
        for cache, at in ((key_cache, 0), (value_cache, 1)):
            copy = pltpu.make_async_copy(
                parcels.at[s, pl.ds(at * span, span)], cache.at[slots[s]], osems.at[at, s]
            )
            copy.start()
            outgoing.append(copy)
    results = attend(
        [query[slots[s]] for s in range(n)],
        [parcels[s, :span, :] for s in range(n)],
        [parcels[s, span : 2 * span, :] for s in range(n)],
        [lengths[s] + 2 for s in range(n)],
    )
    for s in range(n):
        mixed[slots[s]] = results[s]
    project(mixed, weight, out)
    finish(outgoing)


def total(partial, size):
    if size == 2:
        other = lax.ppermute(partial, "tp", [(0, 1), (1, 0)])
        return (partial.astype(jnp.float32) + other.astype(jnp.float32)).astype(jnp.bfloat16)
    return lax.psum(partial, "tp")


def hbm(x):
    return pltpu.with_memory_space_constraint(x, pltpu.HBM)


def shards(
    n,
    tp,
    query_one,
    key_one,
    value_one,
    key_pages,
    value_pages,
    page_table,
    lengths,
    dest_instance,
    dest_slot,
    query_two,
    key_two,
    value_two,
    out_weight,
):
    slots, pages = page_table.shape
    pool, kv_heads, size, width = key_pages.shape
    heads = query_one.shape[1]
    depth, columns = out_weight.shape
    span = pages * size
    assert kv_heads == 1 and slots == n and span <= 256
    key_pages = key_pages.reshape(pool, size, width)
    value_pages = value_pages.reshape(pool, size, width)
    key_one = key_one.reshape(slots, width)
    value_one = value_one.reshape(slots, width)
    key_two = key_two.reshape(slots, width)
    value_two = value_two.reshape(slots, width)

    vmem = pl.BlockSpec(memory_space=pltpu.VMEM)
    far = pl.BlockSpec(memory_space=pltpu.HBM)
    params = pltpu.CompilerParams(vmem_limit_bytes=VMEM_BYTES)
    bf16, f32, i32 = jnp.bfloat16, jnp.float32, jnp.int32
    rows = 2 * span + TAIL
    parcels = pltpu.VMEM((n, rows, width), bf16)

    packed = pl.pallas_call(
        functools.partial(pack_kernel, n, pages),
        out_shape=jax.ShapeDtypeStruct((n, rows, width), bf16),
        in_specs=[far] * 8,
        out_specs=far,
        scratch_shapes=[
            pltpu.SMEM((pages, slots), i32),
            pltpu.SMEM((slots,), i32),
            pltpu.SMEM((slots,), i32),
            pltpu.SMEM((slots,), i32),
            pltpu.VMEM((slots, width), bf16),
            pltpu.VMEM((slots, width), bf16),
            pltpu.VMEM((pool, size, width), bf16),
            pltpu.VMEM((pool, size, width), bf16),
            pltpu.SMEM((n,), i32),
            parcels,
            pltpu.SemaphoreType.DMA((8,)),
            pltpu.SemaphoreType.DMA((n,)),
        ],
        compiler_params=params,
        cost_estimate=pl.CostEstimate(flops=0, bytes_accessed=4 * n * rows * width, transcendentals=0),
        name="pack",
    )(
        hbm(page_table.T),
        hbm(lengths),
        hbm(dest_instance),
        hbm(dest_slot),
        hbm(key_one),
        hbm(value_one),
        hbm(key_pages),
        hbm(value_pages),
    )

    arrived = lax.all_to_all(packed, "inst", split_axis=0, concat_axis=0, tiled=True)

    weight = pltpu.with_memory_space_constraint(out_weight, pltpu.VMEM)
    flops = 4 * slots * heads * span * width + 2 * slots * depth * columns
    moved = 2 * depth * columns + 4 * slots * span * width
    partial_one = pl.pallas_call(
        functools.partial(first_kernel, n, span),
        out_shape=jax.ShapeDtypeStruct((slots, columns), bf16),
        in_specs=[far] * 4 + [vmem],
        out_specs=vmem,
        scratch_shapes=[
            pltpu.SMEM((slots,), i32),
            pltpu.SMEM((slots,), i32),
            pltpu.VMEM((slots, heads, width), bf16),
            parcels,
            pltpu.SMEM((n,), i32),
            pltpu.VMEM((slots, heads, width), f32),
            pltpu.SemaphoreType.DMA((3,)),
            pltpu.SemaphoreType.DMA((GROUPS,)),
        ],
        compiler_params=params,
        cost_estimate=pl.CostEstimate(flops=flops, bytes_accessed=moved, transcendentals=slots * heads * span),
        name="first",
    )(hbm(lengths), hbm(dest_instance), hbm(query_one), hbm(packed), weight)
    out_one = total(partial_one, tp)

    cache = jax.ShapeDtypeStruct((slots, span, width), bf16)
    partial_two, key_cache, value_cache = pl.pallas_call(
        functools.partial(second_kernel, n, pages),
        out_shape=[jax.ShapeDtypeStruct((slots, columns), bf16), cache, cache],
        in_specs=[far] * 4 + [vmem],
        out_specs=[vmem, far, far],
        scratch_shapes=[
            pltpu.VMEM((slots, heads, width), bf16),
            pltpu.VMEM((slots, width), bf16),
            pltpu.VMEM((slots, width), bf16),
            parcels,
            pltpu.VMEM((slots, width), f32),
            pltpu.VMEM((slots, width), f32),
            pltpu.VMEM((slots, heads, width), f32),
            pltpu.SemaphoreType.DMA((3,)),
            pltpu.SemaphoreType.DMA((GROUPS,)),
            pltpu.SemaphoreType.DMA((2, n)),
        ],
        compiler_params=params,
        cost_estimate=pl.CostEstimate(
            flops=flops, bytes_accessed=moved + 4 * slots * span * width, transcendentals=slots * heads * span
        ),
        name="second",
    )(hbm(arrived), hbm(query_two), hbm(key_two), hbm(value_two), weight)
    out_two = total(partial_two, tp)
    shape = (slots * pages, kv_heads, size, width)
    return (out_one, out_two, key_cache.reshape(shape), value_cache.reshape(shape))


def solution(mesh):
    sizes = dict(mesh.shape)
    return jax.shard_map(
        functools.partial(shards, sizes["inst"], sizes["tp"]),
        mesh=mesh,
        in_specs=(
            P("inst", "tp", None),
            P("inst", "tp", None),
            P("inst", "tp", None),
            P("inst", "tp", None, None),
            P("inst", "tp", None, None),
            P("inst", None),
            P("inst"),
            P("inst"),
            P("inst"),
            P("inst", "tp", None),
            P("inst", "tp", None),
            P("inst", "tp", None),
            P("tp", None),
        ),
        out_specs=(
            P("inst", None),
            P("inst", None),
            P("inst", "tp", None, None),
            P("inst", "tp", None, None),
        ),
        check_vma=False,
    )
```

time: 91.7 us -> 72.2 us (0.79)
  the two profiles are of different devices: /device:TPU:0 before, /device:TPU:13 now
where the time goes in v2:
time: 72.2 us; the launch traced here: 71.8 us
  waiting for transfers between devices  41.4 us (57%)
  Pallas kernels  10.8 us (15%)
  starting transfers between devices  9.44 us (13%)
  local copies, waits for them, and re-layouts  8.11 us (11%)
  other arithmetic  1.38 us (2%)
    all_to_all x1, waiting for transfers between devices, shards(): lax.all_to_all(packed, 'inst', split_axis=0, concat_axis=0, tiled=True)  41.1 us
    unnamed x6, local copies, waits for them, and re-layouts  8.11 us
    all_to_all x1, starting transfers between devices, shards(): lax.all_to_all(packed, 'inst', split_axis=0, concat_axis=0, tiled=True)  6.62 us
    pallas_call x1, Pallas kernels, shards(): pl.pallas_call(functools.partial(second_kernel, n, pages), out_shape=[jax...  4.19 us
    pallas_call x1, Pallas kernels, shards(): pl.pallas_call(functools.partial(first_kernel, n, span), out_shape=jax.Sh...  3.48 us
    pallas_call x1, Pallas kernels, shards(): pl.pallas_call(functools.partial(pack_kernel, n, pages), out_shape=jax.Sh...  3.16 us
    ppermute x2, starting transfers between devices, total(): other = lax.ppermute(partial, 'tp', [(0, 1), (1, 0)])  2.82 us
  transfers between devices with their start and end apart: 3, of which 2 were waited for; matrix products, arithmetic and copies ran while one was open for 1% of the time, Pallas kernels for 11%

profile of v2, /device:TPU:13, one launch (start us, length us, event | category | flops | bytes accessed | tf_op | source)
XLA Modules:
  0.0 71.8 jit_solution(13988644690687744409)
XLA Ops:
  0.6 3.2 %pack.1.refs_3_ = bf16[16,528,128]{2,1,0:T(8,128)(2,1)} custom-call(s32[4,16]{1,0:T(4,128)} %bitcast.19, s32[16]{0:T(128)} %refs_0_.1, s32[16]{0:T(128)} %refs_1_.4, s32[16]{0:T(128)} %refs_3_.1, bf16[16,128]{1,0:T(8,128)(2,1)} %bitcast.15, bf16[16,128]{1,0:T(8,128)(2,1)} %bitcast.16, bf16[64,64,128]{2,1,0:T(8,128)(2,1)} %bitcast.13, ...), custom_call_target="tpu_custom_call" | custom-call | bytes 4325376 | tf_op jit(solution)/shard_map/pack/pallas_call | solution.py:228
  3.8 6.6 %all-to-all-start = ((bf16[16,528,128]{2,1,0:T(8,128)(2,1)}), bf16[16,528,128]{2,1,0:T(8,128)(2,1)S(1)}, u32[]{:S(2)}, u32[]{:S(2)}) async-start(bf16[16,528,128]{2,1,0:T(8,128)(2,1)} %pack.1.refs_3_), calls=%async_computation | async-start | bytes 4325376 | tf_op jit(solution)/shard_map/all_to_all | solution.py:261
  10.4 0.0 copy-start
  10.4 3.4 %copy-done = bf16[1024,4096]{1,0:T(8,128)(2,1)S(1)} copy-done((bf16[1024,4096]{1,0:T(8,128)(2,1)S(1)}, bf16[1024,4096]{1,0:T(8,128)(2,1)}, u32[]{:S(2)}) %copy-start) | copy-done | bytes 8388632
  13.8 3.5 %first.1 = bf16[16,4096]{1,0:T(8,128)(2,1)S(1)} custom-call(s32[16]{0:T(128)} %refs_0_.1, s32[16]{0:T(128)} %refs_1_.4, bf16[16,8,128]{2,1,0:T(8,128)(2,1)} %refs_2_.3, bf16[16,528,128]{2,1,0:T(8,128)(2,1)} %pack.1.refs_3_, bf16[1024,4096]{1,0:T(8,128)(2,1)S(1)} %copy-done), custom_call_target="tpu_custom_call" | custom-call | flops 150994944 | bytes 10485760 | tf_op jit(solution)/shard_map/first/pallas_call | solution.py:266
  17.3 1.3 %collective-permute-start = (bf16[16,4096]{1,0:T(8,128)(2,1)S(1)}, bf16[16,4096]{1,0:T(8,128)(2,1)S(1)}, u32[]{:S(2)}, u32[]{:S(2)}) collective-permute-start(bf16[16,4096]{1,0:T(8,128)(2,1)S(1)} %first.1), channel_id=1, source_target_pairs={{0,1},{1,0},{2,3},{3,2},{4,5},{5,4},{6,7},{7,6},{8,9},{9,8},{10,11... | collective-permute-start | bytes 393224 | tf_op jit(solution)/shard_map/ppermute | solution.py:182
  18.6 41.1 %all-to-all-done.refs_0_ = bf16[16,528,128]{2,1,0:T(8,128)(2,1)S(1)} async-done(((bf16[16,528,128]{2,1,0:T(8,128)(2,1)}), bf16[16,528,128]{2,1,0:T(8,128)(2,1)S(1)}, u32[]{:S(2)}, u32[]{:S(2)}) %all-to-all-start) | async-done | bytes 2162720 | tf_op jit(solution)/shard_map/all_to_all | solution.py:261
  59.7 0.0 copy-start.2
  59.7 1.3 %copy-done.2 = bf16[16,528,128]{2,1,0:T(8,128)(2,1)} copy-done((bf16[16,528,128]{2,1,0:T(8,128)(2,1)}, bf16[16,528,128]{2,1,0:T(8,128)(2,1)S(1)}, u32[]{:S(2)}) %copy-start.2) | copy-done | bytes 2162712
  61.1 0.0 copy-start.1
  61.1 3.4 %copy-done.1 = bf16[1024,4096]{1,0:T(8,128)(2,1)S(1)} copy-done((bf16[1024,4096]{1,0:T(8,128)(2,1)S(1)}, bf16[1024,4096]{1,0:T(8,128)(2,1)}, u32[]{:S(2)}) %copy-start.1) | copy-done | bytes 8388632
  64.4 4.2 %second.1 = (bf16[16,4096]{1,0:T(8,128)(2,1)S(1)}, bf16[16,256,128]{2,1,0:T(8,128)(2,1)}, bf16[16,256,128]{2,1,0:T(8,128)(2,1)}) custom-call(bf16[16,528,128]{2,1,0:T(8,128)(2,1)} %copy-done.2, bf16[16,8,128]{2,1,0:T(8,128)(2,1)} %refs_1_.5, bf16[16,128]{1,0:T(8,128)(2,1)} %bitcast.17, bf16[16,128]{1,0:T(8,128)(2,1)} %bitcast.18, ...), custom_call_target="tpu_custom_call" | custom-call | flops 150994944 | bytes 12582912 | tf_op jit(solution)/shard_map/second/pallas_call | solution.py:288
  68.6 1.5 %collective-permute-start.1 = (bf16[16,4096]{1,0:T(8,128)(2,1)S(1)}, bf16[16,4096]{1,0:T(8,128)(2,1)S(1)}, u32[]{:S(2)}, u32[]{:S(2)}) collective-permute-start(bf16[16,4096]{1,0:T(8,128)(2,1)S(1)} %get-tuple-element.7), channel_id=1, source_target_pairs={{0,1},{1,0},{2,3},{3,2},{4,5},{5,4},{6,7},{7,6},{8,9},{9,8},{10,11... | collective-permute-start | bytes 393224 | tf_op jit(solution)/shard_map/ppermute | solution.py:182
  70.2 0.0 collective-permute-done
  70.2 0.7 add_convert_fusion.1
  70.8 0.3 collective-permute-done.1
  71.1 0.7 add_convert_fusion
Async XLA Ops:
  3.8 55.9 %all-to-all-start = ((bf16[16,528,128]{2,1,0:T(8,128)(2,1)}), bf16[16,528,128]{2,1,0:T(8,128)(2,1)S(1)}, u32[]{:S(2)}, u32[]{:S(2)}) async-start(bf16[16,528,128]{2,1,0:T(8,128)(2,1)} %pack.1.refs_3_), calls=%async_computation | async-start | bytes 4325376 | tf_op jit(solution)/shard_map/all_to_all | solution.py:261
  10.4 3.4 %copy-start = (bf16[1024,4096]{1,0:T(8,128)(2,1)S(1)}, bf16[1024,4096]{1,0:T(8,128)(2,1)}, u32[]{:S(2)}) copy-start(bf16[1024,4096]{1,0:T(8,128)(2,1)} %refs_4_.3) | copy-start | bytes 25165828
  17.3 52.9 %collective-permute-start = (bf16[16,4096]{1,0:T(8,128)(2,1)S(1)}, bf16[16,4096]{1,0:T(8,128)(2,1)S(1)}, u32[]{:S(2)}, u32[]{:S(2)}) collective-permute-start(bf16[16,4096]{1,0:T(8,128)(2,1)S(1)} %first.1), channel_id=1, source_target_pairs={{0,1},{1,0},{2,3},{3,2},{4,5},{5,4},{6,7},{7,6},{8,9},{9,8},{10,11... | collective-permute-start | bytes 393224 | tf_op jit(solution)/shard_map/ppermute | solution.py:182
  59.7 1.3 %copy-start.2 = (bf16[16,528,128]{2,1,0:T(8,128)(2,1)}, bf16[16,528,128]{2,1,0:T(8,128)(2,1)S(1)}, u32[]{:S(2)}) copy-start(bf16[16,528,128]{2,1,0:T(8,128)(2,1)S(1)} %all-to-all-done.refs_0_) | copy-start | bytes 6488068
  61.1 3.4 %copy-start.1 = (bf16[1024,4096]{1,0:T(8,128)(2,1)S(1)}, bf16[1024,4096]{1,0:T(8,128)(2,1)}, u32[]{:S(2)}) copy-start(bf16[1024,4096]{1,0:T(8,128)(2,1)} %refs_4_.3) | copy-start | bytes 25165828
  68.6 2.5 %collective-permute-start.1 = (bf16[16,4096]{1,0:T(8,128)(2,1)S(1)}, bf16[16,4096]{1,0:T(8,128)(2,1)S(1)}, u32[]{:S(2)}, u32[]{:S(2)}) collective-permute-start(bf16[16,4096]{1,0:T(8,128)(2,1)S(1)} %get-tuple-element.7), channel_id=1, source_target_pairs={{0,1},{1,0},{2,3},{3,2},{4,5},{5,4},{6,7},{7,6},{8,9},{9,8},{10,11... | collective-permute-start | bytes 393224 | tf_op jit(solution)/shard_map/ppermute | solution.py:182

commit v3 on v2

v3 whole, which is shorter than its diff:
```python
import functools

import jax
import jax.numpy as jnp
from jax import lax
from jax.experimental import pallas as pl
from jax.experimental.pallas import tpu as pltpu
from jax.sharding import PartitionSpec as P

NEG = -1e30
TAIL = 16
CHUNKS = 8
AHEAD = 6
LATE = 4
VMEM_BYTES = 24 * 1024 * 1024


def row_of(block, at):
    rows = lax.broadcasted_iota(jnp.int32, block.shape, 0)
    return jnp.sum(jnp.where(rows == at, block, 0.0), axis=0, keepdims=True)


def put_row(parcel, offset, row, position):
    base = pl.multiple_of(offset + position // TAIL * TAIL, TAIL)
    block = parcel[pl.ds(base, TAIL), :]
    at = lax.broadcasted_iota(jnp.int32, block.shape, 0)
    mixed = jnp.where(at == position % TAIL, row, block.astype(jnp.float32))
    parcel[pl.ds(base, TAIL), :] = mixed.astype(jnp.bfloat16)


def invert(dest, source, n):
    def note(r, carry):
        source[dest[r]] = r
        return carry

    lax.fori_loop(0, n, note, 0)


def begin(pairs, sem):
    copies = [pltpu.make_async_copy(a, b, sem.at[i]) for i, (a, b) in enumerate(pairs)]
    for copy in copies:
        copy.start()
    return copies


def finish(copies):
    for copy in copies:
        copy.wait()


def pack_kernel(n, pages, *refs):
    far, outs = refs[:8], refs[8 : 8 + n]
    table, lengths, dest, slot, key_one, value_one, key_pool, value_pool, source, sems = refs[8 + n :]
    copies = begin(list(zip(far, (table, lengths, dest, slot, key_one, value_one, key_pool, value_pool))), sems)
    me = lax.axis_index("inst")
    size = key_pool.shape[1]
    span = pages * size
    finish(copies[:6])
    invert(dest, source, n)
    keys = key_one[...].astype(jnp.float32)
    values = value_one[...].astype(jnp.float32)
    at = lax.broadcasted_iota(jnp.int32, (TAIL, keys.shape[1]), 0)
    for pool, token, offset, copy in ((key_pool, keys, 0, copies[6]), (value_pool, values, span, copies[7])):
        copy.wait()
        for s in range(n):
            r = source[me ^ s]
            for p in range(pages):
                outs[s][offset + p * size : offset + (p + 1) * size, :] = pool[table[p, r]]
            put_row(outs[s], offset, row_of(token, r), lengths[r])
    for s in range(n):
        r = source[me ^ s]
        tail = jnp.where(at == 0, slot[r].astype(jnp.float32), lengths[r].astype(jnp.float32))
        outs[s][2 * span : 2 * span + TAIL, :] = tail.astype(jnp.bfloat16)


def attend(queries, keys, values, counts):
    width = queries[0].shape[1]
    scores = []
    for q, k, count in zip(queries, keys, counts):
        s = lax.dot_general(q, k, (((1,), (1,)), ((), ())), preferred_element_type=jnp.float32)
        live = lax.broadcasted_iota(jnp.int32, s.shape, 1) < count
        scores.append(jnp.where(live, s * width ** (-0.5), NEG))
    group = scores[0].shape[0]
    score = jnp.concatenate(scores, axis=0)
    top = jnp.max(score, axis=-1, keepdims=True)
    expo = jnp.exp(score - top)
    weights = (expo / jnp.sum(expo, axis=-1, keepdims=True)).astype(jnp.bfloat16)
    return [
        jnp.dot(weights[i * group : (i + 1) * group], v, preferred_element_type=jnp.float32)
        for i, v in enumerate(values)
    ]


def project(mixed, weight, out):
    heads = mixed.shape[1]
    rows = jnp.concatenate([mixed[:, h, :] for h in range(heads)], axis=1).astype(jnp.bfloat16)
    width = weight.shape[1] // CHUNKS
    for c in range(CHUNKS):
        part = jnp.dot(
            rows, weight[:, c * width : (c + 1) * width], preferred_element_type=jnp.float32
        )
        out[:, c * width : (c + 1) * width] = part.astype(jnp.bfloat16)


def first_kernel(n, *refs):
    far, parcels, out, weight = refs[:4], refs[4 : 4 + n], refs[4 + n], refs[5 + n]
    lengths, dest, query, source, mixed, sems = refs[6 + n :]
    copies = begin(list(zip(far, (lengths, dest, query, weight))), sems)
    me = lax.axis_index("inst")
    span = (parcels[0].shape[0] - TAIL) // 2
    finish(copies[:3])
    invert(dest, source, n)
    at = [source[me ^ s] for s in range(n)]
    results = attend(
        [query[r] for r in at],
        [parcel[:span, :] for parcel in parcels],
        [parcel[span : 2 * span, :] for parcel in parcels],
        [lengths[r] + 1 for r in at],
    )
    for r, result in zip(at, results):
        mixed[r] = result
    copies[3].wait()
    project(mixed, weight, out)


def place(arrived, query, key_two, value_two, key_cache, value_cache, parcels, mixed, osems):
    span = (arrived[0].shape[0] - TAIL) // 2
    count = len(arrived)
    slots = []
    lengths = []
    for parcel in arrived:
        tail = parcel[2 * span : 2 * span + TAIL, :].astype(jnp.float32)
        slots.append(jnp.max(tail[0:1, :]).astype(jnp.int32))
        lengths.append(jnp.max(tail[1:2, :]).astype(jnp.int32))
    for i, parcel in enumerate(arrived):
        parcels[i] = parcel[: 2 * span, :]
    outgoing = []
    for i in range(count):
        held = parcels.at[i]
        put_row(held, 0, key_two[pl.ds(slots[i], 1), :], lengths[i] + 1)
        put_row(held, span, value_two[pl.ds(slots[i], 1), :], lengths[i] + 1)
        for cache, at in ((key_cache, 0), (value_cache, 1)):
            copy = pltpu.make_async_copy(
                held.at[pl.ds(at * span, span)], cache.at[slots[i]], osems.at[at, i]
            )
            copy.start()
            outgoing.append(copy)
    results = attend(
        [query[j] for j in slots],
        [parcels[i, :span, :] for i in range(count)],
        [parcels[i, span : 2 * span, :] for i in range(count)],
        [length + 2 for length in lengths],
    )
    for j, result in zip(slots, results):
        mixed[j] = result
    return outgoing


def early_kernel(count, pair, *refs):
    arrived, far, halves = refs[:count], refs[count : count + 3], refs[count + 3 : count + 3 + pair]
    key_cache, value_cache, mixed = refs[count + 3 + pair : count + 6 + pair]
    query, key_two, value_two, new_k, new_v, parcels, sems, osems = refs[-8:]
    copies = begin(list(zip(far, (query, key_two, value_two))), sems)
    if pair:
        out = refs[count + 6 + pair]
        both = halves[0][...].astype(jnp.float32) + halves[1][...].astype(jnp.float32)
        out[...] = both.astype(jnp.bfloat16)
    finish(copies)
    new_k[...] = key_two[...].astype(jnp.float32)
    new_v[...] = value_two[...].astype(jnp.float32)
    finish(place(arrived, query, new_k, new_v, key_cache, value_cache, parcels, mixed, osems))


def late_kernel(count, *refs):
    arrived, far, weight, before = refs[:count], refs[count : count + 3], refs[count + 3], refs[count + 4]
    out, key_cache, value_cache = refs[count + 7 : count + 10]
    query, key_two, value_two, new_k, new_v, parcels, mixed, sems, osems = refs[-9:]
    copies = begin(list(zip(far, (query, key_two, value_two))), sems)
    mixed[...] = before[...]
    finish(copies)
    new_k[...] = key_two[...].astype(jnp.float32)
    new_v[...] = value_two[...].astype(jnp.float32)
    outgoing = place(arrived, query, new_k, new_v, key_cache, value_cache, parcels, mixed, osems)
    project(mixed, weight, out)
    finish(outgoing)


def swap(partial):
    return lax.ppermute(partial, "tp", [(0, 1), (1, 0)])


def near(x):
    return pltpu.with_memory_space_constraint(x, pltpu.VMEM)


def hbm(x):
    return pltpu.with_memory_space_constraint(x, pltpu.HBM)


def step_order(n):
    far = list(range(n // 2, n))
    close = list(range(1, n // 2))
    return [s for pair in zip(far, close) for s in pair] + far[len(close) :]


def shards(
    n,
    tp,
    query_one,
    key_one,
    value_one,
    key_pages,
    value_pages,
    page_table,
    lengths,
    dest_instance,
    dest_slot,
    query_two,
    key_two,
    value_two,
    out_weight,
):
    slots, pages = page_table.shape
    pool, kv_heads, size, width = key_pages.shape
    heads = query_one.shape[1]
    depth, columns = out_weight.shape
    span = pages * size
    assert kv_heads == 1 and slots == n and span <= 256
    key_pages = key_pages.reshape(pool, size, width)
    value_pages = value_pages.reshape(pool, size, width)
    key_one = key_one.reshape(slots, width)
    value_one = value_one.reshape(slots, width)
    key_two = key_two.reshape(slots, width)
    value_two = value_two.reshape(slots, width)

    vmem = pl.BlockSpec(memory_space=pltpu.VMEM)
    far = pl.BlockSpec(memory_space=pltpu.HBM)
    params = pltpu.CompilerParams(vmem_limit_bytes=VMEM_BYTES)
    bf16, f32, i32 = jnp.bfloat16, jnp.float32, jnp.int32
    rows = 2 * span + TAIL
    parcel = jax.ShapeDtypeStruct((rows, width), bf16)

    packed = pl.pallas_call(
        functools.partial(pack_kernel, n, pages),
        out_shape=[parcel] * n,
        in_specs=[far] * 8,
        out_specs=[vmem] * n,
        scratch_shapes=[
            pltpu.SMEM((pages, slots), i32),
            pltpu.SMEM((slots,), i32),
            pltpu.SMEM((slots,), i32),
            pltpu.SMEM((slots,), i32),
            pltpu.VMEM((slots, width), bf16),
            pltpu.VMEM((slots, width), bf16),
            pltpu.VMEM((pool, size, width), bf16),
            pltpu.VMEM((pool, size, width), bf16),
            pltpu.SMEM((n,), i32),
            pltpu.SemaphoreType.DMA((8,)),
        ],
        compiler_params=params,
        cost_estimate=pl.CostEstimate(flops=0, bytes_accessed=4 * n * rows * width, transcendentals=0),
        name="pack",
    )(
        hbm(page_table.T),
        hbm(lengths),
        hbm(dest_instance),
        hbm(dest_slot),
        hbm(key_one),
        hbm(value_one),
        hbm(key_pages),
        hbm(value_pages),
    )

    flops = 4 * slots * heads * span * width + 2 * slots * depth * columns
    moved = 2 * depth * columns + 4 * slots * span * width
    order = step_order(n)
    late = order[-LATE:]
    arrived = {0: packed[0]}

    def send(s, block):
        arrived[s] = lax.ppermute(block, "inst", [(i, i ^ s) for i in range(n)])

    for s in order[:AHEAD]:
        send(s, packed[s])
    query_late = lax.optimization_barrier((query_one, arrived[order[0]]))[0]
    partial_one, weight = pl.pallas_call(
        functools.partial(first_kernel, n),
        out_shape=[
            jax.ShapeDtypeStruct((slots, columns), bf16),
            jax.ShapeDtypeStruct((depth, columns), bf16),
        ],
        in_specs=[far] * 4 + [vmem] * n,
        out_specs=[vmem, vmem],
        scratch_shapes=[
            pltpu.SMEM((slots,), i32),
            pltpu.SMEM((slots,), i32),
            pltpu.VMEM((slots, heads, width), bf16),
            pltpu.SMEM((n,), i32),
            pltpu.VMEM((slots, heads, width), f32),
            pltpu.SemaphoreType.DMA((4,)),
        ],
        compiler_params=params,
        cost_estimate=pl.CostEstimate(flops=flops, bytes_accessed=moved, transcendentals=slots * heads * span),
        name="first",
    )(hbm(lengths), hbm(dest_instance), hbm(query_late), hbm(out_weight), *packed)

    for s in order[AHEAD:]:
        send(s, lax.optimization_barrier((packed[s], partial_one))[0])
    early = [0] + order[:-LATE]

    halves = [partial_one, swap(partial_one)] if tp == 2 else []
    cache = jax.ShapeDtypeStruct((slots, span, width), bf16)
    common = [
        pltpu.VMEM((slots, heads, width), bf16),
        pltpu.VMEM((slots, width), bf16),
        pltpu.VMEM((slots, width), bf16),
        pltpu.VMEM((slots, width), f32),
        pltpu.VMEM((slots, width), f32),
    ]
    mixed = jax.ShapeDtypeStruct((slots, heads, width), f32)
    some = len(early)
    results = pl.pallas_call(
        functools.partial(early_kernel, some, len(halves)),
        out_shape=[cache, cache, mixed] + [jax.ShapeDtypeStruct((slots, columns), bf16)] * (len(halves) // 2),
        in_specs=[vmem] * some + [far] * 3 + [vmem] * len(halves),
        out_specs=[far, far, vmem] + [vmem] * (len(halves) // 2),
        scratch_shapes=common
        + [
            pltpu.VMEM((some, 2 * span, width), bf16),
            pltpu.SemaphoreType.DMA((3,)),
            pltpu.SemaphoreType.DMA((2, some)),
        ],
        compiler_params=params,
        cost_estimate=pl.CostEstimate(
            flops=4 * some * heads * span * width,
            bytes_accessed=8 * some * span * width,
            transcendentals=some * heads * span,
        ),
        name="early",
    )(*[arrived[s] for s in early], hbm(query_two), hbm(key_two), hbm(value_two), *halves)
    key_cache, value_cache, mixed = results[:3]
    out_one = results[3] if halves else lax.psum(partial_one, "tp")

    partial_two, key_cache, value_cache = pl.pallas_call(
        functools.partial(late_kernel, LATE),
        out_shape=[jax.ShapeDtypeStruct((slots, columns), bf16), cache, cache],
        in_specs=[vmem] * LATE + [far] * 3 + [vmem] * 2 + [far] * 2,
        out_specs=[vmem, far, far],
        input_output_aliases={LATE + 5: 1, LATE + 6: 2},
        scratch_shapes=common
        + [
            pltpu.VMEM((LATE, 2 * span, width), bf16),
            pltpu.VMEM((slots, heads, width), f32),
            pltpu.SemaphoreType.DMA((3,)),
            pltpu.SemaphoreType.DMA((2, LATE)),
        ],
        compiler_params=params,
        cost_estimate=pl.CostEstimate(flops=flops, bytes_accessed=moved, transcendentals=LATE * heads * span),
        name="late",
    )(
        *[arrived[s] for s in late],
        hbm(query_two),
        hbm(key_two),
        hbm(value_two),
        near(weight),
        mixed,
        hbm(key_cache),
        hbm(value_cache),
    )
    if tp == 2:
        both = partial_two.astype(f32) + swap(partial_two).astype(f32)
        out_two = both.astype(bf16)
    else:
        out_two = lax.psum(partial_two, "tp")
    shape = (slots * pages, kv_heads, size, width)
    return (out_one, out_two, key_cache.reshape(shape), value_cache.reshape(shape))


def solution(mesh):
    sizes = dict(mesh.shape)
    return jax.shard_map(
        functools.partial(shards, sizes["inst"], sizes["tp"]),
        mesh=mesh,
        in_specs=(
            P("inst", "tp", None),
            P("inst", "tp", None),
            P("inst", "tp", None),
            P("inst", "tp", None, None),
            P("inst", "tp", None, None),
            P("inst", None),
            P("inst"),
            P("inst"),
            P("inst"),
            P("inst", "tp", None),
            P("inst", "tp", None),
            P("inst", "tp", None),
            P("tp", None),
        ),
        out_specs=(
            P("inst", None),
            P("inst", None),
            P("inst", "tp", None, None),
            P("inst", "tp", None, None),
        ),
        check_vma=False,
    )
```

time: 72.2 us -> 62.5 us (0.87)
  the two profiles are of different devices: /device:TPU:13 before, /device:TPU:0 now
where the time goes in v3:
time: 62.5 us; the launch traced here: 62.2 us
  starting transfers between devices  29.3 us (47%)
  waiting for transfers between devices  19.3 us (31%)
  Pallas kernels  12.2 us (20%)
  between operations  0.72 us (1%)
  other arithmetic  0.69 us (1%)
    ppermute x15, starting transfers between devices, send(): arrived[s] = lax.ppermute(block, 'inst', [(i, i ^ s) for i in range(n)])  29.2 us
    ppermute x15, waiting for transfers between devices, send(): arrived[s] = lax.ppermute(block, 'inst', [(i, i ^ s) for i in range(n)])  16.7 us
    pallas_call x1, Pallas kernels, shards(): pl.pallas_call(functools.partial(first_kernel, n), out_shape=[jax.ShapeDt...  4.64 us
    pallas_call x1, Pallas kernels, shards(): pl.pallas_call(functools.partial(early_kernel, some, len(halves)), out_sh...  2.92 us
    pallas_call x1, Pallas kernels, shards(): pl.pallas_call(functools.partial(late_kernel, LATE), out_shape=[jax.Shape...  2.71 us
    ppermute x2, waiting for transfers between devices, swap(): return lax.ppermute(partial, 'tp', [(0, 1), (1, 0)])  2.68 us
    pallas_call x1, Pallas kernels, shards(): pl.pallas_call(functools.partial(pack_kernel, n, pages), out_shape=[parce...  1.9 us
  transfers between devices with their start and end apart: 17, of which 8 were waited for; matrix products, arithmetic and copies ran while one was open for 0% of the time, Pallas kernels for 12%

profile of v3, /device:TPU:0, one launch (start us, length us, event | category | flops | bytes accessed | tf_op | source)
XLA Modules:
  0.0 62.2 jit_solution(7267312065860372960)
XLA Ops:
  0.6 1.9 %pack.1 = (bf16[528,128]{1,0:T(8,128)(2,1)S(1)}, bf16[528,128]{1,0:T(8,128)(2,1)S(1)}, bf16[528,128]{1,0:T(8,128)(2,1)S(1)}, bf16[528,128]{1,0:T(8,128)(2,1)S(1)...) custom-call(s32[4,16]{1,0:T(4,128)} %bitcast.23, ...), custom_call_target="tpu_custom_call" | custom-call | bytes 4325376 | tf_op jit(solution)/shard_map/pack/pallas_call | solution.py:243
  2.5 4.1 %collective-permute-start = (bf16[528,128]{1,0:T(8,128)(2,1)S(1)}, bf16[528,128]{1,0:T(8,128)(2,1)S(1)}, u32[]{:S(2)}, u32[]{:S(2)}) collective-permute-start(bf16[528,128]{1,0:T(8,128)(2,1)S(1)} %get-tuple-element.40.refs_12_), channel_id=1, source_target_pairs={{0,16},{2,18},{4,20},{6,22},{8,24},{10,26},{12,28},{14,30},{16,0},... | collective-permute-start | bytes 405512 | tf_op jit(solution)/shard_map/ppermute | solution.py:281
  6.6 1.5 %collective-permute-start.1 = (bf16[528,128]{1,0:T(8,128)(2,1)S(1)}, bf16[528,128]{1,0:T(8,128)(2,1)S(1)}, u32[]{:S(2)}, u32[]{:S(2)}) collective-permute-start(bf16[528,128]{1,0:T(8,128)(2,1)S(1)} %get-tuple-element.41.refs_5_), channel_id=1, source_target_pairs={{0,2},{2,0},{4,6},{6,4},{8,10},{10,8},{12,14},{14,12},{16,18},{18,... | collective-permute-start | bytes 405512 | tf_op jit(solution)/shard_map/ppermute | solution.py:281
  8.1 0.0 collective-permute-start.2
  8.2 1.8 %collective-permute-start.3 = (bf16[528,128]{1,0:T(8,128)(2,1)S(1)}, bf16[528,128]{1,0:T(8,128)(2,1)S(1)}, u32[]{:S(2)}, u32[]{:S(2)}) collective-permute-start(bf16[528,128]{1,0:T(8,128)(2,1)S(1)} %get-tuple-element.43.refs_6_), channel_id=1, source_target_pairs={{0,4},{2,6},{4,0},{6,2},{8,12},{10,14},{12,8},{14,10},{16,20},{18,... | collective-permute-start | bytes 405512 | tf_op jit(solution)/shard_map/ppermute | solution.py:281
  10.0 2.5 %collective-permute-start.4 = (bf16[528,128]{1,0:T(8,128)(2,1)S(1)}, bf16[528,128]{1,0:T(8,128)(2,1)S(1)}, u32[]{:S(2)}, u32[]{:S(2)}) collective-permute-start(bf16[528,128]{1,0:T(8,128)(2,1)S(1)} %get-tuple-element.44.refs_14_), channel_id=1, source_target_pairs={{0,20},{2,22},{4,16},{6,18},{8,28},{10,30},{12,24},{14,26},{16,4},... | collective-permute-start | bytes 405512 | tf_op jit(solution)/shard_map/ppermute | solution.py:281
  12.5 7.3 %collective-permute-done.refs_1_ = bf16[528,128]{1,0:T(8,128)(2,1)S(1)} collective-permute-done((bf16[528,128]{1,0:T(8,128)(2,1)S(1)}, bf16[528,128]{1,0:T(8,128)(2,1)S(1)}, u32[]{:S(2)}, u32[]{:S(2)}) %collective-permute-start) | collective-permute-done | bytes 135200 | tf_op jit(solution)/shard_map/ppermute | solution.py:281
  19.7 2.8 %collective-permute-start.5 = (bf16[528,128]{1,0:T(8,128)(2,1)S(1)}, bf16[528,128]{1,0:T(8,128)(2,1)S(1)}, u32[]{:S(2)}, u32[]{:S(2)}) collective-permute-start(bf16[528,128]{1,0:T(8,128)(2,1)S(1)} %get-tuple-element.45.refs_7_), channel_id=1, source_target_pairs={{0,6},{2,4},{4,2},{6,0},{8,14},{10,12},{12,10},{14,8},{16,22},{18,... | collective-permute-start | bytes 405512 | tf_op jit(solution)/shard_map/ppermute | solution.py:281
  22.5 4.6 %first.1 = (bf16[16,4096]{1,0:T(8,128)(2,1)S(1)}, bf16[1024,4096]{1,0:T(8,128)(2,1)S(1)}) custom-call(s32[16]{0:T(128)} %refs_0_.1, s32[16]{0:T(128)} %refs_1_.3, bf16[16,8,128]{2,1,0:T(8,128)(2,1)} %refs_2_.2, bf16[1024,4096]{1,0:T(8,128)(2,1)} %refs_3_.3, bf16[528,128]{1,0:T(8,128)(2,1)S(1)} %get-tuple-element.39.refs_4_.refs_0_, ...), custom_call_target="tpu_custom_call" | custom-call | flops 150994944 | bytes 10485760 | tf_op jit(solution)/shard_map/first/pallas_call | solution.py:286
  27.2 0.0 collective-permute-done.1.refs_2_
  27.2 0.1 collective-permute-start.6
  27.3 0.0 collective-permute-done.2.refs_3_
  27.3 2.9 %collective-permute-start.7 = (bf16[528,128]{1,0:T(8,128)(2,1)S(1)}, bf16[528,128]{1,0:T(8,128)(2,1)S(1)}, u32[]{:S(2)}, u32[]{:S(2)}) collective-permute-start(bf16[528,128]{1,0:T(8,128)(2,1)S(1)} %get-tuple-element.58.refs_8_), channel_id=1, source_target_pairs={{0,8},{2,10},{4,12},{6,14},{8,0},{10,2},{12,4},{14,6},{16,24},{18,... | collective-permute-start | bytes 405512 | tf_op jit(solution)/shard_map/ppermute | solution.py:281
  30.2 0.0 collective-permute-done.3.refs_4_
  30.2 1.0 %collective-permute-start.8 = (bf16[528,128]{1,0:T(8,128)(2,1)S(1)}, bf16[528,128]{1,0:T(8,128)(2,1)S(1)}, u32[]{:S(2)}, u32[]{:S(2)}) collective-permute-start(bf16[528,128]{1,0:T(8,128)(2,1)S(1)} %get-tuple-element.59.refs_16_), channel_id=1, source_target_pairs={{0,24},{2,26},{4,28},{6,30},{8,16},{10,18},{12,20},{14,22},{16,8},... | collective-permute-start | bytes 405512 | tf_op jit(solution)/shard_map/ppermute | solution.py:281
  31.2 0.0 collective-permute-done.4.refs_5_
  31.2 0.4 collective-permute-start.9
  31.7 0.0 collective-permute-done.5.refs_6_
  31.7 0.0 collective-permute-start.11
  31.7 1.3 %collective-permute-done.11.refs_16_ = bf16[16,4096]{1,0:T(8,128)(2,1)S(1)} collective-permute-done((bf16[16,4096]{1,0:T(8,128)(2,1)S(1)}, bf16[16,4096]{1,0:T(8,128)(2,1)S(1)}, u32[]{:S(2)}, u32[]{:S(2)}) %collective-permute-start.11) | collective-permute-done | bytes 131104 | tf_op jit(solution)/shard_map/ppermute | solution.py:189
  33.0 3.4 %collective-permute-start.10 = (bf16[528,128]{1,0:T(8,128)(2,1)S(1)}, bf16[528,128]{1,0:T(8,128)(2,1)S(1)}, u32[]{:S(2)}, u32[]{:S(2)}) collective-permute-start(bf16[528,128]{1,0:T(8,128)(2,1)S(1)} %get-tuple-element.61.refs_17_), channel_id=1, source_target_pairs={{0,26},{2,24},{4,30},{6,28},{8,18},{10,16},{12,22},{14,20},{16,10}... | collective-permute-start | bytes 405512 | tf_op jit(solution)/shard_map/ppermute | solution.py:281
  36.4 2.9 %collective-permute-done.6.refs_7_ = bf16[528,128]{1,0:T(8,128)(2,1)S(1)} collective-permute-done((bf16[528,128]{1,0:T(8,128)(2,1)S(1)}, bf16[528,128]{1,0:T(8,128)(2,1)S(1)}, u32[]{:S(2)}, u32[]{:S(2)}) %collective-permute-start.6) | collective-permute-done | bytes 135200 | tf_op jit(solution)/shard_map/ppermute | solution.py:281
  39.3 0.0 collective-permute-start.12
  39.3 0.0 collective-permute-done.7.refs_8_
  39.3 2.5 %collective-permute-start.13 = (bf16[528,128]{1,0:T(8,128)(2,1)S(1)}, bf16[528,128]{1,0:T(8,128)(2,1)S(1)}, u32[]{:S(2)}, u32[]{:S(2)}) collective-permute-start(bf16[528,128]{1,0:T(8,128)(2,1)S(1)} %get-tuple-element.64.refs_18_), channel_id=1, source_target_pairs={{0,28},{2,30},{4,24},{6,26},{8,20},{10,22},{12,16},{14,18},{16,12}... | collective-permute-start | bytes 405512 | tf_op jit(solution)/shard_map/ppermute | solution.py:281
  41.8 0.0 collective-permute-done.8.refs_9_
  41.8 2.9 %collective-permute-start.14 = (bf16[528,128]{1,0:T(8,128)(2,1)S(1)}, bf16[528,128]{1,0:T(8,128)(2,1)S(1)}, u32[]{:S(2)}, u32[]{:S(2)}) collective-permute-start(bf16[528,128]{1,0:T(8,128)(2,1)S(1)} %get-tuple-element.65.refs_11_), channel_id=1, source_target_pairs={{0,14},{2,12},{4,10},{6,8},{8,6},{10,4},{12,2},{14,0},{16,30},{18,... | collective-permute-start | bytes 405512 | tf_op jit(solution)/shard_map/ppermute | solution.py:281
  44.7 0.6 collective-permute-done.9.refs_10_
  45.2 3.3 %collective-permute-start.15 = (bf16[528,128]{1,0:T(8,128)(2,1)S(1)}, bf16[528,128]{1,0:T(8,128)(2,1)S(1)}, u32[]{:S(2)}, u32[]{:S(2)}) collective-permute-start(bf16[528,128]{1,0:T(8,128)(2,1)S(1)} %get-tuple-element.66.refs_19_), channel_id=1, source_target_pairs={{0,30},{2,28},{4,26},{6,24},{8,22},{10,20},{12,18},{14,16},{16,14}... | collective-permute-start | bytes 405512 | tf_op jit(solution)/shard_map/ppermute | solution.py:281
  48.5 0.0 collective-permute-done.10.refs_11_
  48.5 2.9 %early.1 = (bf16[16,256,128]{2,1,0:T(8,128)(2,1)}, bf16[16,256,128]{2,1,0:T(8,128)(2,1)}, f32[16,8,128]{2,1,0:T(8,128)S(1)}, bf16[16,4096]{1,0:T(8,128)(2,1)}) custom-call(bf16[528,128]{1,0:T(8,128)(2,1)S(1)} %get-tuple-element.39.refs_4_.refs_0_, bf16[528,128]{1,0:T(8,128)(2,1)S(1)} %collective-permute-done.refs_1_, ...), custom_call_target="tpu_custom_call" | custom-call | flops 12582912 | bytes 3145728 | tf_op jit(solution)/shard_map/early/pallas_call | solution.py:322
  51.4 0.0 collective-permute-done.12.refs_0_
  51.5 0.5 collective-permute-done.13.refs_1_
  52.0 3.3 %collective-permute-done.14.refs_2_ = bf16[528,128]{1,0:T(8,128)(2,1)S(1)} collective-permute-done((bf16[528,128]{1,0:T(8,128)(2,1)S(1)}, bf16[528,128]{1,0:T(8,128)(2,1)S(1)}, u32[]{:S(2)}, u32[]{:S(2)}) %collective-permute-start.14) | collective-permute-done | bytes 135200 | tf_op jit(solution)/shard_map/ppermute | solution.py:281
  55.3 2.1 %collective-permute-done.15.refs_3_ = bf16[528,128]{1,0:T(8,128)(2,1)S(1)} collective-permute-done((bf16[528,128]{1,0:T(8,128)(2,1)S(1)}, bf16[528,128]{1,0:T(8,128)(2,1)S(1)}, u32[]{:S(2)}, u32[]{:S(2)}) %collective-permute-start.15) | collective-permute-done | bytes 135200 | tf_op jit(solution)/shard_map/ppermute | solution.py:281
  57.4 2.7 %late.1 = (bf16[16,4096]{1,0:T(8,128)(2,1)S(1)}, bf16[16,256,128]{2,1,0:T(8,128)(2,1)}, bf16[16,256,128]{2,1,0:T(8,128)(2,1)}) custom-call(bf16[528,128]{1,0:T(8,128)(2,1)S(1)} %collective-permute-done.12.refs_0_, bf16[528,128]{1,0:T(8,128)(2,1)S(1)} %collective-permute-done.13.refs_1_, ...), custom_call_target="tpu_custom_call", output_to_operand_aliasing={{1}: (9, {}), {2}: (10, {})} | custom-call | flops 150994944 | bytes 10485760 | tf_op jit(solution)/shard_map/late/pallas_call | solution.py:344
  60.1 0.1 collective-permute-start.16
  60.2 1.3 %collective-permute-done.16 = bf16[16,4096]{1,0:T(8,128)(2,1)S(1)} collective-permute-done((bf16[16,4096]{1,0:T(8,128)(2,1)S(1)}, bf16[16,4096]{1,0:T(8,128)(2,1)S(1)}, u32[]{:S(2)}, u32[]{:S(2)}) %collective-permute-start.16) | collective-permute-done | bytes 131104 | tf_op jit(solution)/shard_map/ppermute | solution.py:189
  61.5 0.7 %add_convert_fusion = bf16[16,4096]{1,0:T(8,128)(2,1)} fusion(bf16[16,4096]{1,0:T(8,128)(2,1)S(1)} %collective-permute-done.16, bf16[16,4096]{1,0:T(8,128)(2,1)S(1)} %get-tuple-element.71), kind=kLoop, calls=%fused_computation | loop fusion | flops 262144 | bytes 393216 | tf_op jit(solution)/shard_map/convert_element_type | solution.py:372
Async XLA Ops:
  2.5 17.2 %collective-permute-start = (bf16[528,128]{1,0:T(8,128)(2,1)S(1)}, bf16[528,128]{1,0:T(8,128)(2,1)S(1)}, u32[]{:S(2)}, u32[]{:S(2)}) collective-permute-start(bf16[528,128]{1,0:T(8,128)(2,1)S(1)} %get-tuple-element.40.refs_12_), channel_id=1, source_target_pairs={{0,16},{2,18},{4,20},{6,22},{8,24},{10,26},{12,28},{14,30},{16,0},... | collective-permute-start | bytes 405512 | tf_op jit(solution)/shard_map/ppermute | solution.py:281
  6.6 20.6 %collective-permute-start.1 = (bf16[528,128]{1,0:T(8,128)(2,1)S(1)}, bf16[528,128]{1,0:T(8,128)(2,1)S(1)}, u32[]{:S(2)}, u32[]{:S(2)}) collective-permute-start(bf16[528,128]{1,0:T(8,128)(2,1)S(1)} %get-tuple-element.41.refs_5_), channel_id=1, source_target_pairs={{0,2},{2,0},{4,6},{6,4},{8,10},{10,8},{12,14},{14,12},{16,18},{18,... | collective-permute-start | bytes 405512 | tf_op jit(solution)/shard_map/ppermute | solution.py:281
  8.1 19.1 %collective-permute-start.2 = (bf16[528,128]{1,0:T(8,128)(2,1)S(1)}, bf16[528,128]{1,0:T(8,128)(2,1)S(1)}, u32[]{:S(2)}, u32[]{:S(2)}) collective-permute-start(bf16[528,128]{1,0:T(8,128)(2,1)S(1)} %get-tuple-element.42.refs_13_), channel_id=1, source_target_pairs={{0,18},{2,16},{4,22},{6,20},{8,26},{10,24},{12,30},{14,28},{16,2},... | collective-permute-start | bytes 405512 | tf_op jit(solution)/shard_map/ppermute | solution.py:281
  8.2 22.0 %collective-permute-start.3 = (bf16[528,128]{1,0:T(8,128)(2,1)S(1)}, bf16[528,128]{1,0:T(8,128)(2,1)S(1)}, u32[]{:S(2)}, u32[]{:S(2)}) collective-permute-start(bf16[528,128]{1,0:T(8,128)(2,1)S(1)} %get-tuple-element.43.refs_6_), channel_id=1, source_target_pairs={{0,4},{2,6},{4,0},{6,2},{8,12},{10,14},{12,8},{14,10},{16,20},{18,... | collective-permute-start | bytes 405512 | tf_op jit(solution)/shard_map/ppermute | solution.py:281
  10.0 21.3 %collective-permute-start.4 = (bf16[528,128]{1,0:T(8,128)(2,1)S(1)}, bf16[528,128]{1,0:T(8,128)(2,1)S(1)}, u32[]{:S(2)}, u32[]{:S(2)}) collective-permute-start(bf16[528,128]{1,0:T(8,128)(2,1)S(1)} %get-tuple-element.44.refs_14_), channel_id=1, source_target_pairs={{0,20},{2,22},{4,16},{6,18},{8,28},{10,30},{12,24},{14,26},{16,4},... | collective-permute-start | bytes 405512 | tf_op jit(solution)/shard_map/ppermute | solution.py:281
  19.7 11.9 %collective-permute-start.5 = (bf16[528,128]{1,0:T(8,128)(2,1)S(1)}, bf16[528,128]{1,0:T(8,128)(2,1)S(1)}, u32[]{:S(2)}, u32[]{:S(2)}) collective-permute-start(bf16[528,128]{1,0:T(8,128)(2,1)S(1)} %get-tuple-element.45.refs_7_), channel_id=1, source_target_pairs={{0,6},{2,4},{4,2},{6,0},{8,14},{10,12},{12,10},{14,8},{16,22},{18,... | collective-permute-start | bytes 405512 | tf_op jit(solution)/shard_map/ppermute | solution.py:281
  27.2 12.1 %collective-permute-start.6 = (bf16[528,128]{1,0:T(8,128)(2,1)S(1)}, bf16[528,128]{1,0:T(8,128)(2,1)S(1)}, u32[]{:S(2)}, u32[]{:S(2)}) collective-permute-start(bf16[528,128]{1,0:T(8,128)(2,1)S(1)} %get-tuple-element.57.refs_15_), channel_id=1, source_target_pairs={{0,22},{2,20},{4,18},{6,16},{8,30},{10,28},{12,26},{14,24},{16,6},... | collective-permute-start | bytes 405512 | tf_op jit(solution)/shard_map/ppermute | solution.py:281
  27.3 12.0 %collective-permute-start.7 = (bf16[528,128]{1,0:T(8,128)(2,1)S(1)}, bf16[528,128]{1,0:T(8,128)(2,1)S(1)}, u32[]{:S(2)}, u32[]{:S(2)}) collective-permute-start(bf16[528,128]{1,0:T(8,128)(2,1)S(1)} %get-tuple-element.58.refs_8_), channel_id=1, source_target_pairs={{0,8},{2,10},{4,12},{6,14},{8,0},{10,2},{12,4},{14,6},{16,24},{18,... | collective-permute-start | bytes 405512 | tf_op jit(solution)/shard_map/ppermute | solution.py:281
  30.2 11.6 %collective-permute-start.8 = (bf16[528,128]{1,0:T(8,128)(2,1)S(1)}, bf16[528,128]{1,0:T(8,128)(2,1)S(1)}, u32[]{:S(2)}, u32[]{:S(2)}) collective-permute-start(bf16[528,128]{1,0:T(8,128)(2,1)S(1)} %get-tuple-element.59.refs_16_), channel_id=1, source_target_pairs={{0,24},{2,26},{4,28},{6,30},{8,16},{10,18},{12,20},{14,22},{16,8},... | collective-permute-start | bytes 405512 | tf_op jit(solution)/shard_map/ppermute | solution.py:281
  31.2 14.0 %collective-permute-start.9 = (bf16[528,128]{1,0:T(8,128)(2,1)S(1)}, bf16[528,128]{1,0:T(8,128)(2,1)S(1)}, u32[]{:S(2)}, u32[]{:S(2)}) collective-permute-start(bf16[528,128]{1,0:T(8,128)(2,1)S(1)} %get-tuple-element.60.refs_9_), channel_id=1, source_target_pairs={{0,10},{2,8},{4,14},{6,12},{8,2},{10,0},{12,6},{14,4},{16,26},{18,... | collective-permute-start | bytes 405512 | tf_op jit(solution)/shard_map/ppermute | solution.py:281
  31.7 1.3 %collective-permute-start.11 = (bf16[16,4096]{1,0:T(8,128)(2,1)S(1)}, bf16[16,4096]{1,0:T(8,128)(2,1)S(1)}, u32[]{:S(2)}, u32[]{:S(2)}) collective-permute-start(bf16[16,4096]{1,0:T(8,128)(2,1)S(1)} %get-tuple-element.56.refs_15_), channel_id=1, source_target_pairs={{0,1},{1,0},{2,3},{3,2},{4,5},{5,4},{6,7},{7,6},{8,9},{9,8},{10,11... | collective-permute-start | bytes 393224 | tf_op jit(solution)/shard_map/ppermute | solution.py:189
  33.0 15.5 %collective-permute-start.10 = (bf16[528,128]{1,0:T(8,128)(2,1)S(1)}, bf16[528,128]{1,0:T(8,128)(2,1)S(1)}, u32[]{:S(2)}, u32[]{:S(2)}) collective-permute-start(bf16[528,128]{1,0:T(8,128)(2,1)S(1)} %get-tuple-element.61.refs_17_), channel_id=1, source_target_pairs={{0,26},{2,24},{4,30},{6,28},{8,18},{10,16},{12,22},{14,20},{16,10}... | collective-permute-start | bytes 405512 | tf_op jit(solution)/shard_map/ppermute | solution.py:281
  39.3 12.2 %collective-permute-start.12 = (bf16[528,128]{1,0:T(8,128)(2,1)S(1)}, bf16[528,128]{1,0:T(8,128)(2,1)S(1)}, u32[]{:S(2)}, u32[]{:S(2)}) collective-permute-start(bf16[528,128]{1,0:T(8,128)(2,1)S(1)} %get-tuple-element.63.refs_10_), channel_id=1, source_target_pairs={{0,12},{2,14},{4,8},{6,10},{8,4},{10,6},{12,0},{14,2},{16,28},{18,... | collective-permute-start | bytes 405512 | tf_op jit(solution)/shard_map/ppermute | solution.py:281
  39.3 12.7 %collective-permute-start.13 = (bf16[528,128]{1,0:T(8,128)(2,1)S(1)}, bf16[528,128]{1,0:T(8,128)(2,1)S(1)}, u32[]{:S(2)}, u32[]{:S(2)}) collective-permute-start(bf16[528,128]{1,0:T(8,128)(2,1)S(1)} %get-tuple-element.64.refs_18_), channel_id=1, source_target_pairs={{0,28},{2,30},{4,24},{6,26},{8,20},{10,22},{12,16},{14,18},{16,12}... | collective-permute-start | bytes 405512 | tf_op jit(solution)/shard_map/ppermute | solution.py:281
  41.8 13.5 %collective-permute-start.14 = (bf16[528,128]{1,0:T(8,128)(2,1)S(1)}, bf16[528,128]{1,0:T(8,128)(2,1)S(1)}, u32[]{:S(2)}, u32[]{:S(2)}) collective-permute-start(bf16[528,128]{1,0:T(8,128)(2,1)S(1)} %get-tuple-element.65.refs_11_), channel_id=1, source_target_pairs={{0,14},{2,12},{4,10},{6,8},{8,6},{10,4},{12,2},{14,0},{16,30},{18,... | collective-permute-start | bytes 405512 | tf_op jit(solution)/shard_map/ppermute | solution.py:281
  45.2 12.2 %collective-permute-start.15 = (bf16[528,128]{1,0:T(8,128)(2,1)S(1)}, bf16[528,128]{1,0:T(8,128)(2,1)S(1)}, u32[]{:S(2)}, u32[]{:S(2)}) collective-permute-start(bf16[528,128]{1,0:T(8,128)(2,1)S(1)} %get-tuple-element.66.refs_19_), channel_id=1, source_target_pairs={{0,30},{2,28},{4,26},{6,24},{8,22},{10,20},{12,18},{14,16},{16,14}... | collective-permute-start | bytes 405512 | tf_op jit(solution)/shard_map/ppermute | solution.py:281
  60.1 1.4 %collective-permute-start.16 = (bf16[16,4096]{1,0:T(8,128)(2,1)S(1)}, bf16[16,4096]{1,0:T(8,128)(2,1)S(1)}, u32[]{:S(2)}, u32[]{:S(2)}) collective-permute-start(bf16[16,4096]{1,0:T(8,128)(2,1)S(1)} %get-tuple-element.71), channel_id=1, source_target_pairs={{0,1},{1,0},{2,3},{3,2},{4,5},{5,4},{6,7},{7,6},{8,9},{9,8},{10,11... | collective-permute-start | bytes 393224 | tf_op jit(solution)/shard_map/ppermute | solution.py:189

commit v4 on v3

v4 whole, which is shorter than its diff:
```python
import functools

import jax
import jax.numpy as jnp
from jax import lax
from jax.experimental import pallas as pl
from jax.experimental.pallas import tpu as pltpu
from jax.sharding import PartitionSpec as P

NEG = -1e30
TAIL = 16
CHUNKS = 8
AHEAD = 5
LATE = 3
VMEM_BYTES = 24 * 1024 * 1024


def row_of(block, at):
    rows = lax.broadcasted_iota(jnp.int32, block.shape, 0)
    return jnp.sum(jnp.where(rows == at, block, 0.0), axis=0, keepdims=True)


def put_row(block, row, position):
    base = pl.multiple_of(position // TAIL * TAIL, TAIL)
    part = block[pl.ds(base, TAIL), :]
    at = lax.broadcasted_iota(jnp.int32, part.shape, 0)
    mixed = jnp.where(at == position % TAIL, row, part.astype(jnp.float32))
    block[pl.ds(base, TAIL), :] = mixed.astype(jnp.bfloat16)


def invert(dest, source, n):
    def note(r, carry):
        source[dest[r]] = r
        return carry

    lax.fori_loop(0, n, note, 0)


def begin(pairs, sem):
    copies = [pltpu.make_async_copy(a, b, sem.at[i]) for i, (a, b) in enumerate(pairs)]
    for copy in copies:
        copy.start()
    return copies


def finish(copies):
    for copy in copies:
        copy.wait()


def views(ref, span):
    return ref.at[pl.ds(0, span)], ref.at[pl.ds(span, span)], ref.at[pl.ds(2 * span, TAIL)]


def parcels_of(refs, half, span):
    home, keys, rest, others = refs[0], refs[1], refs[2], refs[3:]
    near = [views(home.at[d], span) for d in range(half)]
    split = (keys, rest.at[pl.ds(0, span)], rest.at[pl.ds(span, TAIL)])
    return near + [split] + [views(ref, span) for ref in others]


def sources(source, half):
    me = lax.axis_index("inst")
    base = me // half * half
    return [source[base + d] for d in range(half)] + [source[me ^ s] for s in range(half, 2 * half)]


def pack_kernel(half, pages, *refs):
    far, outs = refs[:8], refs[8 : 10 + half]
    table, lengths, dest, slot, key_one, value_one, key_pool, value_pool, source, sems = refs[10 + half :]
    copies = begin(list(zip(far, (table, lengths, dest, slot, key_one, value_one, key_pool, value_pool))), sems)
    size = key_pool.shape[1]
    parcels = parcels_of(outs, half, pages * size)
    finish(copies[:6])
    invert(dest, source, 2 * half)
    at = sources(source, half)
    tokens = (key_one[...].astype(jnp.float32), value_one[...].astype(jnp.float32))
    for which, pool in ((0, key_pool), (1, value_pool)):
        copies[6 + which].wait()
        for r, parcel in zip(at, parcels):
            for p in range(pages):
                parcel[which][p * size : (p + 1) * size, :] = pool[table[p, r]]
            put_row(parcel[which], row_of(tokens[which], r), lengths[r])
    rows = lax.broadcasted_iota(jnp.int32, (TAIL, key_one.shape[1]), 0)
    for r, parcel in zip(at, parcels):
        tail = jnp.where(rows == 0, slot[r].astype(jnp.float32), lengths[r].astype(jnp.float32))
        parcel[2][...] = tail.astype(jnp.bfloat16)


def attend(queries, keys, values, counts):
    width = queries[0].shape[1]
    scores = []
    for q, k, count in zip(queries, keys, counts):
        s = lax.dot_general(q, k, (((1,), (1,)), ((), ())), preferred_element_type=jnp.float32)
        live = lax.broadcasted_iota(jnp.int32, s.shape, 1) < count
        scores.append(jnp.where(live, s * width ** (-0.5), NEG))
    group = scores[0].shape[0]
    score = jnp.concatenate(scores, axis=0)
    top = jnp.max(score, axis=-1, keepdims=True)
    expo = jnp.exp(score - top)
    weights = (expo / jnp.sum(expo, axis=-1, keepdims=True)).astype(jnp.bfloat16)
    return [
        jnp.dot(weights[i * group : (i + 1) * group], v, preferred_element_type=jnp.float32)
        for i, v in enumerate(values)
    ]


def project(mixed, weight, out):
    heads = mixed.shape[1]
    rows = jnp.concatenate([mixed[:, h, :] for h in range(heads)], axis=1).astype(jnp.bfloat16)
    width = weight.shape[1] // CHUNKS
    for c in range(CHUNKS):
        part = jnp.dot(
            rows, weight[:, c * width : (c + 1) * width], preferred_element_type=jnp.float32
        )
        out[:, c * width : (c + 1) * width] = part.astype(jnp.bfloat16)


def first_kernel(half, span, *refs):
    far, parcels, out, weight = refs[:4], refs[4 : 6 + half], refs[6 + half], refs[7 + half]
    lengths, dest, query, source, mixed, sems = refs[8 + half :]
    copies = begin(list(zip(far, (lengths, dest, query, weight))), sems)
    parcels = parcels_of(parcels, half, span)
    finish(copies[:3])
    invert(dest, source, 2 * half)
    at = sources(source, half)
    results = attend(
        [query[r] for r in at],
        [parcel[0][...] for parcel in parcels],
        [parcel[1][...] for parcel in parcels],
        [lengths[r] + 1 for r in at],
    )
    for r, result in zip(at, results):
        mixed[r] = result
    copies[3].wait()
    project(mixed, weight, out)


def place(arrived, query, key_two, value_two, key_cache, value_cache, held, mixed, osems):
    count = len(arrived)
    slots = []
    lengths = []
    for parcel in arrived:
        tail = parcel[2][...].astype(jnp.float32)
        slots.append(jnp.max(tail[0:1, :]).astype(jnp.int32))
        lengths.append(jnp.max(tail[1:2, :]).astype(jnp.int32))
    for i, parcel in enumerate(arrived):
        held[0, i] = parcel[0][...]
        held[1, i] = parcel[1][...]
    outgoing = []
    for i in range(count):
        for which, (token, cache) in enumerate(((key_two, key_cache), (value_two, value_cache))):
            put_row(held.at[which, i], token[pl.ds(slots[i], 1), :], lengths[i] + 1)
            copy = pltpu.make_async_copy(held.at[which, i], cache.at[slots[i]], osems.at[which, i])
            copy.start()
            outgoing.append(copy)
    results = attend(
        [query[j] for j in slots],
        [held[0, i] for i in range(count)],
        [held[1, i] for i in range(count)],
        [length + 2 for length in lengths],
    )
    for j, result in zip(slots, results):
        mixed[j] = result
    return outgoing


def early_kernel(half, count, span, pair, *refs):
    arrived, far, halves = refs[: count + 1], refs[count + 1 : count + 4], refs[count + 4 : count + 4 + pair]
    key_cache, value_cache, mixed = refs[count + 4 + pair : count + 7 + pair]
    query, key_two, value_two, new_k, new_v, held, sems, osems = refs[-8:]
    copies = begin(list(zip(far, (query, key_two, value_two))), sems)
    if pair:
        out = refs[count + 7 + pair]
        both = halves[0][...].astype(jnp.float32) + halves[1][...].astype(jnp.float32)
        out[...] = both.astype(jnp.bfloat16)
    finish(copies)
    new_k[...] = key_two[...].astype(jnp.float32)
    new_v[...] = value_two[...].astype(jnp.float32)
    parcels = [views(arrived[0].at[d], span) for d in range(half)] + [views(ref, span) for ref in arrived[1:]]
    finish(place(parcels, query, new_k, new_v, key_cache, value_cache, held, mixed, osems))


def late_kernel(count, span, *refs):
    arrived, far, weight, before = refs[: count + 1], refs[count + 1 : count + 4], refs[count + 4], refs[count + 5]
    out, key_cache, value_cache = refs[count + 8 : count + 11]
    query, key_two, value_two, new_k, new_v, held, mixed, sems, osems = refs[-9:]
    copies = begin(list(zip(far, (query, key_two, value_two))), sems)
    mixed[...] = before[...]
    finish(copies)
    new_k[...] = key_two[...].astype(jnp.float32)
    new_v[...] = value_two[...].astype(jnp.float32)
    keys, rest = arrived[0], arrived[1]
    parcels = [(keys, rest.at[pl.ds(0, span)], rest.at[pl.ds(span, TAIL)])] + [views(ref, span) for ref in arrived[2:]]
    outgoing = place(parcels, query, new_k, new_v, key_cache, value_cache, held, mixed, osems)
    project(mixed, weight, out)
    finish(outgoing)


def swap(partial):
    return lax.ppermute(partial, "tp", [(0, 1), (1, 0)])


def near(x):
    return pltpu.with_memory_space_constraint(x, pltpu.VMEM)


def hbm(x):
    return pltpu.with_memory_space_constraint(x, pltpu.HBM)


def shards(
    n,
    tp,
    query_one,
    key_one,
    value_one,
    key_pages,
    value_pages,
    page_table,
    lengths,
    dest_instance,
    dest_slot,
    query_two,
    key_two,
    value_two,
    out_weight,
):
    slots, pages = page_table.shape
    pool, kv_heads, size, width = key_pages.shape
    heads = query_one.shape[1]
    depth, columns = out_weight.shape
    span = pages * size
    assert kv_heads == 1 and slots == n and n % 2 == 0 and span <= 256
    key_pages = key_pages.reshape(pool, size, width)
    value_pages = value_pages.reshape(pool, size, width)
    key_one = key_one.reshape(slots, width)
    value_one = value_one.reshape(slots, width)
    key_two = key_two.reshape(slots, width)
    value_two = value_two.reshape(slots, width)

    vmem = pl.BlockSpec(memory_space=pltpu.VMEM)
    far = pl.BlockSpec(memory_space=pltpu.HBM)
    params = pltpu.CompilerParams(vmem_limit_bytes=VMEM_BYTES)
    bf16, f32, i32 = jnp.bfloat16, jnp.float32, jnp.int32
    rows = 2 * span + TAIL
    half = n // 2

    def block(*lead):
        return jax.ShapeDtypeStruct((*lead, width), bf16)

    shapes = [block(half, rows), block(span), block(span + TAIL)] + [block(rows)] * (half - 1)

    packed = pl.pallas_call(
        functools.partial(pack_kernel, half, pages),
        out_shape=shapes,
        in_specs=[far] * 8,
        out_specs=[vmem] * len(shapes),
        scratch_shapes=[
            pltpu.SMEM((pages, slots), i32),
            pltpu.SMEM((slots,), i32),
            pltpu.SMEM((slots,), i32),
            pltpu.SMEM((slots,), i32),
            pltpu.VMEM((slots, width), bf16),
            pltpu.VMEM((slots, width), bf16),
            pltpu.VMEM((pool, size, width), bf16),
            pltpu.VMEM((pool, size, width), bf16),
            pltpu.SMEM((n,), i32),
            pltpu.SemaphoreType.DMA((8,)),
        ],
        compiler_params=params,
        cost_estimate=pl.CostEstimate(flops=0, bytes_accessed=4 * n * rows * width, transcendentals=0),
        name="pack",
    )(
        hbm(page_table.T),
        hbm(lengths),
        hbm(dest_instance),
        hbm(dest_slot),
        hbm(key_one),
        hbm(value_one),
        hbm(key_pages),
        hbm(value_pages),
    )

    flops = 4 * slots * heads * span * width + 2 * slots * depth * columns
    moved = 2 * depth * columns + 4 * slots * span * width
    def send(s, block):
        return lax.ppermute(block, "inst", [(i, i ^ s) for i in range(n)])

    def after(x, y):
        return lax.optimization_barrier((x, y))[0]

    home, split_keys, split_rest, others = packed[0], packed[1], packed[2], packed[3:]
    arrived_keys = send(half, split_keys)
    arrived = [send(half + 1 + i, others[i]) for i in range(AHEAD)]
    groups = [list(range(half)), list(range(half, n))]
    arrived_home = lax.all_to_all(home, "inst", 0, 0, axis_index_groups=groups, tiled=True)
    partial_one, weight = pl.pallas_call(
        functools.partial(first_kernel, half, span),
        out_shape=[
            jax.ShapeDtypeStruct((slots, columns), bf16),
            jax.ShapeDtypeStruct((depth, columns), bf16),
        ],
        in_specs=[far] * 4 + [vmem] * len(shapes),
        out_specs=[vmem, vmem],
        scratch_shapes=[
            pltpu.SMEM((slots,), i32),
            pltpu.SMEM((slots,), i32),
            pltpu.VMEM((slots, heads, width), bf16),
            pltpu.SMEM((n,), i32),
            pltpu.VMEM((slots, heads, width), f32),
            pltpu.SemaphoreType.DMA((4,)),
        ],
        compiler_params=params,
        cost_estimate=pl.CostEstimate(flops=flops, bytes_accessed=moved, transcendentals=slots * heads * span),
        name="first",
    )(hbm(lengths), hbm(dest_instance), hbm(after(query_one, arrived_home)), hbm(out_weight), *packed)

    arrived += [send(half + 1 + i, after(others[i], partial_one)) for i in range(AHEAD, half - 1)]
    arrived_rest = send(half, after(split_rest, partial_one))
    early, late = arrived[: half - LATE], [arrived_keys, arrived_rest] + arrived[half - LATE :]

    halves = [partial_one, swap(partial_one)] if tp == 2 else []
    cache = jax.ShapeDtypeStruct((slots, span, width), bf16)
    common = [
        pltpu.VMEM((slots, heads, width), bf16),
        pltpu.VMEM((slots, width), bf16),
        pltpu.VMEM((slots, width), bf16),
        pltpu.VMEM((slots, width), f32),
        pltpu.VMEM((slots, width), f32),
    ]
    mixed = jax.ShapeDtypeStruct((slots, heads, width), f32)
    some = half + len(early)
    results = pl.pallas_call(
        functools.partial(early_kernel, half, len(early), span, len(halves)),
        out_shape=[cache, cache, mixed] + [jax.ShapeDtypeStruct((slots, columns), bf16)] * (len(halves) // 2),
        in_specs=[vmem] * (1 + len(early)) + [far] * 3 + [vmem] * len(halves),
        out_specs=[far, far, vmem] + [vmem] * (len(halves) // 2),
        scratch_shapes=common
        + [
            pltpu.VMEM((2, some, span, width), bf16),
            pltpu.SemaphoreType.DMA((3,)),
            pltpu.SemaphoreType.DMA((2, some)),
        ],
        compiler_params=params,
        cost_estimate=pl.CostEstimate(
            flops=4 * some * heads * span * width,
            bytes_accessed=8 * some * span * width,
            transcendentals=some * heads * span,
        ),
        name="early",
    )(near(arrived_home), *early, hbm(query_two), hbm(key_two), hbm(value_two), *halves)
    key_cache, value_cache, mixed = results[:3]
    out_one = results[3] if halves else lax.psum(partial_one, "tp")

    partial_two, key_cache, value_cache = pl.pallas_call(
        functools.partial(late_kernel, LATE, span),
        out_shape=[jax.ShapeDtypeStruct((slots, columns), bf16), cache, cache],
        in_specs=[vmem] * len(late) + [far] * 3 + [vmem] * 2 + [far] * 2,
        out_specs=[vmem, far, far],
        input_output_aliases={len(late) + 5: 1, len(late) + 6: 2},
        scratch_shapes=common
        + [
            pltpu.VMEM((2, LATE, span, width), bf16),
            pltpu.VMEM((slots, heads, width), f32),
            pltpu.SemaphoreType.DMA((3,)),
            pltpu.SemaphoreType.DMA((2, LATE)),
        ],
        compiler_params=params,
        cost_estimate=pl.CostEstimate(flops=flops, bytes_accessed=moved, transcendentals=LATE * heads * span),
        name="late",
    )(
        *late,
        hbm(query_two),
        hbm(key_two),
        hbm(value_two),
        near(weight),
        mixed,
        hbm(key_cache),
        hbm(value_cache),
    )
    if tp == 2:
        both = partial_two.astype(f32) + swap(partial_two).astype(f32)
        out_two = both.astype(bf16)
    else:
        out_two = lax.psum(partial_two, "tp")
    shape = (slots * pages, kv_heads, size, width)
    return (out_one, out_two, key_cache.reshape(shape), value_cache.reshape(shape))


def solution(mesh):
    sizes = dict(mesh.shape)
    return jax.shard_map(
        functools.partial(shards, sizes["inst"], sizes["tp"]),
        mesh=mesh,
        in_specs=(
            P("inst", "tp", None),
            P("inst", "tp", None),
            P("inst", "tp", None),
            P("inst", "tp", None, None),
            P("inst", "tp", None, None),
            P("inst", None),
            P("inst"),
            P("inst"),
            P("inst"),
            P("inst", "tp", None),
            P("inst", "tp", None),
            P("inst", "tp", None),
            P("tp", None),
        ),
        out_specs=(
            P("inst", None),
            P("inst", None),
            P("inst", "tp", None, None),
            P("inst", "tp", None, None),
        ),
        check_vma=False,
    )
```

time: 62.5 us -> 65.8 us (1.053)
  starting transfers between devices: 29.3 us -> 35.2 us
  waiting for transfers between devices: 19.3 us -> 14.4 us
  Pallas kernels: 12.2 us -> 14.4 us
    ppermute x15 -> x9, waiting for transfers between devices: 16.7 us -> 2.5 us  [send(): return lax.ppermute(block, 'inst', [(i, i ^ s) for i in range(n)])]
    all_to_all x0 -> x1, waiting for transfers between devices: none -> 10.6 us  [shards(): lax.all_to_all(home, 'inst', 0, 0, axis_index_groups=groups, tiled=True)]
    all_to_all x0 -> x1, starting transfers between devices: none -> 6.2 us  [shards(): lax.all_to_all(home, 'inst', 0, 0, axis_index_groups=groups, tiled=True)]
    pallas_call x4, Pallas kernels: 12.2 us -> 14.4 us  [the longest x1 5.89 us: shards(): pl.pallas_call(functools.partial(first_kernel, half, span), out_shape=[ja...]
    ppermute x2, waiting for transfers between devices: 2.68 us -> 1.34 us  [swap(): return lax.ppermute(partial, 'tp', [(0, 1), (1, 0)])]
    ppermute x15 -> x9, starting transfers between devices: 29.2 us -> 28.9 us  [send(): return lax.ppermute(block, 'inst', [(i, i ^ s) for i in range(n)])]
  transfers between devices with their start and end apart: 17 -> 12, of which waited for: 8 -> 3; matrix products, arithmetic and copies ran while one was open for 0% -> 0% of each run, Pallas kernels for 12% -> 14%
where the time goes in v4:
time: 65.8 us; the launch traced here: 65.4 us
  starting transfers between devices  35.2 us (53%)
  Pallas kernels  14.4 us (22%)
  waiting for transfers between devices  14.4 us (22%)
  between operations  0.7 us (1%)
  other arithmetic  0.69 us (1%)
    ppermute x9, starting transfers between devices, send(): return lax.ppermute(block, 'inst', [(i, i ^ s) for i in range(n)])  28.9 us
    all_to_all x1, waiting for transfers between devices, shards(): lax.all_to_all(home, 'inst', 0, 0, axis_index_groups=groups, tiled=True)  10.6 us
    all_to_all x1, starting transfers between devices, shards(): lax.all_to_all(home, 'inst', 0, 0, axis_index_groups=groups, tiled=True)  6.2 us
    pallas_call x1, Pallas kernels, shards(): pl.pallas_call(functools.partial(first_kernel, half, span), out_shape=[ja...  5.89 us
    pallas_call x1, Pallas kernels, shards(): pl.pallas_call(functools.partial(early_kernel, half, len(early), span, le...  2.98 us
    pallas_call x1, Pallas kernels, shards(): pl.pallas_call(functools.partial(pack_kernel, half, pages), out_shape=sha...  2.84 us
    pallas_call x1, Pallas kernels, shards(): pl.pallas_call(functools.partial(late_kernel, LATE, span), out_shape=[jax...  2.68 us
    ppermute x9, waiting for transfers between devices, send(): return lax.ppermute(block, 'inst', [(i, i ^ s) for i in range(n)])  2.5 us
  transfers between devices with their start and end apart: 12, of which 3 were waited for; matrix products, arithmetic and copies ran while one was open for 0% of the time, Pallas kernels for 14%

profile of v4, /device:TPU:0, one launch (start us, length us, event | category | flops | bytes accessed | tf_op | source)
XLA Modules:
  0.0 65.4 jit_solution(9356976482461225459)
XLA Ops:
  0.6 2.8 %pack.1 = (bf16[8,528,128]{2,1,0:T(8,128)(2,1)}, bf16[256,128]{1,0:T(8,128)(2,1)S(1)}, bf16[272,128]{1,0:T(8,128)(2,1)S(1)}, bf16[528,128]{1,0:T(8,128)(2,1)S(1)...) custom-call(s32[4,16]{1,0:T(4,128)} %bitcast.23, ...), custom_call_target="tpu_custom_call" | custom-call | bytes 4325376 | tf_op jit(solution)/shard_map/pack/pallas_call | solution.py:254
  3.5 6.2 %all-to-all-start = ((bf16[8,528,128]{2,1,0:T(8,128)(2,1)}), bf16[8,528,128]{2,1,0:T(8,128)(2,1)S(1)}, u32[]{:S(2)}, u32[]{:S(2)}) async-start(bf16[8,528,128]{2,1,0:T(8,128)(2,1)} %get-tuple-element.27.refs_4_), calls=%async_computation | async-start | bytes 2162688 | tf_op jit(solution)/shard_map/all_to_all | solution.py:297
  9.7 4.0 %collective-permute-start = (bf16[528,128]{1,0:T(8,128)(2,1)S(1)}, bf16[528,128]{1,0:T(8,128)(2,1)S(1)}, u32[]{:S(2)}, u32[]{:S(2)}) collective-permute-start(bf16[528,128]{1,0:T(8,128)(2,1)S(1)} %get-tuple-element.28.refs_7_), channel_id=1, source_target_pairs={{0,18},{2,16},{4,22},{6,20},{8,26},{10,24},{12,30},{14,28},{16,2},... | collective-permute-start | bytes 405512 | tf_op jit(solution)/shard_map/ppermute | solution.py:288
  13.7 1.2 %collective-permute-start.1 = (bf16[528,128]{1,0:T(8,128)(2,1)S(1)}, bf16[528,128]{1,0:T(8,128)(2,1)S(1)}, u32[]{:S(2)}, u32[]{:S(2)}) collective-permute-start(bf16[528,128]{1,0:T(8,128)(2,1)S(1)} %get-tuple-element.29.refs_8_), channel_id=1, source_target_pairs={{0,20},{2,22},{4,16},{6,18},{8,28},{10,30},{12,24},{14,26},{16,4},... | collective-permute-start | bytes 405512 | tf_op jit(solution)/shard_map/ppermute | solution.py:288
  15.0 2.0 %collective-permute-start.2 = (bf16[528,128]{1,0:T(8,128)(2,1)S(1)}, bf16[528,128]{1,0:T(8,128)(2,1)S(1)}, u32[]{:S(2)}, u32[]{:S(2)}) collective-permute-start(bf16[528,128]{1,0:T(8,128)(2,1)S(1)} %get-tuple-element.30.refs_9_), channel_id=1, source_target_pairs={{0,22},{2,20},{4,18},{6,16},{8,30},{10,28},{12,26},{14,24},{16,6},... | collective-permute-start | bytes 405512 | tf_op jit(solution)/shard_map/ppermute | solution.py:288
  17.0 1.8 %collective-permute-start.3 = (bf16[528,128]{1,0:T(8,128)(2,1)S(1)}, bf16[528,128]{1,0:T(8,128)(2,1)S(1)}, u32[]{:S(2)}, u32[]{:S(2)}) collective-permute-start(bf16[528,128]{1,0:T(8,128)(2,1)S(1)} %get-tuple-element.31.refs_10_), channel_id=1, source_target_pairs={{0,24},{2,26},{4,28},{6,30},{8,16},{10,18},{12,20},{14,22},{16,8},... | collective-permute-start | bytes 405512 | tf_op jit(solution)/shard_map/ppermute | solution.py:288
  18.8 3.5 %collective-permute-start.4 = (bf16[528,128]{1,0:T(8,128)(2,1)S(1)}, bf16[528,128]{1,0:T(8,128)(2,1)S(1)}, u32[]{:S(2)}, u32[]{:S(2)}) collective-permute-start(bf16[528,128]{1,0:T(8,128)(2,1)S(1)} %get-tuple-element.32.refs_11_), channel_id=1, source_target_pairs={{0,26},{2,24},{4,30},{6,28},{8,18},{10,16},{12,22},{14,20},{16,10}... | collective-permute-start | bytes 405512 | tf_op jit(solution)/shard_map/ppermute | solution.py:288
  22.3 10.6 %all-to-all-done.refs_0_ = bf16[8,528,128]{2,1,0:T(8,128)(2,1)S(1)} async-done(((bf16[8,528,128]{2,1,0:T(8,128)(2,1)}), bf16[8,528,128]{2,1,0:T(8,128)(2,1)S(1)}, u32[]{:S(2)}, u32[]{:S(2)}) %all-to-all-start) | async-done | bytes 1081376 | tf_op jit(solution)/shard_map/all_to_all | solution.py:297
  32.9 5.9 %first.1 = (bf16[16,4096]{1,0:T(8,128)(2,1)S(1)}, bf16[1024,4096]{1,0:T(8,128)(2,1)S(1)}) custom-call(s32[16]{0:T(128)} %refs_0_.1, s32[16]{0:T(128)} %refs_1_.3, bf16[16,8,128]{2,1,0:T(8,128)(2,1)} %refs_2_.2, bf16[1024,4096]{1,0:T(8,128)(2,1)} %refs_3_.3, bf16[8,528,128]{2,1,0:T(8,128)(2,1)} %get-tuple-element.27.refs_4_, ...), custom_call_target="tpu_custom_call" | custom-call | flops 150994944 | bytes 10485760 | tf_op jit(solution)/shard_map/first/pallas_call | solution.py:298
  38.8 0.0 collective-permute-done.refs_1_
  38.8 2.8 %collective-permute-start.8 = (bf16[528,128]{1,0:T(8,128)(2,1)S(1)}, bf16[528,128]{1,0:T(8,128)(2,1)S(1)}, u32[]{:S(2)}, u32[]{:S(2)}) collective-permute-start(bf16[528,128]{1,0:T(8,128)(2,1)S(1)} %get-tuple-element.41.refs_12_), channel_id=1, source_target_pairs={{0,28},{2,30},{4,24},{6,26},{8,20},{10,22},{12,16},{14,18},{16,12}... | collective-permute-start | bytes 405512 | tf_op jit(solution)/shard_map/ppermute | solution.py:288
  41.6 0.0 collective-permute-done.1.refs_2_
  41.6 2.7 %collective-permute-start.9 = (bf16[528,128]{1,0:T(8,128)(2,1)S(1)}, bf16[528,128]{1,0:T(8,128)(2,1)S(1)}, u32[]{:S(2)}, u32[]{:S(2)}) collective-permute-start(bf16[528,128]{1,0:T(8,128)(2,1)S(1)} %get-tuple-element.42.refs_13_), channel_id=1, source_target_pairs={{0,30},{2,28},{4,26},{6,24},{8,22},{10,20},{12,18},{14,16},{16,14}... | collective-permute-start | bytes 405512 | tf_op jit(solution)/shard_map/ppermute | solution.py:288
  44.3 0.0 collective-permute-done.2.refs_3_
  44.3 0.0 collective-permute-start.5
  44.3 0.0 collective-permute-done.3.refs_4_
  44.3 1.5 %collective-permute-start.7 = (bf16[272,128]{1,0:T(8,128)(2,1)S(1)}, bf16[272,128]{1,0:T(8,128)(2,1)S(1)}, u32[]{:S(2)}, u32[]{:S(2)}) collective-permute-start(bf16[272,128]{1,0:T(8,128)(2,1)S(1)} %get-tuple-element.40.refs_6_), channel_id=1, source_target_pairs={{0,16},{2,18},{4,20},{6,22},{8,24},{10,26},{12,28},{14,30},{16,0},... | collective-permute-start | bytes 208904 | tf_op jit(solution)/shard_map/ppermute | solution.py:288
  45.8 0.0 collective-permute-done.4.refs_5_
  45.8 9.3 %collective-permute-start.6 = (bf16[256,128]{1,0:T(8,128)(2,1)S(1)}, bf16[256,128]{1,0:T(8,128)(2,1)S(1)}, u32[]{:S(2)}, u32[]{:S(2)}) collective-permute-start(bf16[256,128]{1,0:T(8,128)(2,1)S(1)} %get-tuple-element.34.refs_5_), channel_id=1, source_target_pairs={{0,16},{2,18},{4,20},{6,22},{8,24},{10,26},{12,28},{14,30},{16,0},... | collective-permute-start | bytes 196616 | tf_op jit(solution)/shard_map/ppermute | solution.py:288
  55.1 0.0 collective-permute-done.5.refs_10_
  55.1 3.0 %early.1 = (bf16[16,256,128]{2,1,0:T(8,128)(2,1)}, bf16[16,256,128]{2,1,0:T(8,128)(2,1)}, f32[16,8,128]{2,1,0:T(8,128)S(1)}, bf16[16,4096]{1,0:T(8,128)(2,1)}) custom-call(bf16[8,528,128]{2,1,0:T(8,128)(2,1)S(1)} %all-to-all-done.refs_0_, bf16[528,128]{1,0:T(8,128)(2,1)S(1)} %collective-permute-done.refs_1_, ...), custom_call_target="tpu_custom_call" | custom-call | flops 13631488 | bytes 3407872 | tf_op jit(solution)/shard_map/early/pallas_call | solution.py:334
  58.1 2.5 %collective-permute-done.6.refs_0_ = bf16[256,128]{1,0:T(8,128)(2,1)S(1)} collective-permute-done((bf16[256,128]{1,0:T(8,128)(2,1)S(1)}, bf16[256,128]{1,0:T(8,128)(2,1)S(1)}, u32[]{:S(2)}, u32[]{:S(2)}) %collective-permute-start.6) | collective-permute-done | bytes 65568 | tf_op jit(solution)/shard_map/ppermute | solution.py:288
  60.6 0.0 collective-permute-done.7.refs_1_
  60.6 0.0 collective-permute-done.8.refs_2_
  60.6 0.0 collective-permute-done.9.refs_3_
  60.6 2.7 %late.1 = (bf16[16,4096]{1,0:T(8,128)(2,1)S(1)}, bf16[16,256,128]{2,1,0:T(8,128)(2,1)}, bf16[16,256,128]{2,1,0:T(8,128)(2,1)}) custom-call(bf16[256,128]{1,0:T(8,128)(2,1)S(1)} %collective-permute-done.6.refs_0_, bf16[272,128]{1,0:T(8,128)(2,1)S(1)} %collective-permute-done.7.refs_1_, ...), custom_call_target="tpu_custom_call", output_to_operand_aliasing={{1}: (9, {}), {2}: (10, {})} | custom-call | flops 150994944 | bytes 10485760 | tf_op jit(solution)/shard_map/late/pallas_call | solution.py:356
  63.3 0.1 collective-permute-start.10
  63.3 1.3 %collective-permute-done.10 = bf16[16,4096]{1,0:T(8,128)(2,1)S(1)} collective-permute-done((bf16[16,4096]{1,0:T(8,128)(2,1)S(1)}, bf16[16,4096]{1,0:T(8,128)(2,1)S(1)}, u32[]{:S(2)}, u32[]{:S(2)}) %collective-permute-start.10) | collective-permute-done | bytes 131104 | tf_op jit(solution)/shard_map/ppermute | solution.py:201
  64.7 0.7 %add_convert_fusion = bf16[16,4096]{1,0:T(8,128)(2,1)} fusion(bf16[16,4096]{1,0:T(8,128)(2,1)S(1)} %collective-permute-done.10, bf16[16,4096]{1,0:T(8,128)(2,1)S(1)} %get-tuple-element.47), kind=kLoop, calls=%fused_computation | loop fusion | flops 262144 | bytes 393216 | tf_op jit(solution)/shard_map/convert_element_type | solution.py:384
Async XLA Ops:
  3.5 29.4 %all-to-all-start = ((bf16[8,528,128]{2,1,0:T(8,128)(2,1)}), bf16[8,528,128]{2,1,0:T(8,128)(2,1)S(1)}, u32[]{:S(2)}, u32[]{:S(2)}) async-start(bf16[8,528,128]{2,1,0:T(8,128)(2,1)} %get-tuple-element.27.refs_4_), calls=%async_computation | async-start | bytes 2162688 | tf_op jit(solution)/shard_map/all_to_all | solution.py:297
  9.7 29.1 %collective-permute-start = (bf16[528,128]{1,0:T(8,128)(2,1)S(1)}, bf16[528,128]{1,0:T(8,128)(2,1)S(1)}, u32[]{:S(2)}, u32[]{:S(2)}) collective-permute-start(bf16[528,128]{1,0:T(8,128)(2,1)S(1)} %get-tuple-element.28.refs_7_), channel_id=1, source_target_pairs={{0,18},{2,16},{4,22},{6,20},{8,26},{10,24},{12,30},{14,28},{16,2},... | collective-permute-start | bytes 405512 | tf_op jit(solution)/shard_map/ppermute | solution.py:288
  13.7 27.9 %collective-permute-start.1 = (bf16[528,128]{1,0:T(8,128)(2,1)S(1)}, bf16[528,128]{1,0:T(8,128)(2,1)S(1)}, u32[]{:S(2)}, u32[]{:S(2)}) collective-permute-start(bf16[528,128]{1,0:T(8,128)(2,1)S(1)} %get-tuple-element.29.refs_8_), channel_id=1, source_target_pairs={{0,20},{2,22},{4,16},{6,18},{8,28},{10,30},{12,24},{14,26},{16,4},... | collective-permute-start | bytes 405512 | tf_op jit(solution)/shard_map/ppermute | solution.py:288
  15.0 29.3 %collective-permute-start.2 = (bf16[528,128]{1,0:T(8,128)(2,1)S(1)}, bf16[528,128]{1,0:T(8,128)(2,1)S(1)}, u32[]{:S(2)}, u32[]{:S(2)}) collective-permute-start(bf16[528,128]{1,0:T(8,128)(2,1)S(1)} %get-tuple-element.30.refs_9_), channel_id=1, source_target_pairs={{0,22},{2,20},{4,18},{6,16},{8,30},{10,28},{12,26},{14,24},{16,6},... | collective-permute-start | bytes 405512 | tf_op jit(solution)/shard_map/ppermute | solution.py:288
  17.0 27.3 %collective-permute-start.3 = (bf16[528,128]{1,0:T(8,128)(2,1)S(1)}, bf16[528,128]{1,0:T(8,128)(2,1)S(1)}, u32[]{:S(2)}, u32[]{:S(2)}) collective-permute-start(bf16[528,128]{1,0:T(8,128)(2,1)S(1)} %get-tuple-element.31.refs_10_), channel_id=1, source_target_pairs={{0,24},{2,26},{4,28},{6,30},{8,16},{10,18},{12,20},{14,22},{16,8},... | collective-permute-start | bytes 405512 | tf_op jit(solution)/shard_map/ppermute | solution.py:288
  18.8 27.0 %collective-permute-start.4 = (bf16[528,128]{1,0:T(8,128)(2,1)S(1)}, bf16[528,128]{1,0:T(8,128)(2,1)S(1)}, u32[]{:S(2)}, u32[]{:S(2)}) collective-permute-start(bf16[528,128]{1,0:T(8,128)(2,1)S(1)} %get-tuple-element.32.refs_11_), channel_id=1, source_target_pairs={{0,26},{2,24},{4,30},{6,28},{8,18},{10,16},{12,22},{14,20},{16,10}... | collective-permute-start | bytes 405512 | tf_op jit(solution)/shard_map/ppermute | solution.py:288
  38.8 21.8 %collective-permute-start.8 = (bf16[528,128]{1,0:T(8,128)(2,1)S(1)}, bf16[528,128]{1,0:T(8,128)(2,1)S(1)}, u32[]{:S(2)}, u32[]{:S(2)}) collective-permute-start(bf16[528,128]{1,0:T(8,128)(2,1)S(1)} %get-tuple-element.41.refs_12_), channel_id=1, source_target_pairs={{0,28},{2,30},{4,24},{6,26},{8,20},{10,22},{12,16},{14,18},{16,12}... | collective-permute-start | bytes 405512 | tf_op jit(solution)/shard_map/ppermute | solution.py:288
  41.6 19.0 %collective-permute-start.9 = (bf16[528,128]{1,0:T(8,128)(2,1)S(1)}, bf16[528,128]{1,0:T(8,128)(2,1)S(1)}, u32[]{:S(2)}, u32[]{:S(2)}) collective-permute-start(bf16[528,128]{1,0:T(8,128)(2,1)S(1)} %get-tuple-element.42.refs_13_), channel_id=1, source_target_pairs={{0,30},{2,28},{4,26},{6,24},{8,22},{10,20},{12,18},{14,16},{16,14}... | collective-permute-start | bytes 405512 | tf_op jit(solution)/shard_map/ppermute | solution.py:288
  44.3 10.8 %collective-permute-start.5 = (bf16[16,4096]{1,0:T(8,128)(2,1)S(1)}, bf16[16,4096]{1,0:T(8,128)(2,1)S(1)}, u32[]{:S(2)}, u32[]{:S(2)}) collective-permute-start(bf16[16,4096]{1,0:T(8,128)(2,1)S(1)} %get-tuple-element.38.refs_9_), channel_id=1, source_target_pairs={{0,1},{1,0},{2,3},{3,2},{4,5},{5,4},{6,7},{7,6},{8,9},{9,8},{10,11... | collective-permute-start | bytes 393224 | tf_op jit(solution)/shard_map/ppermute | solution.py:201
  44.3 16.3 %collective-permute-start.7 = (bf16[272,128]{1,0:T(8,128)(2,1)S(1)}, bf16[272,128]{1,0:T(8,128)(2,1)S(1)}, u32[]{:S(2)}, u32[]{:S(2)}) collective-permute-start(bf16[272,128]{1,0:T(8,128)(2,1)S(1)} %get-tuple-element.40.refs_6_), channel_id=1, source_target_pairs={{0,16},{2,18},{4,20},{6,22},{8,24},{10,26},{12,28},{14,30},{16,0},... | collective-permute-start | bytes 208904 | tf_op jit(solution)/shard_map/ppermute | solution.py:288
  45.8 14.8 %collective-permute-start.6 = (bf16[256,128]{1,0:T(8,128)(2,1)S(1)}, bf16[256,128]{1,0:T(8,128)(2,1)S(1)}, u32[]{:S(2)}, u32[]{:S(2)}) collective-permute-start(bf16[256,128]{1,0:T(8,128)(2,1)S(1)} %get-tuple-element.34.refs_5_), channel_id=1, source_target_pairs={{0,16},{2,18},{4,20},{6,22},{8,24},{10,26},{12,28},{14,30},{16,0},... | collective-permute-start | bytes 196616 | tf_op jit(solution)/shard_map/ppermute | solution.py:288
  63.3 1.4 %collective-permute-start.10 = (bf16[16,4096]{1,0:T(8,128)(2,1)S(1)}, bf16[16,4096]{1,0:T(8,128)(2,1)S(1)}, u32[]{:S(2)}, u32[]{:S(2)}) collective-permute-start(bf16[16,4096]{1,0:T(8,128)(2,1)S(1)} %get-tuple-element.47), channel_id=1, source_target_pairs={{0,1},{1,0},{2,3},{3,2},{4,5},{5,4},{6,7},{7,6},{8,9},{9,8},{10,11... | collective-permute-start | bytes 393224 | tf_op jit(solution)/shard_map/ppermute | solution.py:201

commit v5 on v4

--- a/solution.py
+++ b/solution.py
@@ -10,7 +10,7 @@
 NEG = -1e30
 TAIL = 16
 CHUNKS = 8
-AHEAD = 5
+AHEAD = 6
 LATE = 3
 VMEM_BYTES = 24 * 1024 * 1024
 
@@ -48,32 +48,27 @@
         copy.wait()
 
 
-def views(ref, span):
-    return ref.at[pl.ds(0, span)], ref.at[pl.ds(span, span)], ref.at[pl.ds(2 * span, TAIL)]
-
-
-def parcels_of(refs, half, span):
-    home, keys, rest, others = refs[0], refs[1], refs[2], refs[3:]
-    near = [views(home.at[d], span) for d in range(half)]
-    split = (keys, rest.at[pl.ds(0, span)], rest.at[pl.ds(span, TAIL)])
-    return near + [split] + [views(ref, span) for ref in others]
-
-
-def sources(source, half):
+def parcels_of(refs, span):
+    return [
+        (ref.at[pl.ds(0, span)], ref.at[pl.ds(span, span)], ref.at[pl.ds(2 * span, TAIL)]) for ref in refs
+    ]
+
+
+def sources(source, steps):
     me = lax.axis_index("inst")
-    base = me // half * half
-    return [source[base + d] for d in range(half)] + [source[me ^ s] for s in range(half, 2 * half)]
-
-
-def pack_kernel(half, pages, *refs):
-    far, outs = refs[:8], refs[8 : 10 + half]
-    table, lengths, dest, slot, key_one, value_one, key_pool, value_pool, source, sems = refs[10 + half :]
+    return [source[me ^ s] for s in steps]
+
+
+def pack_kernel(steps, pages, *refs):
+    n = len(steps)
+    far, outs = refs[:8], refs[8 : 8 + n]
+    table, lengths, dest, slot, key_one, value_one, key_pool, value_pool, source, sems = refs[8 + n :]
     copies = begin(list(zip(far, (table, lengths, dest, slot, key_one, value_one, key_pool, value_pool))), sems)
     size = key_pool.shape[1]
-    parcels = parcels_of(outs, half, pages * size)
+    parcels = parcels_of(outs, pages * size)
     finish(copies[:6])
-    invert(dest, source, 2 * half)
-    at = sources(source, half)
+    invert(dest, source, n)
+    at = sources(source, steps)
     tokens = (key_one[...].astype(jnp.float32), value_one[...].astype(jnp.float32))
     for which, pool in ((0, key_pool), (1, value_pool)):
         copies[6 + which].wait()
@@ -116,14 +111,15 @@
         out[:, c * width : (c + 1) * width] = part.astype(jnp.bfloat16)
 
 
-def first_kernel(half, span, *refs):
-    far, parcels, out, weight = refs[:4], refs[4 : 6 + half], refs[6 + half], refs[7 + half]
-    lengths, dest, query, source, mixed, sems = refs[8 + half :]
+def first_kernel(steps, span, *refs):
+    n = len(steps)
+    far, parcels, out, weight = refs[:4], refs[4 : 4 + n], refs[4 + n], refs[5 + n]
+    lengths, dest, query, source, mixed, sems = refs[6 + n :]
     copies = begin(list(zip(far, (lengths, dest, query, weight))), sems)
-    parcels = parcels_of(parcels, half, span)
+    parcels = parcels_of(parcels, span)
     finish(copies[:3])
-    invert(dest, source, 2 * half)
-    at = sources(source, half)
+    invert(dest, source, n)
+    at = sources(source, steps)
     results = attend(
         [query[r] for r in at],
         [parcel[0][...] for parcel in parcels],
@@ -165,33 +161,27 @@
     return outgoing
 
 
-def early_kernel(half, count, span, pair, *refs):
-    arrived, far, halves = refs[: count + 1], refs[count + 1 : count + 4], refs[count + 4 : count + 4 + pair]
-    key_cache, value_cache, mixed = refs[count + 4 + pair : count + 7 + pair]
-    query, key_two, value_two, new_k, new_v, held, sems, osems = refs[-8:]
+def early_kernel(count, span, pair, *refs):
+    arrived, far, halves = refs[:count], refs[count : count + 3], refs[count + 3 : count + 3 + pair]
+    key_cache, value_cache, mixed, query, new_k, new_v = refs[count + 3 + pair : count + 9 + pair]
+    key_two, value_two, held, sems, osems = refs[-5:]
     copies = begin(list(zip(far, (query, key_two, value_two))), sems)
     if pair:
-        out = refs[count + 7 + pair]
+        out = refs[count + 9 + pair]
         both = halves[0][...].astype(jnp.float32) + halves[1][...].astype(jnp.float32)
         out[...] = both.astype(jnp.bfloat16)
     finish(copies)
     new_k[...] = key_two[...].astype(jnp.float32)
     new_v[...] = value_two[...].astype(jnp.float32)
-    parcels = [views(arrived[0].at[d], span) for d in range(half)] + [views(ref, span) for ref in arrived[1:]]
+    parcels = parcels_of(arrived, span)
     finish(place(parcels, query, new_k, new_v, key_cache, value_cache, held, mixed, osems))
 
 
 def late_kernel(count, span, *refs):
-    arrived, far, weight, before = refs[: count + 1], refs[count + 1 : count + 4], refs[count + 4], refs[count + 5]
-    out, key_cache, value_cache = refs[count + 8 : count + 11]
-    query, key_two, value_two, new_k, new_v, held, mixed, sems, osems = refs[-9:]
-    copies = begin(list(zip(far, (query, key_two, value_two))), sems)
+    arrived, (query, new_k, new_v, weight, before) = refs[:count], refs[count : count + 5]
+    out, key_cache, value_cache, held, mixed, osems = refs[count + 7 :]
     mixed[...] = before[...]
-    finish(copies)
-    new_k[...] = key_two[...].astype(jnp.float32)
-    new_v[...] = value_two[...].astype(jnp.float32)
-    keys, rest = arrived[0], arrived[1]
-    parcels = [(keys, rest.at[pl.ds(0, span)], rest.at[pl.ds(span, TAIL)])] + [views(ref, span) for ref in arrived[2:]]
+    parcels = parcels_of(arrived, span)
     outgoing = place(parcels, query, new_k, new_v, key_cache, value_cache, held, mixed, osems)
     project(mixed, weight, out)
     finish(outgoing)
@@ -207,6 +197,21 @@
 
 def hbm(x):
     return pltpu.with_memory_space_constraint(x, pltpu.HBM)
+
+
+def step_order(n):
+    half = n // 2
+    crossing = [s for pair in zip(range(half, half + half // 2), range(half + half // 2, n)) for s in pair]
+    staying = list(range(1, half))
+    order = []
+    for kind in "cnnccncnccncncn":
+        queue = crossing if kind == "c" else staying
+        if queue:
+            order.append(queue.pop(0))
+    while crossing or staying:
+        order += crossing[:1] + staying[:1]
+        del crossing[:1], staying[:1]
+    return order
 
 
 def shards(
@@ -231,7 +236,7 @@
     heads = query_one.shape[1]
     depth, columns = out_weight.shape
     span = pages * size
-    assert kv_heads == 1 and slots == n and n % 2 == 0 and span <= 256
+    assert kv_heads == 1 and slots == n and n >= 16 and span <= 256
     key_pages = key_pages.reshape(pool, size, width)
     value_pages = value_pages.reshape(pool, size, width)
     key_one = key_one.reshape(slots, width)
@@ -244,15 +249,16 @@
     params = pltpu.CompilerParams(vmem_limit_bytes=VMEM_BYTES)
     bf16, f32, i32 = jnp.bfloat16, jnp.float32, jnp.int32
     rows = 2 * span + TAIL
-    half = n // 2
-
-    def block(*lead):
-        return jax.ShapeDtypeStruct((*lead, width), bf16)
-
-    shapes = [block(half, rows), block(span), block(span + TAIL)] + [block(rows)] * (half - 1)
+    order = step_order(n)
+    steps = [0] + order
+
+    def block(height):
+        return jax.ShapeDtypeStruct((height, width), bf16)
+
+    shapes = [block(rows)] * n
 
     packed = pl.pallas_call(
-        functools.partial(pack_kernel, half, pages),
+        functools.partial(pack_kernel, steps, pages),
         out_shape=shapes,
         in_specs=[far] * 8,
         out_specs=[vmem] * len(shapes),
@@ -284,19 +290,17 @@
 
     flops = 4 * slots * heads * span * width + 2 * slots * depth * columns
     moved = 2 * depth * columns + 4 * slots * span * width
-    def send(s, block):
-        return lax.ppermute(block, "inst", [(i, i ^ s) for i in range(n)])
-
-    def after(x, y):
-        return lax.optimization_barrier((x, y))[0]
-
-    home, split_keys, split_rest, others = packed[0], packed[1], packed[2], packed[3:]
-    arrived_keys = send(half, split_keys)
-    arrived = [send(half + 1 + i, others[i]) for i in range(AHEAD)]
-    groups = [list(range(half)), list(range(half, n))]
-    arrived_home = lax.all_to_all(home, "inst", 0, 0, axis_index_groups=groups, tiled=True)
+    arrived = [packed[0]]
+
+    def send(i, *after):
+        block = lax.optimization_barrier((packed[i], *after))[0] if after else packed[i]
+        arrived.append(lax.ppermute(block, "inst", [(d, d ^ steps[i]) for d in range(n)]))
+
+    for i in range(1, 1 + AHEAD):
+        send(i)
+    query_late = lax.optimization_barrier((query_one, arrived[1]))[0]
     partial_one, weight = pl.pallas_call(
-        functools.partial(first_kernel, half, span),
+        functools.partial(first_kernel, steps, span),
         out_shape=[
             jax.ShapeDtypeStruct((slots, columns), bf16),
             jax.ShapeDtypeStruct((depth, columns), bf16),
@@ -314,30 +318,27 @@
         compiler_params=params,
         cost_estimate=pl.CostEstimate(flops=flops, bytes_accessed=moved, transcendentals=slots * heads * span),
         name="first",
-    )(hbm(lengths), hbm(dest_instance), hbm(after(query_one, arrived_home)), hbm(out_weight), *packed)
-
-    arrived += [send(half + 1 + i, after(others[i], partial_one)) for i in range(AHEAD, half - 1)]
-    arrived_rest = send(half, after(split_rest, partial_one))
-    early, late = arrived[: half - LATE], [arrived_keys, arrived_rest] + arrived[half - LATE :]
-
+    )(hbm(lengths), hbm(dest_instance), hbm(query_late), hbm(out_weight), *packed)
+
+    for i in range(1 + AHEAD, n):
+        send(i, partial_one)
+    early, late = arrived[:-LATE], arrived[-LATE:]
     halves = [partial_one, swap(partial_one)] if tp == 2 else []
+
     cache = jax.ShapeDtypeStruct((slots, span, width), bf16)
-    common = [
-        pltpu.VMEM((slots, heads, width), bf16),
-        pltpu.VMEM((slots, width), bf16),
-        pltpu.VMEM((slots, width), bf16),
-        pltpu.VMEM((slots, width), f32),
-        pltpu.VMEM((slots, width), f32),
-    ]
     mixed = jax.ShapeDtypeStruct((slots, heads, width), f32)
-    some = half + len(early)
+    some = len(early)
     results = pl.pallas_call(
-        functools.partial(early_kernel, half, len(early), span, len(halves)),
-        out_shape=[cache, cache, mixed] + [jax.ShapeDtypeStruct((slots, columns), bf16)] * (len(halves) // 2),
-        in_specs=[vmem] * (1 + len(early)) + [far] * 3 + [vmem] * len(halves),
-        out_specs=[far, far, vmem] + [vmem] * (len(halves) // 2),
-        scratch_shapes=common
-        + [
+        functools.partial(early_kernel, some, span, len(halves)),
+        out_shape=[cache, cache, mixed]
+        + [jax.ShapeDtypeStruct((slots, heads, width), bf16)]
+        + [jax.ShapeDtypeStruct((slots, width), f32)] * 2
+        + [jax.ShapeDtypeStruct((slots, columns), bf16)] * (len(halves) // 2),
+        in_specs=[vmem] * some + [far] * 3 + [vmem] * len(halves),
+        out_specs=[far, far] + [vmem] * (4 + len(halves) // 2),
+        scratch_shapes=[
+            pltpu.VMEM((slots, width), bf16),
+            pltpu.VMEM((slots, width), bf16),
             pltpu.VMEM((2, some, span, width), bf16),
             pltpu.SemaphoreType.DMA((3,)),
             pltpu.SemaphoreType.DMA((2, some)),
@@ -349,21 +350,19 @@
             transcendentals=some * heads * span,
         ),
         name="early",
-    )(near(arrived_home), *early, hbm(query_two), hbm(key_two), hbm(value_two), *halves)
-    key_cache, value_cache, mixed = results[:3]
-    out_one = results[3] if halves else lax.psum(partial_one, "tp")
+    )(*early, hbm(query_two), hbm(key_two), hbm(value_two), *halves)
+    key_cache, value_cache, *carried = results[:6]
+    out_one = results[6] if halves else lax.psum(partial_one, "tp")
 
     partial_two, key_cache, value_cache = pl.pallas_call(
         functools.partial(late_kernel, LATE, span),
         out_shape=[jax.ShapeDtypeStruct((slots, columns), bf16), cache, cache],
-        in_specs=[vmem] * len(late) + [far] * 3 + [vmem] * 2 + [far] * 2,
+        in_specs=[vmem] * (len(late) + 5) + [far] * 2,
         out_specs=[vmem, far, far],
         input_output_aliases={len(late) + 5: 1, len(late) + 6: 2},
-        scratch_shapes=common
-        + [
+        scratch_shapes=[
             pltpu.VMEM((2, LATE, span, width), bf16),
             pltpu.VMEM((slots, heads, width), f32),
-            pltpu.SemaphoreType.DMA((3,)),
             pltpu.SemaphoreType.DMA((2, LATE)),
         ],
         compiler_params=params,
@@ -371,11 +370,9 @@
         name="late",
     )(
         *late,
-        hbm(query_two),
-        hbm(key_two),
-        hbm(value_two),
+        *[near(x) for x in carried[1:]],
         near(weight),
-        mixed,
+        near(carried[0]),
         hbm(key_cache),
         hbm(value_cache),
     )

time: 65.8 us -> 63.5 us (0.965)
  Pallas kernels: 14.4 us -> 11.4 us
  waiting for transfers between devices: 14.4 us -> 16.9 us
  starting transfers between devices: 35.2 us -> 33.6 us
    ppermute x9 -> x15, waiting for transfers between devices: 2.5 us -> 14.2 us  [send(): lax.ppermute(block, 'inst', [(d, d ^ steps[i]) for d in range(n)])]
    all_to_all x1 -> x0, waiting for transfers between devices: 10.6 us -> none  [shards(): lax.all_to_all(home, 'inst', 0, 0, axis_index_groups=groups, tiled=True)]
    all_to_all x1 -> x0, starting transfers between devices: 6.2 us -> none  [shards(): lax.all_to_all(home, 'inst', 0, 0, axis_index_groups=groups, tiled=True)]
    ppermute x9 -> x15, starting transfers between devices: 28.9 us -> 33.5 us  [send(): lax.ppermute(block, 'inst', [(d, d ^ steps[i]) for d in range(n)])]
    pallas_call x3, Pallas kernels: 11.7 us -> 9.51 us  [the longest x1 4.66 us: shards(): pl.pallas_call(functools.partial(first_kernel, steps, span), out_shape=[j...]
    ppermute x2, waiting for transfers between devices: 1.34 us -> 2.68 us  [swap(): return lax.ppermute(partial, 'tp', [(0, 1), (1, 0)])]
    pallas_call x1, Pallas kernels: 2.68 us -> 1.9 us  [shards(): pl.pallas_call(functools.partial(late_kernel, LATE, span), out_shape=[jax...]
  transfers between devices with their start and end apart: 12 -> 17, of which waited for: 3 -> 6; matrix products, arithmetic and copies ran while one was open for 0% -> 0% of each run, Pallas kernels for 14% -> 12%
where the time goes in v5:
time: 63.5 us; the launch traced here: 63.3 us
  starting transfers between devices  33.6 us (53%)
  waiting for transfers between devices  16.9 us (27%)
  Pallas kernels  11.4 us (18%)
  between operations  0.72 us (1%)
  other arithmetic  0.69 us (1%)
    ppermute x15, starting transfers between devices, send(): lax.ppermute(block, 'inst', [(d, d ^ steps[i]) for d in range(n)])  33.5 us
    ppermute x15, waiting for transfers between devices, send(): lax.ppermute(block, 'inst', [(d, d ^ steps[i]) for d in range(n)])  14.2 us
    pallas_call x1, Pallas kernels, shards(): pl.pallas_call(functools.partial(first_kernel, steps, span), out_shape=[j...  4.66 us
    pallas_call x1, Pallas kernels, shards(): pl.pallas_call(functools.partial(early_kernel, some, span, len(halves)),...  2.98 us
    ppermute x2, waiting for transfers between devices, swap(): return lax.ppermute(partial, 'tp', [(0, 1), (1, 0)])  2.68 us
    pallas_call x1, Pallas kernels, shards(): pl.pallas_call(functools.partial(late_kernel, LATE, span), out_shape=[jax...  1.9 us
    pallas_call x1, Pallas kernels, shards(): pl.pallas_call(functools.partial(pack_kernel, steps, pages), out_shape=sh...  1.87 us
  transfers between devices with their start and end apart: 17, of which 6 were waited for; matrix products, arithmetic and copies ran while one was open for 0% of the time, Pallas kernels for 12%

profile of v5, /device:TPU:0, one launch (start us, length us, event | category | flops | bytes accessed | tf_op | source)
XLA Modules:
  0.0 63.3 jit_solution(11939829038673241140)
XLA Ops:
  0.6 1.9 %pack.1 = (bf16[528,128]{1,0:T(8,128)(2,1)S(1)}, bf16[528,128]{1,0:T(8,128)(2,1)S(1)}, bf16[528,128]{1,0:T(8,128)(2,1)S(1)}, bf16[528,128]{1,0:T(8,128)(2,1)S(1)...) custom-call(s32[4,16]{1,0:T(4,128)} %bitcast.21, ...), custom_call_target="tpu_custom_call" | custom-call | bytes 4325376 | tf_op jit(solution)/shard_map/pack/pallas_call | solution.py:260
  2.5 4.1 %collective-permute-start = (bf16[528,128]{1,0:T(8,128)(2,1)S(1)}, bf16[528,128]{1,0:T(8,128)(2,1)S(1)}, u32[]{:S(2)}, u32[]{:S(2)}) collective-permute-start(bf16[528,128]{1,0:T(8,128)(2,1)S(1)} %get-tuple-element.43.refs_5_), channel_id=1, source_target_pairs={{0,16},{2,18},{4,20},{6,22},{8,24},{10,26},{12,28},{14,30},{16,0},... | collective-permute-start | bytes 405512 | tf_op jit(solution)/shard_map/ppermute | solution.py:297
  6.6 1.5 %collective-permute-start.1 = (bf16[528,128]{1,0:T(8,128)(2,1)S(1)}, bf16[528,128]{1,0:T(8,128)(2,1)S(1)}, u32[]{:S(2)}, u32[]{:S(2)}) collective-permute-start(bf16[528,128]{1,0:T(8,128)(2,1)S(1)} %get-tuple-element.44.refs_6_), channel_id=1, source_target_pairs={{0,2},{2,0},{4,6},{6,4},{8,10},{10,8},{12,14},{14,12},{16,18},{18,... | collective-permute-start | bytes 405512 | tf_op jit(solution)/shard_map/ppermute | solution.py:297
  8.1 1.5 %collective-permute-start.2 = (bf16[528,128]{1,0:T(8,128)(2,1)S(1)}, bf16[528,128]{1,0:T(8,128)(2,1)S(1)}, u32[]{:S(2)}, u32[]{:S(2)}) collective-permute-start(bf16[528,128]{1,0:T(8,128)(2,1)S(1)} %get-tuple-element.45.refs_7_), channel_id=1, source_target_pairs={{0,4},{2,6},{4,0},{6,2},{8,12},{10,14},{12,8},{14,10},{16,20},{18,... | collective-permute-start | bytes 405512 | tf_op jit(solution)/shard_map/ppermute | solution.py:297
  9.6 1.3 %collective-permute-start.3 = (bf16[528,128]{1,0:T(8,128)(2,1)S(1)}, bf16[528,128]{1,0:T(8,128)(2,1)S(1)}, u32[]{:S(2)}, u32[]{:S(2)}) collective-permute-start(bf16[528,128]{1,0:T(8,128)(2,1)S(1)} %get-tuple-element.46.refs_8_), channel_id=1, source_target_pairs={{0,24},{2,26},{4,28},{6,30},{8,16},{10,18},{12,20},{14,22},{16,8},... | collective-permute-start | bytes 405512 | tf_op jit(solution)/shard_map/ppermute | solution.py:297
  11.0 1.7 %collective-permute-start.4 = (bf16[528,128]{1,0:T(8,128)(2,1)S(1)}, bf16[528,128]{1,0:T(8,128)(2,1)S(1)}, u32[]{:S(2)}, u32[]{:S(2)}) collective-permute-start(bf16[528,128]{1,0:T(8,128)(2,1)S(1)} %get-tuple-element.47.refs_9_), channel_id=1, source_target_pairs={{0,18},{2,16},{4,22},{6,20},{8,26},{10,24},{12,30},{14,28},{16,2},... | collective-permute-start | bytes 405512 | tf_op jit(solution)/shard_map/ppermute | solution.py:297
  12.6 7.1 %collective-permute-done.refs_1_ = bf16[528,128]{1,0:T(8,128)(2,1)S(1)} collective-permute-done((bf16[528,128]{1,0:T(8,128)(2,1)S(1)}, bf16[528,128]{1,0:T(8,128)(2,1)S(1)}, u32[]{:S(2)}, u32[]{:S(2)}) %collective-permute-start) | collective-permute-done | bytes 135200 | tf_op jit(solution)/shard_map/ppermute | solution.py:297
  19.7 2.8 %collective-permute-start.5 = (bf16[528,128]{1,0:T(8,128)(2,1)S(1)}, bf16[528,128]{1,0:T(8,128)(2,1)S(1)}, u32[]{:S(2)}, u32[]{:S(2)}) collective-permute-start(bf16[528,128]{1,0:T(8,128)(2,1)S(1)} %get-tuple-element.48.refs_10_), channel_id=1, source_target_pairs={{0,6},{2,4},{4,2},{6,0},{8,14},{10,12},{12,10},{14,8},{16,22},{18,... | collective-permute-start | bytes 405512 | tf_op jit(solution)/shard_map/ppermute | solution.py:297
  22.5 4.7 %first.1 = (bf16[16,4096]{1,0:T(8,128)(2,1)S(1)}, bf16[1024,4096]{1,0:T(8,128)(2,1)S(1)}) custom-call(s32[16]{0:T(128)} %refs_0_.1, s32[16]{0:T(128)} %refs_1_.3, bf16[16,8,128]{2,1,0:T(8,128)(2,1)} %refs_2_.2, bf16[1024,4096]{1,0:T(8,128)(2,1)} %refs_3_.3, bf16[528,128]{1,0:T(8,128)(2,1)S(1)} %get-tuple-element.42.refs_4_.refs_0_, ...), custom_call_target="tpu_custom_call" | custom-call | flops 150994944 | bytes 10485760 | tf_op jit(solution)/shard_map/first/pallas_call | solution.py:302
  27.2 0.0 collective-permute-done.1.refs_2_
  27.2 2.5 %collective-permute-start.6 = (bf16[528,128]{1,0:T(8,128)(2,1)S(1)}, bf16[528,128]{1,0:T(8,128)(2,1)S(1)}, u32[]{:S(2)}, u32[]{:S(2)}) collective-permute-start(bf16[528,128]{1,0:T(8,128)(2,1)S(1)} %get-tuple-element.60.refs_11_), channel_id=1, source_target_pairs={{0,26},{2,24},{4,30},{6,28},{8,18},{10,16},{12,22},{14,20},{16,10}... | collective-permute-start | bytes 405512 | tf_op jit(solution)/shard_map/ppermute | solution.py:297
  29.7 0.0 collective-permute-done.2.refs_3_
  29.7 0.0 collective-permute-start.7
  29.7 0.0 collective-permute-done.3.refs_4_
  29.7 1.5 %collective-permute-start.8 = (bf16[528,128]{1,0:T(8,128)(2,1)S(1)}, bf16[528,128]{1,0:T(8,128)(2,1)S(1)}, u32[]{:S(2)}, u32[]{:S(2)}) collective-permute-start(bf16[528,128]{1,0:T(8,128)(2,1)S(1)} %get-tuple-element.62.refs_13_), channel_id=1, source_target_pairs={{0,20},{2,22},{4,16},{6,18},{8,28},{10,30},{12,24},{14,26},{16,4},... | collective-permute-start | bytes 405512 | tf_op jit(solution)/shard_map/ppermute | solution.py:297
  31.2 0.0 collective-permute-done.4.refs_5_
  31.2 3.8 %collective-permute-start.9 = (bf16[528,128]{1,0:T(8,128)(2,1)S(1)}, bf16[528,128]{1,0:T(8,128)(2,1)S(1)}, u32[]{:S(2)}, u32[]{:S(2)}) collective-permute-start(bf16[528,128]{1,0:T(8,128)(2,1)S(1)} %get-tuple-element.63.refs_14_), channel_id=1, source_target_pairs={{0,28},{2,30},{4,24},{6,26},{8,20},{10,22},{12,16},{14,18},{16,12}... | collective-permute-start | bytes 405512 | tf_op jit(solution)/shard_map/ppermute | solution.py:297
  35.0 0.0 collective-permute-done.5.refs_6_
  35.0 0.0 collective-permute-start.12
  35.0 1.3 %collective-permute-done.12.refs_17_ = bf16[16,4096]{1,0:T(8,128)(2,1)S(1)} collective-permute-done((bf16[16,4096]{1,0:T(8,128)(2,1)S(1)}, bf16[16,4096]{1,0:T(8,128)(2,1)S(1)}, u32[]{:S(2)}, u32[]{:S(2)}) %collective-permute-start.12) | collective-permute-done | bytes 131104 | tf_op jit(solution)/shard_map/ppermute | solution.py:191
  36.3 0.1 collective-permute-start.10
  36.4 0.0 collective-permute-done.6.refs_7_
  36.4 2.3 %collective-permute-start.11 = (bf16[528,128]{1,0:T(8,128)(2,1)S(1)}, bf16[528,128]{1,0:T(8,128)(2,1)S(1)}, u32[]{:S(2)}, u32[]{:S(2)}) collective-permute-start(bf16[528,128]{1,0:T(8,128)(2,1)S(1)} %get-tuple-element.65.refs_16_), channel_id=1, source_target_pairs={{0,22},{2,20},{4,18},{6,16},{8,30},{10,28},{12,26},{14,24},{16,6},... | collective-permute-start | bytes 405512 | tf_op jit(solution)/shard_map/ppermute | solution.py:297
  38.8 0.3 collective-permute-done.7.refs_8_
  39.1 1.3 %collective-permute-start.13 = (bf16[528,128]{1,0:T(8,128)(2,1)S(1)}, bf16[528,128]{1,0:T(8,128)(2,1)S(1)}, u32[]{:S(2)}, u32[]{:S(2)}) collective-permute-start(bf16[528,128]{1,0:T(8,128)(2,1)S(1)} %get-tuple-element.67.refs_17_), channel_id=1, source_target_pairs={{0,12},{2,14},{4,8},{6,10},{8,4},{10,6},{12,0},{14,2},{16,28},{18,... | collective-permute-start | bytes 405512 | tf_op jit(solution)/shard_map/ppermute | solution.py:297
  40.4 3.5 %collective-permute-done.8.refs_9_ = bf16[528,128]{1,0:T(8,128)(2,1)S(1)} collective-permute-done((bf16[528,128]{1,0:T(8,128)(2,1)S(1)}, bf16[528,128]{1,0:T(8,128)(2,1)S(1)}, u32[]{:S(2)}, u32[]{:S(2)}) %collective-permute-start.8) | collective-permute-done | bytes 135200 | tf_op jit(solution)/shard_map/ppermute | solution.py:297
  43.9 2.3 %collective-permute-start.14 = (bf16[528,128]{1,0:T(8,128)(2,1)S(1)}, bf16[528,128]{1,0:T(8,128)(2,1)S(1)}, u32[]{:S(2)}, u32[]{:S(2)}) collective-permute-start(bf16[528,128]{1,0:T(8,128)(2,1)S(1)} %get-tuple-element.68.refs_18_), channel_id=1, source_target_pairs={{0,30},{2,28},{4,26},{6,24},{8,22},{10,20},{12,18},{14,16},{16,14}... | collective-permute-start | bytes 405512 | tf_op jit(solution)/shard_map/ppermute | solution.py:297
  46.2 0.0 collective-permute-done.9.refs_10_
  46.2 6.8 %collective-permute-start.15 = (bf16[528,128]{1,0:T(8,128)(2,1)S(1)}, bf16[528,128]{1,0:T(8,128)(2,1)S(1)}, u32[]{:S(2)}, u32[]{:S(2)}) collective-permute-start(bf16[528,128]{1,0:T(8,128)(2,1)S(1)} %get-tuple-element.69.refs_19_), channel_id=1, source_target_pairs={{0,14},{2,12},{4,10},{6,8},{8,6},{10,4},{12,2},{14,0},{16,30},{18,... | collective-permute-start | bytes 405512 | tf_op jit(solution)/shard_map/ppermute | solution.py:297
  53.0 0.0 collective-permute-done.10.refs_11_
  53.0 3.2 %collective-permute-done.11.refs_12_ = bf16[528,128]{1,0:T(8,128)(2,1)S(1)} collective-permute-done((bf16[528,128]{1,0:T(8,128)(2,1)S(1)}, bf16[528,128]{1,0:T(8,128)(2,1)S(1)}, u32[]{:S(2)}, u32[]{:S(2)}) %collective-permute-start.11) | collective-permute-done | bytes 135200 | tf_op jit(solution)/shard_map/ppermute | solution.py:297
  56.3 3.0 %early.1 = (bf16[16,256,128]{2,1,0:T(8,128)(2,1)}, bf16[16,256,128]{2,1,0:T(8,128)(2,1)}, f32[16,8,128]{2,1,0:T(8,128)S(1)}, bf16[16,8,128]{2,1,0:T(8,128)(2,1)S...) custom-call(bf16[528,128]{1,0:T(8,128)(2,1)S(1)} %get-tuple-element.42.refs_4_.refs_0_, ...), custom_call_target="tpu_custom_call" | custom-call | flops 13631488 | bytes 3407872 | tf_op jit(solution)/shard_map/early/pallas_call | solution.py:331
  59.2 0.0 collective-permute-done.13.refs_0_
  59.3 0.0 collective-permute-done.14.refs_1_
  59.3 0.0 collective-permute-done.15.refs_2_
  59.3 1.9 %late.1 = (bf16[16,4096]{1,0:T(8,128)(2,1)S(1)}, bf16[16,256,128]{2,1,0:T(8,128)(2,1)}, bf16[16,256,128]{2,1,0:T(8,128)(2,1)}) custom-call(bf16[528,128]{1,0:T(8,128)(2,1)S(1)} %collective-permute-done.13.refs_0_, bf16[528,128]{1,0:T(8,128)(2,1)S(1)} %collective-permute-done.14.refs_1_, ...), custom_call_target="tpu_custom_call", output_to_operand_aliasing={{1}: (8, {}), {2}: (9, {})} | custom-call | flops 150994944 | bytes 10485760 | tf_op jit(solution)/shard_map/late/pallas_call | solution.py:357
  61.2 0.1 collective-permute-start.16
  61.3 1.3 %collective-permute-done.16 = bf16[16,4096]{1,0:T(8,128)(2,1)S(1)} collective-permute-done((bf16[16,4096]{1,0:T(8,128)(2,1)S(1)}, bf16[16,4096]{1,0:T(8,128)(2,1)S(1)}, u32[]{:S(2)}, u32[]{:S(2)}) %collective-permute-start.16) | collective-permute-done | bytes 131104 | tf_op jit(solution)/shard_map/ppermute | solution.py:191
  62.6 0.7 %add_convert_fusion = bf16[16,4096]{1,0:T(8,128)(2,1)} fusion(bf16[16,4096]{1,0:T(8,128)(2,1)S(1)} %collective-permute-done.16, bf16[16,4096]{1,0:T(8,128)(2,1)S(1)} %get-tuple-element.77), kind=kLoop, calls=%fused_computation | loop fusion | flops 262144 | bytes 393216 | tf_op jit(solution)/shard_map/convert_element_type | solution.py:381
Async XLA Ops:
  2.5 17.2 %collective-permute-start = (bf16[528,128]{1,0:T(8,128)(2,1)S(1)}, bf16[528,128]{1,0:T(8,128)(2,1)S(1)}, u32[]{:S(2)}, u32[]{:S(2)}) collective-permute-start(bf16[528,128]{1,0:T(8,128)(2,1)S(1)} %get-tuple-element.43.refs_5_), channel_id=1, source_target_pairs={{0,16},{2,18},{4,20},{6,22},{8,24},{10,26},{12,28},{14,30},{16,0},... | collective-permute-start | bytes 405512 | tf_op jit(solution)/shard_map/ppermute | solution.py:297
  6.6 20.6 %collective-permute-start.1 = (bf16[528,128]{1,0:T(8,128)(2,1)S(1)}, bf16[528,128]{1,0:T(8,128)(2,1)S(1)}, u32[]{:S(2)}, u32[]{:S(2)}) collective-permute-start(bf16[528,128]{1,0:T(8,128)(2,1)S(1)} %get-tuple-element.44.refs_6_), channel_id=1, source_target_pairs={{0,2},{2,0},{4,6},{6,4},{8,10},{10,8},{12,14},{14,12},{16,18},{18,... | collective-permute-start | bytes 405512 | tf_op jit(solution)/shard_map/ppermute | solution.py:297
  8.1 21.6 %collective-permute-start.2 = (bf16[528,128]{1,0:T(8,128)(2,1)S(1)}, bf16[528,128]{1,0:T(8,128)(2,1)S(1)}, u32[]{:S(2)}, u32[]{:S(2)}) collective-permute-start(bf16[528,128]{1,0:T(8,128)(2,1)S(1)} %get-tuple-element.45.refs_7_), channel_id=1, source_target_pairs={{0,4},{2,6},{4,0},{6,2},{8,12},{10,14},{12,8},{14,10},{16,20},{18,... | collective-permute-start | bytes 405512 | tf_op jit(solution)/shard_map/ppermute | solution.py:297
  9.6 20.1 %collective-permute-start.3 = (bf16[528,128]{1,0:T(8,128)(2,1)S(1)}, bf16[528,128]{1,0:T(8,128)(2,1)S(1)}, u32[]{:S(2)}, u32[]{:S(2)}) collective-permute-start(bf16[528,128]{1,0:T(8,128)(2,1)S(1)} %get-tuple-element.46.refs_8_), channel_id=1, source_target_pairs={{0,24},{2,26},{4,28},{6,30},{8,16},{10,18},{12,20},{14,22},{16,8},... | collective-permute-start | bytes 405512 | tf_op jit(solution)/shard_map/ppermute | solution.py:297
  11.0 20.2 %collective-permute-start.4 = (bf16[528,128]{1,0:T(8,128)(2,1)S(1)}, bf16[528,128]{1,0:T(8,128)(2,1)S(1)}, u32[]{:S(2)}, u32[]{:S(2)}) collective-permute-start(bf16[528,128]{1,0:T(8,128)(2,1)S(1)} %get-tuple-element.47.refs_9_), channel_id=1, source_target_pairs={{0,18},{2,16},{4,22},{6,20},{8,26},{10,24},{12,30},{14,28},{16,2},... | collective-permute-start | bytes 405512 | tf_op jit(solution)/shard_map/ppermute | solution.py:297
  19.7 15.3 %collective-permute-start.5 = (bf16[528,128]{1,0:T(8,128)(2,1)S(1)}, bf16[528,128]{1,0:T(8,128)(2,1)S(1)}, u32[]{:S(2)}, u32[]{:S(2)}) collective-permute-start(bf16[528,128]{1,0:T(8,128)(2,1)S(1)} %get-tuple-element.48.refs_10_), channel_id=1, source_target_pairs={{0,6},{2,4},{4,2},{6,0},{8,14},{10,12},{12,10},{14,8},{16,22},{18,... | collective-permute-start | bytes 405512 | tf_op jit(solution)/shard_map/ppermute | solution.py:297
  27.2 9.2 %collective-permute-start.6 = (bf16[528,128]{1,0:T(8,128)(2,1)S(1)}, bf16[528,128]{1,0:T(8,128)(2,1)S(1)}, u32[]{:S(2)}, u32[]{:S(2)}) collective-permute-start(bf16[528,128]{1,0:T(8,128)(2,1)S(1)} %get-tuple-element.60.refs_11_), channel_id=1, source_target_pairs={{0,26},{2,24},{4,30},{6,28},{8,18},{10,16},{12,22},{14,20},{16,10}... | collective-permute-start | bytes 405512 | tf_op jit(solution)/shard_map/ppermute | solution.py:297
  29.7 9.4 %collective-permute-start.7 = (bf16[528,128]{1,0:T(8,128)(2,1)S(1)}, bf16[528,128]{1,0:T(8,128)(2,1)S(1)}, u32[]{:S(2)}, u32[]{:S(2)}) collective-permute-start(bf16[528,128]{1,0:T(8,128)(2,1)S(1)} %get-tuple-element.61.refs_12_), channel_id=1, source_target_pairs={{0,8},{2,10},{4,12},{6,14},{8,0},{10,2},{12,4},{14,6},{16,24},{18,... | collective-permute-start | bytes 405512 | tf_op jit(solution)/shard_map/ppermute | solution.py:297
  29.7 14.2 %collective-permute-start.8 = (bf16[528,128]{1,0:T(8,128)(2,1)S(1)}, bf16[528,128]{1,0:T(8,128)(2,1)S(1)}, u32[]{:S(2)}, u32[]{:S(2)}) collective-permute-start(bf16[528,128]{1,0:T(8,128)(2,1)S(1)} %get-tuple-element.62.refs_13_), channel_id=1, source_target_pairs={{0,20},{2,22},{4,16},{6,18},{8,28},{10,30},{12,24},{14,26},{16,4},... | collective-permute-start | bytes 405512 | tf_op jit(solution)/shard_map/ppermute | solution.py:297
  31.2 15.0 %collective-permute-start.9 = (bf16[528,128]{1,0:T(8,128)(2,1)S(1)}, bf16[528,128]{1,0:T(8,128)(2,1)S(1)}, u32[]{:S(2)}, u32[]{:S(2)}) collective-permute-start(bf16[528,128]{1,0:T(8,128)(2,1)S(1)} %get-tuple-element.63.refs_14_), channel_id=1, source_target_pairs={{0,28},{2,30},{4,24},{6,26},{8,20},{10,22},{12,16},{14,18},{16,12}... | collective-permute-start | bytes 405512 | tf_op jit(solution)/shard_map/ppermute | solution.py:297
  35.0 1.3 %collective-permute-start.12 = (bf16[16,4096]{1,0:T(8,128)(2,1)S(1)}, bf16[16,4096]{1,0:T(8,128)(2,1)S(1)}, u32[]{:S(2)}, u32[]{:S(2)}) collective-permute-start(bf16[16,4096]{1,0:T(8,128)(2,1)S(1)} %get-tuple-element.59.refs_16_), channel_id=1, source_target_pairs={{0,1},{1,0},{2,3},{3,2},{4,5},{5,4},{6,7},{7,6},{8,9},{9,8},{10,11... | collective-permute-start | bytes 393224 | tf_op jit(solution)/shard_map/ppermute | solution.py:191
  36.3 16.7 %collective-permute-start.10 = (bf16[528,128]{1,0:T(8,128)(2,1)S(1)}, bf16[528,128]{1,0:T(8,128)(2,1)S(1)}, u32[]{:S(2)}, u32[]{:S(2)}) collective-permute-start(bf16[528,128]{1,0:T(8,128)(2,1)S(1)} %get-tuple-element.64.refs_15_), channel_id=1, source_target_pairs={{0,10},{2,8},{4,14},{6,12},{8,2},{10,0},{12,6},{14,4},{16,26},{18,... | collective-permute-start | bytes 405512 | tf_op jit(solution)/shard_map/ppermute | solution.py:297
  36.4 19.8 %collective-permute-start.11 = (bf16[528,128]{1,0:T(8,128)(2,1)S(1)}, bf16[528,128]{1,0:T(8,128)(2,1)S(1)}, u32[]{:S(2)}, u32[]{:S(2)}) collective-permute-start(bf16[528,128]{1,0:T(8,128)(2,1)S(1)} %get-tuple-element.65.refs_16_), channel_id=1, source_target_pairs={{0,22},{2,20},{4,18},{6,16},{8,30},{10,28},{12,26},{14,24},{16,6},... | collective-permute-start | bytes 405512 | tf_op jit(solution)/shard_map/ppermute | solution.py:297
  39.1 20.2 %collective-permute-start.13 = (bf16[528,128]{1,0:T(8,128)(2,1)S(1)}, bf16[528,128]{1,0:T(8,128)(2,1)S(1)}, u32[]{:S(2)}, u32[]{:S(2)}) collective-permute-start(bf16[528,128]{1,0:T(8,128)(2,1)S(1)} %get-tuple-element.67.refs_17_), channel_id=1, source_target_pairs={{0,12},{2,14},{4,8},{6,10},{8,4},{10,6},{12,0},{14,2},{16,28},{18,... | collective-permute-start | bytes 405512 | tf_op jit(solution)/shard_map/ppermute | solution.py:297
  43.9 15.3 %collective-permute-start.14 = (bf16[528,128]{1,0:T(8,128)(2,1)S(1)}, bf16[528,128]{1,0:T(8,128)(2,1)S(1)}, u32[]{:S(2)}, u32[]{:S(2)}) collective-permute-start(bf16[528,128]{1,0:T(8,128)(2,1)S(1)} %get-tuple-element.68.refs_18_), channel_id=1, source_target_pairs={{0,30},{2,28},{4,26},{6,24},{8,22},{10,20},{12,18},{14,16},{16,14}... | collective-permute-start | bytes 405512 | tf_op jit(solution)/shard_map/ppermute | solution.py:297
  46.2 13.1 %collective-permute-start.15 = (bf16[528,128]{1,0:T(8,128)(2,1)S(1)}, bf16[528,128]{1,0:T(8,128)(2,1)S(1)}, u32[]{:S(2)}, u32[]{:S(2)}) collective-permute-start(bf16[528,128]{1,0:T(8,128)(2,1)S(1)} %get-tuple-element.69.refs_19_), channel_id=1, source_target_pairs={{0,14},{2,12},{4,10},{6,8},{8,6},{10,4},{12,2},{14,0},{16,30},{18,... | collective-permute-start | bytes 405512 | tf_op jit(solution)/shard_map/ppermute | solution.py:297
  61.2 1.4 %collective-permute-start.16 = (bf16[16,4096]{1,0:T(8,128)(2,1)S(1)}, bf16[16,4096]{1,0:T(8,128)(2,1)S(1)}, u32[]{:S(2)}, u32[]{:S(2)}) collective-permute-start(bf16[16,4096]{1,0:T(8,128)(2,1)S(1)} %get-tuple-element.77), channel_id=1, source_target_pairs={{0,1},{1,0},{2,3},{3,2},{4,5},{5,4},{6,7},{7,6},{8,9},{9,8},{10,11... | collective-permute-start | bytes 393224 | tf_op jit(solution)/shard_map/ppermute | solution.py:191

commit v6 on v5

--- a/solution.py
+++ b/solution.py
@@ -10,8 +10,8 @@
 NEG = -1e30
 TAIL = 16
 CHUNKS = 8
-AHEAD = 6
-LATE = 3
+AHEAD = 5
+LATE = 5
 VMEM_BYTES = 24 * 1024 * 1024
 
 
@@ -201,10 +201,10 @@
 
 def step_order(n):
     half = n // 2
-    crossing = [s for pair in zip(range(half, half + half // 2), range(half + half // 2, n)) for s in pair]
+    crossing = list(range(half, n))
     staying = list(range(1, half))
     order = []
-    for kind in "cnnccncnccncncn":
+    for kind in "cncncncncncncnc":
         queue = crossing if kind == "c" else staying
         if queue:
             order.append(queue.pop(0))
@@ -298,7 +298,6 @@
 
     for i in range(1, 1 + AHEAD):
         send(i)
-    query_late = lax.optimization_barrier((query_one, arrived[1]))[0]
     partial_one, weight = pl.pallas_call(
         functools.partial(first_kernel, steps, span),
         out_shape=[
@@ -318,12 +317,14 @@
         compiler_params=params,
         cost_estimate=pl.CostEstimate(flops=flops, bytes_accessed=moved, transcendentals=slots * heads * span),
         name="first",
-    )(hbm(lengths), hbm(dest_instance), hbm(query_late), hbm(out_weight), *packed)
+    )(hbm(lengths), hbm(dest_instance), hbm(query_one), hbm(out_weight), *packed)
 
     for i in range(1 + AHEAD, n):
         send(i, partial_one)
     early, late = arrived[:-LATE], arrived[-LATE:]
-    halves = [partial_one, swap(partial_one)] if tp == 2 else []
+    halves = []
+    if tp == 2:
+        halves = [partial_one, swap(lax.optimization_barrier((partial_one, arrived[n // 2]))[0])]
 
     cache = jax.ShapeDtypeStruct((slots, span, width), bf16)
     mixed = jax.ShapeDtypeStruct((slots, heads, width), f32)

time: 63.5 us -> 59.7 us (0.940)
  the two profiles are of different devices: /device:TPU:0 before, /device:TPU:17 now
where the time goes in v6:
time: 59.7 us; the launch traced here: 59.5 us
  starting transfers between devices  34.8 us (58%)
  waiting for transfers between devices  11.9 us (20%)
  Pallas kernels  11.4 us (19%)
  other arithmetic  0.69 us (1%)
  between operations  0.69 us (1%)
    ppermute x15, starting transfers between devices, send(): lax.ppermute(block, 'inst', [(d, d ^ steps[i]) for d in range(n)])  28.6 us
    ppermute x15, waiting for transfers between devices, send(): lax.ppermute(block, 'inst', [(d, d ^ steps[i]) for d in range(n)])  10.9 us
    ppermute x2, starting transfers between devices, swap(): return lax.ppermute(partial, 'tp', [(0, 1), (1, 0)])  6.19 us
    pallas_call x1, Pallas kernels, shards(): pl.pallas_call(functools.partial(first_kernel, steps, span), out_shape=[j...  4.66 us
    pallas_call x1, Pallas kernels, shards(): pl.pallas_call(functools.partial(early_kernel, some, span, len(halves)),...  2.85 us
    pallas_call x1, Pallas kernels, shards(): pl.pallas_call(functools.partial(late_kernel, LATE, span), out_shape=[jax...  2 us
    pallas_call x1, Pallas kernels, shards(): pl.pallas_call(functools.partial(pack_kernel, steps, pages), out_shape=sh...  1.87 us
  transfers between devices with their start and end apart: 17, of which 5 were waited for; matrix products, arithmetic and copies ran while one was open for 0% of the time, Pallas kernels for 13%

profile of v6, /device:TPU:17, one launch (start us, length us, event | category | flops | bytes accessed | tf_op | source)
XLA Modules:
  0.0 59.5 jit_solution(9299631301004676777)
XLA Ops:
  0.6 1.9 %pack.1 = (bf16[528,128]{1,0:T(8,128)(2,1)S(1)}, bf16[528,128]{1,0:T(8,128)(2,1)S(1)}, bf16[528,128]{1,0:T(8,128)(2,1)S(1)}, bf16[528,128]{1,0:T(8,128)(2,1)S(1)...) custom-call(s32[4,16]{1,0:T(4,128)} %bitcast.21, ...), custom_call_target="tpu_custom_call" | custom-call | bytes 4325376 | tf_op jit(solution)/shard_map/pack/pallas_call | solution.py:260
  2.5 0.1 collective-permute-start
  2.6 1.3 %collective-permute-start.1 = (bf16[528,128]{1,0:T(8,128)(2,1)S(1)}, bf16[528,128]{1,0:T(8,128)(2,1)S(1)}, u32[]{:S(2)}, u32[]{:S(2)}) collective-permute-start(bf16[528,128]{1,0:T(8,128)(2,1)S(1)} %get-tuple-element.45.refs_6_), channel_id=1, source_target_pairs={{0,2},{2,0},{4,6},{6,4},{8,10},{10,8},{12,14},{14,12},{16,18},{18,... | collective-permute-start | bytes 405512 | tf_op jit(solution)/shard_map/ppermute | solution.py:297
  3.9 2.3 %collective-permute-start.2 = (bf16[528,128]{1,0:T(8,128)(2,1)S(1)}, bf16[528,128]{1,0:T(8,128)(2,1)S(1)}, u32[]{:S(2)}, u32[]{:S(2)}) collective-permute-start(bf16[528,128]{1,0:T(8,128)(2,1)S(1)} %get-tuple-element.46.refs_7_), channel_id=1, source_target_pairs={{0,18},{2,16},{4,22},{6,20},{8,26},{10,24},{12,30},{14,28},{16,2},... | collective-permute-start | bytes 405512 | tf_op jit(solution)/shard_map/ppermute | solution.py:297
  6.1 1.2 %collective-permute-start.3 = (bf16[528,128]{1,0:T(8,128)(2,1)S(1)}, bf16[528,128]{1,0:T(8,128)(2,1)S(1)}, u32[]{:S(2)}, u32[]{:S(2)}) collective-permute-start(bf16[528,128]{1,0:T(8,128)(2,1)S(1)} %get-tuple-element.47.refs_8_), channel_id=1, source_target_pairs={{0,4},{2,6},{4,0},{6,2},{8,12},{10,14},{12,8},{14,10},{16,20},{18,... | collective-permute-start | bytes 405512 | tf_op jit(solution)/shard_map/ppermute | solution.py:297
  7.4 4.7 %first.1 = (bf16[16,4096]{1,0:T(8,128)(2,1)S(1)}, bf16[1024,4096]{1,0:T(8,128)(2,1)S(1)}) custom-call(s32[16]{0:T(128)} %refs_0_.1, s32[16]{0:T(128)} %refs_1_.3, bf16[16,8,128]{2,1,0:T(8,128)(2,1)} %refs_2_.3, bf16[1024,4096]{1,0:T(8,128)(2,1)} %refs_3_.3, bf16[528,128]{1,0:T(8,128)(2,1)S(1)} %get-tuple-element.43.refs_4_.refs_0_, ...), custom_call_target="tpu_custom_call" | custom-call | flops 150994944 | bytes 10485760 | tf_op jit(solution)/shard_map/first/pallas_call | solution.py:301
  12.0 1.4 %collective-permute-start.7 = (bf16[528,128]{1,0:T(8,128)(2,1)S(1)}, bf16[528,128]{1,0:T(8,128)(2,1)S(1)}, u32[]{:S(2)}, u32[]{:S(2)}) collective-permute-start(bf16[528,128]{1,0:T(8,128)(2,1)S(1)} %get-tuple-element.62.refs_12_), channel_id=1, source_target_pairs={{0,8},{2,10},{4,12},{6,14},{8,0},{10,2},{12,4},{14,6},{16,24},{18,... | collective-permute-start | bytes 405512 | tf_op jit(solution)/shard_map/ppermute | solution.py:297
  13.4 0.0 collective-permute-done.refs_1_
  13.4 0.0 collective-permute-start.4
  13.4 0.0 collective-permute-done.1.refs_2_
  13.4 2.2 %collective-permute-start.5 = (bf16[528,128]{1,0:T(8,128)(2,1)S(1)}, bf16[528,128]{1,0:T(8,128)(2,1)S(1)}, u32[]{:S(2)}, u32[]{:S(2)}) collective-permute-start(bf16[528,128]{1,0:T(8,128)(2,1)S(1)} %get-tuple-element.60.refs_10_), channel_id=1, source_target_pairs={{0,6},{2,4},{4,2},{6,0},{8,14},{10,12},{12,10},{14,8},{16,22},{18,... | collective-permute-start | bytes 405512 | tf_op jit(solution)/shard_map/ppermute | solution.py:297
  15.6 0.0 collective-permute-done.2.refs_3_
  15.6 3.0 %collective-permute-start.6 = (bf16[528,128]{1,0:T(8,128)(2,1)S(1)}, bf16[528,128]{1,0:T(8,128)(2,1)S(1)}, u32[]{:S(2)}, u32[]{:S(2)}) collective-permute-start(bf16[528,128]{1,0:T(8,128)(2,1)S(1)} %get-tuple-element.61.refs_11_), channel_id=1, source_target_pairs={{0,22},{2,20},{4,18},{6,16},{8,30},{10,28},{12,26},{14,24},{16,6},... | collective-permute-start | bytes 405512 | tf_op jit(solution)/shard_map/ppermute | solution.py:297
  18.6 0.0 collective-permute-done.3.refs_4_
  18.6 4.8 %collective-permute-start.8 = (bf16[528,128]{1,0:T(8,128)(2,1)S(1)}, bf16[528,128]{1,0:T(8,128)(2,1)S(1)}, u32[]{:S(2)}, u32[]{:S(2)}) collective-permute-start(bf16[528,128]{1,0:T(8,128)(2,1)S(1)} %get-tuple-element.63.refs_13_), channel_id=1, source_target_pairs={{0,24},{2,26},{4,28},{6,30},{8,16},{10,18},{12,20},{14,22},{16,8},... | collective-permute-start | bytes 405512 | tf_op jit(solution)/shard_map/ppermute | solution.py:297
  23.4 0.0 collective-permute-done.7.refs_8_
  23.4 0.0 collective-permute-start.9
  23.4 0.0 collective-permute-done.4.refs_5_
  23.4 5.6 %collective-permute-start.10 = (bf16[16,4096]{1,0:T(8,128)(2,1)S(1)}, bf16[16,4096]{1,0:T(8,128)(2,1)S(1)}, u32[]{:S(2)}, u32[]{:S(2)}) collective-permute-start(bf16[16,4096]{1,0:T(8,128)(2,1)S(1)} %get-tuple-element.65.refs_14_), channel_id=1, source_target_pairs={{0,1},{1,0},{2,3},{3,2},{4,5},{5,4},{6,7},{7,6},{8,9},{9,8},{10,11... | collective-permute-start | bytes 393224 | tf_op jit(solution)/shard_map/ppermute | solution.py:191
  29.0 0.0 collective-permute-done.5.refs_6_
  29.0 1.5 %collective-permute-start.11 = (bf16[528,128]{1,0:T(8,128)(2,1)S(1)}, bf16[528,128]{1,0:T(8,128)(2,1)S(1)}, u32[]{:S(2)}, u32[]{:S(2)}) collective-permute-start(bf16[528,128]{1,0:T(8,128)(2,1)S(1)} %get-tuple-element.67.refs_15_), channel_id=1, source_target_pairs={{0,26},{2,24},{4,30},{6,28},{8,18},{10,16},{12,22},{14,20},{16,10}... | collective-permute-start | bytes 405512 | tf_op jit(solution)/shard_map/ppermute | solution.py:297
  30.6 0.0 collective-permute-done.6.refs_7_
  30.6 4.7 %collective-permute-start.12 = (bf16[528,128]{1,0:T(8,128)(2,1)S(1)}, bf16[528,128]{1,0:T(8,128)(2,1)S(1)}, u32[]{:S(2)}, u32[]{:S(2)}) collective-permute-start(bf16[528,128]{1,0:T(8,128)(2,1)S(1)} %get-tuple-element.68.refs_16_), channel_id=1, source_target_pairs={{0,12},{2,14},{4,8},{6,10},{8,4},{10,6},{12,0},{14,2},{16,28},{18,... | collective-permute-start | bytes 405512 | tf_op jit(solution)/shard_map/ppermute | solution.py:297
  35.3 0.0 collective-permute-done.8.refs_9_
  35.3 1.0 %collective-permute-start.13 = (bf16[528,128]{1,0:T(8,128)(2,1)S(1)}, bf16[528,128]{1,0:T(8,128)(2,1)S(1)}, u32[]{:S(2)}, u32[]{:S(2)}) collective-permute-start(bf16[528,128]{1,0:T(8,128)(2,1)S(1)} %get-tuple-element.69.refs_17_), channel_id=1, source_target_pairs={{0,28},{2,30},{4,24},{6,26},{8,20},{10,22},{12,16},{14,18},{16,12}... | collective-permute-start | bytes 405512 | tf_op jit(solution)/shard_map/ppermute | solution.py:297
  36.3 0.0 collective-permute-done.9.refs_10_
  36.3 1.3 %collective-permute-start.14 = (bf16[528,128]{1,0:T(8,128)(2,1)S(1)}, bf16[528,128]{1,0:T(8,128)(2,1)S(1)}, u32[]{:S(2)}, u32[]{:S(2)}) collective-permute-start(bf16[528,128]{1,0:T(8,128)(2,1)S(1)} %get-tuple-element.70.refs_18_), channel_id=1, source_target_pairs={{0,14},{2,12},{4,10},{6,8},{8,6},{10,4},{12,2},{14,0},{16,30},{18,... | collective-permute-start | bytes 405512 | tf_op jit(solution)/shard_map/ppermute | solution.py:297
  37.6 0.0 collective-permute-done.10.refs_15_
  37.6 3.8 %collective-permute-start.15 = (bf16[528,128]{1,0:T(8,128)(2,1)S(1)}, bf16[528,128]{1,0:T(8,128)(2,1)S(1)}, u32[]{:S(2)}, u32[]{:S(2)}) collective-permute-start(bf16[528,128]{1,0:T(8,128)(2,1)S(1)} %get-tuple-element.71.refs_19_), channel_id=1, source_target_pairs={{0,30},{2,28},{4,26},{6,24},{8,22},{10,20},{12,18},{14,16},{16,14}... | collective-permute-start | bytes 405512 | tf_op jit(solution)/shard_map/ppermute | solution.py:297
  41.5 2.9 %early.1 = (bf16[16,256,128]{2,1,0:T(8,128)(2,1)}, bf16[16,256,128]{2,1,0:T(8,128)(2,1)}, f32[16,8,128]{2,1,0:T(8,128)S(1)}, bf16[16,8,128]{2,1,0:T(8,128)(2,1)S...) custom-call(bf16[528,128]{1,0:T(8,128)(2,1)S(1)} %get-tuple-element.43.refs_4_.refs_0_, ...), custom_call_target="tpu_custom_call" | custom-call | flops 11534336 | bytes 2883584 | tf_op jit(solution)/shard_map/early/pallas_call | solution.py:332
  44.3 1.5 %collective-permute-done.11.refs_0_ = bf16[528,128]{1,0:T(8,128)(2,1)S(1)} collective-permute-done((bf16[528,128]{1,0:T(8,128)(2,1)S(1)}, bf16[528,128]{1,0:T(8,128)(2,1)S(1)}, u32[]{:S(2)}, u32[]{:S(2)}) %collective-permute-start.11) | collective-permute-done | bytes 135200 | tf_op jit(solution)/shard_map/ppermute | solution.py:297
  45.8 0.0 collective-permute-done.12.refs_1_
  45.8 2.8 %collective-permute-done.13.refs_2_ = bf16[528,128]{1,0:T(8,128)(2,1)S(1)} collective-permute-done((bf16[528,128]{1,0:T(8,128)(2,1)S(1)}, bf16[528,128]{1,0:T(8,128)(2,1)S(1)}, u32[]{:S(2)}, u32[]{:S(2)}) %collective-permute-start.13) | collective-permute-done | bytes 135200 | tf_op jit(solution)/shard_map/ppermute | solution.py:297
  48.6 0.3 collective-permute-done.14.refs_3_
  48.9 6.4 %collective-permute-done.15.refs_4_ = bf16[528,128]{1,0:T(8,128)(2,1)S(1)} collective-permute-done((bf16[528,128]{1,0:T(8,128)(2,1)S(1)}, bf16[528,128]{1,0:T(8,128)(2,1)S(1)}, u32[]{:S(2)}, u32[]{:S(2)}) %collective-permute-start.15) | collective-permute-done | bytes 135200 | tf_op jit(solution)/shard_map/ppermute | solution.py:297
  55.2 2.0 %late.1 = (bf16[16,4096]{1,0:T(8,128)(2,1)S(1)}, bf16[16,256,128]{2,1,0:T(8,128)(2,1)}, bf16[16,256,128]{2,1,0:T(8,128)(2,1)}) custom-call(bf16[528,128]{1,0:T(8,128)(2,1)S(1)} %collective-permute-done.11.refs_0_, bf16[528,128]{1,0:T(8,128)(2,1)S(1)} %collective-permute-done.12.refs_1_, ...), custom_call_target="tpu_custom_call", output_to_operand_aliasing={{1}: (10, {}), {2}: (11, {})} | custom-call | flops 150994944 | bytes 10485760 | tf_op jit(solution)/shard_map/late/pallas_call | solution.py:358
  57.2 0.6 collective-permute-start.16
  57.8 1.0 %collective-permute-done.16 = bf16[16,4096]{1,0:T(8,128)(2,1)S(1)} collective-permute-done((bf16[16,4096]{1,0:T(8,128)(2,1)S(1)}, bf16[16,4096]{1,0:T(8,128)(2,1)S(1)}, u32[]{:S(2)}, u32[]{:S(2)}) %collective-permute-start.16) | collective-permute-done | bytes 131104 | tf_op jit(solution)/shard_map/ppermute | solution.py:191
  58.8 0.7 %add_convert_fusion = bf16[16,4096]{1,0:T(8,128)(2,1)} fusion(bf16[16,4096]{1,0:T(8,128)(2,1)S(1)} %collective-permute-done.16, bf16[16,4096]{1,0:T(8,128)(2,1)S(1)} %get-tuple-element.79), kind=kLoop, calls=%fused_computation | loop fusion | flops 262144 | bytes 393216 | tf_op jit(solution)/shard_map/convert_element_type | solution.py:382
Async XLA Ops:
  2.5 10.9 %collective-permute-start = (bf16[528,128]{1,0:T(8,128)(2,1)S(1)}, bf16[528,128]{1,0:T(8,128)(2,1)S(1)}, u32[]{:S(2)}, u32[]{:S(2)}) collective-permute-start(bf16[528,128]{1,0:T(8,128)(2,1)S(1)} %get-tuple-element.44.refs_5_), channel_id=1, source_target_pairs={{0,16},{2,18},{4,20},{6,22},{8,24},{10,26},{12,28},{14,30},{16,0},... | collective-permute-start | bytes 405512 | tf_op jit(solution)/shard_map/ppermute | solution.py:297
  2.6 10.8 %collective-permute-start.1 = (bf16[528,128]{1,0:T(8,128)(2,1)S(1)}, bf16[528,128]{1,0:T(8,128)(2,1)S(1)}, u32[]{:S(2)}, u32[]{:S(2)}) collective-permute-start(bf16[528,128]{1,0:T(8,128)(2,1)S(1)} %get-tuple-element.45.refs_6_), channel_id=1, source_target_pairs={{0,2},{2,0},{4,6},{6,4},{8,10},{10,8},{12,14},{14,12},{16,18},{18,... | collective-permute-start | bytes 405512 | tf_op jit(solution)/shard_map/ppermute | solution.py:297
  3.9 11.7 %collective-permute-start.2 = (bf16[528,128]{1,0:T(8,128)(2,1)S(1)}, bf16[528,128]{1,0:T(8,128)(2,1)S(1)}, u32[]{:S(2)}, u32[]{:S(2)}) collective-permute-start(bf16[528,128]{1,0:T(8,128)(2,1)S(1)} %get-tuple-element.46.refs_7_), channel_id=1, source_target_pairs={{0,18},{2,16},{4,22},{6,20},{8,26},{10,24},{12,30},{14,28},{16,2},... | collective-permute-start | bytes 405512 | tf_op jit(solution)/shard_map/ppermute | solution.py:297
  6.1 12.5 %collective-permute-start.3 = (bf16[528,128]{1,0:T(8,128)(2,1)S(1)}, bf16[528,128]{1,0:T(8,128)(2,1)S(1)}, u32[]{:S(2)}, u32[]{:S(2)}) collective-permute-start(bf16[528,128]{1,0:T(8,128)(2,1)S(1)} %get-tuple-element.47.refs_8_), channel_id=1, source_target_pairs={{0,4},{2,6},{4,0},{6,2},{8,12},{10,14},{12,8},{14,10},{16,20},{18,... | collective-permute-start | bytes 405512 | tf_op jit(solution)/shard_map/ppermute | solution.py:297
  12.0 11.4 %collective-permute-start.7 = (bf16[528,128]{1,0:T(8,128)(2,1)S(1)}, bf16[528,128]{1,0:T(8,128)(2,1)S(1)}, u32[]{:S(2)}, u32[]{:S(2)}) collective-permute-start(bf16[528,128]{1,0:T(8,128)(2,1)S(1)} %get-tuple-element.62.refs_12_), channel_id=1, source_target_pairs={{0,8},{2,10},{4,12},{6,14},{8,0},{10,2},{12,4},{14,6},{16,24},{18,... | collective-permute-start | bytes 405512 | tf_op jit(solution)/shard_map/ppermute | solution.py:297
  13.4 10.0 %collective-permute-start.4 = (bf16[528,128]{1,0:T(8,128)(2,1)S(1)}, bf16[528,128]{1,0:T(8,128)(2,1)S(1)}, u32[]{:S(2)}, u32[]{:S(2)}) collective-permute-start(bf16[528,128]{1,0:T(8,128)(2,1)S(1)} %get-tuple-element.48.refs_9_), channel_id=1, source_target_pairs={{0,20},{2,22},{4,16},{6,18},{8,28},{10,30},{12,24},{14,26},{16,4},... | collective-permute-start | bytes 405512 | tf_op jit(solution)/shard_map/ppermute | solution.py:297
  13.4 15.6 %collective-permute-start.5 = (bf16[528,128]{1,0:T(8,128)(2,1)S(1)}, bf16[528,128]{1,0:T(8,128)(2,1)S(1)}, u32[]{:S(2)}, u32[]{:S(2)}) collective-permute-start(bf16[528,128]{1,0:T(8,128)(2,1)S(1)} %get-tuple-element.60.refs_10_), channel_id=1, source_target_pairs={{0,6},{2,4},{4,2},{6,0},{8,14},{10,12},{12,10},{14,8},{16,22},{18,... | collective-permute-start | bytes 405512 | tf_op jit(solution)/shard_map/ppermute | solution.py:297
  15.6 15.0 %collective-permute-start.6 = (bf16[528,128]{1,0:T(8,128)(2,1)S(1)}, bf16[528,128]{1,0:T(8,128)(2,1)S(1)}, u32[]{:S(2)}, u32[]{:S(2)}) collective-permute-start(bf16[528,128]{1,0:T(8,128)(2,1)S(1)} %get-tuple-element.61.refs_11_), channel_id=1, source_target_pairs={{0,22},{2,20},{4,18},{6,16},{8,30},{10,28},{12,26},{14,24},{16,6},... | collective-permute-start | bytes 405512 | tf_op jit(solution)/shard_map/ppermute | solution.py:297
  18.6 16.7 %collective-permute-start.8 = (bf16[528,128]{1,0:T(8,128)(2,1)S(1)}, bf16[528,128]{1,0:T(8,128)(2,1)S(1)}, u32[]{:S(2)}, u32[]{:S(2)}) collective-permute-start(bf16[528,128]{1,0:T(8,128)(2,1)S(1)} %get-tuple-element.63.refs_13_), channel_id=1, source_target_pairs={{0,24},{2,26},{4,28},{6,30},{8,16},{10,18},{12,20},{14,22},{16,8},... | collective-permute-start | bytes 405512 | tf_op jit(solution)/shard_map/ppermute | solution.py:297
  23.4 12.9 %collective-permute-start.9 = (bf16[528,128]{1,0:T(8,128)(2,1)S(1)}, bf16[528,128]{1,0:T(8,128)(2,1)S(1)}, u32[]{:S(2)}, u32[]{:S(2)}) collective-permute-start(bf16[528,128]{1,0:T(8,128)(2,1)S(1)} %get-tuple-element.64.refs_14_), channel_id=1, source_target_pairs={{0,10},{2,8},{4,14},{6,12},{8,2},{10,0},{12,6},{14,4},{16,26},{18,... | collective-permute-start | bytes 405512 | tf_op jit(solution)/shard_map/ppermute | solution.py:297
  23.4 14.2 %collective-permute-start.10 = (bf16[16,4096]{1,0:T(8,128)(2,1)S(1)}, bf16[16,4096]{1,0:T(8,128)(2,1)S(1)}, u32[]{:S(2)}, u32[]{:S(2)}) collective-permute-start(bf16[16,4096]{1,0:T(8,128)(2,1)S(1)} %get-tuple-element.65.refs_14_), channel_id=1, source_target_pairs={{0,1},{1,0},{2,3},{3,2},{4,5},{5,4},{6,7},{7,6},{8,9},{9,8},{10,11... | collective-permute-start | bytes 393224 | tf_op jit(solution)/shard_map/ppermute | solution.py:191
  29.0 16.8 %collective-permute-start.11 = (bf16[528,128]{1,0:T(8,128)(2,1)S(1)}, bf16[528,128]{1,0:T(8,128)(2,1)S(1)}, u32[]{:S(2)}, u32[]{:S(2)}) collective-permute-start(bf16[528,128]{1,0:T(8,128)(2,1)S(1)} %get-tuple-element.67.refs_15_), channel_id=1, source_target_pairs={{0,26},{2,24},{4,30},{6,28},{8,18},{10,16},{12,22},{14,20},{16,10}... | collective-permute-start | bytes 405512 | tf_op jit(solution)/shard_map/ppermute | solution.py:297
  30.6 15.2 %collective-permute-start.12 = (bf16[528,128]{1,0:T(8,128)(2,1)S(1)}, bf16[528,128]{1,0:T(8,128)(2,1)S(1)}, u32[]{:S(2)}, u32[]{:S(2)}) collective-permute-start(bf16[528,128]{1,0:T(8,128)(2,1)S(1)} %get-tuple-element.68.refs_16_), channel_id=1, source_target_pairs={{0,12},{2,14},{4,8},{6,10},{8,4},{10,6},{12,0},{14,2},{16,28},{18,... | collective-permute-start | bytes 405512 | tf_op jit(solution)/shard_map/ppermute | solution.py:297
  35.3 13.2 %collective-permute-start.13 = (bf16[528,128]{1,0:T(8,128)(2,1)S(1)}, bf16[528,128]{1,0:T(8,128)(2,1)S(1)}, u32[]{:S(2)}, u32[]{:S(2)}) collective-permute-start(bf16[528,128]{1,0:T(8,128)(2,1)S(1)} %get-tuple-element.69.refs_17_), channel_id=1, source_target_pairs={{0,28},{2,30},{4,24},{6,26},{8,20},{10,22},{12,16},{14,18},{16,12}... | collective-permute-start | bytes 405512 | tf_op jit(solution)/shard_map/ppermute | solution.py:297
  36.3 12.5 %collective-permute-start.14 = (bf16[528,128]{1,0:T(8,128)(2,1)S(1)}, bf16[528,128]{1,0:T(8,128)(2,1)S(1)}, u32[]{:S(2)}, u32[]{:S(2)}) collective-permute-start(bf16[528,128]{1,0:T(8,128)(2,1)S(1)} %get-tuple-element.70.refs_18_), channel_id=1, source_target_pairs={{0,14},{2,12},{4,10},{6,8},{8,6},{10,4},{12,2},{14,0},{16,30},{18,... | collective-permute-start | bytes 405512 | tf_op jit(solution)/shard_map/ppermute | solution.py:297
  37.6 17.6 %collective-permute-start.15 = (bf16[528,128]{1,0:T(8,128)(2,1)S(1)}, bf16[528,128]{1,0:T(8,128)(2,1)S(1)}, u32[]{:S(2)}, u32[]{:S(2)}) collective-permute-start(bf16[528,128]{1,0:T(8,128)(2,1)S(1)} %get-tuple-element.71.refs_19_), channel_id=1, source_target_pairs={{0,30},{2,28},{4,26},{6,24},{8,22},{10,20},{12,18},{14,16},{16,14}... | collective-permute-start | bytes 405512 | tf_op jit(solution)/shard_map/ppermute | solution.py:297
  57.2 1.5 %collective-permute-start.16 = (bf16[16,4096]{1,0:T(8,128)(2,1)S(1)}, bf16[16,4096]{1,0:T(8,128)(2,1)S(1)}, u32[]{:S(2)}, u32[]{:S(2)}) collective-permute-start(bf16[16,4096]{1,0:T(8,128)(2,1)S(1)} %get-tuple-element.79), channel_id=1, source_target_pairs={{0,1},{1,0},{2,3},{3,2},{4,5},{5,4},{6,7},{7,6},{8,9},{9,8},{10,11... | collective-permute-start | bytes 393224 | tf_op jit(solution)/shard_map/ppermute | solution.py:191

commit v7 on v6

--- a/solution.py
+++ b/solution.py
@@ -8,7 +8,8 @@
 from jax.sharding import PartitionSpec as P
 
 NEG = -1e30
-TAIL = 16
+TILE = 16
+SPLIT = 64
 CHUNKS = 8
 AHEAD = 5
 LATE = 5
@@ -20,12 +21,30 @@
     return jnp.sum(jnp.where(rows == at, block, 0.0), axis=0, keepdims=True)
 
 
+def row_at(block, position):
+    base = pl.multiple_of(position // TILE * TILE, TILE)
+    return row_of(block[pl.ds(base, TILE), :].astype(jnp.float32), position % TILE)
+
+
 def put_row(block, row, position):
-    base = pl.multiple_of(position // TAIL * TAIL, TAIL)
-    part = block[pl.ds(base, TAIL), :]
+    base = pl.multiple_of(position // TILE * TILE, TILE)
+    part = block[pl.ds(base, TILE), :]
     at = lax.broadcasted_iota(jnp.int32, part.shape, 0)
-    mixed = jnp.where(at == position % TAIL, row, part.astype(jnp.float32))
-    block[pl.ds(base, TAIL), :] = mixed.astype(jnp.bfloat16)
+    mixed = jnp.where(at == position % TILE, row, part.astype(jnp.float32))
+    block[pl.ds(base, TILE), :] = mixed.astype(jnp.bfloat16)
+
+
+def put_last(block, row):
+    end = block.shape[0]
+    part = block[end - TILE : end, :]
+    at = lax.broadcasted_iota(jnp.int32, part.shape, 0)
+    mixed = jnp.where(at == TILE - 1, row, part.astype(jnp.float32))
+    block[end - TILE : end, :] = mixed.astype(jnp.bfloat16)
+
+
+def last_row(block):
+    end = block.shape[0]
+    return block[end - TILE : end, :].astype(jnp.float32)[TILE - 1 : TILE, :]
 
 
 def invert(dest, source, n):
@@ -49,9 +68,7 @@
 
 
 def parcels_of(refs, span):
-    return [
-        (ref.at[pl.ds(0, span)], ref.at[pl.ds(span, span)], ref.at[pl.ds(2 * span, TAIL)]) for ref in refs
-    ]
+    return [(ref.at[pl.ds(0, span)], ref.at[pl.ds(span, span)]) for ref in refs]
 
 
 def sources(source, steps):
@@ -59,10 +76,10 @@
     return [source[me ^ s] for s in steps]
 
 
-def pack_kernel(steps, pages, *refs):
-    n = len(steps)
-    far, outs = refs[:8], refs[8 : 8 + n]
-    table, lengths, dest, slot, key_one, value_one, key_pool, value_pool, source, sems = refs[8 + n :]
+def pack_kernel(n, steps, pages, *refs):
+    count = len(steps)
+    far, outs = refs[:8], refs[8 : 8 + count]
+    table, lengths, dest, slot, key_one, value_one, key_pool, value_pool, source, sems = refs[8 + count :]
     copies = begin(list(zip(far, (table, lengths, dest, slot, key_one, value_one, key_pool, value_pool))), sems)
     size = key_pool.shape[1]
     parcels = parcels_of(outs, pages * size)
@@ -70,16 +87,17 @@
     invert(dest, source, n)
     at = sources(source, steps)
     tokens = (key_one[...].astype(jnp.float32), value_one[...].astype(jnp.float32))
+    lanes = lax.broadcasted_iota(jnp.int32, (1, key_one.shape[1]), 1)
     for which, pool in ((0, key_pool), (1, value_pool)):
         copies[6 + which].wait()
         for r, parcel in zip(at, parcels):
             for p in range(pages):
                 parcel[which][p * size : (p + 1) * size, :] = pool[table[p, r]]
             put_row(parcel[which], row_of(tokens[which], r), lengths[r])
-    rows = lax.broadcasted_iota(jnp.int32, (TAIL, key_one.shape[1]), 0)
-    for r, parcel in zip(at, parcels):
-        tail = jnp.where(rows == 0, slot[r].astype(jnp.float32), lengths[r].astype(jnp.float32))
-        parcel[2][...] = tail.astype(jnp.bfloat16)
+            if which == 0:
+                put_row(parcel[0], last_row(parcel[0]), lengths[r] + 1)
+                note = jnp.where(lanes < SPLIT, slot[r], lengths[r]).astype(jnp.float32)
+                put_last(parcel[0], note)
 
 
 def attend(queries, keys, values, counts):
@@ -137,12 +155,14 @@
     slots = []
     lengths = []
     for parcel in arrived:
-        tail = parcel[2][...].astype(jnp.float32)
-        slots.append(jnp.max(tail[0:1, :]).astype(jnp.int32))
-        lengths.append(jnp.max(tail[1:2, :]).astype(jnp.int32))
+        note = last_row(parcel[0])
+        lanes = lax.broadcasted_iota(jnp.int32, note.shape, 1)
+        slots.append(jnp.max(jnp.where(lanes < SPLIT, note, 0.0)).astype(jnp.int32))
+        lengths.append(jnp.max(jnp.where(lanes < SPLIT, 0.0, note)).astype(jnp.int32))
     for i, parcel in enumerate(arrived):
         held[0, i] = parcel[0][...]
         held[1, i] = parcel[1][...]
+        put_last(held.at[0, i], row_at(parcel[0], lengths[i] + 1))
     outgoing = []
     for i in range(count):
         for which, (token, cache) in enumerate(((key_two, key_cache), (value_two, value_cache))):
@@ -248,7 +268,7 @@
     far = pl.BlockSpec(memory_space=pltpu.HBM)
     params = pltpu.CompilerParams(vmem_limit_bytes=VMEM_BYTES)
     bf16, f32, i32 = jnp.bfloat16, jnp.float32, jnp.int32
-    rows = 2 * span + TAIL
+    rows = 2 * span
     order = step_order(n)
     steps = [0] + order
 
@@ -257,47 +277,50 @@
 
     shapes = [block(rows)] * n
 
-    packed = pl.pallas_call(
-        functools.partial(pack_kernel, steps, pages),
-        out_shape=shapes,
-        in_specs=[far] * 8,
-        out_specs=[vmem] * len(shapes),
-        scratch_shapes=[
-            pltpu.SMEM((pages, slots), i32),
-            pltpu.SMEM((slots,), i32),
-            pltpu.SMEM((slots,), i32),
-            pltpu.SMEM((slots,), i32),
-            pltpu.VMEM((slots, width), bf16),
-            pltpu.VMEM((slots, width), bf16),
-            pltpu.VMEM((pool, size, width), bf16),
-            pltpu.VMEM((pool, size, width), bf16),
-            pltpu.SMEM((n,), i32),
-            pltpu.SemaphoreType.DMA((8,)),
-        ],
-        compiler_params=params,
-        cost_estimate=pl.CostEstimate(flops=0, bytes_accessed=4 * n * rows * width, transcendentals=0),
-        name="pack",
-    )(
-        hbm(page_table.T),
-        hbm(lengths),
-        hbm(dest_instance),
-        hbm(dest_slot),
-        hbm(key_one),
-        hbm(value_one),
-        hbm(key_pages),
-        hbm(value_pages),
-    )
+    def pack(chosen):
+        return pl.pallas_call(
+            functools.partial(pack_kernel, n, chosen, pages),
+            out_shape=[jax.ShapeDtypeStruct((rows, width), bf16)] * len(chosen),
+            in_specs=[far] * 8,
+            out_specs=[vmem] * len(chosen),
+            scratch_shapes=[
+                pltpu.SMEM((pages, slots), i32),
+                pltpu.SMEM((slots,), i32),
+                pltpu.SMEM((slots,), i32),
+                pltpu.SMEM((slots,), i32),
+                pltpu.VMEM((slots, width), bf16),
+                pltpu.VMEM((slots, width), bf16),
+                pltpu.VMEM((pool, size, width), bf16),
+                pltpu.VMEM((pool, size, width), bf16),
+                pltpu.SMEM((n,), i32),
+                pltpu.SemaphoreType.DMA((8,)),
+            ],
+            compiler_params=params,
+            cost_estimate=pl.CostEstimate(
+                flops=0, bytes_accessed=4 * len(chosen) * rows * width, transcendentals=0
+            ),
+            name="pack",
+        )(
+            hbm(page_table.T),
+            hbm(lengths),
+            hbm(dest_instance),
+            hbm(dest_slot),
+            hbm(key_one),
+            hbm(value_one),
+            hbm(key_pages),
+            hbm(value_pages),
+        )
+
+    steps = step_order(n) + [0]
+    packed = pack(steps[:AHEAD]) + pack(steps[AHEAD:])
 
     flops = 4 * slots * heads * span * width + 2 * slots * depth * columns
     moved = 2 * depth * columns + 4 * slots * span * width
-    arrived = [packed[0]]
-
     def send(i, *after):
         block = lax.optimization_barrier((packed[i], *after))[0] if after else packed[i]
-        arrived.append(lax.ppermute(block, "inst", [(d, d ^ steps[i]) for d in range(n)]))
-
-    for i in range(1, 1 + AHEAD):
-        send(i)
+        return lax.ppermute(block, "inst", [(d, d ^ steps[i]) for d in range(n)])
+
+    arrived = [send(i) for i in range(AHEAD)]
     partial_one, weight = pl.pallas_call(
         functools.partial(first_kernel, steps, span),
         out_shape=[
@@ -319,12 +342,11 @@
         name="first",
     )(hbm(lengths), hbm(dest_instance), hbm(query_one), hbm(out_weight), *packed)
 
-    for i in range(1 + AHEAD, n):
-        send(i, partial_one)
-    early, late = arrived[:-LATE], arrived[-LATE:]
+    arrived += [send(i, partial_one) for i in range(AHEAD, n - 1)]
+    early, late = [packed[-1]] + arrived[:-LATE], arrived[-LATE:]
     halves = []
     if tp == 2:
-        halves = [partial_one, swap(lax.optimization_barrier((partial_one, arrived[n // 2]))[0])]
+        halves = [partial_one, swap(lax.optimization_barrier((partial_one, arrived[0]))[0])]
 
     cache = jax.ShapeDtypeStruct((slots, span, width), bf16)
     mixed = jax.ShapeDtypeStruct((slots, heads, width), f32)

time: 59.7 us -> 58.1 us (0.973)
  the two profiles are of different devices: /device:TPU:17 before, /device:TPU:0 now
where the time goes in v7:
time: 58.1 us; the launch traced here: 57.8 us
  starting transfers between devices  30 us (52%)
  waiting for transfers between devices  13.3 us (23%)
  Pallas kernels  13.1 us (23%)
  between operations  0.7 us (1%)
  other arithmetic  0.69 us (1%)
    ppermute x15, starting transfers between devices, send(): return lax.ppermute(block, 'inst', [(d, d ^ steps[i]) for d in range(n)])  29.9 us
    ppermute x15, waiting for transfers between devices, send(): return lax.ppermute(block, 'inst', [(d, d ^ steps[i]) for d in range(n)])  12 us
    pallas_call x1, Pallas kernels, shards(): pl.pallas_call(functools.partial(first_kernel, steps, span), out_shape=[j...  4.66 us
    pallas_call x2, Pallas kernels, pack(): pl.pallas_call(functools.partial(pack_kernel, n, chosen, pages), out_shap...  3.48 us
    pallas_call x1, Pallas kernels, shards(): pl.pallas_call(functools.partial(early_kernel, some, span, len(halves)),...  2.97 us
    pallas_call x1, Pallas kernels, shards(): pl.pallas_call(functools.partial(late_kernel, LATE, span), out_shape=[jax...  2.01 us
    ppermute x2, waiting for transfers between devices, swap(): return lax.ppermute(partial, 'tp', [(0, 1), (1, 0)])  1.34 us
  transfers between devices with their start and end apart: 17, of which 7 were waited for; matrix products, arithmetic and copies ran while one was open for 0% of the time, Pallas kernels for 16%

profile of v7, /device:TPU:0, one launch (start us, length us, event | category | flops | bytes accessed | tf_op | source)
XLA Modules:
  0.0 57.8 jit_solution(16861096121202956931)
XLA Ops:
  0.6 1.7 %pack.3 = (bf16[512,128]{1,0:T(8,128)(2,1)S(1)}, bf16[512,128]{1,0:T(8,128)(2,1)S(1)}, bf16[512,128]{1,0:T(8,128)(2,1)S(1)}, bf16[512,128]{1,0:T(8,128)(2,1)S(1)}, bf16[512,128]{1,0:T(8,128)(2,1)S(1)}) custom-call(s32[4,16]{1,0:T(4,128)} %bitcast.23, s32[16]{0:T(128)} %refs_0_.1, s32[16]{0:T(128)} %refs_1_.5, s32[16]{0:T(128)} %refs_3_.4, ...), custom_call_target="tpu_custom_call" | custom-call | bytes 1310720 | tf_op jit(solution)/shard_map/pack/pallas_call | solution.py:281
  2.3 4.1 %collective-permute-start = (bf16[512,128]{1,0:T(8,128)(2,1)S(1)}, bf16[512,128]{1,0:T(8,128)(2,1)S(1)}, u32[]{:S(2)}, u32[]{:S(2)}) collective-permute-start(bf16[512,128]{1,0:T(8,128)(2,1)S(1)} %get-tuple-element.44.refs_4_), channel_id=1, source_target_pairs={{0,16},{2,18},{4,20},{6,22},{8,24},{10,26},{12,28},{14,30},{16,0},... | collective-permute-start | bytes 393224 | tf_op jit(solution)/shard_map/ppermute | solution.py:321
  6.5 1.5 %collective-permute-start.1 = (bf16[512,128]{1,0:T(8,128)(2,1)S(1)}, bf16[512,128]{1,0:T(8,128)(2,1)S(1)}, u32[]{:S(2)}, u32[]{:S(2)}) collective-permute-start(bf16[512,128]{1,0:T(8,128)(2,1)S(1)} %get-tuple-element.45.refs_5_), channel_id=1, source_target_pairs={{0,2},{2,0},{4,6},{6,4},{8,10},{10,8},{12,14},{14,12},{16,18},{18,... | collective-permute-start | bytes 393224 | tf_op jit(solution)/shard_map/ppermute | solution.py:321
  7.9 0.0 collective-permute-start.2
  8.0 1.8 %collective-permute-start.3 = (bf16[512,128]{1,0:T(8,128)(2,1)S(1)}, bf16[512,128]{1,0:T(8,128)(2,1)S(1)}, u32[]{:S(2)}, u32[]{:S(2)}) collective-permute-start(bf16[512,128]{1,0:T(8,128)(2,1)S(1)} %get-tuple-element.47.refs_7_), channel_id=1, source_target_pairs={{0,4},{2,6},{4,0},{6,2},{8,12},{10,14},{12,8},{14,10},{16,20},{18,... | collective-permute-start | bytes 393224 | tf_op jit(solution)/shard_map/ppermute | solution.py:321
  9.8 2.5 %collective-permute-start.4 = (bf16[512,128]{1,0:T(8,128)(2,1)S(1)}, bf16[512,128]{1,0:T(8,128)(2,1)S(1)}, u32[]{:S(2)}, u32[]{:S(2)}) collective-permute-start(bf16[512,128]{1,0:T(8,128)(2,1)S(1)} %get-tuple-element.48.refs_8_), channel_id=1, source_target_pairs={{0,20},{2,22},{4,16},{6,18},{8,28},{10,30},{12,24},{14,26},{16,4},... | collective-permute-start | bytes 393224 | tf_op jit(solution)/shard_map/ppermute | solution.py:321
  12.3 1.8 %pack.2 = (bf16[512,128]{1,0:T(8,128)(2,1)S(1)}, bf16[512,128]{1,0:T(8,128)(2,1)S(1)}, bf16[512,128]{1,0:T(8,128)(2,1)S(1)}, bf16[512,128]{1,0:T(8,128)(2,1)S(1)...) custom-call(s32[4,16]{1,0:T(4,128)} %bitcast.24, ...), custom_call_target="tpu_custom_call" | custom-call | bytes 2883584 | tf_op jit(solution)/shard_map/pack/pallas_call | solution.py:281
  14.1 4.7 %first.1 = (bf16[16,4096]{1,0:T(8,128)(2,1)S(1)}, bf16[1024,4096]{1,0:T(8,128)(2,1)S(1)}) custom-call(s32[16]{0:T(128)} %refs_0_.1, s32[16]{0:T(128)} %refs_1_.5, bf16[16,8,128]{2,1,0:T(8,128)(2,1)} %refs_2_.5, bf16[1024,4096]{1,0:T(8,128)(2,1)} %refs_3_.5, bf16[512,128]{1,0:T(8,128)(2,1)S(1)} %get-tuple-element.44.refs_4_, ...), custom_call_target="tpu_custom_call" | custom-call | flops 150994944 | bytes 10485760 | tf_op jit(solution)/shard_map/first/pallas_call | solution.py:324
  18.7 0.5 collective-permute-done.refs_1_
  19.2 2.8 %collective-permute-start.5 = (bf16[512,128]{1,0:T(8,128)(2,1)S(1)}, bf16[512,128]{1,0:T(8,128)(2,1)S(1)}, u32[]{:S(2)}, u32[]{:S(2)}) collective-permute-start(bf16[512,128]{1,0:T(8,128)(2,1)S(1)} %get-tuple-element.60.refs_9_), channel_id=1, source_target_pairs={{0,6},{2,4},{4,2},{6,0},{8,14},{10,12},{12,10},{14,8},{16,22},{18,... | collective-permute-start | bytes 393224 | tf_op jit(solution)/shard_map/ppermute | solution.py:321
  22.0 0.0 collective-permute-done.1.refs_2_
  22.0 0.0 collective-permute-start.6
  22.0 1.3 %collective-permute-done.2.refs_3_ = bf16[512,128]{1,0:T(8,128)(2,1)S(1)} collective-permute-done((bf16[512,128]{1,0:T(8,128)(2,1)S(1)}, bf16[512,128]{1,0:T(8,128)(2,1)S(1)}, u32[]{:S(2)}, u32[]{:S(2)}) %collective-permute-start.2) | collective-permute-done | bytes 131104 | tf_op jit(solution)/shard_map/ppermute | solution.py:321
  23.3 1.7 %collective-permute-start.7 = (bf16[512,128]{1,0:T(8,128)(2,1)S(1)}, bf16[512,128]{1,0:T(8,128)(2,1)S(1)}, u32[]{:S(2)}, u32[]{:S(2)}) collective-permute-start(bf16[512,128]{1,0:T(8,128)(2,1)S(1)} %get-tuple-element.62.refs_11_), channel_id=1, source_target_pairs={{0,8},{2,10},{4,12},{6,14},{8,0},{10,2},{12,4},{14,6},{16,24},{18,... | collective-permute-start | bytes 393224 | tf_op jit(solution)/shard_map/ppermute | solution.py:321
  24.9 0.0 collective-permute-done.3.refs_4_
  24.9 2.2 %collective-permute-start.8 = (bf16[512,128]{1,0:T(8,128)(2,1)S(1)}, bf16[512,128]{1,0:T(8,128)(2,1)S(1)}, u32[]{:S(2)}, u32[]{:S(2)}) collective-permute-start(bf16[512,128]{1,0:T(8,128)(2,1)S(1)} %get-tuple-element.63.refs_12_), channel_id=1, source_target_pairs={{0,24},{2,26},{4,28},{6,30},{8,16},{10,18},{12,20},{14,22},{16,8},... | collective-permute-start | bytes 393224 | tf_op jit(solution)/shard_map/ppermute | solution.py:321
  27.2 0.5 collective-permute-done.4.refs_5_
  27.7 1.0 %collective-permute-start.9 = (bf16[512,128]{1,0:T(8,128)(2,1)S(1)}, bf16[512,128]{1,0:T(8,128)(2,1)S(1)}, u32[]{:S(2)}, u32[]{:S(2)}) collective-permute-start(bf16[512,128]{1,0:T(8,128)(2,1)S(1)} %get-tuple-element.64.refs_13_), channel_id=1, source_target_pairs={{0,10},{2,8},{4,14},{6,12},{8,2},{10,0},{12,6},{14,4},{16,26},{18,... | collective-permute-start | bytes 393224 | tf_op jit(solution)/shard_map/ppermute | solution.py:321
  28.7 0.0 collective-permute-done.5.refs_6_
  28.7 0.0 collective-permute-start.10
  28.7 5.1 %collective-permute-done.6.refs_7_ = bf16[512,128]{1,0:T(8,128)(2,1)S(1)} collective-permute-done((bf16[512,128]{1,0:T(8,128)(2,1)S(1)}, bf16[512,128]{1,0:T(8,128)(2,1)S(1)}, u32[]{:S(2)}, u32[]{:S(2)}) %collective-permute-start.6) | collective-permute-done | bytes 131104 | tf_op jit(solution)/shard_map/ppermute | solution.py:321
  33.8 4.5 %collective-permute-start.11 = (bf16[512,128]{1,0:T(8,128)(2,1)S(1)}, bf16[512,128]{1,0:T(8,128)(2,1)S(1)}, u32[]{:S(2)}, u32[]{:S(2)}) collective-permute-start(bf16[512,128]{1,0:T(8,128)(2,1)S(1)} %get-tuple-element.67.refs_14_), channel_id=1, source_target_pairs={{0,26},{2,24},{4,30},{6,28},{8,18},{10,16},{12,22},{14,20},{16,10}... | collective-permute-start | bytes 393224 | tf_op jit(solution)/shard_map/ppermute | solution.py:321
  38.3 0.0 collective-permute-done.7.refs_8_
  38.3 0.0 collective-permute-start.12
  38.3 0.0 collective-permute-done.8.refs_9_
  38.3 1.9 %collective-permute-start.13 = (bf16[512,128]{1,0:T(8,128)(2,1)S(1)}, bf16[512,128]{1,0:T(8,128)(2,1)S(1)}, u32[]{:S(2)}, u32[]{:S(2)}) collective-permute-start(bf16[512,128]{1,0:T(8,128)(2,1)S(1)} %get-tuple-element.69.refs_16_), channel_id=1, source_target_pairs={{0,28},{2,30},{4,24},{6,26},{8,20},{10,22},{12,16},{14,18},{16,12}... | collective-permute-start | bytes 393224 | tf_op jit(solution)/shard_map/ppermute | solution.py:321
  40.2 0.0 collective-permute-done.9.refs_10_
  40.2 2.6 %collective-permute-start.14 = (bf16[512,128]{1,0:T(8,128)(2,1)S(1)}, bf16[512,128]{1,0:T(8,128)(2,1)S(1)}, u32[]{:S(2)}, u32[]{:S(2)}) collective-permute-start(bf16[512,128]{1,0:T(8,128)(2,1)S(1)} %get-tuple-element.70.refs_17_), channel_id=1, source_target_pairs={{0,14},{2,12},{4,10},{6,8},{8,6},{10,4},{12,2},{14,0},{16,30},{18,... | collective-permute-start | bytes 393224 | tf_op jit(solution)/shard_map/ppermute | solution.py:321
  42.8 0.0 collective-permute-done.10.refs_15_
  42.8 3.3 %collective-permute-start.15 = (bf16[512,128]{1,0:T(8,128)(2,1)S(1)}, bf16[512,128]{1,0:T(8,128)(2,1)S(1)}, u32[]{:S(2)}, u32[]{:S(2)}) collective-permute-start(bf16[512,128]{1,0:T(8,128)(2,1)S(1)} %get-tuple-element.71.refs_18_), channel_id=1, source_target_pairs={{0,30},{2,28},{4,26},{6,24},{8,22},{10,20},{12,18},{14,16},{16,14}... | collective-permute-start | bytes 393224 | tf_op jit(solution)/shard_map/ppermute | solution.py:321
  46.1 3.0 %early.1 = (bf16[16,256,128]{2,1,0:T(8,128)(2,1)}, bf16[16,256,128]{2,1,0:T(8,128)(2,1)}, f32[16,8,128]{2,1,0:T(8,128)S(1)}, bf16[16,8,128]{2,1,0:T(8,128)(2,1)S...) custom-call(bf16[512,128]{1,0:T(8,128)(2,1)S(1)} %get-tuple-element.43.refs_19_.refs_0_, ...), custom_call_target="tpu_custom_call" | custom-call | flops 11534336 | bytes 2883584 | tf_op jit(solution)/shard_map/early/pallas_call | solution.py:354
  49.0 0.0 collective-permute-done.11.refs_0_
  49.0 0.1 collective-permute-done.12.refs_1_
  49.2 0.0 collective-permute-done.13.refs_2_
  49.2 4.5 %collective-permute-done.14.refs_3_ = bf16[512,128]{1,0:T(8,128)(2,1)S(1)} collective-permute-done((bf16[512,128]{1,0:T(8,128)(2,1)S(1)}, bf16[512,128]{1,0:T(8,128)(2,1)S(1)}, u32[]{:S(2)}, u32[]{:S(2)}) %collective-permute-start.14) | collective-permute-done | bytes 131104 | tf_op jit(solution)/shard_map/ppermute | solution.py:321
  53.7 0.0 collective-permute-done.15.refs_4_
  53.7 2.0 %late.1 = (bf16[16,4096]{1,0:T(8,128)(2,1)S(1)}, bf16[16,256,128]{2,1,0:T(8,128)(2,1)}, bf16[16,256,128]{2,1,0:T(8,128)(2,1)}) custom-call(bf16[512,128]{1,0:T(8,128)(2,1)S(1)} %collective-permute-done.11.refs_0_, bf16[512,128]{1,0:T(8,128)(2,1)S(1)} %collective-permute-done.12.refs_1_, ...), custom_call_target="tpu_custom_call", output_to_operand_aliasing={{1}: (10, {}), {2}: (11, {})} | custom-call | flops 150994944 | bytes 10485760 | tf_op jit(solution)/shard_map/late/pallas_call | solution.py:380
  55.7 0.1 collective-permute-start.16
  55.8 1.3 %collective-permute-done.16 = bf16[16,4096]{1,0:T(8,128)(2,1)S(1)} collective-permute-done((bf16[16,4096]{1,0:T(8,128)(2,1)S(1)}, bf16[16,4096]{1,0:T(8,128)(2,1)S(1)}, u32[]{:S(2)}, u32[]{:S(2)}) %collective-permute-start.16) | collective-permute-done | bytes 131104 | tf_op jit(solution)/shard_map/ppermute | solution.py:211
  57.1 0.7 %add_convert_fusion = bf16[16,4096]{1,0:T(8,128)(2,1)} fusion(bf16[16,4096]{1,0:T(8,128)(2,1)S(1)} %collective-permute-done.16, bf16[16,4096]{1,0:T(8,128)(2,1)S(1)} %get-tuple-element.79), kind=kLoop, calls=%fused_computation | loop fusion | flops 262144 | bytes 393216 | tf_op jit(solution)/shard_map/convert_element_type | solution.py:404
Async XLA Ops:
  2.3 16.9 %collective-permute-start = (bf16[512,128]{1,0:T(8,128)(2,1)S(1)}, bf16[512,128]{1,0:T(8,128)(2,1)S(1)}, u32[]{:S(2)}, u32[]{:S(2)}) collective-permute-start(bf16[512,128]{1,0:T(8,128)(2,1)S(1)} %get-tuple-element.44.refs_4_), channel_id=1, source_target_pairs={{0,16},{2,18},{4,20},{6,22},{8,24},{10,26},{12,28},{14,30},{16,0},... | collective-permute-start | bytes 393224 | tf_op jit(solution)/shard_map/ppermute | solution.py:321
  6.5 15.5 %collective-permute-start.1 = (bf16[512,128]{1,0:T(8,128)(2,1)S(1)}, bf16[512,128]{1,0:T(8,128)(2,1)S(1)}, u32[]{:S(2)}, u32[]{:S(2)}) collective-permute-start(bf16[512,128]{1,0:T(8,128)(2,1)S(1)} %get-tuple-element.45.refs_5_), channel_id=1, source_target_pairs={{0,2},{2,0},{4,6},{6,4},{8,10},{10,8},{12,14},{14,12},{16,18},{18,... | collective-permute-start | bytes 393224 | tf_op jit(solution)/shard_map/ppermute | solution.py:321
  7.9 15.3 %collective-permute-start.2 = (bf16[512,128]{1,0:T(8,128)(2,1)S(1)}, bf16[512,128]{1,0:T(8,128)(2,1)S(1)}, u32[]{:S(2)}, u32[]{:S(2)}) collective-permute-start(bf16[512,128]{1,0:T(8,128)(2,1)S(1)} %get-tuple-element.46.refs_6_), channel_id=1, source_target_pairs={{0,18},{2,16},{4,22},{6,20},{8,26},{10,24},{12,30},{14,28},{16,2},... | collective-permute-start | bytes 393224 | tf_op jit(solution)/shard_map/ppermute | solution.py:321
  8.0 16.9 %collective-permute-start.3 = (bf16[512,128]{1,0:T(8,128)(2,1)S(1)}, bf16[512,128]{1,0:T(8,128)(2,1)S(1)}, u32[]{:S(2)}, u32[]{:S(2)}) collective-permute-start(bf16[512,128]{1,0:T(8,128)(2,1)S(1)} %get-tuple-element.47.refs_7_), channel_id=1, source_target_pairs={{0,4},{2,6},{4,0},{6,2},{8,12},{10,14},{12,8},{14,10},{16,20},{18,... | collective-permute-start | bytes 393224 | tf_op jit(solution)/shard_map/ppermute | solution.py:321
  9.8 17.9 %collective-permute-start.4 = (bf16[512,128]{1,0:T(8,128)(2,1)S(1)}, bf16[512,128]{1,0:T(8,128)(2,1)S(1)}, u32[]{:S(2)}, u32[]{:S(2)}) collective-permute-start(bf16[512,128]{1,0:T(8,128)(2,1)S(1)} %get-tuple-element.48.refs_8_), channel_id=1, source_target_pairs={{0,20},{2,22},{4,16},{6,18},{8,28},{10,30},{12,24},{14,26},{16,4},... | collective-permute-start | bytes 393224 | tf_op jit(solution)/shard_map/ppermute | solution.py:321
  19.2 9.5 %collective-permute-start.5 = (bf16[512,128]{1,0:T(8,128)(2,1)S(1)}, bf16[512,128]{1,0:T(8,128)(2,1)S(1)}, u32[]{:S(2)}, u32[]{:S(2)}) collective-permute-start(bf16[512,128]{1,0:T(8,128)(2,1)S(1)} %get-tuple-element.60.refs_9_), channel_id=1, source_target_pairs={{0,6},{2,4},{4,2},{6,0},{8,14},{10,12},{12,10},{14,8},{16,22},{18,... | collective-permute-start | bytes 393224 | tf_op jit(solution)/shard_map/ppermute | solution.py:321
  22.0 11.8 %collective-permute-start.6 = (bf16[512,128]{1,0:T(8,128)(2,1)S(1)}, bf16[512,128]{1,0:T(8,128)(2,1)S(1)}, u32[]{:S(2)}, u32[]{:S(2)}) collective-permute-start(bf16[512,128]{1,0:T(8,128)(2,1)S(1)} %get-tuple-element.61.refs_10_), channel_id=1, source_target_pairs={{0,22},{2,20},{4,18},{6,16},{8,30},{10,28},{12,26},{14,24},{16,6},... | collective-permute-start | bytes 393224 | tf_op jit(solution)/shard_map/ppermute | solution.py:321
  23.3 15.0 %collective-permute-start.7 = (bf16[512,128]{1,0:T(8,128)(2,1)S(1)}, bf16[512,128]{1,0:T(8,128)(2,1)S(1)}, u32[]{:S(2)}, u32[]{:S(2)}) collective-permute-start(bf16[512,128]{1,0:T(8,128)(2,1)S(1)} %get-tuple-element.62.refs_11_), channel_id=1, source_target_pairs={{0,8},{2,10},{4,12},{6,14},{8,0},{10,2},{12,4},{14,6},{16,24},{18,... | collective-permute-start | bytes 393224 | tf_op jit(solution)/shard_map/ppermute | solution.py:321
  24.9 13.4 %collective-permute-start.8 = (bf16[512,128]{1,0:T(8,128)(2,1)S(1)}, bf16[512,128]{1,0:T(8,128)(2,1)S(1)}, u32[]{:S(2)}, u32[]{:S(2)}) collective-permute-start(bf16[512,128]{1,0:T(8,128)(2,1)S(1)} %get-tuple-element.63.refs_12_), channel_id=1, source_target_pairs={{0,24},{2,26},{4,28},{6,30},{8,16},{10,18},{12,20},{14,22},{16,8},... | collective-permute-start | bytes 393224 | tf_op jit(solution)/shard_map/ppermute | solution.py:321
  27.7 12.5 %collective-permute-start.9 = (bf16[512,128]{1,0:T(8,128)(2,1)S(1)}, bf16[512,128]{1,0:T(8,128)(2,1)S(1)}, u32[]{:S(2)}, u32[]{:S(2)}) collective-permute-start(bf16[512,128]{1,0:T(8,128)(2,1)S(1)} %get-tuple-element.64.refs_13_), channel_id=1, source_target_pairs={{0,10},{2,8},{4,14},{6,12},{8,2},{10,0},{12,6},{14,4},{16,26},{18,... | collective-permute-start | bytes 393224 | tf_op jit(solution)/shard_map/ppermute | solution.py:321
  28.7 14.1 %collective-permute-start.10 = (bf16[16,4096]{1,0:T(8,128)(2,1)S(1)}, bf16[16,4096]{1,0:T(8,128)(2,1)S(1)}, u32[]{:S(2)}, u32[]{:S(2)}) collective-permute-start(bf16[16,4096]{1,0:T(8,128)(2,1)S(1)} %get-tuple-element.65.refs_14_), channel_id=1, source_target_pairs={{0,1},{1,0},{2,3},{3,2},{4,5},{5,4},{6,7},{7,6},{8,9},{9,8},{10,11... | collective-permute-start | bytes 393224 | tf_op jit(solution)/shard_map/ppermute | solution.py:211
  33.8 15.3 %collective-permute-start.11 = (bf16[512,128]{1,0:T(8,128)(2,1)S(1)}, bf16[512,128]{1,0:T(8,128)(2,1)S(1)}, u32[]{:S(2)}, u32[]{:S(2)}) collective-permute-start(bf16[512,128]{1,0:T(8,128)(2,1)S(1)} %get-tuple-element.67.refs_14_), channel_id=1, source_target_pairs={{0,26},{2,24},{4,30},{6,28},{8,18},{10,16},{12,22},{14,20},{16,10}... | collective-permute-start | bytes 393224 | tf_op jit(solution)/shard_map/ppermute | solution.py:321
  38.3 10.9 %collective-permute-start.12 = (bf16[512,128]{1,0:T(8,128)(2,1)S(1)}, bf16[512,128]{1,0:T(8,128)(2,1)S(1)}, u32[]{:S(2)}, u32[]{:S(2)}) collective-permute-start(bf16[512,128]{1,0:T(8,128)(2,1)S(1)} %get-tuple-element.68.refs_15_), channel_id=1, source_target_pairs={{0,12},{2,14},{4,8},{6,10},{8,4},{10,6},{12,0},{14,2},{16,28},{18,... | collective-permute-start | bytes 393224 | tf_op jit(solution)/shard_map/ppermute | solution.py:321
  38.3 10.9 %collective-permute-start.13 = (bf16[512,128]{1,0:T(8,128)(2,1)S(1)}, bf16[512,128]{1,0:T(8,128)(2,1)S(1)}, u32[]{:S(2)}, u32[]{:S(2)}) collective-permute-start(bf16[512,128]{1,0:T(8,128)(2,1)S(1)} %get-tuple-element.69.refs_16_), channel_id=1, source_target_pairs={{0,28},{2,30},{4,24},{6,26},{8,20},{10,22},{12,16},{14,18},{16,12}... | collective-permute-start | bytes 393224 | tf_op jit(solution)/shard_map/ppermute | solution.py:321
  40.2 13.5 %collective-permute-start.14 = (bf16[512,128]{1,0:T(8,128)(2,1)S(1)}, bf16[512,128]{1,0:T(8,128)(2,1)S(1)}, u32[]{:S(2)}, u32[]{:S(2)}) collective-permute-start(bf16[512,128]{1,0:T(8,128)(2,1)S(1)} %get-tuple-element.70.refs_17_), channel_id=1, source_target_pairs={{0,14},{2,12},{4,10},{6,8},{8,6},{10,4},{12,2},{14,0},{16,30},{18,... | collective-permute-start | bytes 393224 | tf_op jit(solution)/shard_map/ppermute | solution.py:321
  42.8 10.9 %collective-permute-start.15 = (bf16[512,128]{1,0:T(8,128)(2,1)S(1)}, bf16[512,128]{1,0:T(8,128)(2,1)S(1)}, u32[]{:S(2)}, u32[]{:S(2)}) collective-permute-start(bf16[512,128]{1,0:T(8,128)(2,1)S(1)} %get-tuple-element.71.refs_18_), channel_id=1, source_target_pairs={{0,30},{2,28},{4,26},{6,24},{8,22},{10,20},{12,18},{14,16},{16,14}... | collective-permute-start | bytes 393224 | tf_op jit(solution)/shard_map/ppermute | solution.py:321
  55.7 1.4 %collective-permute-start.16 = (bf16[16,4096]{1,0:T(8,128)(2,1)S(1)}, bf16[16,4096]{1,0:T(8,128)(2,1)S(1)}, u32[]{:S(2)}, u32[]{:S(2)}) collective-permute-start(bf16[16,4096]{1,0:T(8,128)(2,1)S(1)} %get-tuple-element.79), channel_id=1, source_target_pairs={{0,1},{1,0},{2,3},{3,2},{4,5},{5,4},{6,7},{7,6},{8,9},{9,8},{10,11... | collective-permute-start | bytes 393224 | tf_op jit(solution)/shard_map/ppermute | solution.py:211

commit v8 on v7

--- a/solution.py
+++ b/solution.py
@@ -12,7 +12,7 @@
 SPLIT = 64
 CHUNKS = 8
 AHEAD = 5
-LATE = 5
+LATE = 4
 VMEM_BYTES = 24 * 1024 * 1024
 
 
@@ -181,15 +181,11 @@
     return outgoing
 
 
-def early_kernel(count, span, pair, *refs):
-    arrived, far, halves = refs[:count], refs[count : count + 3], refs[count + 3 : count + 3 + pair]
-    key_cache, value_cache, mixed, query, new_k, new_v = refs[count + 3 + pair : count + 9 + pair]
+def early_kernel(count, span, *refs):
+    arrived, far = refs[:count], refs[count : count + 3]
+    key_cache, value_cache, mixed, query, new_k, new_v = refs[count + 3 : count + 9]
     key_two, value_two, held, sems, osems = refs[-5:]
     copies = begin(list(zip(far, (query, key_two, value_two))), sems)
-    if pair:
-        out = refs[count + 9 + pair]
-        both = halves[0][...].astype(jnp.float32) + halves[1][...].astype(jnp.float32)
-        out[...] = both.astype(jnp.bfloat16)
     finish(copies)
     new_k[...] = key_two[...].astype(jnp.float32)
     new_v[...] = value_two[...].astype(jnp.float32)
@@ -197,12 +193,16 @@
     finish(place(parcels, query, new_k, new_v, key_cache, value_cache, held, mixed, osems))
 
 
-def late_kernel(count, span, *refs):
+def late_kernel(count, span, pair, *refs):
     arrived, (query, new_k, new_v, weight, before) = refs[:count], refs[count : count + 5]
-    out, key_cache, value_cache, held, mixed, osems = refs[count + 7 :]
+    halves, (out, key_cache, value_cache) = refs[count + 7 : count + 7 + pair], refs[count + 7 + pair : count + 10 + pair]
+    held, mixed, osems = refs[-3:]
     mixed[...] = before[...]
     parcels = parcels_of(arrived, span)
     outgoing = place(parcels, query, new_k, new_v, key_cache, value_cache, held, mixed, osems)
+    if pair:
+        both = halves[0][...].astype(jnp.float32) + halves[1][...].astype(jnp.float32)
+        refs[count + 10 + pair][...] = both.astype(jnp.bfloat16)
     project(mixed, weight, out)
     finish(outgoing)
 
@@ -221,10 +221,10 @@
 
 def step_order(n):
     half = n // 2
-    crossing = list(range(half, n))
-    staying = list(range(1, half))
+    crossing = list(range(half, n))[::-1]
+    staying = list(range(1, half))[::-1]
     order = []
-    for kind in "cncncncncncncnc":
+    for kind in "cnccncnccncncnn":
         queue = crossing if kind == "c" else staying
         if queue:
             order.append(queue.pop(0))
@@ -352,13 +352,12 @@
     mixed = jax.ShapeDtypeStruct((slots, heads, width), f32)
     some = len(early)
     results = pl.pallas_call(
-        functools.partial(early_kernel, some, span, len(halves)),
+        functools.partial(early_kernel, some, span),
         out_shape=[cache, cache, mixed]
         + [jax.ShapeDtypeStruct((slots, heads, width), bf16)]
-        + [jax.ShapeDtypeStruct((slots, width), f32)] * 2
-        + [jax.ShapeDtypeStruct((slots, columns), bf16)] * (len(halves) // 2),
-        in_specs=[vmem] * some + [far] * 3 + [vmem] * len(halves),
-        out_specs=[far, far] + [vmem] * (4 + len(halves) // 2),
+        + [jax.ShapeDtypeStruct((slots, width), f32)] * 2,
+        in_specs=[vmem] * some + [far] * 3,
+        out_specs=[far, far] + [vmem] * 4,
         scratch_shapes=[
             pltpu.VMEM((slots, width), bf16),
             pltpu.VMEM((slots, width), bf16),
@@ -373,15 +372,15 @@
             transcendentals=some * heads * span,
         ),
         name="early",
-    )(*early, hbm(query_two), hbm(key_two), hbm(value_two), *halves)
-    key_cache, value_cache, *carried = results[:6]
-    out_one = results[6] if halves else lax.psum(partial_one, "tp")
-
-    partial_two, key_cache, value_cache = pl.pallas_call(
-        functools.partial(late_kernel, LATE, span),
-        out_shape=[jax.ShapeDtypeStruct((slots, columns), bf16), cache, cache],
-        in_specs=[vmem] * (len(late) + 5) + [far] * 2,
-        out_specs=[vmem, far, far],
+    )(*early, hbm(query_two), hbm(key_two), hbm(value_two))
+    key_cache, value_cache, *carried = results
+
+    partial_two, key_cache, value_cache, *sums = pl.pallas_call(
+        functools.partial(late_kernel, LATE, span, len(halves)),
+        out_shape=[jax.ShapeDtypeStruct((slots, columns), bf16), cache, cache]
+        + [jax.ShapeDtypeStruct((slots, columns), bf16)] * (len(halves) // 2),
+        in_specs=[vmem] * (len(late) + 5) + [far] * 2 + [vmem] * len(halves),
+        out_specs=[vmem, far, far] + [vmem] * (len(halves) // 2),
         input_output_aliases={len(late) + 5: 1, len(late) + 6: 2},
         scratch_shapes=[
             pltpu.VMEM((2, LATE, span, width), bf16),
@@ -398,7 +397,9 @@
         near(carried[0]),
         hbm(key_cache),
         hbm(value_cache),
+        *halves,
     )
+    out_one = sums[0] if sums else lax.psum(partial_one, "tp")
     if tp == 2:
         both = partial_two.astype(f32) + swap(partial_two).astype(f32)
         out_two = both.astype(bf16)

time: 58.1 us -> 60.8 us (1.046)
  starting transfers between devices: 30 us -> 33.8 us
  waiting for transfers between devices: 13.3 us -> 12.3 us
    ppermute x15, starting transfers between devices: 29.9 us -> 33.7 us  [send(): return lax.ppermute(block, 'inst', [(d, d ^ steps[i]) for d in range(n)])]
    ppermute x15, waiting for transfers between devices: 12 us -> 10.9 us  [send(): return lax.ppermute(block, 'inst', [(d, d ^ steps[i]) for d in range(n)])]
  transfers between devices with their start and end apart: 17 -> 17, of which waited for: 7 -> 5; matrix products, arithmetic and copies ran while one was open for 0% -> 0% of each run, Pallas kernels for 16% -> 15%
where the time goes in v8:
time: 60.8 us; the launch traced here: 60.6 us
  starting transfers between devices  33.8 us (56%)
  Pallas kernels  13.1 us (22%)
  waiting for transfers between devices  12.3 us (20%)
  between operations  0.72 us (1%)
  other arithmetic  0.69 us (1%)
    ppermute x15, starting transfers between devices, send(): return lax.ppermute(block, 'inst', [(d, d ^ steps[i]) for d in range(n)])  33.7 us
    ppermute x15, waiting for transfers between devices, send(): return lax.ppermute(block, 'inst', [(d, d ^ steps[i]) for d in range(n)])  10.9 us
    pallas_call x1, Pallas kernels, shards(): pl.pallas_call(functools.partial(first_kernel, steps, span), out_shape=[j...  4.66 us
    pallas_call x2, Pallas kernels, pack(): pl.pallas_call(functools.partial(pack_kernel, n, chosen, pages), out_shap...  3.48 us
    pallas_call x1, Pallas kernels, shards(): pl.pallas_call(functools.partial(late_kernel, LATE, span, len(halves)), o...  2.6 us
    pallas_call x1, Pallas kernels, shards(): pl.pallas_call(functools.partial(early_kernel, some, span), out_shape=[ca...  2.38 us
    ppermute x2, waiting for transfers between devices, swap(): return lax.ppermute(partial, 'tp', [(0, 1), (1, 0)])  1.34 us
  transfers between devices with their start and end apart: 17, of which 5 were waited for; matrix products, arithmetic and copies ran while one was open for 0% of the time, Pallas kernels for 15%

profile of v8, /device:TPU:0, one launch (start us, length us, event | category | flops | bytes accessed | tf_op | source)
XLA Modules:
  0.0 60.6 jit_solution(5766437554953221835)
XLA Ops:
  0.6 1.7 %pack.3 = (bf16[512,128]{1,0:T(8,128)(2,1)S(1)}, bf16[512,128]{1,0:T(8,128)(2,1)S(1)}, bf16[512,128]{1,0:T(8,128)(2,1)S(1)}, bf16[512,128]{1,0:T(8,128)(2,1)S(1)}, bf16[512,128]{1,0:T(8,128)(2,1)S(1)}) custom-call(s32[4,16]{1,0:T(4,128)} %bitcast.23, s32[16]{0:T(128)} %refs_0_.1, s32[16]{0:T(128)} %refs_1_.5, s32[16]{0:T(128)} %refs_3_.4, ...), custom_call_target="tpu_custom_call" | custom-call | bytes 1310720 | tf_op jit(solution)/shard_map/pack/pallas_call | solution.py:281
  2.3 7.0 %collective-permute-start.4 = (bf16[512,128]{1,0:T(8,128)(2,1)S(1)}, bf16[512,128]{1,0:T(8,128)(2,1)S(1)}, u32[]{:S(2)}, u32[]{:S(2)}) collective-permute-start(bf16[512,128]{1,0:T(8,128)(2,1)S(1)} %get-tuple-element.44.refs_4_), channel_id=1, source_target_pairs={{0,30},{2,28},{4,26},{6,24},{8,22},{10,20},{12,18},{14,16},{16,14}... | collective-permute-start | bytes 393224 | tf_op jit(solution)/shard_map/ppermute | solution.py:321
  9.3 0.0 collective-permute-start.5
  9.3 1.8 %collective-permute-start.6 = (bf16[512,128]{1,0:T(8,128)(2,1)S(1)}, bf16[512,128]{1,0:T(8,128)(2,1)S(1)}, u32[]{:S(2)}, u32[]{:S(2)}) collective-permute-start(bf16[512,128]{1,0:T(8,128)(2,1)S(1)} %get-tuple-element.46.refs_6_), channel_id=1, source_target_pairs={{0,28},{2,30},{4,24},{6,26},{8,20},{10,22},{12,16},{14,18},{16,12}... | collective-permute-start | bytes 393224 | tf_op jit(solution)/shard_map/ppermute | solution.py:321
  11.1 3.4 %collective-permute-start.7 = (bf16[512,128]{1,0:T(8,128)(2,1)S(1)}, bf16[512,128]{1,0:T(8,128)(2,1)S(1)}, u32[]{:S(2)}, u32[]{:S(2)}) collective-permute-start(bf16[512,128]{1,0:T(8,128)(2,1)S(1)} %get-tuple-element.47.refs_7_), channel_id=1, source_target_pairs={{0,26},{2,24},{4,30},{6,28},{8,18},{10,16},{12,22},{14,20},{16,10}... | collective-permute-start | bytes 393224 | tf_op jit(solution)/shard_map/ppermute | solution.py:321
  14.5 0.6 %collective-permute-start.8 = (bf16[512,128]{1,0:T(8,128)(2,1)S(1)}, bf16[512,128]{1,0:T(8,128)(2,1)S(1)}, u32[]{:S(2)}, u32[]{:S(2)}) collective-permute-start(bf16[512,128]{1,0:T(8,128)(2,1)S(1)} %get-tuple-element.48.refs_8_), channel_id=1, source_target_pairs={{0,12},{2,14},{4,8},{6,10},{8,4},{10,6},{12,0},{14,2},{16,28},{18,... | collective-permute-start | bytes 393224 | tf_op jit(solution)/shard_map/ppermute | solution.py:321
  15.1 1.8 %pack.2 = (bf16[512,128]{1,0:T(8,128)(2,1)S(1)}, bf16[512,128]{1,0:T(8,128)(2,1)S(1)}, bf16[512,128]{1,0:T(8,128)(2,1)S(1)}, bf16[512,128]{1,0:T(8,128)(2,1)S(1)...) custom-call(s32[4,16]{1,0:T(4,128)} %bitcast.24, ...), custom_call_target="tpu_custom_call" | custom-call | bytes 2883584 | tf_op jit(solution)/shard_map/pack/pallas_call | solution.py:281
  16.9 4.7 %first.1 = (bf16[16,4096]{1,0:T(8,128)(2,1)S(1)}, bf16[1024,4096]{1,0:T(8,128)(2,1)S(1)}) custom-call(s32[16]{0:T(128)} %refs_0_.1, s32[16]{0:T(128)} %refs_1_.5, bf16[16,8,128]{2,1,0:T(8,128)(2,1)} %refs_2_.5, bf16[1024,4096]{1,0:T(8,128)(2,1)} %refs_3_.5, bf16[512,128]{1,0:T(8,128)(2,1)S(1)} %get-tuple-element.44.refs_4_, ...), custom_call_target="tpu_custom_call" | custom-call | flops 150994944 | bytes 10485760 | tf_op jit(solution)/shard_map/first/pallas_call | solution.py:324
  21.6 0.0 collective-permute-done.4.refs_1_
  21.6 1.0 %collective-permute-start.9 = (bf16[512,128]{1,0:T(8,128)(2,1)S(1)}, bf16[512,128]{1,0:T(8,128)(2,1)S(1)}, u32[]{:S(2)}, u32[]{:S(2)}) collective-permute-start(bf16[512,128]{1,0:T(8,128)(2,1)S(1)} %get-tuple-element.64.refs_9_), channel_id=1, source_target_pairs={{0,24},{2,26},{4,28},{6,30},{8,16},{10,18},{12,20},{14,22},{16,8},... | collective-permute-start | bytes 393224 | tf_op jit(solution)/shard_map/ppermute | solution.py:321
  22.6 0.0 collective-permute-done.5.refs_2_
  22.6 1.0 %collective-permute-start.10 = (bf16[512,128]{1,0:T(8,128)(2,1)S(1)}, bf16[512,128]{1,0:T(8,128)(2,1)S(1)}, u32[]{:S(2)}, u32[]{:S(2)}) collective-permute-start(bf16[512,128]{1,0:T(8,128)(2,1)S(1)} %get-tuple-element.65.refs_10_), channel_id=1, source_target_pairs={{0,10},{2,8},{4,14},{6,12},{8,2},{10,0},{12,6},{14,4},{16,26},{18,... | collective-permute-start | bytes 393224 | tf_op jit(solution)/shard_map/ppermute | solution.py:321
  23.6 0.0 collective-permute-done.6.refs_3_
  23.6 4.3 %collective-permute-start.11 = (bf16[512,128]{1,0:T(8,128)(2,1)S(1)}, bf16[512,128]{1,0:T(8,128)(2,1)S(1)}, u32[]{:S(2)}, u32[]{:S(2)}) collective-permute-start(bf16[512,128]{1,0:T(8,128)(2,1)S(1)} %get-tuple-element.66.refs_11_), channel_id=1, source_target_pairs={{0,22},{2,20},{4,18},{6,16},{8,30},{10,28},{12,26},{14,24},{16,6},... | collective-permute-start | bytes 393224 | tf_op jit(solution)/shard_map/ppermute | solution.py:321
  27.9 0.0 collective-permute-done.7.refs_4_
  27.9 3.0 %collective-permute-start.12 = (bf16[512,128]{1,0:T(8,128)(2,1)S(1)}, bf16[512,128]{1,0:T(8,128)(2,1)S(1)}, u32[]{:S(2)}, u32[]{:S(2)}) collective-permute-start(bf16[512,128]{1,0:T(8,128)(2,1)S(1)} %get-tuple-element.67.refs_12_), channel_id=1, source_target_pairs={{0,20},{2,22},{4,16},{6,18},{8,28},{10,30},{12,24},{14,26},{16,4},... | collective-permute-start | bytes 393224 | tf_op jit(solution)/shard_map/ppermute | solution.py:321
  30.9 0.0 collective-permute-done.8.refs_5_
  30.9 1.1 %collective-permute-start.13 = (bf16[512,128]{1,0:T(8,128)(2,1)S(1)}, bf16[512,128]{1,0:T(8,128)(2,1)S(1)}, u32[]{:S(2)}, u32[]{:S(2)}) collective-permute-start(bf16[512,128]{1,0:T(8,128)(2,1)S(1)} %get-tuple-element.68.refs_13_), channel_id=1, source_target_pairs={{0,8},{2,10},{4,12},{6,14},{8,0},{10,2},{12,4},{14,6},{16,24},{18,... | collective-permute-start | bytes 393224 | tf_op jit(solution)/shard_map/ppermute | solution.py:321
  32.0 0.0 collective-permute-done.9.refs_6_
  32.0 7.5 %collective-permute-start.14 = (bf16[512,128]{1,0:T(8,128)(2,1)S(1)}, bf16[512,128]{1,0:T(8,128)(2,1)S(1)}, u32[]{:S(2)}, u32[]{:S(2)}) collective-permute-start(bf16[512,128]{1,0:T(8,128)(2,1)S(1)} %get-tuple-element.69.refs_14_), channel_id=1, source_target_pairs={{0,18},{2,16},{4,22},{6,20},{8,26},{10,24},{12,30},{14,28},{16,2},... | collective-permute-start | bytes 393224 | tf_op jit(solution)/shard_map/ppermute | solution.py:321
  39.6 0.0 collective-permute-done.10.refs_7_
  39.6 1.4 %collective-permute-start = (bf16[512,128]{1,0:T(8,128)(2,1)S(1)}, bf16[512,128]{1,0:T(8,128)(2,1)S(1)}, u32[]{:S(2)}, u32[]{:S(2)}) collective-permute-start(bf16[512,128]{1,0:T(8,128)(2,1)S(1)} %get-tuple-element.60.refs_15_), channel_id=1, source_target_pairs={{0,6},{2,4},{4,2},{6,0},{8,14},{10,12},{12,10},{14,8},{16,22},{18,... | collective-permute-start | bytes 393224 | tf_op jit(solution)/shard_map/ppermute | solution.py:321
  41.0 2.7 %collective-permute-done.11.refs_8_ = bf16[512,128]{1,0:T(8,128)(2,1)S(1)} collective-permute-done((bf16[512,128]{1,0:T(8,128)(2,1)S(1)}, bf16[512,128]{1,0:T(8,128)(2,1)S(1)}, u32[]{:S(2)}, u32[]{:S(2)}) %collective-permute-start.11) | collective-permute-done | bytes 131104 | tf_op jit(solution)/shard_map/ppermute | solution.py:321
  43.7 0.0 collective-permute-start.1
  43.7 5.7 %collective-permute-done.12.refs_9_ = bf16[512,128]{1,0:T(8,128)(2,1)S(1)} collective-permute-done((bf16[512,128]{1,0:T(8,128)(2,1)S(1)}, bf16[512,128]{1,0:T(8,128)(2,1)S(1)}, u32[]{:S(2)}, u32[]{:S(2)}) %collective-permute-start.12) | collective-permute-done | bytes 131104 | tf_op jit(solution)/shard_map/ppermute | solution.py:321
  49.4 1.5 %collective-permute-start.2 = (bf16[512,128]{1,0:T(8,128)(2,1)S(1)}, bf16[512,128]{1,0:T(8,128)(2,1)S(1)}, u32[]{:S(2)}, u32[]{:S(2)}) collective-permute-start(bf16[512,128]{1,0:T(8,128)(2,1)S(1)} %get-tuple-element.62.refs_17_), channel_id=1, source_target_pairs={{0,4},{2,6},{4,0},{6,2},{8,12},{10,14},{12,8},{14,10},{16,20},{18,... | collective-permute-start | bytes 393224 | tf_op jit(solution)/shard_map/ppermute | solution.py:321
  50.9 0.0 collective-permute-done.13.refs_10_
  50.9 0.0 collective-permute-start.3
  50.9 1.0 %collective-permute-done.14.refs_11_ = bf16[512,128]{1,0:T(8,128)(2,1)S(1)} collective-permute-done((bf16[512,128]{1,0:T(8,128)(2,1)S(1)}, bf16[512,128]{1,0:T(8,128)(2,1)S(1)}, u32[]{:S(2)}, u32[]{:S(2)}) %collective-permute-start.14) | collective-permute-done | bytes 131104 | tf_op jit(solution)/shard_map/ppermute | solution.py:321
  51.9 0.0 collective-permute-start.15
  51.9 2.4 %early.1 = (bf16[16,256,128]{2,1,0:T(8,128)(2,1)}, bf16[16,256,128]{2,1,0:T(8,128)(2,1)}, f32[16,8,128]{2,1,0:T(8,128)S(1)}, bf16[16,8,128]{2,1,0:T(8,128)(2,1)S...) custom-call(bf16[512,128]{1,0:T(8,128)(2,1)S(1)} %get-tuple-element.58.refs_19_.refs_0_, ...), custom_call_target="tpu_custom_call" | custom-call | flops 12582912 | bytes 3145728 | tf_op jit(solution)/shard_map/early/pallas_call | solution.py:354
  54.3 0.0 collective-permute-done.refs_0_
  54.3 0.0 collective-permute-done.1.refs_1_
  54.3 0.0 collective-permute-done.2.refs_2_
  54.3 1.5 %collective-permute-done.3.refs_3_ = bf16[512,128]{1,0:T(8,128)(2,1)S(1)} collective-permute-done((bf16[512,128]{1,0:T(8,128)(2,1)S(1)}, bf16[512,128]{1,0:T(8,128)(2,1)S(1)}, u32[]{:S(2)}, u32[]{:S(2)}) %collective-permute-start.3) | collective-permute-done | bytes 131104 | tf_op jit(solution)/shard_map/ppermute | solution.py:321
  55.8 0.0 collective-permute-done.15.refs_12_
  55.9 2.6 %late.1 = (bf16[16,4096]{1,0:T(8,128)(2,1)S(1)}, bf16[16,256,128]{2,1,0:T(8,128)(2,1)}, bf16[16,256,128]{2,1,0:T(8,128)(2,1)}, bf16[16,4096]{1,0:T(8,128)(2,1)}) custom-call(bf16[512,128]{1,0:T(8,128)(2,1)S(1)} %collective-permute-done.refs_0_, bf16[512,128]{1,0:T(8,128)(2,1)S(1)} %collective-permute-done.1.refs_1_, ...), custom_call_target="tpu_custom_call", output_to_operand_aliasing={{1}: (9, {}), {2}: (10, {})} | custom-call | flops 150994944 | bytes 10485760 | tf_op jit(solution)/shard_map/late/pallas_call | solution.py:378
  58.5 0.1 collective-permute-start.16
  58.5 1.3 %collective-permute-done.16 = bf16[16,4096]{1,0:T(8,128)(2,1)S(1)} collective-permute-done((bf16[16,4096]{1,0:T(8,128)(2,1)S(1)}, bf16[16,4096]{1,0:T(8,128)(2,1)S(1)}, u32[]{:S(2)}, u32[]{:S(2)}) %collective-permute-start.16) | collective-permute-done | bytes 131104 | tf_op jit(solution)/shard_map/ppermute | solution.py:211
  59.9 0.7 %add_convert_fusion = bf16[16,4096]{1,0:T(8,128)(2,1)} fusion(bf16[16,4096]{1,0:T(8,128)(2,1)S(1)} %collective-permute-done.16, bf16[16,4096]{1,0:T(8,128)(2,1)S(1)} %get-tuple-element.79), kind=kLoop, calls=%fused_computation | loop fusion | flops 262144 | bytes 393216 | tf_op jit(solution)/shard_map/convert_element_type | solution.py:405
Async XLA Ops:
  2.3 19.2 %collective-permute-start.4 = (bf16[512,128]{1,0:T(8,128)(2,1)S(1)}, bf16[512,128]{1,0:T(8,128)(2,1)S(1)}, u32[]{:S(2)}, u32[]{:S(2)}) collective-permute-start(bf16[512,128]{1,0:T(8,128)(2,1)S(1)} %get-tuple-element.44.refs_4_), channel_id=1, source_target_pairs={{0,30},{2,28},{4,26},{6,24},{8,22},{10,20},{12,18},{14,16},{16,14}... | collective-permute-start | bytes 393224 | tf_op jit(solution)/shard_map/ppermute | solution.py:321
  9.3 13.3 %collective-permute-start.5 = (bf16[512,128]{1,0:T(8,128)(2,1)S(1)}, bf16[512,128]{1,0:T(8,128)(2,1)S(1)}, u32[]{:S(2)}, u32[]{:S(2)}) collective-permute-start(bf16[512,128]{1,0:T(8,128)(2,1)S(1)} %get-tuple-element.45.refs_5_), channel_id=1, source_target_pairs={{0,14},{2,12},{4,10},{6,8},{8,6},{10,4},{12,2},{14,0},{16,30},{18,... | collective-permute-start | bytes 393224 | tf_op jit(solution)/shard_map/ppermute | solution.py:321
  9.3 14.3 %collective-permute-start.6 = (bf16[512,128]{1,0:T(8,128)(2,1)S(1)}, bf16[512,128]{1,0:T(8,128)(2,1)S(1)}, u32[]{:S(2)}, u32[]{:S(2)}) collective-permute-start(bf16[512,128]{1,0:T(8,128)(2,1)S(1)} %get-tuple-element.46.refs_6_), channel_id=1, source_target_pairs={{0,28},{2,30},{4,24},{6,26},{8,20},{10,22},{12,16},{14,18},{16,12}... | collective-permute-start | bytes 393224 | tf_op jit(solution)/shard_map/ppermute | solution.py:321
  11.1 16.8 %collective-permute-start.7 = (bf16[512,128]{1,0:T(8,128)(2,1)S(1)}, bf16[512,128]{1,0:T(8,128)(2,1)S(1)}, u32[]{:S(2)}, u32[]{:S(2)}) collective-permute-start(bf16[512,128]{1,0:T(8,128)(2,1)S(1)} %get-tuple-element.47.refs_7_), channel_id=1, source_target_pairs={{0,26},{2,24},{4,30},{6,28},{8,18},{10,16},{12,22},{14,20},{16,10}... | collective-permute-start | bytes 393224 | tf_op jit(solution)/shard_map/ppermute | solution.py:321
  14.5 16.4 %collective-permute-start.8 = (bf16[512,128]{1,0:T(8,128)(2,1)S(1)}, bf16[512,128]{1,0:T(8,128)(2,1)S(1)}, u32[]{:S(2)}, u32[]{:S(2)}) collective-permute-start(bf16[512,128]{1,0:T(8,128)(2,1)S(1)} %get-tuple-element.48.refs_8_), channel_id=1, source_target_pairs={{0,12},{2,14},{4,8},{6,10},{8,4},{10,6},{12,0},{14,2},{16,28},{18,... | collective-permute-start | bytes 393224 | tf_op jit(solution)/shard_map/ppermute | solution.py:321
  21.6 10.4 %collective-permute-start.9 = (bf16[512,128]{1,0:T(8,128)(2,1)S(1)}, bf16[512,128]{1,0:T(8,128)(2,1)S(1)}, u32[]{:S(2)}, u32[]{:S(2)}) collective-permute-start(bf16[512,128]{1,0:T(8,128)(2,1)S(1)} %get-tuple-element.64.refs_9_), channel_id=1, source_target_pairs={{0,24},{2,26},{4,28},{6,30},{8,16},{10,18},{12,20},{14,22},{16,8},... | collective-permute-start | bytes 393224 | tf_op jit(solution)/shard_map/ppermute | solution.py:321
  22.6 16.9 %collective-permute-start.10 = (bf16[512,128]{1,0:T(8,128)(2,1)S(1)}, bf16[512,128]{1,0:T(8,128)(2,1)S(1)}, u32[]{:S(2)}, u32[]{:S(2)}) collective-permute-start(bf16[512,128]{1,0:T(8,128)(2,1)S(1)} %get-tuple-element.65.refs_10_), channel_id=1, source_target_pairs={{0,10},{2,8},{4,14},{6,12},{8,2},{10,0},{12,6},{14,4},{16,26},{18,... | collective-permute-start | bytes 393224 | tf_op jit(solution)/shard_map/ppermute | solution.py:321
  23.6 20.1 %collective-permute-start.11 = (bf16[512,128]{1,0:T(8,128)(2,1)S(1)}, bf16[512,128]{1,0:T(8,128)(2,1)S(1)}, u32[]{:S(2)}, u32[]{:S(2)}) collective-permute-start(bf16[512,128]{1,0:T(8,128)(2,1)S(1)} %get-tuple-element.66.refs_11_), channel_id=1, source_target_pairs={{0,22},{2,20},{4,18},{6,16},{8,30},{10,28},{12,26},{14,24},{16,6},... | collective-permute-start | bytes 393224 | tf_op jit(solution)/shard_map/ppermute | solution.py:321
  27.9 21.4 %collective-permute-start.12 = (bf16[512,128]{1,0:T(8,128)(2,1)S(1)}, bf16[512,128]{1,0:T(8,128)(2,1)S(1)}, u32[]{:S(2)}, u32[]{:S(2)}) collective-permute-start(bf16[512,128]{1,0:T(8,128)(2,1)S(1)} %get-tuple-element.67.refs_12_), channel_id=1, source_target_pairs={{0,20},{2,22},{4,16},{6,18},{8,28},{10,30},{12,24},{14,26},{16,4},... | collective-permute-start | bytes 393224 | tf_op jit(solution)/shard_map/ppermute | solution.py:321
  30.9 20.0 %collective-permute-start.13 = (bf16[512,128]{1,0:T(8,128)(2,1)S(1)}, bf16[512,128]{1,0:T(8,128)(2,1)S(1)}, u32[]{:S(2)}, u32[]{:S(2)}) collective-permute-start(bf16[512,128]{1,0:T(8,128)(2,1)S(1)} %get-tuple-element.68.refs_13_), channel_id=1, source_target_pairs={{0,8},{2,10},{4,12},{6,14},{8,0},{10,2},{12,4},{14,6},{16,24},{18,... | collective-permute-start | bytes 393224 | tf_op jit(solution)/shard_map/ppermute | solution.py:321
  32.0 19.9 %collective-permute-start.14 = (bf16[512,128]{1,0:T(8,128)(2,1)S(1)}, bf16[512,128]{1,0:T(8,128)(2,1)S(1)}, u32[]{:S(2)}, u32[]{:S(2)}) collective-permute-start(bf16[512,128]{1,0:T(8,128)(2,1)S(1)} %get-tuple-element.69.refs_14_), channel_id=1, source_target_pairs={{0,18},{2,16},{4,22},{6,20},{8,26},{10,24},{12,30},{14,28},{16,2},... | collective-permute-start | bytes 393224 | tf_op jit(solution)/shard_map/ppermute | solution.py:321
  39.6 14.8 %collective-permute-start = (bf16[512,128]{1,0:T(8,128)(2,1)S(1)}, bf16[512,128]{1,0:T(8,128)(2,1)S(1)}, u32[]{:S(2)}, u32[]{:S(2)}) collective-permute-start(bf16[512,128]{1,0:T(8,128)(2,1)S(1)} %get-tuple-element.60.refs_15_), channel_id=1, source_target_pairs={{0,6},{2,4},{4,2},{6,0},{8,14},{10,12},{12,10},{14,8},{16,22},{18,... | collective-permute-start | bytes 393224 | tf_op jit(solution)/shard_map/ppermute | solution.py:321
  43.7 10.6 %collective-permute-start.1 = (bf16[512,128]{1,0:T(8,128)(2,1)S(1)}, bf16[512,128]{1,0:T(8,128)(2,1)S(1)}, u32[]{:S(2)}, u32[]{:S(2)}) collective-permute-start(bf16[512,128]{1,0:T(8,128)(2,1)S(1)} %get-tuple-element.61.refs_16_), channel_id=1, source_target_pairs={{0,16},{2,18},{4,20},{6,22},{8,24},{10,26},{12,28},{14,30},{16,0},... | collective-permute-start | bytes 393224 | tf_op jit(solution)/shard_map/ppermute | solution.py:321
  49.4 5.0 %collective-permute-start.2 = (bf16[512,128]{1,0:T(8,128)(2,1)S(1)}, bf16[512,128]{1,0:T(8,128)(2,1)S(1)}, u32[]{:S(2)}, u32[]{:S(2)}) collective-permute-start(bf16[512,128]{1,0:T(8,128)(2,1)S(1)} %get-tuple-element.62.refs_17_), channel_id=1, source_target_pairs={{0,4},{2,6},{4,0},{6,2},{8,12},{10,14},{12,8},{14,10},{16,20},{18,... | collective-permute-start | bytes 393224 | tf_op jit(solution)/shard_map/ppermute | solution.py:321
  50.9 5.0 %collective-permute-start.3 = (bf16[512,128]{1,0:T(8,128)(2,1)S(1)}, bf16[512,128]{1,0:T(8,128)(2,1)S(1)}, u32[]{:S(2)}, u32[]{:S(2)}) collective-permute-start(bf16[512,128]{1,0:T(8,128)(2,1)S(1)} %get-tuple-element.63.refs_18_), channel_id=1, source_target_pairs={{0,2},{2,0},{4,6},{6,4},{8,10},{10,8},{12,14},{14,12},{16,18},{18,... | collective-permute-start | bytes 393224 | tf_op jit(solution)/shard_map/ppermute | solution.py:321
  51.9 3.9 %collective-permute-start.15 = (bf16[16,4096]{1,0:T(8,128)(2,1)S(1)}, bf16[16,4096]{1,0:T(8,128)(2,1)S(1)}, u32[]{:S(2)}, u32[]{:S(2)}) collective-permute-start(bf16[16,4096]{1,0:T(8,128)(2,1)S(1)} %get-tuple-element.77.refs_11_), channel_id=1, source_target_pairs={{0,1},{1,0},{2,3},{3,2},{4,5},{5,4},{6,7},{7,6},{8,9},{9,8},{10,11... | collective-permute-start | bytes 393224 | tf_op jit(solution)/shard_map/ppermute | solution.py:211
  58.5 1.4 %collective-permute-start.16 = (bf16[16,4096]{1,0:T(8,128)(2,1)S(1)}, bf16[16,4096]{1,0:T(8,128)(2,1)S(1)}, u32[]{:S(2)}, u32[]{:S(2)}) collective-permute-start(bf16[16,4096]{1,0:T(8,128)(2,1)S(1)} %get-tuple-element.79), channel_id=1, source_target_pairs={{0,1},{1,0},{2,3},{3,2},{4,5},{5,4},{6,7},{7,6},{8,9},{9,8},{10,11... | collective-permute-start | bytes 393224 | tf_op jit(solution)/shard_map/ppermute | solution.py:211

commit v9 on v8

--- a/solution.py
+++ b/solution.py
@@ -12,7 +12,7 @@
 SPLIT = 64
 CHUNKS = 8
 AHEAD = 5
-LATE = 4
+LATE = 5
 VMEM_BYTES = 24 * 1024 * 1024
 
 
@@ -193,22 +193,21 @@
     finish(place(parcels, query, new_k, new_v, key_cache, value_cache, held, mixed, osems))
 
 
-def late_kernel(count, span, pair, *refs):
+def late_kernel(count, span, *refs):
     arrived, (query, new_k, new_v, weight, before) = refs[:count], refs[count : count + 5]
-    halves, (out, key_cache, value_cache) = refs[count + 7 : count + 7 + pair], refs[count + 7 + pair : count + 10 + pair]
-    held, mixed, osems = refs[-3:]
+    out, key_cache, value_cache, held, mixed, osems = refs[count + 7 :]
     mixed[...] = before[...]
     parcels = parcels_of(arrived, span)
     outgoing = place(parcels, query, new_k, new_v, key_cache, value_cache, held, mixed, osems)
-    if pair:
-        both = halves[0][...].astype(jnp.float32) + halves[1][...].astype(jnp.float32)
-        refs[count + 10 + pair][...] = both.astype(jnp.bfloat16)
     project(mixed, weight, out)
     finish(outgoing)
 
 
-def swap(partial):
-    return lax.ppermute(partial, "tp", [(0, 1), (1, 0)])
+def total(partial, size):
+    if size == 2:
+        other = lax.ppermute(partial, "tp", [(0, 1), (1, 0)])
+        return (partial.astype(jnp.float32) + other.astype(jnp.float32)).astype(jnp.bfloat16)
+    return lax.psum(partial, "tp")
 
 
 def near(x):
@@ -221,7 +220,7 @@
 
 def step_order(n):
     half = n // 2
-    crossing = list(range(half, n))[::-1]
+    crossing = [half] + list(range(half + 1, n))[::-1]
     staying = list(range(1, half))[::-1]
     order = []
     for kind in "cnccncnccncncnn":
@@ -344,10 +343,6 @@
 
     arrived += [send(i, partial_one) for i in range(AHEAD, n - 1)]
     early, late = [packed[-1]] + arrived[:-LATE], arrived[-LATE:]
-    halves = []
-    if tp == 2:
-        halves = [partial_one, swap(lax.optimization_barrier((partial_one, arrived[0]))[0])]
-
     cache = jax.ShapeDtypeStruct((slots, span, width), bf16)
     mixed = jax.ShapeDtypeStruct((slots, heads, width), f32)
     some = len(early)
@@ -374,13 +369,14 @@
         name="early",
     )(*early, hbm(query_two), hbm(key_two), hbm(value_two))
     key_cache, value_cache, *carried = results
-
-    partial_two, key_cache, value_cache, *sums = pl.pallas_call(
-        functools.partial(late_kernel, LATE, span, len(halves)),
-        out_shape=[jax.ShapeDtypeStruct((slots, columns), bf16), cache, cache]
-        + [jax.ShapeDtypeStruct((slots, columns), bf16)] * (len(halves) // 2),
-        in_specs=[vmem] * (len(late) + 5) + [far] * 2 + [vmem] * len(halves),
-        out_specs=[vmem, far, far] + [vmem] * (len(halves) // 2),
+    partial_one = lax.optimization_barrier((partial_one, carried[0]))[0]
+    out_one = total(partial_one, tp)
+
+    partial_two, key_cache, value_cache = pl.pallas_call(
+        functools.partial(late_kernel, LATE, span),
+        out_shape=[jax.ShapeDtypeStruct((slots, columns), bf16), cache, cache],
+        in_specs=[vmem] * (len(late) + 5) + [far] * 2,
+        out_specs=[vmem, far, far],
         input_output_aliases={len(late) + 5: 1, len(late) + 6: 2},
         scratch_shapes=[
             pltpu.VMEM((2, LATE, span, width), bf16),
@@ -397,14 +393,8 @@
         near(carried[0]),
         hbm(key_cache),
         hbm(value_cache),
-        *halves,
     )
-    out_one = sums[0] if sums else lax.psum(partial_one, "tp")
-    if tp == 2:
-        both = partial_two.astype(f32) + swap(partial_two).astype(f32)
-        out_two = both.astype(bf16)
-    else:
-        out_two = lax.psum(partial_two, "tp")
+    out_two = total(partial_two, tp)
     shape = (slots * pages, kv_heads, size, width)
     return (out_one, out_two, key_cache.reshape(shape), value_cache.reshape(shape))
 

time: 60.8 us -> 60.8 us (level)
  waiting for transfers between devices: 12.3 us -> 9.29 us
  starting transfers between devices: 33.8 us -> 36.6 us
  other arithmetic: 0.69 us -> 1.38 us
    ppermute x15, starting transfers between devices: 33.7 us -> 36.5 us  [send(): return lax.ppermute(block, 'inst', [(d, d ^ steps[i]) for d in range(n)])]
    ppermute x15, waiting for transfers between devices: 10.9 us -> 8.65 us  [send(): return lax.ppermute(block, 'inst', [(d, d ^ steps[i]) for d in range(n)])]
    ppermute x2, waiting for transfers between devices: 1.34 us -> 0.64 us  [total(): other = lax.ppermute(partial, 'tp', [(0, 1), (1, 0)])]
    convert_element_type x1 -> x2, other arithmetic: 0.69 us -> 1.38 us  [total(): (partial.astype(jnp.float32) + other.astype(jnp.float32)).astype(jnp.bflo...]
  transfers between devices with their start and end apart: 17 -> 17, of which waited for: 5 -> 5; matrix products, arithmetic and copies ran while one was open for 0% -> 1% of each run, Pallas kernels for 15% -> 18%
where the time goes in v9:
time: 60.8 us; the launch traced here: 60.5 us
  starting transfers between devices  36.6 us (60%)
  Pallas kernels  12.5 us (21%)
  waiting for transfers between devices  9.29 us (15%)
  other arithmetic  1.38 us (2%)
  between operations  0.73 us (1%)
    ppermute x15, starting transfers between devices, send(): return lax.ppermute(block, 'inst', [(d, d ^ steps[i]) for d in range(n)])  36.5 us
    ppermute x15, waiting for transfers between devices, send(): return lax.ppermute(block, 'inst', [(d, d ^ steps[i]) for d in range(n)])  8.65 us
    pallas_call x1, Pallas kernels, shards(): pl.pallas_call(functools.partial(first_kernel, steps, span), out_shape=[j...  4.66 us
    pallas_call x2, Pallas kernels, pack(): pl.pallas_call(functools.partial(pack_kernel, n, chosen, pages), out_shap...  3.48 us
    pallas_call x1, Pallas kernels, shards(): pl.pallas_call(functools.partial(early_kernel, some, span), out_shape=[ca...  2.31 us
    pallas_call x1, Pallas kernels, shards(): pl.pallas_call(functools.partial(late_kernel, LATE, span), out_shape=[jax...  2.01 us
    convert_element_type x2, other arithmetic, total(): (partial.astype(jnp.float32) + other.astype(jnp.float32)).astype(jnp.bflo...  1.38 us
  transfers between devices with their start and end apart: 17, of which 5 were waited for; matrix products, arithmetic and copies ran while one was open for 1% of the time, Pallas kernels for 18%

profile of v9, /device:TPU:0, one launch (start us, length us, event | category | flops | bytes accessed | tf_op | source)
XLA Modules:
  0.0 60.5 jit_solution(6397894485951051935)
XLA Ops:
  0.6 1.7 %pack.2 = (bf16[512,128]{1,0:T(8,128)(2,1)S(1)}, bf16[512,128]{1,0:T(8,128)(2,1)S(1)}, bf16[512,128]{1,0:T(8,128)(2,1)S(1)}, bf16[512,128]{1,0:T(8,128)(2,1)S(1)}, bf16[512,128]{1,0:T(8,128)(2,1)S(1)}) custom-call(s32[4,16]{1,0:T(4,128)} %bitcast.23, s32[16]{0:T(128)} %refs_0_.1, s32[16]{0:T(128)} %refs_1_.5, s32[16]{0:T(128)} %refs_3_.4, ...), custom_call_target="tpu_custom_call" | custom-call | bytes 1310720 | tf_op jit(solution)/shard_map/pack/pallas_call | solution.py:280
  2.3 4.1 %collective-permute-start = (bf16[512,128]{1,0:T(8,128)(2,1)S(1)}, bf16[512,128]{1,0:T(8,128)(2,1)S(1)}, u32[]{:S(2)}, u32[]{:S(2)}) collective-permute-start(bf16[512,128]{1,0:T(8,128)(2,1)S(1)} %get-tuple-element.42.refs_4_), channel_id=1, source_target_pairs={{0,16},{2,18},{4,20},{6,22},{8,24},{10,26},{12,28},{14,30},{16,0},... | collective-permute-start | bytes 393224 | tf_op jit(solution)/shard_map/ppermute | solution.py:320
  6.5 3.5 %collective-permute-start.1 = (bf16[512,128]{1,0:T(8,128)(2,1)S(1)}, bf16[512,128]{1,0:T(8,128)(2,1)S(1)}, u32[]{:S(2)}, u32[]{:S(2)}) collective-permute-start(bf16[512,128]{1,0:T(8,128)(2,1)S(1)} %get-tuple-element.43.refs_5_), channel_id=1, source_target_pairs={{0,14},{2,12},{4,10},{6,8},{8,6},{10,4},{12,2},{14,0},{16,30},{18,... | collective-permute-start | bytes 393224 | tf_op jit(solution)/shard_map/ppermute | solution.py:320
  9.9 0.0 collective-permute-start.2
  9.9 4.7 %collective-permute-start.3 = (bf16[512,128]{1,0:T(8,128)(2,1)S(1)}, bf16[512,128]{1,0:T(8,128)(2,1)S(1)}, u32[]{:S(2)}, u32[]{:S(2)}) collective-permute-start(bf16[512,128]{1,0:T(8,128)(2,1)S(1)} %get-tuple-element.45.refs_7_), channel_id=1, source_target_pairs={{0,28},{2,30},{4,24},{6,26},{8,20},{10,22},{12,16},{14,18},{16,12}... | collective-permute-start | bytes 393224 | tf_op jit(solution)/shard_map/ppermute | solution.py:320
  14.6 0.0 collective-permute-start.4
  14.6 1.8 %pack.3 = (bf16[512,128]{1,0:T(8,128)(2,1)S(1)}, bf16[512,128]{1,0:T(8,128)(2,1)S(1)}, bf16[512,128]{1,0:T(8,128)(2,1)S(1)}, bf16[512,128]{1,0:T(8,128)(2,1)S(1)...) custom-call(s32[4,16]{1,0:T(4,128)} %bitcast.24, ...), custom_call_target="tpu_custom_call" | custom-call | bytes 2883584 | tf_op jit(solution)/shard_map/pack/pallas_call | solution.py:280
  16.4 4.7 %first.1 = (bf16[16,4096]{1,0:T(8,128)(2,1)S(1)}, bf16[1024,4096]{1,0:T(8,128)(2,1)S(1)}) custom-call(s32[16]{0:T(128)} %refs_0_.1, s32[16]{0:T(128)} %refs_1_.5, bf16[16,8,128]{2,1,0:T(8,128)(2,1)} %refs_2_.5, bf16[1024,4096]{1,0:T(8,128)(2,1)} %refs_3_.5, bf16[512,128]{1,0:T(8,128)(2,1)S(1)} %get-tuple-element.42.refs_4_, ...), custom_call_target="tpu_custom_call" | custom-call | flops 150994944 | bytes 10485760 | tf_op jit(solution)/shard_map/first/pallas_call | solution.py:323
  21.1 0.0 collective-permute-done.refs_1_
  21.1 1.2 %collective-permute-start.5 = (bf16[512,128]{1,0:T(8,128)(2,1)S(1)}, bf16[512,128]{1,0:T(8,128)(2,1)S(1)}, u32[]{:S(2)}, u32[]{:S(2)}) collective-permute-start(bf16[512,128]{1,0:T(8,128)(2,1)S(1)} %get-tuple-element.59.refs_9_), channel_id=1, source_target_pairs={{0,26},{2,24},{4,30},{6,28},{8,18},{10,16},{12,22},{14,20},{16,10}... | collective-permute-start | bytes 393224 | tf_op jit(solution)/shard_map/ppermute | solution.py:320
  22.3 0.0 collective-permute-done.1.refs_2_
  22.3 1.8 %collective-permute-start.6 = (bf16[512,128]{1,0:T(8,128)(2,1)S(1)}, bf16[512,128]{1,0:T(8,128)(2,1)S(1)}, u32[]{:S(2)}, u32[]{:S(2)}) collective-permute-start(bf16[512,128]{1,0:T(8,128)(2,1)S(1)} %get-tuple-element.60.refs_10_), channel_id=1, source_target_pairs={{0,10},{2,8},{4,14},{6,12},{8,2},{10,0},{12,6},{14,4},{16,26},{18,... | collective-permute-start | bytes 393224 | tf_op jit(solution)/shard_map/ppermute | solution.py:320
  24.1 0.0 collective-permute-done.2.refs_3_
  24.1 2.8 %collective-permute-start.7 = (bf16[512,128]{1,0:T(8,128)(2,1)S(1)}, bf16[512,128]{1,0:T(8,128)(2,1)S(1)}, u32[]{:S(2)}, u32[]{:S(2)}) collective-permute-start(bf16[512,128]{1,0:T(8,128)(2,1)S(1)} %get-tuple-element.61.refs_11_), channel_id=1, source_target_pairs={{0,24},{2,26},{4,28},{6,30},{8,16},{10,18},{12,20},{14,22},{16,8},... | collective-permute-start | bytes 393224 | tf_op jit(solution)/shard_map/ppermute | solution.py:320
  26.9 0.0 collective-permute-done.3.refs_4_
  26.9 6.0 %collective-permute-start.8 = (bf16[512,128]{1,0:T(8,128)(2,1)S(1)}, bf16[512,128]{1,0:T(8,128)(2,1)S(1)}, u32[]{:S(2)}, u32[]{:S(2)}) collective-permute-start(bf16[512,128]{1,0:T(8,128)(2,1)S(1)} %get-tuple-element.62.refs_12_), channel_id=1, source_target_pairs={{0,22},{2,20},{4,18},{6,16},{8,30},{10,28},{12,26},{14,24},{16,6},... | collective-permute-start | bytes 393224 | tf_op jit(solution)/shard_map/ppermute | solution.py:320
  32.9 0.0 collective-permute-done.4.refs_5_
  32.9 0.0 collective-permute-start.9
  32.9 0.0 collective-permute-done.5.refs_6_
  32.9 5.9 %collective-permute-start.11 = (bf16[512,128]{1,0:T(8,128)(2,1)S(1)}, bf16[512,128]{1,0:T(8,128)(2,1)S(1)}, u32[]{:S(2)}, u32[]{:S(2)}) collective-permute-start(bf16[512,128]{1,0:T(8,128)(2,1)S(1)} %get-tuple-element.66.refs_14_), channel_id=1, source_target_pairs={{0,20},{2,22},{4,16},{6,18},{8,28},{10,30},{12,24},{14,26},{16,4},... | collective-permute-start | bytes 393224 | tf_op jit(solution)/shard_map/ppermute | solution.py:320
  38.9 0.0 collective-permute-done.6.refs_7_
  38.9 0.3 collective-permute-start.12
  39.2 0.0 collective-permute-done.7.refs_8_
  39.2 4.4 %collective-permute-start.13 = (bf16[512,128]{1,0:T(8,128)(2,1)S(1)}, bf16[512,128]{1,0:T(8,128)(2,1)S(1)}, u32[]{:S(2)}, u32[]{:S(2)}) collective-permute-start(bf16[512,128]{1,0:T(8,128)(2,1)S(1)} %get-tuple-element.68.refs_16_), channel_id=1, source_target_pairs={{0,18},{2,16},{4,22},{6,20},{8,26},{10,24},{12,30},{14,28},{16,2},... | collective-permute-start | bytes 393224 | tf_op jit(solution)/shard_map/ppermute | solution.py:320
  43.6 6.1 %collective-permute-done.8.refs_9_ = bf16[512,128]{1,0:T(8,128)(2,1)S(1)} collective-permute-done((bf16[512,128]{1,0:T(8,128)(2,1)S(1)}, bf16[512,128]{1,0:T(8,128)(2,1)S(1)}, u32[]{:S(2)}, u32[]{:S(2)}) %collective-permute-start.8) | collective-permute-done | bytes 131104 | tf_op jit(solution)/shard_map/ppermute | solution.py:320
  49.7 1.7 %collective-permute-start.14 = (bf16[512,128]{1,0:T(8,128)(2,1)S(1)}, bf16[512,128]{1,0:T(8,128)(2,1)S(1)}, u32[]{:S(2)}, u32[]{:S(2)}) collective-permute-start(bf16[512,128]{1,0:T(8,128)(2,1)S(1)} %get-tuple-element.69.refs_17_), channel_id=1, source_target_pairs={{0,4},{2,6},{4,0},{6,2},{8,12},{10,14},{12,8},{14,10},{16,20},{18,... | collective-permute-start | bytes 393224 | tf_op jit(solution)/shard_map/ppermute | solution.py:320
  51.4 0.0 collective-permute-done.9.refs_10_
  51.4 0.0 collective-permute-start.15
  51.4 2.3 %early.1 = (bf16[16,256,128]{2,1,0:T(8,128)(2,1)}, bf16[16,256,128]{2,1,0:T(8,128)(2,1)}, f32[16,8,128]{2,1,0:T(8,128)S(1)}, bf16[16,8,128]{2,1,0:T(8,128)(2,1)S...) custom-call(bf16[512,128]{1,0:T(8,128)(2,1)S(1)} %get-tuple-element.57.refs_19_.refs_0_, ...), custom_call_target="tpu_custom_call" | custom-call | flops 11534336 | bytes 2883584 | tf_op jit(solution)/shard_map/early/pallas_call | solution.py:349
  53.7 0.0 collective-permute-done.11.refs_0_
  53.8 0.1 collective-permute-start.10
  53.8 0.0 collective-permute-done.12.refs_1_
  53.8 0.4 collective-permute-done.13.refs_2_
  54.2 0.4 collective-permute-done.14.refs_3_
  54.7 1.7 %collective-permute-done.15.refs_4_ = bf16[512,128]{1,0:T(8,128)(2,1)S(1)} collective-permute-done((bf16[512,128]{1,0:T(8,128)(2,1)S(1)}, bf16[512,128]{1,0:T(8,128)(2,1)S(1)}, u32[]{:S(2)}, u32[]{:S(2)}) %collective-permute-start.15) | collective-permute-done | bytes 131104 | tf_op jit(solution)/shard_map/ppermute | solution.py:320
  56.4 2.0 %late.1 = (bf16[16,4096]{1,0:T(8,128)(2,1)S(1)}, bf16[16,256,128]{2,1,0:T(8,128)(2,1)}, bf16[16,256,128]{2,1,0:T(8,128)(2,1)}) custom-call(bf16[512,128]{1,0:T(8,128)(2,1)S(1)} %collective-permute-done.11.refs_0_, bf16[512,128]{1,0:T(8,128)(2,1)S(1)} %collective-permute-done.12.refs_1_, ...), custom_call_target="tpu_custom_call", output_to_operand_aliasing={{1}: (10, {}), {2}: (11, {})} | custom-call | flops 150994944 | bytes 10485760 | tf_op jit(solution)/shard_map/late/pallas_call | solution.py:375
  58.4 0.1 collective-permute-start.16
  58.5 0.0 collective-permute-done.10
  58.5 0.7 %add_convert_fusion.1 = bf16[16,4096]{1,0:T(8,128)(2,1)} fusion(bf16[16,4096]{1,0:T(8,128)(2,1)S(1)} %collective-permute-done.10, bf16[16,4096]{1,0:T(8,128)(2,1)S(1)} %get-tuple-element.65), kind=kLoop, calls=%fused_computation.1 | loop fusion | flops 262144 | bytes 393216 | tf_op jit(solution)/shard_map/convert_element_type | solution.py:209
  59.2 0.6 %collective-permute-done.16 = bf16[16,4096]{1,0:T(8,128)(2,1)S(1)} collective-permute-done((bf16[16,4096]{1,0:T(8,128)(2,1)S(1)}, bf16[16,4096]{1,0:T(8,128)(2,1)S(1)}, u32[]{:S(2)}, u32[]{:S(2)}) %collective-permute-start.16) | collective-permute-done | bytes 131104 | tf_op jit(solution)/shard_map/ppermute | solution.py:208
  59.8 0.7 %add_convert_fusion = bf16[16,4096]{1,0:T(8,128)(2,1)} fusion(bf16[16,4096]{1,0:T(8,128)(2,1)S(1)} %collective-permute-done.16, bf16[16,4096]{1,0:T(8,128)(2,1)S(1)} %get-tuple-element.77), kind=kLoop, calls=%fused_computation | loop fusion | flops 262144 | bytes 393216 | tf_op jit(solution)/shard_map/convert_element_type | solution.py:209
Async XLA Ops:
  2.3 18.7 %collective-permute-start = (bf16[512,128]{1,0:T(8,128)(2,1)S(1)}, bf16[512,128]{1,0:T(8,128)(2,1)S(1)}, u32[]{:S(2)}, u32[]{:S(2)}) collective-permute-start(bf16[512,128]{1,0:T(8,128)(2,1)S(1)} %get-tuple-element.42.refs_4_), channel_id=1, source_target_pairs={{0,16},{2,18},{4,20},{6,22},{8,24},{10,26},{12,28},{14,30},{16,0},... | collective-permute-start | bytes 393224 | tf_op jit(solution)/shard_map/ppermute | solution.py:320
  6.5 15.8 %collective-permute-start.1 = (bf16[512,128]{1,0:T(8,128)(2,1)S(1)}, bf16[512,128]{1,0:T(8,128)(2,1)S(1)}, u32[]{:S(2)}, u32[]{:S(2)}) collective-permute-start(bf16[512,128]{1,0:T(8,128)(2,1)S(1)} %get-tuple-element.43.refs_5_), channel_id=1, source_target_pairs={{0,14},{2,12},{4,10},{6,8},{8,6},{10,4},{12,2},{14,0},{16,30},{18,... | collective-permute-start | bytes 393224 | tf_op jit(solution)/shard_map/ppermute | solution.py:320
  9.9 14.2 %collective-permute-start.2 = (bf16[512,128]{1,0:T(8,128)(2,1)S(1)}, bf16[512,128]{1,0:T(8,128)(2,1)S(1)}, u32[]{:S(2)}, u32[]{:S(2)}) collective-permute-start(bf16[512,128]{1,0:T(8,128)(2,1)S(1)} %get-tuple-element.44.refs_6_), channel_id=1, source_target_pairs={{0,30},{2,28},{4,26},{6,24},{8,22},{10,20},{12,18},{14,16},{16,14}... | collective-permute-start | bytes 393224 | tf_op jit(solution)/shard_map/ppermute | solution.py:320
  9.9 17.0 %collective-permute-start.3 = (bf16[512,128]{1,0:T(8,128)(2,1)S(1)}, bf16[512,128]{1,0:T(8,128)(2,1)S(1)}, u32[]{:S(2)}, u32[]{:S(2)}) collective-permute-start(bf16[512,128]{1,0:T(8,128)(2,1)S(1)} %get-tuple-element.45.refs_7_), channel_id=1, source_target_pairs={{0,28},{2,30},{4,24},{6,26},{8,20},{10,22},{12,16},{14,18},{16,12}... | collective-permute-start | bytes 393224 | tf_op jit(solution)/shard_map/ppermute | solution.py:320
  14.6 18.3 %collective-permute-start.4 = (bf16[512,128]{1,0:T(8,128)(2,1)S(1)}, bf16[512,128]{1,0:T(8,128)(2,1)S(1)}, u32[]{:S(2)}, u32[]{:S(2)}) collective-permute-start(bf16[512,128]{1,0:T(8,128)(2,1)S(1)} %get-tuple-element.46.refs_8_), channel_id=1, source_target_pairs={{0,12},{2,14},{4,8},{6,10},{8,4},{10,6},{12,0},{14,2},{16,28},{18,... | collective-permute-start | bytes 393224 | tf_op jit(solution)/shard_map/ppermute | solution.py:320
  21.1 11.9 %collective-permute-start.5 = (bf16[512,128]{1,0:T(8,128)(2,1)S(1)}, bf16[512,128]{1,0:T(8,128)(2,1)S(1)}, u32[]{:S(2)}, u32[]{:S(2)}) collective-permute-start(bf16[512,128]{1,0:T(8,128)(2,1)S(1)} %get-tuple-element.59.refs_9_), channel_id=1, source_target_pairs={{0,26},{2,24},{4,30},{6,28},{8,18},{10,16},{12,22},{14,20},{16,10}... | collective-permute-start | bytes 393224 | tf_op jit(solution)/shard_map/ppermute | solution.py:320
  22.3 16.6 %collective-permute-start.6 = (bf16[512,128]{1,0:T(8,128)(2,1)S(1)}, bf16[512,128]{1,0:T(8,128)(2,1)S(1)}, u32[]{:S(2)}, u32[]{:S(2)}) collective-permute-start(bf16[512,128]{1,0:T(8,128)(2,1)S(1)} %get-tuple-element.60.refs_10_), channel_id=1, source_target_pairs={{0,10},{2,8},{4,14},{6,12},{8,2},{10,0},{12,6},{14,4},{16,26},{18,... | collective-permute-start | bytes 393224 | tf_op jit(solution)/shard_map/ppermute | solution.py:320
  24.1 15.1 %collective-permute-start.7 = (bf16[512,128]{1,0:T(8,128)(2,1)S(1)}, bf16[512,128]{1,0:T(8,128)(2,1)S(1)}, u32[]{:S(2)}, u32[]{:S(2)}) collective-permute-start(bf16[512,128]{1,0:T(8,128)(2,1)S(1)} %get-tuple-element.61.refs_11_), channel_id=1, source_target_pairs={{0,24},{2,26},{4,28},{6,30},{8,16},{10,18},{12,20},{14,22},{16,8},... | collective-permute-start | bytes 393224 | tf_op jit(solution)/shard_map/ppermute | solution.py:320
  26.9 22.8 %collective-permute-start.8 = (bf16[512,128]{1,0:T(8,128)(2,1)S(1)}, bf16[512,128]{1,0:T(8,128)(2,1)S(1)}, u32[]{:S(2)}, u32[]{:S(2)}) collective-permute-start(bf16[512,128]{1,0:T(8,128)(2,1)S(1)} %get-tuple-element.62.refs_12_), channel_id=1, source_target_pairs={{0,22},{2,20},{4,18},{6,16},{8,30},{10,28},{12,26},{14,24},{16,6},... | collective-permute-start | bytes 393224 | tf_op jit(solution)/shard_map/ppermute | solution.py:320
  32.9 18.5 %collective-permute-start.9 = (bf16[512,128]{1,0:T(8,128)(2,1)S(1)}, bf16[512,128]{1,0:T(8,128)(2,1)S(1)}, u32[]{:S(2)}, u32[]{:S(2)}) collective-permute-start(bf16[512,128]{1,0:T(8,128)(2,1)S(1)} %get-tuple-element.63.refs_13_), channel_id=1, source_target_pairs={{0,8},{2,10},{4,12},{6,14},{8,0},{10,2},{12,4},{14,6},{16,24},{18,... | collective-permute-start | bytes 393224 | tf_op jit(solution)/shard_map/ppermute | solution.py:320
  32.9 20.8 %collective-permute-start.11 = (bf16[512,128]{1,0:T(8,128)(2,1)S(1)}, bf16[512,128]{1,0:T(8,128)(2,1)S(1)}, u32[]{:S(2)}, u32[]{:S(2)}) collective-permute-start(bf16[512,128]{1,0:T(8,128)(2,1)S(1)} %get-tuple-element.66.refs_14_), channel_id=1, source_target_pairs={{0,20},{2,22},{4,16},{6,18},{8,28},{10,30},{12,24},{14,26},{16,4},... | collective-permute-start | bytes 393224 | tf_op jit(solution)/shard_map/ppermute | solution.py:320
  38.9 15.0 %collective-permute-start.12 = (bf16[512,128]{1,0:T(8,128)(2,1)S(1)}, bf16[512,128]{1,0:T(8,128)(2,1)S(1)}, u32[]{:S(2)}, u32[]{:S(2)}) collective-permute-start(bf16[512,128]{1,0:T(8,128)(2,1)S(1)} %get-tuple-element.67.refs_15_), channel_id=1, source_target_pairs={{0,6},{2,4},{4,2},{6,0},{8,14},{10,12},{12,10},{14,8},{16,22},{18,... | collective-permute-start | bytes 393224 | tf_op jit(solution)/shard_map/ppermute | solution.py:320
  39.2 15.0 %collective-permute-start.13 = (bf16[512,128]{1,0:T(8,128)(2,1)S(1)}, bf16[512,128]{1,0:T(8,128)(2,1)S(1)}, u32[]{:S(2)}, u32[]{:S(2)}) collective-permute-start(bf16[512,128]{1,0:T(8,128)(2,1)S(1)} %get-tuple-element.68.refs_16_), channel_id=1, source_target_pairs={{0,18},{2,16},{4,22},{6,20},{8,26},{10,24},{12,30},{14,28},{16,2},... | collective-permute-start | bytes 393224 | tf_op jit(solution)/shard_map/ppermute | solution.py:320
  49.7 5.0 %collective-permute-start.14 = (bf16[512,128]{1,0:T(8,128)(2,1)S(1)}, bf16[512,128]{1,0:T(8,128)(2,1)S(1)}, u32[]{:S(2)}, u32[]{:S(2)}) collective-permute-start(bf16[512,128]{1,0:T(8,128)(2,1)S(1)} %get-tuple-element.69.refs_17_), channel_id=1, source_target_pairs={{0,4},{2,6},{4,0},{6,2},{8,12},{10,14},{12,8},{14,10},{16,20},{18,... | collective-permute-start | bytes 393224 | tf_op jit(solution)/shard_map/ppermute | solution.py:320
  51.4 5.0 %collective-permute-start.15 = (bf16[512,128]{1,0:T(8,128)(2,1)S(1)}, bf16[512,128]{1,0:T(8,128)(2,1)S(1)}, u32[]{:S(2)}, u32[]{:S(2)}) collective-permute-start(bf16[512,128]{1,0:T(8,128)(2,1)S(1)} %get-tuple-element.70.refs_18_), channel_id=1, source_target_pairs={{0,2},{2,0},{4,6},{6,4},{8,10},{10,8},{12,14},{14,12},{16,18},{18,... | collective-permute-start | bytes 393224 | tf_op jit(solution)/shard_map/ppermute | solution.py:320
  53.8 4.7 %collective-permute-start.10 = (bf16[16,4096]{1,0:T(8,128)(2,1)S(1)}, bf16[16,4096]{1,0:T(8,128)(2,1)S(1)}, u32[]{:S(2)}, u32[]{:S(2)}) collective-permute-start(bf16[16,4096]{1,0:T(8,128)(2,1)S(1)} %get-tuple-element.65), channel_id=1, source_target_pairs={{0,1},{1,0},{2,3},{3,2},{4,5},{5,4},{6,7},{7,6},{8,9},{9,8},{10,11... | collective-permute-start | bytes 393224 | tf_op jit(solution)/shard_map/ppermute | solution.py:208
  58.4 1.4 %collective-permute-start.16 = (bf16[16,4096]{1,0:T(8,128)(2,1)S(1)}, bf16[16,4096]{1,0:T(8,128)(2,1)S(1)}, u32[]{:S(2)}, u32[]{:S(2)}) collective-permute-start(bf16[16,4096]{1,0:T(8,128)(2,1)S(1)} %get-tuple-element.77), channel_id=1, source_target_pairs={{0,1},{1,0},{2,3},{3,2},{4,5},{5,4},{6,7},{7,6},{8,9},{9,8},{10,11... | collective-permute-start | bytes 393224 | tf_op jit(solution)/shard_map/ppermute | solution.py:208

commit v10 on v9

--- a/solution.py
+++ b/solution.py
@@ -223,7 +223,7 @@
     crossing = [half] + list(range(half + 1, n))[::-1]
     staying = list(range(1, half))[::-1]
     order = []
-    for kind in "cnccncnccncncnn":
+    for kind in "cncncncncncncnc":
         queue = crossing if kind == "c" else staying
         if queue:
             order.append(queue.pop(0))

time: 60.8 us -> 57.9 us (0.952)
  starting transfers between devices: 36.6 us -> 34.4 us
  waiting for transfers between devices: 9.29 us -> 8.67 us
    ppermute x15, starting transfers between devices: 36.5 us -> 34.3 us  [send(): return lax.ppermute(block, 'inst', [(d, d ^ steps[i]) for d in range(n)])]
    ppermute x15, waiting for transfers between devices: 8.65 us -> 8.03 us  [send(): return lax.ppermute(block, 'inst', [(d, d ^ steps[i]) for d in range(n)])]
  transfers between devices with their start and end apart: 17 -> 17, of which waited for: 5 -> 7; matrix products, arithmetic and copies ran while one was open for 1% -> 1% of each run, Pallas kernels for 18% -> 19%
where the time goes in v10:
time: 57.9 us; the launch traced here: 57.7 us
  starting transfers between devices  34.4 us (59%)
  Pallas kernels  12.5 us (22%)
  waiting for transfers between devices  8.67 us (15%)
  other arithmetic  1.38 us (2%)
  between operations  0.73 us (1%)
    ppermute x15, starting transfers between devices, send(): return lax.ppermute(block, 'inst', [(d, d ^ steps[i]) for d in range(n)])  34.3 us
    ppermute x15, waiting for transfers between devices, send(): return lax.ppermute(block, 'inst', [(d, d ^ steps[i]) for d in range(n)])  8.03 us
    pallas_call x1, Pallas kernels, shards(): pl.pallas_call(functools.partial(first_kernel, steps, span), out_shape=[j...  4.66 us
    pallas_call x2, Pallas kernels, pack(): pl.pallas_call(functools.partial(pack_kernel, n, chosen, pages), out_shap...  3.48 us
    pallas_call x1, Pallas kernels, shards(): pl.pallas_call(functools.partial(early_kernel, some, span), out_shape=[ca...  2.31 us
    pallas_call x1, Pallas kernels, shards(): pl.pallas_call(functools.partial(late_kernel, LATE, span), out_shape=[jax...  2.01 us
    convert_element_type x2, other arithmetic, total(): (partial.astype(jnp.float32) + other.astype(jnp.float32)).astype(jnp.bflo...  1.38 us
  transfers between devices with their start and end apart: 17, of which 7 were waited for; matrix products, arithmetic and copies ran while one was open for 1% of the time, Pallas kernels for 19%

profile of v10, /device:TPU:0, one launch (start us, length us, event | category | flops | bytes accessed | tf_op | source)
XLA Modules:
  0.0 57.7 jit_solution(18361267436215902181)
XLA Ops:
  0.6 1.7 %pack.2 = (bf16[512,128]{1,0:T(8,128)(2,1)S(1)}, bf16[512,128]{1,0:T(8,128)(2,1)S(1)}, bf16[512,128]{1,0:T(8,128)(2,1)S(1)}, bf16[512,128]{1,0:T(8,128)(2,1)S(1)}, bf16[512,128]{1,0:T(8,128)(2,1)S(1)}) custom-call(s32[4,16]{1,0:T(4,128)} %bitcast.23, s32[16]{0:T(128)} %refs_0_.1, s32[16]{0:T(128)} %refs_1_.5, s32[16]{0:T(128)} %refs_3_.4, ...), custom_call_target="tpu_custom_call" | custom-call | bytes 1310720 | tf_op jit(solution)/shard_map/pack/pallas_call | solution.py:280
  2.3 4.1 %collective-permute-start = (bf16[512,128]{1,0:T(8,128)(2,1)S(1)}, bf16[512,128]{1,0:T(8,128)(2,1)S(1)}, u32[]{:S(2)}, u32[]{:S(2)}) collective-permute-start(bf16[512,128]{1,0:T(8,128)(2,1)S(1)} %get-tuple-element.42.refs_4_), channel_id=1, source_target_pairs={{0,16},{2,18},{4,20},{6,22},{8,24},{10,26},{12,28},{14,30},{16,0},... | collective-permute-start | bytes 393224 | tf_op jit(solution)/shard_map/ppermute | solution.py:320
  6.5 3.5 %collective-permute-start.1 = (bf16[512,128]{1,0:T(8,128)(2,1)S(1)}, bf16[512,128]{1,0:T(8,128)(2,1)S(1)}, u32[]{:S(2)}, u32[]{:S(2)}) collective-permute-start(bf16[512,128]{1,0:T(8,128)(2,1)S(1)} %get-tuple-element.43.refs_5_), channel_id=1, source_target_pairs={{0,14},{2,12},{4,10},{6,8},{8,6},{10,4},{12,2},{14,0},{16,30},{18,... | collective-permute-start | bytes 393224 | tf_op jit(solution)/shard_map/ppermute | solution.py:320
  9.9 0.0 collective-permute-start.2
  9.9 1.8 %collective-permute-start.3 = (bf16[512,128]{1,0:T(8,128)(2,1)S(1)}, bf16[512,128]{1,0:T(8,128)(2,1)S(1)}, u32[]{:S(2)}, u32[]{:S(2)}) collective-permute-start(bf16[512,128]{1,0:T(8,128)(2,1)S(1)} %get-tuple-element.45.refs_7_), channel_id=1, source_target_pairs={{0,12},{2,14},{4,8},{6,10},{8,4},{10,6},{12,0},{14,2},{16,28},{18,... | collective-permute-start | bytes 393224 | tf_op jit(solution)/shard_map/ppermute | solution.py:320
  11.7 2.9 %collective-permute-start.4 = (bf16[512,128]{1,0:T(8,128)(2,1)S(1)}, bf16[512,128]{1,0:T(8,128)(2,1)S(1)}, u32[]{:S(2)}, u32[]{:S(2)}) collective-permute-start(bf16[512,128]{1,0:T(8,128)(2,1)S(1)} %get-tuple-element.46.refs_8_), channel_id=1, source_target_pairs={{0,28},{2,30},{4,24},{6,26},{8,20},{10,22},{12,16},{14,18},{16,12}... | collective-permute-start | bytes 393224 | tf_op jit(solution)/shard_map/ppermute | solution.py:320
  14.6 1.8 %pack.3 = (bf16[512,128]{1,0:T(8,128)(2,1)S(1)}, bf16[512,128]{1,0:T(8,128)(2,1)S(1)}, bf16[512,128]{1,0:T(8,128)(2,1)S(1)}, bf16[512,128]{1,0:T(8,128)(2,1)S(1)...) custom-call(s32[4,16]{1,0:T(4,128)} %bitcast.24, ...), custom_call_target="tpu_custom_call" | custom-call | bytes 2883584 | tf_op jit(solution)/shard_map/pack/pallas_call | solution.py:280
  16.4 4.7 %first.1 = (bf16[16,4096]{1,0:T(8,128)(2,1)S(1)}, bf16[1024,4096]{1,0:T(8,128)(2,1)S(1)}) custom-call(s32[16]{0:T(128)} %refs_0_.1, s32[16]{0:T(128)} %refs_1_.5, bf16[16,8,128]{2,1,0:T(8,128)(2,1)} %refs_2_.5, bf16[1024,4096]{1,0:T(8,128)(2,1)} %refs_3_.5, bf16[512,128]{1,0:T(8,128)(2,1)S(1)} %get-tuple-element.42.refs_4_, ...), custom_call_target="tpu_custom_call" | custom-call | flops 150994944 | bytes 10485760 | tf_op jit(solution)/shard_map/first/pallas_call | solution.py:323
  21.1 0.0 collective-permute-done.refs_1_
  21.1 2.1 %collective-permute-start.5 = (bf16[512,128]{1,0:T(8,128)(2,1)S(1)}, bf16[512,128]{1,0:T(8,128)(2,1)S(1)}, u32[]{:S(2)}, u32[]{:S(2)}) collective-permute-start(bf16[512,128]{1,0:T(8,128)(2,1)S(1)} %get-tuple-element.59.refs_9_), channel_id=1, source_target_pairs={{0,10},{2,8},{4,14},{6,12},{8,2},{10,0},{12,6},{14,4},{16,26},{18,... | collective-permute-start | bytes 393224 | tf_op jit(solution)/shard_map/ppermute | solution.py:320
  23.1 0.0 collective-permute-done.1.refs_2_
  23.1 0.9 %collective-permute-start.6 = (bf16[512,128]{1,0:T(8,128)(2,1)S(1)}, bf16[512,128]{1,0:T(8,128)(2,1)S(1)}, u32[]{:S(2)}, u32[]{:S(2)}) collective-permute-start(bf16[512,128]{1,0:T(8,128)(2,1)S(1)} %get-tuple-element.60.refs_10_), channel_id=1, source_target_pairs={{0,26},{2,24},{4,30},{6,28},{8,18},{10,16},{12,22},{14,20},{16,10}... | collective-permute-start | bytes 393224 | tf_op jit(solution)/shard_map/ppermute | solution.py:320
  24.1 0.0 collective-permute-done.2.refs_3_
  24.1 0.1 collective-permute-start.7
  24.2 0.0 collective-permute-done.3.refs_4_
  24.2 3.2 %collective-permute-start.8 = (bf16[512,128]{1,0:T(8,128)(2,1)S(1)}, bf16[512,128]{1,0:T(8,128)(2,1)S(1)}, u32[]{:S(2)}, u32[]{:S(2)}) collective-permute-start(bf16[512,128]{1,0:T(8,128)(2,1)S(1)} %get-tuple-element.62.refs_12_), channel_id=1, source_target_pairs={{0,24},{2,26},{4,28},{6,30},{8,16},{10,18},{12,20},{14,22},{16,8},... | collective-permute-start | bytes 393224 | tf_op jit(solution)/shard_map/ppermute | solution.py:320
  27.3 0.0 collective-permute-done.4.refs_5_
  27.3 2.1 %collective-permute-start.9 = (bf16[512,128]{1,0:T(8,128)(2,1)S(1)}, bf16[512,128]{1,0:T(8,128)(2,1)S(1)}, u32[]{:S(2)}, u32[]{:S(2)}) collective-permute-start(bf16[512,128]{1,0:T(8,128)(2,1)S(1)} %get-tuple-element.63.refs_13_), channel_id=1, source_target_pairs={{0,6},{2,4},{4,2},{6,0},{8,14},{10,12},{12,10},{14,8},{16,22},{18,... | collective-permute-start | bytes 393224 | tf_op jit(solution)/shard_map/ppermute | solution.py:320
  29.5 0.4 collective-permute-done.5.refs_6_
  29.9 1.5 %collective-permute-start.11 = (bf16[512,128]{1,0:T(8,128)(2,1)S(1)}, bf16[512,128]{1,0:T(8,128)(2,1)S(1)}, u32[]{:S(2)}, u32[]{:S(2)}) collective-permute-start(bf16[512,128]{1,0:T(8,128)(2,1)S(1)} %get-tuple-element.66.refs_14_), channel_id=1, source_target_pairs={{0,22},{2,20},{4,18},{6,16},{8,30},{10,28},{12,26},{14,24},{16,6},... | collective-permute-start | bytes 393224 | tf_op jit(solution)/shard_map/ppermute | solution.py:320
  31.4 1.0 %collective-permute-done.6.refs_7_ = bf16[512,128]{1,0:T(8,128)(2,1)S(1)} collective-permute-done((bf16[512,128]{1,0:T(8,128)(2,1)S(1)}, bf16[512,128]{1,0:T(8,128)(2,1)S(1)}, u32[]{:S(2)}, u32[]{:S(2)}) %collective-permute-start.6) | collective-permute-done | bytes 131104 | tf_op jit(solution)/shard_map/ppermute | solution.py:320
  32.4 1.5 %collective-permute-start.12 = (bf16[512,128]{1,0:T(8,128)(2,1)S(1)}, bf16[512,128]{1,0:T(8,128)(2,1)S(1)}, u32[]{:S(2)}, u32[]{:S(2)}) collective-permute-start(bf16[512,128]{1,0:T(8,128)(2,1)S(1)} %get-tuple-element.67.refs_15_), channel_id=1, source_target_pairs={{0,4},{2,6},{4,0},{6,2},{8,12},{10,14},{12,8},{14,10},{16,20},{18,... | collective-permute-start | bytes 393224 | tf_op jit(solution)/shard_map/ppermute | solution.py:320
  34.0 0.1 collective-permute-done.7.refs_8_
  34.0 2.1 %collective-permute-start.13 = (bf16[512,128]{1,0:T(8,128)(2,1)S(1)}, bf16[512,128]{1,0:T(8,128)(2,1)S(1)}, u32[]{:S(2)}, u32[]{:S(2)}) collective-permute-start(bf16[512,128]{1,0:T(8,128)(2,1)S(1)} %get-tuple-element.68.refs_16_), channel_id=1, source_target_pairs={{0,20},{2,22},{4,16},{6,18},{8,28},{10,30},{12,24},{14,26},{16,4},... | collective-permute-start | bytes 393224 | tf_op jit(solution)/shard_map/ppermute | solution.py:320
  36.1 0.8 %collective-permute-done.8.refs_9_ = bf16[512,128]{1,0:T(8,128)(2,1)S(1)} collective-permute-done((bf16[512,128]{1,0:T(8,128)(2,1)S(1)}, bf16[512,128]{1,0:T(8,128)(2,1)S(1)}, u32[]{:S(2)}, u32[]{:S(2)}) %collective-permute-start.8) | collective-permute-done | bytes 131104 | tf_op jit(solution)/shard_map/ppermute | solution.py:320
  37.0 0.5 collective-permute-start.14
  37.4 0.0 collective-permute-done.9.refs_10_
  37.4 8.0 %collective-permute-start.15 = (bf16[512,128]{1,0:T(8,128)(2,1)S(1)}, bf16[512,128]{1,0:T(8,128)(2,1)S(1)}, u32[]{:S(2)}, u32[]{:S(2)}) collective-permute-start(bf16[512,128]{1,0:T(8,128)(2,1)S(1)} %get-tuple-element.70.refs_18_), channel_id=1, source_target_pairs={{0,18},{2,16},{4,22},{6,20},{8,26},{10,24},{12,30},{14,28},{16,2},... | collective-permute-start | bytes 393224 | tf_op jit(solution)/shard_map/ppermute | solution.py:320
  45.4 2.3 %early.1 = (bf16[16,256,128]{2,1,0:T(8,128)(2,1)}, bf16[16,256,128]{2,1,0:T(8,128)(2,1)}, f32[16,8,128]{2,1,0:T(8,128)S(1)}, bf16[16,8,128]{2,1,0:T(8,128)(2,1)S...) custom-call(bf16[512,128]{1,0:T(8,128)(2,1)S(1)} %get-tuple-element.57.refs_19_.refs_0_, ...), custom_call_target="tpu_custom_call" | custom-call | flops 11534336 | bytes 2883584 | tf_op jit(solution)/shard_map/early/pallas_call | solution.py:349
  47.8 0.0 collective-permute-done.11.refs_0_
  47.8 0.1 collective-permute-start.10
  47.8 0.0 collective-permute-done.12.refs_1_
  47.9 2.8 %collective-permute-done.13.refs_2_ = bf16[512,128]{1,0:T(8,128)(2,1)S(1)} collective-permute-done((bf16[512,128]{1,0:T(8,128)(2,1)S(1)}, bf16[512,128]{1,0:T(8,128)(2,1)S(1)}, u32[]{:S(2)}, u32[]{:S(2)}) %collective-permute-start.13) | collective-permute-done | bytes 131104 | tf_op jit(solution)/shard_map/ppermute | solution.py:320
  50.7 0.0 collective-permute-done.14.refs_3_
  50.7 2.9 %collective-permute-done.15.refs_4_ = bf16[512,128]{1,0:T(8,128)(2,1)S(1)} collective-permute-done((bf16[512,128]{1,0:T(8,128)(2,1)S(1)}, bf16[512,128]{1,0:T(8,128)(2,1)S(1)}, u32[]{:S(2)}, u32[]{:S(2)}) %collective-permute-start.15) | collective-permute-done | bytes 131104 | tf_op jit(solution)/shard_map/ppermute | solution.py:320
  53.5 2.0 %late.1 = (bf16[16,4096]{1,0:T(8,128)(2,1)S(1)}, bf16[16,256,128]{2,1,0:T(8,128)(2,1)}, bf16[16,256,128]{2,1,0:T(8,128)(2,1)}) custom-call(bf16[512,128]{1,0:T(8,128)(2,1)S(1)} %collective-permute-done.11.refs_0_, bf16[512,128]{1,0:T(8,128)(2,1)S(1)} %collective-permute-done.12.refs_1_, ...), custom_call_target="tpu_custom_call", output_to_operand_aliasing={{1}: (10, {}), {2}: (11, {})} | custom-call | flops 150994944 | bytes 10485760 | tf_op jit(solution)/shard_map/late/pallas_call | solution.py:375
  55.6 0.1 collective-permute-start.16
  55.6 0.0 collective-permute-done.10
  55.7 0.7 %add_convert_fusion.1 = bf16[16,4096]{1,0:T(8,128)(2,1)} fusion(bf16[16,4096]{1,0:T(8,128)(2,1)S(1)} %collective-permute-done.10, bf16[16,4096]{1,0:T(8,128)(2,1)S(1)} %get-tuple-element.65), kind=kLoop, calls=%fused_computation.1 | loop fusion | flops 262144 | bytes 393216 | tf_op jit(solution)/shard_map/convert_element_type | solution.py:209
  56.3 0.6 %collective-permute-done.16 = bf16[16,4096]{1,0:T(8,128)(2,1)S(1)} collective-permute-done((bf16[16,4096]{1,0:T(8,128)(2,1)S(1)}, bf16[16,4096]{1,0:T(8,128)(2,1)S(1)}, u32[]{:S(2)}, u32[]{:S(2)}) %collective-permute-start.16) | collective-permute-done | bytes 131104 | tf_op jit(solution)/shard_map/ppermute | solution.py:208
  57.0 0.7 %add_convert_fusion = bf16[16,4096]{1,0:T(8,128)(2,1)} fusion(bf16[16,4096]{1,0:T(8,128)(2,1)S(1)} %collective-permute-done.16, bf16[16,4096]{1,0:T(8,128)(2,1)S(1)} %get-tuple-element.77), kind=kLoop, calls=%fused_computation | loop fusion | flops 262144 | bytes 393216 | tf_op jit(solution)/shard_map/convert_element_type | solution.py:209
Async XLA Ops:
  2.3 18.7 %collective-permute-start = (bf16[512,128]{1,0:T(8,128)(2,1)S(1)}, bf16[512,128]{1,0:T(8,128)(2,1)S(1)}, u32[]{:S(2)}, u32[]{:S(2)}) collective-permute-start(bf16[512,128]{1,0:T(8,128)(2,1)S(1)} %get-tuple-element.42.refs_4_), channel_id=1, source_target_pairs={{0,16},{2,18},{4,20},{6,22},{8,24},{10,26},{12,28},{14,30},{16,0},... | collective-permute-start | bytes 393224 | tf_op jit(solution)/shard_map/ppermute | solution.py:320
  6.5 16.7 %collective-permute-start.1 = (bf16[512,128]{1,0:T(8,128)(2,1)S(1)}, bf16[512,128]{1,0:T(8,128)(2,1)S(1)}, u32[]{:S(2)}, u32[]{:S(2)}) collective-permute-start(bf16[512,128]{1,0:T(8,128)(2,1)S(1)} %get-tuple-element.43.refs_5_), channel_id=1, source_target_pairs={{0,14},{2,12},{4,10},{6,8},{8,6},{10,4},{12,2},{14,0},{16,30},{18,... | collective-permute-start | bytes 393224 | tf_op jit(solution)/shard_map/ppermute | solution.py:320
  9.9 14.2 %collective-permute-start.2 = (bf16[512,128]{1,0:T(8,128)(2,1)S(1)}, bf16[512,128]{1,0:T(8,128)(2,1)S(1)}, u32[]{:S(2)}, u32[]{:S(2)}) collective-permute-start(bf16[512,128]{1,0:T(8,128)(2,1)S(1)} %get-tuple-element.44.refs_6_), channel_id=1, source_target_pairs={{0,30},{2,28},{4,26},{6,24},{8,22},{10,20},{12,18},{14,16},{16,14}... | collective-permute-start | bytes 393224 | tf_op jit(solution)/shard_map/ppermute | solution.py:320
  9.9 14.3 %collective-permute-start.3 = (bf16[512,128]{1,0:T(8,128)(2,1)S(1)}, bf16[512,128]{1,0:T(8,128)(2,1)S(1)}, u32[]{:S(2)}, u32[]{:S(2)}) collective-permute-start(bf16[512,128]{1,0:T(8,128)(2,1)S(1)} %get-tuple-element.45.refs_7_), channel_id=1, source_target_pairs={{0,12},{2,14},{4,8},{6,10},{8,4},{10,6},{12,0},{14,2},{16,28},{18,... | collective-permute-start | bytes 393224 | tf_op jit(solution)/shard_map/ppermute | solution.py:320
  11.7 15.7 %collective-permute-start.4 = (bf16[512,128]{1,0:T(8,128)(2,1)S(1)}, bf16[512,128]{1,0:T(8,128)(2,1)S(1)}, u32[]{:S(2)}, u32[]{:S(2)}) collective-permute-start(bf16[512,128]{1,0:T(8,128)(2,1)S(1)} %get-tuple-element.46.refs_8_), channel_id=1, source_target_pairs={{0,28},{2,30},{4,24},{6,26},{8,20},{10,22},{12,16},{14,18},{16,12}... | collective-permute-start | bytes 393224 | tf_op jit(solution)/shard_map/ppermute | solution.py:320
  21.1 8.8 %collective-permute-start.5 = (bf16[512,128]{1,0:T(8,128)(2,1)S(1)}, bf16[512,128]{1,0:T(8,128)(2,1)S(1)}, u32[]{:S(2)}, u32[]{:S(2)}) collective-permute-start(bf16[512,128]{1,0:T(8,128)(2,1)S(1)} %get-tuple-element.59.refs_9_), channel_id=1, source_target_pairs={{0,10},{2,8},{4,14},{6,12},{8,2},{10,0},{12,6},{14,4},{16,26},{18,... | collective-permute-start | bytes 393224 | tf_op jit(solution)/shard_map/ppermute | solution.py:320
  23.1 9.3 %collective-permute-start.6 = (bf16[512,128]{1,0:T(8,128)(2,1)S(1)}, bf16[512,128]{1,0:T(8,128)(2,1)S(1)}, u32[]{:S(2)}, u32[]{:S(2)}) collective-permute-start(bf16[512,128]{1,0:T(8,128)(2,1)S(1)} %get-tuple-element.60.refs_10_), channel_id=1, source_target_pairs={{0,26},{2,24},{4,30},{6,28},{8,18},{10,16},{12,22},{14,20},{16,10}... | collective-permute-start | bytes 393224 | tf_op jit(solution)/shard_map/ppermute | solution.py:320
  24.1 10.0 %collective-permute-start.7 = (bf16[512,128]{1,0:T(8,128)(2,1)S(1)}, bf16[512,128]{1,0:T(8,128)(2,1)S(1)}, u32[]{:S(2)}, u32[]{:S(2)}) collective-permute-start(bf16[512,128]{1,0:T(8,128)(2,1)S(1)} %get-tuple-element.61.refs_11_), channel_id=1, source_target_pairs={{0,8},{2,10},{4,12},{6,14},{8,0},{10,2},{12,4},{14,6},{16,24},{18,... | collective-permute-start | bytes 393224 | tf_op jit(solution)/shard_map/ppermute | solution.py:320
  24.2 12.8 %collective-permute-start.8 = (bf16[512,128]{1,0:T(8,128)(2,1)S(1)}, bf16[512,128]{1,0:T(8,128)(2,1)S(1)}, u32[]{:S(2)}, u32[]{:S(2)}) collective-permute-start(bf16[512,128]{1,0:T(8,128)(2,1)S(1)} %get-tuple-element.62.refs_12_), channel_id=1, source_target_pairs={{0,24},{2,26},{4,28},{6,30},{8,16},{10,18},{12,20},{14,22},{16,8},... | collective-permute-start | bytes 393224 | tf_op jit(solution)/shard_map/ppermute | solution.py:320
  27.3 10.1 %collective-permute-start.9 = (bf16[512,128]{1,0:T(8,128)(2,1)S(1)}, bf16[512,128]{1,0:T(8,128)(2,1)S(1)}, u32[]{:S(2)}, u32[]{:S(2)}) collective-permute-start(bf16[512,128]{1,0:T(8,128)(2,1)S(1)} %get-tuple-element.63.refs_13_), channel_id=1, source_target_pairs={{0,6},{2,4},{4,2},{6,0},{8,14},{10,12},{12,10},{14,8},{16,22},{18,... | collective-permute-start | bytes 393224 | tf_op jit(solution)/shard_map/ppermute | solution.py:320
  29.9 17.9 %collective-permute-start.11 = (bf16[512,128]{1,0:T(8,128)(2,1)S(1)}, bf16[512,128]{1,0:T(8,128)(2,1)S(1)}, u32[]{:S(2)}, u32[]{:S(2)}) collective-permute-start(bf16[512,128]{1,0:T(8,128)(2,1)S(1)} %get-tuple-element.66.refs_14_), channel_id=1, source_target_pairs={{0,22},{2,20},{4,18},{6,16},{8,30},{10,28},{12,26},{14,24},{16,6},... | collective-permute-start | bytes 393224 | tf_op jit(solution)/shard_map/ppermute | solution.py:320
  32.4 15.4 %collective-permute-start.12 = (bf16[512,128]{1,0:T(8,128)(2,1)S(1)}, bf16[512,128]{1,0:T(8,128)(2,1)S(1)}, u32[]{:S(2)}, u32[]{:S(2)}) collective-permute-start(bf16[512,128]{1,0:T(8,128)(2,1)S(1)} %get-tuple-element.67.refs_15_), channel_id=1, source_target_pairs={{0,4},{2,6},{4,0},{6,2},{8,12},{10,14},{12,8},{14,10},{16,20},{18,... | collective-permute-start | bytes 393224 | tf_op jit(solution)/shard_map/ppermute | solution.py:320
  34.0 16.7 %collective-permute-start.13 = (bf16[512,128]{1,0:T(8,128)(2,1)S(1)}, bf16[512,128]{1,0:T(8,128)(2,1)S(1)}, u32[]{:S(2)}, u32[]{:S(2)}) collective-permute-start(bf16[512,128]{1,0:T(8,128)(2,1)S(1)} %get-tuple-element.68.refs_16_), channel_id=1, source_target_pairs={{0,20},{2,22},{4,16},{6,18},{8,28},{10,30},{12,24},{14,26},{16,4},... | collective-permute-start | bytes 393224 | tf_op jit(solution)/shard_map/ppermute | solution.py:320
  37.0 13.7 %collective-permute-start.14 = (bf16[512,128]{1,0:T(8,128)(2,1)S(1)}, bf16[512,128]{1,0:T(8,128)(2,1)S(1)}, u32[]{:S(2)}, u32[]{:S(2)}) collective-permute-start(bf16[512,128]{1,0:T(8,128)(2,1)S(1)} %get-tuple-element.69.refs_17_), channel_id=1, source_target_pairs={{0,2},{2,0},{4,6},{6,4},{8,10},{10,8},{12,14},{14,12},{16,18},{18,... | collective-permute-start | bytes 393224 | tf_op jit(solution)/shard_map/ppermute | solution.py:320
  37.4 16.1 %collective-permute-start.15 = (bf16[512,128]{1,0:T(8,128)(2,1)S(1)}, bf16[512,128]{1,0:T(8,128)(2,1)S(1)}, u32[]{:S(2)}, u32[]{:S(2)}) collective-permute-start(bf16[512,128]{1,0:T(8,128)(2,1)S(1)} %get-tuple-element.70.refs_18_), channel_id=1, source_target_pairs={{0,18},{2,16},{4,22},{6,20},{8,26},{10,24},{12,30},{14,28},{16,2},... | collective-permute-start | bytes 393224 | tf_op jit(solution)/shard_map/ppermute | solution.py:320
  47.8 7.9 %collective-permute-start.10 = (bf16[16,4096]{1,0:T(8,128)(2,1)S(1)}, bf16[16,4096]{1,0:T(8,128)(2,1)S(1)}, u32[]{:S(2)}, u32[]{:S(2)}) collective-permute-start(bf16[16,4096]{1,0:T(8,128)(2,1)S(1)} %get-tuple-element.65), channel_id=1, source_target_pairs={{0,1},{1,0},{2,3},{3,2},{4,5},{5,4},{6,7},{7,6},{8,9},{9,8},{10,11... | collective-permute-start | bytes 393224 | tf_op jit(solution)/shard_map/ppermute | solution.py:208
  55.6 1.4 %collective-permute-start.16 = (bf16[16,4096]{1,0:T(8,128)(2,1)S(1)}, bf16[16,4096]{1,0:T(8,128)(2,1)S(1)}, u32[]{:S(2)}, u32[]{:S(2)}) collective-permute-start(bf16[16,4096]{1,0:T(8,128)(2,1)S(1)} %get-tuple-element.77), channel_id=1, source_target_pairs={{0,1},{1,0},{2,3},{3,2},{4,5},{5,4},{6,7},{7,6},{8,9},{9,8},{10,11... | collective-permute-start | bytes 393224 | tf_op jit(solution)/shard_map/ppermute | solution.py:208

commit v11 on v10

--- a/solution.py
+++ b/solution.py
@@ -220,10 +220,12 @@
 
 def step_order(n):
     half = n // 2
-    crossing = [half] + list(range(half + 1, n))[::-1]
-    staying = list(range(1, half))[::-1]
+    lead = [half, half + half // 2, half + 1]
+    crossing = lead + [s for s in range(n - 1, half, -1) if s not in lead]
+    lead = [1, half // 2]
+    staying = lead + [s for s in range(half - 1, 0, -1) if s not in lead]
     order = []
-    for kind in "cncncncncncncnc":
+    for kind in "ccncncncncncncn":
         queue = crossing if kind == "c" else staying
         if queue:
             order.append(queue.pop(0))

time: 57.9 us -> 59.7 us (1.031)
  waiting for transfers between devices: 8.67 us -> 11.4 us
  starting transfers between devices: 34.4 us -> 33.4 us
    ppermute x15, waiting for transfers between devices: 8.03 us -> 10.8 us  [send(): return lax.ppermute(block, 'inst', [(d, d ^ steps[i]) for d in range(n)])]
    ppermute x15, starting transfers between devices: 34.3 us -> 33.3 us  [send(): return lax.ppermute(block, 'inst', [(d, d ^ steps[i]) for d in range(n)])]
  transfers between devices with their start and end apart: 17 -> 17, of which waited for: 7 -> 6; matrix products, arithmetic and copies ran while one was open for 1% -> 1% of each run, Pallas kernels for 19% -> 18%
where the time goes in v11:
time: 59.7 us; the launch traced here: 59.4 us
  starting transfers between devices  33.4 us (56%)
  Pallas kernels  12.5 us (21%)
  waiting for transfers between devices  11.4 us (19%)
  other arithmetic  1.38 us (2%)
  between operations  0.72 us (1%)
    ppermute x15, starting transfers between devices, send(): return lax.ppermute(block, 'inst', [(d, d ^ steps[i]) for d in range(n)])  33.3 us
    ppermute x15, waiting for transfers between devices, send(): return lax.ppermute(block, 'inst', [(d, d ^ steps[i]) for d in range(n)])  10.8 us
    pallas_call x1, Pallas kernels, shards(): pl.pallas_call(functools.partial(first_kernel, steps, span), out_shape=[j...  4.66 us
    pallas_call x2, Pallas kernels, pack(): pl.pallas_call(functools.partial(pack_kernel, n, chosen, pages), out_shap...  3.48 us
    pallas_call x1, Pallas kernels, shards(): pl.pallas_call(functools.partial(early_kernel, some, span), out_shape=[ca...  2.31 us
    pallas_call x1, Pallas kernels, shards(): pl.pallas_call(functools.partial(late_kernel, LATE, span), out_shape=[jax...  2.01 us
    convert_element_type x2, other arithmetic, total(): (partial.astype(jnp.float32) + other.astype(jnp.float32)).astype(jnp.bflo...  1.38 us
  transfers between devices with their start and end apart: 17, of which 6 were waited for; matrix products, arithmetic and copies ran while one was open for 1% of the time, Pallas kernels for 18%

profile of v11, /device:TPU:0, one launch (start us, length us, event | category | flops | bytes accessed | tf_op | source)
XLA Modules:
  0.0 59.4 jit_solution(696077333679123337)
XLA Ops:
  0.6 1.7 %pack.2 = (bf16[512,128]{1,0:T(8,128)(2,1)S(1)}, bf16[512,128]{1,0:T(8,128)(2,1)S(1)}, bf16[512,128]{1,0:T(8,128)(2,1)S(1)}, bf16[512,128]{1,0:T(8,128)(2,1)S(1)}, bf16[512,128]{1,0:T(8,128)(2,1)S(1)}) custom-call(s32[4,16]{1,0:T(4,128)} %bitcast.23, s32[16]{0:T(128)} %refs_0_.1, s32[16]{0:T(128)} %refs_1_.5, s32[16]{0:T(128)} %refs_3_.4, ...), custom_call_target="tpu_custom_call" | custom-call | bytes 1310720 | tf_op jit(solution)/shard_map/pack/pallas_call | solution.py:282
  2.3 4.1 %collective-permute-start = (bf16[512,128]{1,0:T(8,128)(2,1)S(1)}, bf16[512,128]{1,0:T(8,128)(2,1)S(1)}, u32[]{:S(2)}, u32[]{:S(2)}) collective-permute-start(bf16[512,128]{1,0:T(8,128)(2,1)S(1)} %get-tuple-element.42.refs_4_), channel_id=1, source_target_pairs={{0,16},{2,18},{4,20},{6,22},{8,24},{10,26},{12,28},{14,30},{16,0},... | collective-permute-start | bytes 393224 | tf_op jit(solution)/shard_map/ppermute | solution.py:322
  6.5 1.3 %collective-permute-start.1 = (bf16[512,128]{1,0:T(8,128)(2,1)S(1)}, bf16[512,128]{1,0:T(8,128)(2,1)S(1)}, u32[]{:S(2)}, u32[]{:S(2)}) collective-permute-start(bf16[512,128]{1,0:T(8,128)(2,1)S(1)} %get-tuple-element.43.refs_5_), channel_id=1, source_target_pairs={{0,24},{2,26},{4,28},{6,30},{8,16},{10,18},{12,20},{14,22},{16,8},... | collective-permute-start | bytes 393224 | tf_op jit(solution)/shard_map/ppermute | solution.py:322
  7.8 1.5 %collective-permute-start.2 = (bf16[512,128]{1,0:T(8,128)(2,1)S(1)}, bf16[512,128]{1,0:T(8,128)(2,1)S(1)}, u32[]{:S(2)}, u32[]{:S(2)}) collective-permute-start(bf16[512,128]{1,0:T(8,128)(2,1)S(1)} %get-tuple-element.44.refs_6_), channel_id=1, source_target_pairs={{0,2},{2,0},{4,6},{6,4},{8,10},{10,8},{12,14},{14,12},{16,18},{18,... | collective-permute-start | bytes 393224 | tf_op jit(solution)/shard_map/ppermute | solution.py:322
  9.3 1.7 %collective-permute-start.3 = (bf16[512,128]{1,0:T(8,128)(2,1)S(1)}, bf16[512,128]{1,0:T(8,128)(2,1)S(1)}, u32[]{:S(2)}, u32[]{:S(2)}) collective-permute-start(bf16[512,128]{1,0:T(8,128)(2,1)S(1)} %get-tuple-element.45.refs_7_), channel_id=1, source_target_pairs={{0,18},{2,16},{4,22},{6,20},{8,26},{10,24},{12,30},{14,28},{16,2},... | collective-permute-start | bytes 393224 | tf_op jit(solution)/shard_map/ppermute | solution.py:322
  11.0 1.3 %collective-permute-start.4 = (bf16[512,128]{1,0:T(8,128)(2,1)S(1)}, bf16[512,128]{1,0:T(8,128)(2,1)S(1)}, u32[]{:S(2)}, u32[]{:S(2)}) collective-permute-start(bf16[512,128]{1,0:T(8,128)(2,1)S(1)} %get-tuple-element.46.refs_8_), channel_id=1, source_target_pairs={{0,8},{2,10},{4,12},{6,14},{8,0},{10,2},{12,4},{14,6},{16,24},{18,... | collective-permute-start | bytes 393224 | tf_op jit(solution)/shard_map/ppermute | solution.py:322
  12.3 1.8 %pack.3 = (bf16[512,128]{1,0:T(8,128)(2,1)S(1)}, bf16[512,128]{1,0:T(8,128)(2,1)S(1)}, bf16[512,128]{1,0:T(8,128)(2,1)S(1)}, bf16[512,128]{1,0:T(8,128)(2,1)S(1)...) custom-call(s32[4,16]{1,0:T(4,128)} %bitcast.24, ...), custom_call_target="tpu_custom_call" | custom-call | bytes 2883584 | tf_op jit(solution)/shard_map/pack/pallas_call | solution.py:282
  14.1 4.7 %first.1 = (bf16[16,4096]{1,0:T(8,128)(2,1)S(1)}, bf16[1024,4096]{1,0:T(8,128)(2,1)S(1)}) custom-call(s32[16]{0:T(128)} %refs_0_.1, s32[16]{0:T(128)} %refs_1_.5, bf16[16,8,128]{2,1,0:T(8,128)(2,1)} %refs_2_.5, bf16[1024,4096]{1,0:T(8,128)(2,1)} %refs_3_.5, bf16[512,128]{1,0:T(8,128)(2,1)S(1)} %get-tuple-element.42.refs_4_, ...), custom_call_target="tpu_custom_call" | custom-call | flops 150994944 | bytes 10485760 | tf_op jit(solution)/shard_map/first/pallas_call | solution.py:325
  18.7 0.5 collective-permute-done.refs_1_
  19.2 4.7 %collective-permute-start.5 = (bf16[512,128]{1,0:T(8,128)(2,1)S(1)}, bf16[512,128]{1,0:T(8,128)(2,1)S(1)}, u32[]{:S(2)}, u32[]{:S(2)}) collective-permute-start(bf16[512,128]{1,0:T(8,128)(2,1)S(1)} %get-tuple-element.59.refs_9_), channel_id=1, source_target_pairs={{0,30},{2,28},{4,26},{6,24},{8,22},{10,20},{12,18},{14,16},{16,14}... | collective-permute-start | bytes 393224 | tf_op jit(solution)/shard_map/ppermute | solution.py:322
  23.9 0.0 collective-permute-done.1.refs_2_
  23.9 0.9 %collective-permute-start.6 = (bf16[512,128]{1,0:T(8,128)(2,1)S(1)}, bf16[512,128]{1,0:T(8,128)(2,1)S(1)}, u32[]{:S(2)}, u32[]{:S(2)}) collective-permute-start(bf16[512,128]{1,0:T(8,128)(2,1)S(1)} %get-tuple-element.60.refs_10_), channel_id=1, source_target_pairs={{0,14},{2,12},{4,10},{6,8},{8,6},{10,4},{12,2},{14,0},{16,30},{18,... | collective-permute-start | bytes 393224 | tf_op jit(solution)/shard_map/ppermute | solution.py:322
  24.8 0.0 collective-permute-done.2.refs_3_
  24.8 2.4 %collective-permute-start.7 = (bf16[512,128]{1,0:T(8,128)(2,1)S(1)}, bf16[512,128]{1,0:T(8,128)(2,1)S(1)}, u32[]{:S(2)}, u32[]{:S(2)}) collective-permute-start(bf16[512,128]{1,0:T(8,128)(2,1)S(1)} %get-tuple-element.61.refs_11_), channel_id=1, source_target_pairs={{0,28},{2,30},{4,24},{6,26},{8,20},{10,22},{12,16},{14,18},{16,12}... | collective-permute-start | bytes 393224 | tf_op jit(solution)/shard_map/ppermute | solution.py:322
  27.2 1.7 %collective-permute-done.3.refs_4_ = bf16[512,128]{1,0:T(8,128)(2,1)S(1)} collective-permute-done((bf16[512,128]{1,0:T(8,128)(2,1)S(1)}, bf16[512,128]{1,0:T(8,128)(2,1)S(1)}, u32[]{:S(2)}, u32[]{:S(2)}) %collective-permute-start.3) | collective-permute-done | bytes 131104 | tf_op jit(solution)/shard_map/ppermute | solution.py:322
  28.9 0.0 collective-permute-start.8
  28.9 0.0 collective-permute-done.4.refs_5_
  28.9 1.9 %collective-permute-start.9 = (bf16[512,128]{1,0:T(8,128)(2,1)S(1)}, bf16[512,128]{1,0:T(8,128)(2,1)S(1)}, u32[]{:S(2)}, u32[]{:S(2)}) collective-permute-start(bf16[512,128]{1,0:T(8,128)(2,1)S(1)} %get-tuple-element.63.refs_13_), channel_id=1, source_target_pairs={{0,26},{2,24},{4,30},{6,28},{8,18},{10,16},{12,22},{14,20},{16,10}... | collective-permute-start | bytes 393224 | tf_op jit(solution)/shard_map/ppermute | solution.py:322
  30.8 0.0 collective-permute-done.5.refs_6_
  30.9 5.7 %collective-permute-start.11 = (bf16[512,128]{1,0:T(8,128)(2,1)S(1)}, bf16[512,128]{1,0:T(8,128)(2,1)S(1)}, u32[]{:S(2)}, u32[]{:S(2)}) collective-permute-start(bf16[512,128]{1,0:T(8,128)(2,1)S(1)} %get-tuple-element.66.refs_14_), channel_id=1, source_target_pairs={{0,10},{2,8},{4,14},{6,12},{8,2},{10,0},{12,6},{14,4},{16,26},{18,... | collective-permute-start | bytes 393224 | tf_op jit(solution)/shard_map/ppermute | solution.py:322
  36.6 0.3 collective-permute-done.6.refs_7_
  36.9 0.0 collective-permute-start.12
  36.9 0.0 collective-permute-done.7.refs_8_
  36.9 4.1 %collective-permute-start.13 = (bf16[512,128]{1,0:T(8,128)(2,1)S(1)}, bf16[512,128]{1,0:T(8,128)(2,1)S(1)}, u32[]{:S(2)}, u32[]{:S(2)}) collective-permute-start(bf16[512,128]{1,0:T(8,128)(2,1)S(1)} %get-tuple-element.68.refs_16_), channel_id=1, source_target_pairs={{0,6},{2,4},{4,2},{6,0},{8,14},{10,12},{12,10},{14,8},{16,22},{18,... | collective-permute-start | bytes 393224 | tf_op jit(solution)/shard_map/ppermute | solution.py:322
  41.0 0.0 collective-permute-done.8.refs_9_
  41.0 3.2 %collective-permute-start.14 = (bf16[512,128]{1,0:T(8,128)(2,1)S(1)}, bf16[512,128]{1,0:T(8,128)(2,1)S(1)}, u32[]{:S(2)}, u32[]{:S(2)}) collective-permute-start(bf16[512,128]{1,0:T(8,128)(2,1)S(1)} %get-tuple-element.69.refs_17_), channel_id=1, source_target_pairs={{0,20},{2,22},{4,16},{6,18},{8,28},{10,30},{12,24},{14,26},{16,4},... | collective-permute-start | bytes 393224 | tf_op jit(solution)/shard_map/ppermute | solution.py:322
  44.2 0.0 collective-permute-done.9.refs_10_
  44.2 0.4 collective-permute-start.15
  44.6 2.3 %early.1 = (bf16[16,256,128]{2,1,0:T(8,128)(2,1)}, bf16[16,256,128]{2,1,0:T(8,128)(2,1)}, f32[16,8,128]{2,1,0:T(8,128)S(1)}, bf16[16,8,128]{2,1,0:T(8,128)(2,1)S...) custom-call(bf16[512,128]{1,0:T(8,128)(2,1)S(1)} %get-tuple-element.57.refs_19_.refs_0_, ...), custom_call_target="tpu_custom_call" | custom-call | flops 11534336 | bytes 2883584 | tf_op jit(solution)/shard_map/early/pallas_call | solution.py:351
  46.9 0.0 collective-permute-done.11.refs_0_
  46.9 0.1 collective-permute-start.10
  47.0 7.9 %collective-permute-done.12.refs_1_ = bf16[512,128]{1,0:T(8,128)(2,1)S(1)} collective-permute-done((bf16[512,128]{1,0:T(8,128)(2,1)S(1)}, bf16[512,128]{1,0:T(8,128)(2,1)S(1)}, u32[]{:S(2)}, u32[]{:S(2)}) %collective-permute-start.12) | collective-permute-done | bytes 131104 | tf_op jit(solution)/shard_map/ppermute | solution.py:322
  54.9 0.0 collective-permute-done.13.refs_2_
  54.9 0.4 collective-permute-done.14.refs_3_
  55.3 0.0 collective-permute-done.15.refs_4_
  55.3 2.0 %late.1 = (bf16[16,4096]{1,0:T(8,128)(2,1)S(1)}, bf16[16,256,128]{2,1,0:T(8,128)(2,1)}, bf16[16,256,128]{2,1,0:T(8,128)(2,1)}) custom-call(bf16[512,128]{1,0:T(8,128)(2,1)S(1)} %collective-permute-done.11.refs_0_, bf16[512,128]{1,0:T(8,128)(2,1)S(1)} %collective-permute-done.12.refs_1_, ...), custom_call_target="tpu_custom_call", output_to_operand_aliasing={{1}: (10, {}), {2}: (11, {})} | custom-call | flops 150994944 | bytes 10485760 | tf_op jit(solution)/shard_map/late/pallas_call | solution.py:377
  57.3 0.1 collective-permute-start.16
  57.4 0.0 collective-permute-done.10
  57.4 0.7 %add_convert_fusion.1 = bf16[16,4096]{1,0:T(8,128)(2,1)} fusion(bf16[16,4096]{1,0:T(8,128)(2,1)S(1)} %collective-permute-done.10, bf16[16,4096]{1,0:T(8,128)(2,1)S(1)} %get-tuple-element.65), kind=kLoop, calls=%fused_computation.1 | loop fusion | flops 262144 | bytes 393216 | tf_op jit(solution)/shard_map/convert_element_type | solution.py:209
  58.1 0.6 %collective-permute-done.16 = bf16[16,4096]{1,0:T(8,128)(2,1)S(1)} collective-permute-done((bf16[16,4096]{1,0:T(8,128)(2,1)S(1)}, bf16[16,4096]{1,0:T(8,128)(2,1)S(1)}, u32[]{:S(2)}, u32[]{:S(2)}) %collective-permute-start.16) | collective-permute-done | bytes 131104 | tf_op jit(solution)/shard_map/ppermute | solution.py:208
  58.7 0.7 %add_convert_fusion = bf16[16,4096]{1,0:T(8,128)(2,1)} fusion(bf16[16,4096]{1,0:T(8,128)(2,1)S(1)} %collective-permute-done.16, bf16[16,4096]{1,0:T(8,128)(2,1)S(1)} %get-tuple-element.77), kind=kLoop, calls=%fused_computation | loop fusion | flops 262144 | bytes 393216 | tf_op jit(solution)/shard_map/convert_element_type | solution.py:209
Async XLA Ops:
  2.3 16.9 %collective-permute-start = (bf16[512,128]{1,0:T(8,128)(2,1)S(1)}, bf16[512,128]{1,0:T(8,128)(2,1)S(1)}, u32[]{:S(2)}, u32[]{:S(2)}) collective-permute-start(bf16[512,128]{1,0:T(8,128)(2,1)S(1)} %get-tuple-element.42.refs_4_), channel_id=1, source_target_pairs={{0,16},{2,18},{4,20},{6,22},{8,24},{10,26},{12,28},{14,30},{16,0},... | collective-permute-start | bytes 393224 | tf_op jit(solution)/shard_map/ppermute | solution.py:322
  6.5 17.4 %collective-permute-start.1 = (bf16[512,128]{1,0:T(8,128)(2,1)S(1)}, bf16[512,128]{1,0:T(8,128)(2,1)S(1)}, u32[]{:S(2)}, u32[]{:S(2)}) collective-permute-start(bf16[512,128]{1,0:T(8,128)(2,1)S(1)} %get-tuple-element.43.refs_5_), channel_id=1, source_target_pairs={{0,24},{2,26},{4,28},{6,30},{8,16},{10,18},{12,20},{14,22},{16,8},... | collective-permute-start | bytes 393224 | tf_op jit(solution)/shard_map/ppermute | solution.py:322
  7.8 17.0 %collective-permute-start.2 = (bf16[512,128]{1,0:T(8,128)(2,1)S(1)}, bf16[512,128]{1,0:T(8,128)(2,1)S(1)}, u32[]{:S(2)}, u32[]{:S(2)}) collective-permute-start(bf16[512,128]{1,0:T(8,128)(2,1)S(1)} %get-tuple-element.44.refs_6_), channel_id=1, source_target_pairs={{0,2},{2,0},{4,6},{6,4},{8,10},{10,8},{12,14},{14,12},{16,18},{18,... | collective-permute-start | bytes 393224 | tf_op jit(solution)/shard_map/ppermute | solution.py:322
  9.3 19.6 %collective-permute-start.3 = (bf16[512,128]{1,0:T(8,128)(2,1)S(1)}, bf16[512,128]{1,0:T(8,128)(2,1)S(1)}, u32[]{:S(2)}, u32[]{:S(2)}) collective-permute-start(bf16[512,128]{1,0:T(8,128)(2,1)S(1)} %get-tuple-element.45.refs_7_), channel_id=1, source_target_pairs={{0,18},{2,16},{4,22},{6,20},{8,26},{10,24},{12,30},{14,28},{16,2},... | collective-permute-start | bytes 393224 | tf_op jit(solution)/shard_map/ppermute | solution.py:322
  11.0 18.0 %collective-permute-start.4 = (bf16[512,128]{1,0:T(8,128)(2,1)S(1)}, bf16[512,128]{1,0:T(8,128)(2,1)S(1)}, u32[]{:S(2)}, u32[]{:S(2)}) collective-permute-start(bf16[512,128]{1,0:T(8,128)(2,1)S(1)} %get-tuple-element.46.refs_8_), channel_id=1, source_target_pairs={{0,8},{2,10},{4,12},{6,14},{8,0},{10,2},{12,4},{14,6},{16,24},{18,... | collective-permute-start | bytes 393224 | tf_op jit(solution)/shard_map/ppermute | solution.py:322
  19.2 11.6 %collective-permute-start.5 = (bf16[512,128]{1,0:T(8,128)(2,1)S(1)}, bf16[512,128]{1,0:T(8,128)(2,1)S(1)}, u32[]{:S(2)}, u32[]{:S(2)}) collective-permute-start(bf16[512,128]{1,0:T(8,128)(2,1)S(1)} %get-tuple-element.59.refs_9_), channel_id=1, source_target_pairs={{0,30},{2,28},{4,26},{6,24},{8,22},{10,20},{12,18},{14,16},{16,14}... | collective-permute-start | bytes 393224 | tf_op jit(solution)/shard_map/ppermute | solution.py:322
  23.9 13.0 %collective-permute-start.6 = (bf16[512,128]{1,0:T(8,128)(2,1)S(1)}, bf16[512,128]{1,0:T(8,128)(2,1)S(1)}, u32[]{:S(2)}, u32[]{:S(2)}) collective-permute-start(bf16[512,128]{1,0:T(8,128)(2,1)S(1)} %get-tuple-element.60.refs_10_), channel_id=1, source_target_pairs={{0,14},{2,12},{4,10},{6,8},{8,6},{10,4},{12,2},{14,0},{16,30},{18,... | collective-permute-start | bytes 393224 | tf_op jit(solution)/shard_map/ppermute | solution.py:322
  24.8 12.1 %collective-permute-start.7 = (bf16[512,128]{1,0:T(8,128)(2,1)S(1)}, bf16[512,128]{1,0:T(8,128)(2,1)S(1)}, u32[]{:S(2)}, u32[]{:S(2)}) collective-permute-start(bf16[512,128]{1,0:T(8,128)(2,1)S(1)} %get-tuple-element.61.refs_11_), channel_id=1, source_target_pairs={{0,28},{2,30},{4,24},{6,26},{8,20},{10,22},{12,16},{14,18},{16,12}... | collective-permute-start | bytes 393224 | tf_op jit(solution)/shard_map/ppermute | solution.py:322
  28.9 12.1 %collective-permute-start.8 = (bf16[512,128]{1,0:T(8,128)(2,1)S(1)}, bf16[512,128]{1,0:T(8,128)(2,1)S(1)}, u32[]{:S(2)}, u32[]{:S(2)}) collective-permute-start(bf16[512,128]{1,0:T(8,128)(2,1)S(1)} %get-tuple-element.62.refs_12_), channel_id=1, source_target_pairs={{0,12},{2,14},{4,8},{6,10},{8,4},{10,6},{12,0},{14,2},{16,28},{18,... | collective-permute-start | bytes 393224 | tf_op jit(solution)/shard_map/ppermute | solution.py:322
  28.9 15.3 %collective-permute-start.9 = (bf16[512,128]{1,0:T(8,128)(2,1)S(1)}, bf16[512,128]{1,0:T(8,128)(2,1)S(1)}, u32[]{:S(2)}, u32[]{:S(2)}) collective-permute-start(bf16[512,128]{1,0:T(8,128)(2,1)S(1)} %get-tuple-element.63.refs_13_), channel_id=1, source_target_pairs={{0,26},{2,24},{4,30},{6,28},{8,18},{10,16},{12,22},{14,20},{16,10}... | collective-permute-start | bytes 393224 | tf_op jit(solution)/shard_map/ppermute | solution.py:322
  30.9 16.0 %collective-permute-start.11 = (bf16[512,128]{1,0:T(8,128)(2,1)S(1)}, bf16[512,128]{1,0:T(8,128)(2,1)S(1)}, u32[]{:S(2)}, u32[]{:S(2)}) collective-permute-start(bf16[512,128]{1,0:T(8,128)(2,1)S(1)} %get-tuple-element.66.refs_14_), channel_id=1, source_target_pairs={{0,10},{2,8},{4,14},{6,12},{8,2},{10,0},{12,6},{14,4},{16,26},{18,... | collective-permute-start | bytes 393224 | tf_op jit(solution)/shard_map/ppermute | solution.py:322
  36.9 18.0 %collective-permute-start.12 = (bf16[512,128]{1,0:T(8,128)(2,1)S(1)}, bf16[512,128]{1,0:T(8,128)(2,1)S(1)}, u32[]{:S(2)}, u32[]{:S(2)}) collective-permute-start(bf16[512,128]{1,0:T(8,128)(2,1)S(1)} %get-tuple-element.67.refs_15_), channel_id=1, source_target_pairs={{0,22},{2,20},{4,18},{6,16},{8,30},{10,28},{12,26},{14,24},{16,6},... | collective-permute-start | bytes 393224 | tf_op jit(solution)/shard_map/ppermute | solution.py:322
  36.9 18.0 %collective-permute-start.13 = (bf16[512,128]{1,0:T(8,128)(2,1)S(1)}, bf16[512,128]{1,0:T(8,128)(2,1)S(1)}, u32[]{:S(2)}, u32[]{:S(2)}) collective-permute-start(bf16[512,128]{1,0:T(8,128)(2,1)S(1)} %get-tuple-element.68.refs_16_), channel_id=1, source_target_pairs={{0,6},{2,4},{4,2},{6,0},{8,14},{10,12},{12,10},{14,8},{16,22},{18,... | collective-permute-start | bytes 393224 | tf_op jit(solution)/shard_map/ppermute | solution.py:322
  41.0 14.3 %collective-permute-start.14 = (bf16[512,128]{1,0:T(8,128)(2,1)S(1)}, bf16[512,128]{1,0:T(8,128)(2,1)S(1)}, u32[]{:S(2)}, u32[]{:S(2)}) collective-permute-start(bf16[512,128]{1,0:T(8,128)(2,1)S(1)} %get-tuple-element.69.refs_17_), channel_id=1, source_target_pairs={{0,20},{2,22},{4,16},{6,18},{8,28},{10,30},{12,24},{14,26},{16,4},... | collective-permute-start | bytes 393224 | tf_op jit(solution)/shard_map/ppermute | solution.py:322
  44.2 11.1 %collective-permute-start.15 = (bf16[512,128]{1,0:T(8,128)(2,1)S(1)}, bf16[512,128]{1,0:T(8,128)(2,1)S(1)}, u32[]{:S(2)}, u32[]{:S(2)}) collective-permute-start(bf16[512,128]{1,0:T(8,128)(2,1)S(1)} %get-tuple-element.70.refs_18_), channel_id=1, source_target_pairs={{0,4},{2,6},{4,0},{6,2},{8,12},{10,14},{12,8},{14,10},{16,20},{18,... | collective-permute-start | bytes 393224 | tf_op jit(solution)/shard_map/ppermute | solution.py:322
  46.9 10.5 %collective-permute-start.10 = (bf16[16,4096]{1,0:T(8,128)(2,1)S(1)}, bf16[16,4096]{1,0:T(8,128)(2,1)S(1)}, u32[]{:S(2)}, u32[]{:S(2)}) collective-permute-start(bf16[16,4096]{1,0:T(8,128)(2,1)S(1)} %get-tuple-element.65), channel_id=1, source_target_pairs={{0,1},{1,0},{2,3},{3,2},{4,5},{5,4},{6,7},{7,6},{8,9},{9,8},{10,11... | collective-permute-start | bytes 393224 | tf_op jit(solution)/shard_map/ppermute | solution.py:208
  57.3 1.4 %collective-permute-start.16 = (bf16[16,4096]{1,0:T(8,128)(2,1)S(1)}, bf16[16,4096]{1,0:T(8,128)(2,1)S(1)}, u32[]{:S(2)}, u32[]{:S(2)}) collective-permute-start(bf16[16,4096]{1,0:T(8,128)(2,1)S(1)} %get-tuple-element.77), channel_id=1, source_target_pairs={{0,1},{1,0},{2,3},{3,2},{4,5},{5,4},{6,7},{7,6},{8,9},{9,8},{10,11... | collective-permute-start | bytes 393224 | tf_op jit(solution)/shard_map/ppermute | solution.py:208

commit v12 on v10

--- a/solution.py
+++ b/solution.py
@@ -223,7 +223,7 @@
     crossing = [half] + list(range(half + 1, n))[::-1]
     staying = list(range(1, half))[::-1]
     order = []
-    for kind in "cncncncncncncnc":
+    for kind in "ccncncncncncncn":
         queue = crossing if kind == "c" else staying
         if queue:
             order.append(queue.pop(0))

time: 57.9 us -> 59.6 us (1.029)
  starting transfers between devices: 34.4 us -> 37.3 us
  waiting for transfers between devices: 8.67 us -> 7.46 us
    ppermute x15, starting transfers between devices: 34.3 us -> 37.1 us  [send(): return lax.ppermute(block, 'inst', [(d, d ^ steps[i]) for d in range(n)])]
    ppermute x15, waiting for transfers between devices: 8.03 us -> 6.82 us  [send(): return lax.ppermute(block, 'inst', [(d, d ^ steps[i]) for d in range(n)])]
  transfers between devices with their start and end apart: 17 -> 17, of which waited for: 7 -> 3; matrix products, arithmetic and copies ran while one was open for 1% -> 1% of each run, Pallas kernels for 19% -> 18%
where the time goes in v12:
time: 59.6 us; the launch traced here: 59.3 us
  starting transfers between devices  37.3 us (63%)
  Pallas kernels  12.5 us (21%)
  waiting for transfers between devices  7.46 us (13%)
  other arithmetic  1.38 us (2%)
  between operations  0.75 us (1%)
    ppermute x15, starting transfers between devices, send(): return lax.ppermute(block, 'inst', [(d, d ^ steps[i]) for d in range(n)])  37.1 us
    ppermute x15, waiting for transfers between devices, send(): return lax.ppermute(block, 'inst', [(d, d ^ steps[i]) for d in range(n)])  6.82 us
    pallas_call x1, Pallas kernels, shards(): pl.pallas_call(functools.partial(first_kernel, steps, span), out_shape=[j...  4.66 us
    pallas_call x2, Pallas kernels, pack(): pl.pallas_call(functools.partial(pack_kernel, n, chosen, pages), out_shap...  3.48 us
    pallas_call x1, Pallas kernels, shards(): pl.pallas_call(functools.partial(early_kernel, some, span), out_shape=[ca...  2.31 us
    pallas_call x1, Pallas kernels, shards(): pl.pallas_call(functools.partial(late_kernel, LATE, span), out_shape=[jax...  2.01 us
    convert_element_type x2, other arithmetic, total(): (partial.astype(jnp.float32) + other.astype(jnp.float32)).astype(jnp.bflo...  1.38 us
  transfers between devices with their start and end apart: 17, of which 3 were waited for; matrix products, arithmetic and copies ran while one was open for 1% of the time, Pallas kernels for 18%

profile of v12, /device:TPU:0, one launch (start us, length us, event | category | flops | bytes accessed | tf_op | source)
XLA Modules:
  0.0 59.3 jit_solution(13961677418203261838)
XLA Ops:
  0.6 1.7 %pack.2 = (bf16[512,128]{1,0:T(8,128)(2,1)S(1)}, bf16[512,128]{1,0:T(8,128)(2,1)S(1)}, bf16[512,128]{1,0:T(8,128)(2,1)S(1)}, bf16[512,128]{1,0:T(8,128)(2,1)S(1)}, bf16[512,128]{1,0:T(8,128)(2,1)S(1)}) custom-call(s32[4,16]{1,0:T(4,128)} %bitcast.23, s32[16]{0:T(128)} %refs_0_.1, s32[16]{0:T(128)} %refs_1_.5, s32[16]{0:T(128)} %refs_3_.4, ...), custom_call_target="tpu_custom_call" | custom-call | bytes 1310720 | tf_op jit(solution)/shard_map/pack/pallas_call | solution.py:280
  2.3 4.1 %collective-permute-start = (bf16[512,128]{1,0:T(8,128)(2,1)S(1)}, bf16[512,128]{1,0:T(8,128)(2,1)S(1)}, u32[]{:S(2)}, u32[]{:S(2)}) collective-permute-start(bf16[512,128]{1,0:T(8,128)(2,1)S(1)} %get-tuple-element.42.refs_4_), channel_id=1, source_target_pairs={{0,16},{2,18},{4,20},{6,22},{8,24},{10,26},{12,28},{14,30},{16,0},... | collective-permute-start | bytes 393224 | tf_op jit(solution)/shard_map/ppermute | solution.py:320
  6.5 3.2 %collective-permute-start.1 = (bf16[512,128]{1,0:T(8,128)(2,1)S(1)}, bf16[512,128]{1,0:T(8,128)(2,1)S(1)}, u32[]{:S(2)}, u32[]{:S(2)}) collective-permute-start(bf16[512,128]{1,0:T(8,128)(2,1)S(1)} %get-tuple-element.43.refs_5_), channel_id=1, source_target_pairs={{0,30},{2,28},{4,26},{6,24},{8,22},{10,20},{12,18},{14,16},{16,14}... | collective-permute-start | bytes 393224 | tf_op jit(solution)/shard_map/ppermute | solution.py:320
  9.7 0.2 collective-permute-start.2
  9.9 3.8 %collective-permute-start.3 = (bf16[512,128]{1,0:T(8,128)(2,1)S(1)}, bf16[512,128]{1,0:T(8,128)(2,1)S(1)}, u32[]{:S(2)}, u32[]{:S(2)}) collective-permute-start(bf16[512,128]{1,0:T(8,128)(2,1)S(1)} %get-tuple-element.45.refs_7_), channel_id=1, source_target_pairs={{0,28},{2,30},{4,24},{6,26},{8,20},{10,22},{12,16},{14,18},{16,12}... | collective-permute-start | bytes 393224 | tf_op jit(solution)/shard_map/ppermute | solution.py:320
  13.7 0.4 collective-permute-start.4
  14.1 1.8 %pack.3 = (bf16[512,128]{1,0:T(8,128)(2,1)S(1)}, bf16[512,128]{1,0:T(8,128)(2,1)S(1)}, bf16[512,128]{1,0:T(8,128)(2,1)S(1)}, bf16[512,128]{1,0:T(8,128)(2,1)S(1)...) custom-call(s32[4,16]{1,0:T(4,128)} %bitcast.24, ...), custom_call_target="tpu_custom_call" | custom-call | bytes 2883584 | tf_op jit(solution)/shard_map/pack/pallas_call | solution.py:280
  15.9 4.7 %first.1 = (bf16[16,4096]{1,0:T(8,128)(2,1)S(1)}, bf16[1024,4096]{1,0:T(8,128)(2,1)S(1)}) custom-call(s32[16]{0:T(128)} %refs_0_.1, s32[16]{0:T(128)} %refs_1_.5, bf16[16,8,128]{2,1,0:T(8,128)(2,1)} %refs_2_.5, bf16[1024,4096]{1,0:T(8,128)(2,1)} %refs_3_.5, bf16[512,128]{1,0:T(8,128)(2,1)S(1)} %get-tuple-element.42.refs_4_, ...), custom_call_target="tpu_custom_call" | custom-call | flops 150994944 | bytes 10485760 | tf_op jit(solution)/shard_map/first/pallas_call | solution.py:323
  20.5 0.0 collective-permute-done.refs_1_
  20.6 2.3 %collective-permute-start.5 = (bf16[512,128]{1,0:T(8,128)(2,1)S(1)}, bf16[512,128]{1,0:T(8,128)(2,1)S(1)}, u32[]{:S(2)}, u32[]{:S(2)}) collective-permute-start(bf16[512,128]{1,0:T(8,128)(2,1)S(1)} %get-tuple-element.59.refs_9_), channel_id=1, source_target_pairs={{0,26},{2,24},{4,30},{6,28},{8,18},{10,16},{12,22},{14,20},{16,10}... | collective-permute-start | bytes 393224 | tf_op jit(solution)/shard_map/ppermute | solution.py:320
  22.9 0.0 collective-permute-done.1.refs_2_
  22.9 3.2 %collective-permute-start.6 = (bf16[512,128]{1,0:T(8,128)(2,1)S(1)}, bf16[512,128]{1,0:T(8,128)(2,1)S(1)}, u32[]{:S(2)}, u32[]{:S(2)}) collective-permute-start(bf16[512,128]{1,0:T(8,128)(2,1)S(1)} %get-tuple-element.60.refs_10_), channel_id=1, source_target_pairs={{0,10},{2,8},{4,14},{6,12},{8,2},{10,0},{12,6},{14,4},{16,26},{18,... | collective-permute-start | bytes 393224 | tf_op jit(solution)/shard_map/ppermute | solution.py:320
  26.1 0.0 collective-permute-done.2.refs_3_
  26.1 3.0 %collective-permute-start.7 = (bf16[512,128]{1,0:T(8,128)(2,1)S(1)}, bf16[512,128]{1,0:T(8,128)(2,1)S(1)}, u32[]{:S(2)}, u32[]{:S(2)}) collective-permute-start(bf16[512,128]{1,0:T(8,128)(2,1)S(1)} %get-tuple-element.61.refs_11_), channel_id=1, source_target_pairs={{0,24},{2,26},{4,28},{6,30},{8,16},{10,18},{12,20},{14,22},{16,8},... | collective-permute-start | bytes 393224 | tf_op jit(solution)/shard_map/ppermute | solution.py:320
  29.1 0.0 collective-permute-done.3.refs_4_
  29.1 1.1 %collective-permute-start.8 = (bf16[512,128]{1,0:T(8,128)(2,1)S(1)}, bf16[512,128]{1,0:T(8,128)(2,1)S(1)}, u32[]{:S(2)}, u32[]{:S(2)}) collective-permute-start(bf16[512,128]{1,0:T(8,128)(2,1)S(1)} %get-tuple-element.62.refs_12_), channel_id=1, source_target_pairs={{0,8},{2,10},{4,12},{6,14},{8,0},{10,2},{12,4},{14,6},{16,24},{18,... | collective-permute-start | bytes 393224 | tf_op jit(solution)/shard_map/ppermute | solution.py:320
  30.3 0.0 collective-permute-done.4.refs_5_
  30.3 1.3 %collective-permute-start.9 = (bf16[512,128]{1,0:T(8,128)(2,1)S(1)}, bf16[512,128]{1,0:T(8,128)(2,1)S(1)}, u32[]{:S(2)}, u32[]{:S(2)}) collective-permute-start(bf16[512,128]{1,0:T(8,128)(2,1)S(1)} %get-tuple-element.63.refs_13_), channel_id=1, source_target_pairs={{0,22},{2,20},{4,18},{6,16},{8,30},{10,28},{12,26},{14,24},{16,6},... | collective-permute-start | bytes 393224 | tf_op jit(solution)/shard_map/ppermute | solution.py:320
  31.6 0.0 collective-permute-done.5.refs_6_
  31.6 1.5 %collective-permute-start.11 = (bf16[512,128]{1,0:T(8,128)(2,1)S(1)}, bf16[512,128]{1,0:T(8,128)(2,1)S(1)}, u32[]{:S(2)}, u32[]{:S(2)}) collective-permute-start(bf16[512,128]{1,0:T(8,128)(2,1)S(1)} %get-tuple-element.66.refs_14_), channel_id=1, source_target_pairs={{0,6},{2,4},{4,2},{6,0},{8,14},{10,12},{12,10},{14,8},{16,22},{18,... | collective-permute-start | bytes 393224 | tf_op jit(solution)/shard_map/ppermute | solution.py:320
  33.2 0.0 collective-permute-done.6.refs_7_
  33.2 5.1 %collective-permute-start.12 = (bf16[512,128]{1,0:T(8,128)(2,1)S(1)}, bf16[512,128]{1,0:T(8,128)(2,1)S(1)}, u32[]{:S(2)}, u32[]{:S(2)}) collective-permute-start(bf16[512,128]{1,0:T(8,128)(2,1)S(1)} %get-tuple-element.67.refs_15_), channel_id=1, source_target_pairs={{0,20},{2,22},{4,16},{6,18},{8,28},{10,30},{12,24},{14,26},{16,4},... | collective-permute-start | bytes 393224 | tf_op jit(solution)/shard_map/ppermute | solution.py:320
  38.3 0.0 collective-permute-done.7.refs_8_
  38.3 1.6 %collective-permute-start.13 = (bf16[512,128]{1,0:T(8,128)(2,1)S(1)}, bf16[512,128]{1,0:T(8,128)(2,1)S(1)}, u32[]{:S(2)}, u32[]{:S(2)}) collective-permute-start(bf16[512,128]{1,0:T(8,128)(2,1)S(1)} %get-tuple-element.68.refs_16_), channel_id=1, source_target_pairs={{0,4},{2,6},{4,0},{6,2},{8,12},{10,14},{12,8},{14,10},{16,20},{18,... | collective-permute-start | bytes 393224 | tf_op jit(solution)/shard_map/ppermute | solution.py:320
  39.9 0.0 collective-permute-done.8.refs_9_
  39.9 5.3 %collective-permute-start.14 = (bf16[512,128]{1,0:T(8,128)(2,1)S(1)}, bf16[512,128]{1,0:T(8,128)(2,1)S(1)}, u32[]{:S(2)}, u32[]{:S(2)}) collective-permute-start(bf16[512,128]{1,0:T(8,128)(2,1)S(1)} %get-tuple-element.69.refs_17_), channel_id=1, source_target_pairs={{0,18},{2,16},{4,22},{6,20},{8,26},{10,24},{12,30},{14,28},{16,2},... | collective-permute-start | bytes 393224 | tf_op jit(solution)/shard_map/ppermute | solution.py:320
  45.1 5.1 %collective-permute-done.9.refs_10_ = bf16[512,128]{1,0:T(8,128)(2,1)S(1)} collective-permute-done((bf16[512,128]{1,0:T(8,128)(2,1)S(1)}, bf16[512,128]{1,0:T(8,128)(2,1)S(1)}, u32[]{:S(2)}, u32[]{:S(2)}) %collective-permute-start.9) | collective-permute-done | bytes 131104 | tf_op jit(solution)/shard_map/ppermute | solution.py:320
  50.2 0.8 %collective-permute-start.15 = (bf16[512,128]{1,0:T(8,128)(2,1)S(1)}, bf16[512,128]{1,0:T(8,128)(2,1)S(1)}, u32[]{:S(2)}, u32[]{:S(2)}) collective-permute-start(bf16[512,128]{1,0:T(8,128)(2,1)S(1)} %get-tuple-element.70.refs_18_), channel_id=1, source_target_pairs={{0,2},{2,0},{4,6},{6,4},{8,10},{10,8},{12,14},{14,12},{16,18},{18,... | collective-permute-start | bytes 393224 | tf_op jit(solution)/shard_map/ppermute | solution.py:320
  51.1 2.3 %early.1 = (bf16[16,256,128]{2,1,0:T(8,128)(2,1)}, bf16[16,256,128]{2,1,0:T(8,128)(2,1)}, f32[16,8,128]{2,1,0:T(8,128)S(1)}, bf16[16,8,128]{2,1,0:T(8,128)(2,1)S...) custom-call(bf16[512,128]{1,0:T(8,128)(2,1)S(1)} %get-tuple-element.57.refs_19_.refs_0_, ...), custom_call_target="tpu_custom_call" | custom-call | flops 11534336 | bytes 2883584 | tf_op jit(solution)/shard_map/early/pallas_call | solution.py:349
  53.4 0.0 collective-permute-done.11.refs_0_
  53.4 0.1 collective-permute-start.10
  53.5 0.0 collective-permute-done.12.refs_1_
  53.5 0.0 collective-permute-done.13.refs_2_
  53.5 0.0 collective-permute-done.14.refs_3_
  53.5 1.7 %collective-permute-done.15.refs_4_ = bf16[512,128]{1,0:T(8,128)(2,1)S(1)} collective-permute-done((bf16[512,128]{1,0:T(8,128)(2,1)S(1)}, bf16[512,128]{1,0:T(8,128)(2,1)S(1)}, u32[]{:S(2)}, u32[]{:S(2)}) %collective-permute-start.15) | collective-permute-done | bytes 131104 | tf_op jit(solution)/shard_map/ppermute | solution.py:320
  55.2 2.0 %late.1 = (bf16[16,4096]{1,0:T(8,128)(2,1)S(1)}, bf16[16,256,128]{2,1,0:T(8,128)(2,1)}, bf16[16,256,128]{2,1,0:T(8,128)(2,1)}) custom-call(bf16[512,128]{1,0:T(8,128)(2,1)S(1)} %collective-permute-done.11.refs_0_, bf16[512,128]{1,0:T(8,128)(2,1)S(1)} %collective-permute-done.12.refs_1_, ...), custom_call_target="tpu_custom_call", output_to_operand_aliasing={{1}: (10, {}), {2}: (11, {})} | custom-call | flops 150994944 | bytes 10485760 | tf_op jit(solution)/shard_map/late/pallas_call | solution.py:375
  57.2 0.1 collective-permute-start.16
  57.3 0.0 collective-permute-done.10
  57.3 0.7 %add_convert_fusion.1 = bf16[16,4096]{1,0:T(8,128)(2,1)} fusion(bf16[16,4096]{1,0:T(8,128)(2,1)S(1)} %collective-permute-done.10, bf16[16,4096]{1,0:T(8,128)(2,1)S(1)} %get-tuple-element.65), kind=kLoop, calls=%fused_computation.1 | loop fusion | flops 262144 | bytes 393216 | tf_op jit(solution)/shard_map/convert_element_type | solution.py:209
  58.0 0.6 %collective-permute-done.16 = bf16[16,4096]{1,0:T(8,128)(2,1)S(1)} collective-permute-done((bf16[16,4096]{1,0:T(8,128)(2,1)S(1)}, bf16[16,4096]{1,0:T(8,128)(2,1)S(1)}, u32[]{:S(2)}, u32[]{:S(2)}) %collective-permute-start.16) | collective-permute-done | bytes 131104 | tf_op jit(solution)/shard_map/ppermute | solution.py:208
  58.6 0.7 %add_convert_fusion = bf16[16,4096]{1,0:T(8,128)(2,1)} fusion(bf16[16,4096]{1,0:T(8,128)(2,1)S(1)} %collective-permute-done.16, bf16[16,4096]{1,0:T(8,128)(2,1)S(1)} %get-tuple-element.77), kind=kLoop, calls=%fused_computation | loop fusion | flops 262144 | bytes 393216 | tf_op jit(solution)/shard_map/convert_element_type | solution.py:209
Async XLA Ops:
  2.3 18.2 %collective-permute-start = (bf16[512,128]{1,0:T(8,128)(2,1)S(1)}, bf16[512,128]{1,0:T(8,128)(2,1)S(1)}, u32[]{:S(2)}, u32[]{:S(2)}) collective-permute-start(bf16[512,128]{1,0:T(8,128)(2,1)S(1)} %get-tuple-element.42.refs_4_), channel_id=1, source_target_pairs={{0,16},{2,18},{4,20},{6,22},{8,24},{10,26},{12,28},{14,30},{16,0},... | collective-permute-start | bytes 393224 | tf_op jit(solution)/shard_map/ppermute | solution.py:320
  6.5 16.5 %collective-permute-start.1 = (bf16[512,128]{1,0:T(8,128)(2,1)S(1)}, bf16[512,128]{1,0:T(8,128)(2,1)S(1)}, u32[]{:S(2)}, u32[]{:S(2)}) collective-permute-start(bf16[512,128]{1,0:T(8,128)(2,1)S(1)} %get-tuple-element.43.refs_5_), channel_id=1, source_target_pairs={{0,30},{2,28},{4,26},{6,24},{8,22},{10,20},{12,18},{14,16},{16,14}... | collective-permute-start | bytes 393224 | tf_op jit(solution)/shard_map/ppermute | solution.py:320
  9.7 16.5 %collective-permute-start.2 = (bf16[512,128]{1,0:T(8,128)(2,1)S(1)}, bf16[512,128]{1,0:T(8,128)(2,1)S(1)}, u32[]{:S(2)}, u32[]{:S(2)}) collective-permute-start(bf16[512,128]{1,0:T(8,128)(2,1)S(1)} %get-tuple-element.44.refs_6_), channel_id=1, source_target_pairs={{0,14},{2,12},{4,10},{6,8},{8,6},{10,4},{12,2},{14,0},{16,30},{18,... | collective-permute-start | bytes 393224 | tf_op jit(solution)/shard_map/ppermute | solution.py:320
  9.9 19.2 %collective-permute-start.3 = (bf16[512,128]{1,0:T(8,128)(2,1)S(1)}, bf16[512,128]{1,0:T(8,128)(2,1)S(1)}, u32[]{:S(2)}, u32[]{:S(2)}) collective-permute-start(bf16[512,128]{1,0:T(8,128)(2,1)S(1)} %get-tuple-element.45.refs_7_), channel_id=1, source_target_pairs={{0,28},{2,30},{4,24},{6,26},{8,20},{10,22},{12,16},{14,18},{16,12}... | collective-permute-start | bytes 393224 | tf_op jit(solution)/shard_map/ppermute | solution.py:320
  13.7 16.6 %collective-permute-start.4 = (bf16[512,128]{1,0:T(8,128)(2,1)S(1)}, bf16[512,128]{1,0:T(8,128)(2,1)S(1)}, u32[]{:S(2)}, u32[]{:S(2)}) collective-permute-start(bf16[512,128]{1,0:T(8,128)(2,1)S(1)} %get-tuple-element.46.refs_8_), channel_id=1, source_target_pairs={{0,12},{2,14},{4,8},{6,10},{8,4},{10,6},{12,0},{14,2},{16,28},{18,... | collective-permute-start | bytes 393224 | tf_op jit(solution)/shard_map/ppermute | solution.py:320
  20.6 11.1 %collective-permute-start.5 = (bf16[512,128]{1,0:T(8,128)(2,1)S(1)}, bf16[512,128]{1,0:T(8,128)(2,1)S(1)}, u32[]{:S(2)}, u32[]{:S(2)}) collective-permute-start(bf16[512,128]{1,0:T(8,128)(2,1)S(1)} %get-tuple-element.59.refs_9_), channel_id=1, source_target_pairs={{0,26},{2,24},{4,30},{6,28},{8,18},{10,16},{12,22},{14,20},{16,10}... | collective-permute-start | bytes 393224 | tf_op jit(solution)/shard_map/ppermute | solution.py:320
  22.9 10.3 %collective-permute-start.6 = (bf16[512,128]{1,0:T(8,128)(2,1)S(1)}, bf16[512,128]{1,0:T(8,128)(2,1)S(1)}, u32[]{:S(2)}, u32[]{:S(2)}) collective-permute-start(bf16[512,128]{1,0:T(8,128)(2,1)S(1)} %get-tuple-element.60.refs_10_), channel_id=1, source_target_pairs={{0,10},{2,8},{4,14},{6,12},{8,2},{10,0},{12,6},{14,4},{16,26},{18,... | collective-permute-start | bytes 393224 | tf_op jit(solution)/shard_map/ppermute | solution.py:320
  26.1 12.1 %collective-permute-start.7 = (bf16[512,128]{1,0:T(8,128)(2,1)S(1)}, bf16[512,128]{1,0:T(8,128)(2,1)S(1)}, u32[]{:S(2)}, u32[]{:S(2)}) collective-permute-start(bf16[512,128]{1,0:T(8,128)(2,1)S(1)} %get-tuple-element.61.refs_11_), channel_id=1, source_target_pairs={{0,24},{2,26},{4,28},{6,30},{8,16},{10,18},{12,20},{14,22},{16,8},... | collective-permute-start | bytes 393224 | tf_op jit(solution)/shard_map/ppermute | solution.py:320
  29.1 10.7 %collective-permute-start.8 = (bf16[512,128]{1,0:T(8,128)(2,1)S(1)}, bf16[512,128]{1,0:T(8,128)(2,1)S(1)}, u32[]{:S(2)}, u32[]{:S(2)}) collective-permute-start(bf16[512,128]{1,0:T(8,128)(2,1)S(1)} %get-tuple-element.62.refs_12_), channel_id=1, source_target_pairs={{0,8},{2,10},{4,12},{6,14},{8,0},{10,2},{12,4},{14,6},{16,24},{18,... | collective-permute-start | bytes 393224 | tf_op jit(solution)/shard_map/ppermute | solution.py:320
  30.3 19.9 %collective-permute-start.9 = (bf16[512,128]{1,0:T(8,128)(2,1)S(1)}, bf16[512,128]{1,0:T(8,128)(2,1)S(1)}, u32[]{:S(2)}, u32[]{:S(2)}) collective-permute-start(bf16[512,128]{1,0:T(8,128)(2,1)S(1)} %get-tuple-element.63.refs_13_), channel_id=1, source_target_pairs={{0,22},{2,20},{4,18},{6,16},{8,30},{10,28},{12,26},{14,24},{16,6},... | collective-permute-start | bytes 393224 | tf_op jit(solution)/shard_map/ppermute | solution.py:320
  31.6 21.8 %collective-permute-start.11 = (bf16[512,128]{1,0:T(8,128)(2,1)S(1)}, bf16[512,128]{1,0:T(8,128)(2,1)S(1)}, u32[]{:S(2)}, u32[]{:S(2)}) collective-permute-start(bf16[512,128]{1,0:T(8,128)(2,1)S(1)} %get-tuple-element.66.refs_14_), channel_id=1, source_target_pairs={{0,6},{2,4},{4,2},{6,0},{8,14},{10,12},{12,10},{14,8},{16,22},{18,... | collective-permute-start | bytes 393224 | tf_op jit(solution)/shard_map/ppermute | solution.py:320
  33.2 20.3 %collective-permute-start.12 = (bf16[512,128]{1,0:T(8,128)(2,1)S(1)}, bf16[512,128]{1,0:T(8,128)(2,1)S(1)}, u32[]{:S(2)}, u32[]{:S(2)}) collective-permute-start(bf16[512,128]{1,0:T(8,128)(2,1)S(1)} %get-tuple-element.67.refs_15_), channel_id=1, source_target_pairs={{0,20},{2,22},{4,16},{6,18},{8,28},{10,30},{12,24},{14,26},{16,4},... | collective-permute-start | bytes 393224 | tf_op jit(solution)/shard_map/ppermute | solution.py:320
  38.3 15.2 %collective-permute-start.13 = (bf16[512,128]{1,0:T(8,128)(2,1)S(1)}, bf16[512,128]{1,0:T(8,128)(2,1)S(1)}, u32[]{:S(2)}, u32[]{:S(2)}) collective-permute-start(bf16[512,128]{1,0:T(8,128)(2,1)S(1)} %get-tuple-element.68.refs_16_), channel_id=1, source_target_pairs={{0,4},{2,6},{4,0},{6,2},{8,12},{10,14},{12,8},{14,10},{16,20},{18,... | collective-permute-start | bytes 393224 | tf_op jit(solution)/shard_map/ppermute | solution.py:320
  39.9 13.6 %collective-permute-start.14 = (bf16[512,128]{1,0:T(8,128)(2,1)S(1)}, bf16[512,128]{1,0:T(8,128)(2,1)S(1)}, u32[]{:S(2)}, u32[]{:S(2)}) collective-permute-start(bf16[512,128]{1,0:T(8,128)(2,1)S(1)} %get-tuple-element.69.refs_17_), channel_id=1, source_target_pairs={{0,18},{2,16},{4,22},{6,20},{8,26},{10,24},{12,30},{14,28},{16,2},... | collective-permute-start | bytes 393224 | tf_op jit(solution)/shard_map/ppermute | solution.py:320
  50.2 5.0 %collective-permute-start.15 = (bf16[512,128]{1,0:T(8,128)(2,1)S(1)}, bf16[512,128]{1,0:T(8,128)(2,1)S(1)}, u32[]{:S(2)}, u32[]{:S(2)}) collective-permute-start(bf16[512,128]{1,0:T(8,128)(2,1)S(1)} %get-tuple-element.70.refs_18_), channel_id=1, source_target_pairs={{0,2},{2,0},{4,6},{6,4},{8,10},{10,8},{12,14},{14,12},{16,18},{18,... | collective-permute-start | bytes 393224 | tf_op jit(solution)/shard_map/ppermute | solution.py:320
  53.4 3.9 %collective-permute-start.10 = (bf16[16,4096]{1,0:T(8,128)(2,1)S(1)}, bf16[16,4096]{1,0:T(8,128)(2,1)S(1)}, u32[]{:S(2)}, u32[]{:S(2)}) collective-permute-start(bf16[16,4096]{1,0:T(8,128)(2,1)S(1)} %get-tuple-element.65), channel_id=1, source_target_pairs={{0,1},{1,0},{2,3},{3,2},{4,5},{5,4},{6,7},{7,6},{8,9},{9,8},{10,11... | collective-permute-start | bytes 393224 | tf_op jit(solution)/shard_map/ppermute | solution.py:208
  57.2 1.4 %collective-permute-start.16 = (bf16[16,4096]{1,0:T(8,128)(2,1)S(1)}, bf16[16,4096]{1,0:T(8,128)(2,1)S(1)}, u32[]{:S(2)}, u32[]{:S(2)}) collective-permute-start(bf16[16,4096]{1,0:T(8,128)(2,1)S(1)} %get-tuple-element.77), channel_id=1, source_target_pairs={{0,1},{1,0},{2,3},{3,2},{4,5},{5,4},{6,7},{7,6},{8,9},{9,8},{10,11... | collective-permute-start | bytes 393224 | tf_op jit(solution)/shard_map/ppermute | solution.py:208

commit v13 on v12

--- a/solution.py
+++ b/solution.py
@@ -8,6 +8,7 @@
 from jax.sharding import PartitionSpec as P
 
 NEG = -1e30
+Z = 4
 TILE = 16
 SPLIT = 64
 CHUNKS = 8
@@ -72,8 +73,9 @@
 
 
 def sources(source, steps):
+    n = source.shape[0]
     me = lax.axis_index("inst")
-    return [source[me ^ s] for s in steps]
+    return [source[target(me, step, n)] for step in steps]
 
 
 def pack_kernel(n, steps, pages, *refs):
@@ -219,18 +221,16 @@
 
 
 def step_order(n):
-    half = n // 2
-    crossing = [half] + list(range(half + 1, n))[::-1]
-    staying = list(range(1, half))[::-1]
-    order = []
-    for kind in "ccncncncncncncn":
-        queue = crossing if kind == "c" else staying
-        if queue:
-            order.append(queue.pop(0))
-    while crossing or staying:
-        order += crossing[:1] + staying[:1]
-        del crossing[:1], staying[:1]
-    return order
+    part = n // Z
+    order = [(2, 0)]
+    for b in range(part - 1, 0, -1):
+        order += [(1, b), (2, b), (3, b), (0, b)]
+    return order + [(1, 0), (3, 0)]
+
+
+def target(at, step, n):
+    part = n // Z
+    return (at // part + step[0]) % Z * part + (at % part ^ step[1])
 
 
 def shards(
@@ -255,7 +255,7 @@
     heads = query_one.shape[1]
     depth, columns = out_weight.shape
     span = pages * size
-    assert kv_heads == 1 and slots == n and n >= 16 and span <= 256
+    assert kv_heads == 1 and slots == n and n % 16 == 0 and span <= 256
     key_pages = key_pages.reshape(pool, size, width)
     value_pages = value_pages.reshape(pool, size, width)
     key_one = key_one.reshape(slots, width)
@@ -310,14 +310,14 @@
             hbm(value_pages),
         )
 
-    steps = step_order(n) + [0]
+    steps = step_order(n) + [(0, 0)]
     packed = pack(steps[:AHEAD]) + pack(steps[AHEAD:])
 
     flops = 4 * slots * heads * span * width + 2 * slots * depth * columns
     moved = 2 * depth * columns + 4 * slots * span * width
     def send(i, *after):
         block = lax.optimization_barrier((packed[i], *after))[0] if after else packed[i]
-        return lax.ppermute(block, "inst", [(d, d ^ steps[i]) for d in range(n)])
+        return lax.ppermute(block, "inst", [(d, target(d, steps[i], n)) for d in range(n)])
 
     arrived = [send(i) for i in range(AHEAD)]
     partial_one, weight = pl.pallas_call(

time: 59.6 us -> 58.1 us (0.975)
  the two profiles are of different devices: /device:TPU:0 before, /device:TPU:21 now
where the time goes in v13:
time: 58.1 us; the launch traced here: 57.8 us
  starting transfers between devices  26.1 us (45%)
  waiting for transfers between devices  17.2 us (30%)
  Pallas kernels  12.5 us (22%)
  other arithmetic  1.38 us (2%)
  between operations  0.7 us (1%)
    ppermute x15, starting transfers between devices, send(): lax.ppermute(block, 'inst', [(d, target(d, steps[i], n)) for d in range(n)])  24.8 us
    ppermute x15, waiting for transfers between devices, send(): lax.ppermute(block, 'inst', [(d, target(d, steps[i], n)) for d in range(n)])  16.9 us
    pallas_call x1, Pallas kernels, shards(): pl.pallas_call(functools.partial(first_kernel, steps, span), out_shape=[j...  4.67 us
    pallas_call x2, Pallas kernels, pack(): pl.pallas_call(functools.partial(pack_kernel, n, chosen, pages), out_shap...  3.48 us
    pallas_call x1, Pallas kernels, shards(): pl.pallas_call(functools.partial(early_kernel, some, span), out_shape=[ca...  2.31 us
    pallas_call x1, Pallas kernels, shards(): pl.pallas_call(functools.partial(late_kernel, LATE, span), out_shape=[jax...  2.02 us
    convert_element_type x2, other arithmetic, total(): (partial.astype(jnp.float32) + other.astype(jnp.float32)).astype(jnp.bflo...  1.38 us
    ppermute x2, starting transfers between devices, total(): other = lax.ppermute(partial, 'tp', [(0, 1), (1, 0)])  1.26 us
  transfers between devices with their start and end apart: 17, of which 6 were waited for; matrix products, arithmetic and copies ran while one was open for 1% of the time, Pallas kernels for 19%

profile of v13, /device:TPU:21, one launch (start us, length us, event | category | flops | bytes accessed | tf_op | source)
XLA Modules:
  0.0 57.8 jit_solution(6143923441054431767)
XLA Ops:
  0.6 1.7 %pack.2 = (bf16[512,128]{1,0:T(8,128)(2,1)S(1)}, bf16[512,128]{1,0:T(8,128)(2,1)S(1)}, bf16[512,128]{1,0:T(8,128)(2,1)S(1)}, bf16[512,128]{1,0:T(8,128)(2,1)S(1)}, bf16[512,128]{1,0:T(8,128)(2,1)S(1)}) custom-call(s32[4,16]{1,0:T(4,128)} %bitcast.23, s32[16]{0:T(128)} %refs_0_.1, s32[16]{0:T(128)} %refs_1_.5, s32[16]{0:T(128)} %refs_3_.4, ...), custom_call_target="tpu_custom_call" | custom-call | bytes 1310720 | tf_op jit(solution)/shard_map/pack/pallas_call | solution.py:280
  2.3 0.1 collective-permute-start
  2.5 2.2 %collective-permute-start.1 = (bf16[512,128]{1,0:T(8,128)(2,1)S(1)}, bf16[512,128]{1,0:T(8,128)(2,1)S(1)}, u32[]{:S(2)}, u32[]{:S(2)}) collective-permute-start(bf16[512,128]{1,0:T(8,128)(2,1)S(1)} %get-tuple-element.43.refs_5_), channel_id=1, source_target_pairs={{0,14},{2,12},{4,10},{6,8},{8,22},{10,20},{12,18},{14,16},{16,30},... | collective-permute-start | bytes 393224 | tf_op jit(solution)/shard_map/ppermute | solution.py:320
  4.6 3.2 %collective-permute-start.2 = (bf16[512,128]{1,0:T(8,128)(2,1)S(1)}, bf16[512,128]{1,0:T(8,128)(2,1)S(1)}, u32[]{:S(2)}, u32[]{:S(2)}) collective-permute-start(bf16[512,128]{1,0:T(8,128)(2,1)S(1)} %get-tuple-element.44.refs_6_), channel_id=1, source_target_pairs={{0,22},{2,20},{4,18},{6,16},{8,30},{10,28},{12,26},{14,24},{16,6},... | collective-permute-start | bytes 393224 | tf_op jit(solution)/shard_map/ppermute | solution.py:320
  7.9 1.9 %collective-permute-start.3 = (bf16[512,128]{1,0:T(8,128)(2,1)S(1)}, bf16[512,128]{1,0:T(8,128)(2,1)S(1)}, u32[]{:S(2)}, u32[]{:S(2)}) collective-permute-start(bf16[512,128]{1,0:T(8,128)(2,1)S(1)} %get-tuple-element.45.refs_7_), channel_id=1, source_target_pairs={{0,30},{2,28},{4,26},{6,24},{8,6},{10,4},{12,2},{14,0},{16,14},{18... | collective-permute-start | bytes 393224 | tf_op jit(solution)/shard_map/ppermute | solution.py:320
  9.8 1.2 %collective-permute-start.4 = (bf16[512,128]{1,0:T(8,128)(2,1)S(1)}, bf16[512,128]{1,0:T(8,128)(2,1)S(1)}, u32[]{:S(2)}, u32[]{:S(2)}) collective-permute-start(bf16[512,128]{1,0:T(8,128)(2,1)S(1)} %get-tuple-element.46.refs_8_), channel_id=1, source_target_pairs={{0,6},{2,4},{4,2},{6,0},{8,14},{10,12},{12,10},{14,8},{16,22},{18,... | collective-permute-start | bytes 393224 | tf_op jit(solution)/shard_map/ppermute | solution.py:320
  11.0 1.8 %pack.3 = (bf16[512,128]{1,0:T(8,128)(2,1)S(1)}, bf16[512,128]{1,0:T(8,128)(2,1)S(1)}, bf16[512,128]{1,0:T(8,128)(2,1)S(1)}, bf16[512,128]{1,0:T(8,128)(2,1)S(1)...) custom-call(s32[4,16]{1,0:T(4,128)} %bitcast.24, ...), custom_call_target="tpu_custom_call" | custom-call | bytes 2883584 | tf_op jit(solution)/shard_map/pack/pallas_call | solution.py:280
  12.8 4.7 %first.1 = (bf16[16,4096]{1,0:T(8,128)(2,1)S(1)}, bf16[1024,4096]{1,0:T(8,128)(2,1)S(1)}) custom-call(s32[16]{0:T(128)} %refs_0_.1, s32[16]{0:T(128)} %refs_1_.5, bf16[16,8,128]{2,1,0:T(8,128)(2,1)} %refs_2_.5, bf16[1024,4096]{1,0:T(8,128)(2,1)} %refs_3_.5, bf16[512,128]{1,0:T(8,128)(2,1)S(1)} %get-tuple-element.42.refs_4_, ...), custom_call_target="tpu_custom_call" | custom-call | flops 150994944 | bytes 10485760 | tf_op jit(solution)/shard_map/first/pallas_call | solution.py:323
  17.5 0.0 collective-permute-done.refs_1_
  17.5 0.4 collective-permute-start.5
  17.9 3.1 %collective-permute-done.1.refs_2_ = bf16[512,128]{1,0:T(8,128)(2,1)S(1)} collective-permute-done((bf16[512,128]{1,0:T(8,128)(2,1)S(1)}, bf16[512,128]{1,0:T(8,128)(2,1)S(1)}, u32[]{:S(2)}, u32[]{:S(2)}) %collective-permute-start.1) | collective-permute-done | bytes 131104 | tf_op jit(solution)/shard_map/ppermute | solution.py:320
  21.0 0.0 collective-permute-start.6
  21.0 0.0 collective-permute-done.2.refs_3_
  21.0 1.1 %collective-permute-start.7 = (bf16[512,128]{1,0:T(8,128)(2,1)S(1)}, bf16[512,128]{1,0:T(8,128)(2,1)S(1)}, u32[]{:S(2)}, u32[]{:S(2)}) collective-permute-start(bf16[512,128]{1,0:T(8,128)(2,1)S(1)} %get-tuple-element.61.refs_11_), channel_id=1, source_target_pairs={{0,28},{2,30},{4,24},{6,26},{8,4},{10,6},{12,0},{14,2},{16,12},{18... | collective-permute-start | bytes 393224 | tf_op jit(solution)/shard_map/ppermute | solution.py:320
  22.1 0.0 collective-permute-done.3.refs_4_
  22.1 1.4 %collective-permute-start.8 = (bf16[512,128]{1,0:T(8,128)(2,1)S(1)}, bf16[512,128]{1,0:T(8,128)(2,1)S(1)}, u32[]{:S(2)}, u32[]{:S(2)}) collective-permute-start(bf16[512,128]{1,0:T(8,128)(2,1)S(1)} %get-tuple-element.62.refs_12_), channel_id=1, source_target_pairs={{0,4},{2,6},{4,0},{6,2},{8,12},{10,14},{12,8},{14,10},{16,20},{18,... | collective-permute-start | bytes 393224 | tf_op jit(solution)/shard_map/ppermute | solution.py:320
  23.5 0.5 collective-permute-done.4.refs_5_
  23.9 2.4 %collective-permute-start.9 = (bf16[512,128]{1,0:T(8,128)(2,1)S(1)}, bf16[512,128]{1,0:T(8,128)(2,1)S(1)}, u32[]{:S(2)}, u32[]{:S(2)}) collective-permute-start(bf16[512,128]{1,0:T(8,128)(2,1)S(1)} %get-tuple-element.63.refs_13_), channel_id=1, source_target_pairs={{0,10},{2,8},{4,14},{6,12},{8,18},{10,16},{12,22},{14,20},{16,26},... | collective-permute-start | bytes 393224 | tf_op jit(solution)/shard_map/ppermute | solution.py:320
  26.3 0.0 collective-permute-done.5.refs_6_
  26.3 1.9 %collective-permute-start.11 = (bf16[512,128]{1,0:T(8,128)(2,1)S(1)}, bf16[512,128]{1,0:T(8,128)(2,1)S(1)}, u32[]{:S(2)}, u32[]{:S(2)}) collective-permute-start(bf16[512,128]{1,0:T(8,128)(2,1)S(1)} %get-tuple-element.66.refs_14_), channel_id=1, source_target_pairs={{0,18},{2,16},{4,22},{6,20},{8,26},{10,24},{12,30},{14,28},{16,2},... | collective-permute-start | bytes 393224 | tf_op jit(solution)/shard_map/ppermute | solution.py:320
  28.2 0.1 collective-permute-done.6.refs_7_
  28.4 8.1 %collective-permute-start.12 = (bf16[512,128]{1,0:T(8,128)(2,1)S(1)}, bf16[512,128]{1,0:T(8,128)(2,1)S(1)}, u32[]{:S(2)}, u32[]{:S(2)}) collective-permute-start(bf16[512,128]{1,0:T(8,128)(2,1)S(1)} %get-tuple-element.67.refs_15_), channel_id=1, source_target_pairs={{0,26},{2,24},{4,30},{6,28},{8,2},{10,0},{12,6},{14,4},{16,10},{18... | collective-permute-start | bytes 393224 | tf_op jit(solution)/shard_map/ppermute | solution.py:320
  36.4 0.0 collective-permute-done.7.refs_8_
  36.4 0.9 %collective-permute-start.13 = (bf16[512,128]{1,0:T(8,128)(2,1)S(1)}, bf16[512,128]{1,0:T(8,128)(2,1)S(1)}, u32[]{:S(2)}, u32[]{:S(2)}) collective-permute-start(bf16[512,128]{1,0:T(8,128)(2,1)S(1)} %get-tuple-element.68.refs_16_), channel_id=1, source_target_pairs={{0,2},{2,0},{4,6},{6,4},{8,10},{10,8},{12,14},{14,12},{16,18},{18,... | collective-permute-start | bytes 393224 | tf_op jit(solution)/shard_map/ppermute | solution.py:320
  37.3 0.0 collective-permute-done.8.refs_9_
  37.4 0.0 collective-permute-start.14
  37.4 7.3 %collective-permute-done.9.refs_10_ = bf16[512,128]{1,0:T(8,128)(2,1)S(1)} collective-permute-done((bf16[512,128]{1,0:T(8,128)(2,1)S(1)}, bf16[512,128]{1,0:T(8,128)(2,1)S(1)}, u32[]{:S(2)}, u32[]{:S(2)}) %collective-permute-start.9) | collective-permute-done | bytes 131104 | tf_op jit(solution)/shard_map/ppermute | solution.py:320
  44.7 0.0 collective-permute-start.15
  44.7 2.3 %early.1 = (bf16[16,256,128]{2,1,0:T(8,128)(2,1)}, bf16[16,256,128]{2,1,0:T(8,128)(2,1)}, f32[16,8,128]{2,1,0:T(8,128)S(1)}, bf16[16,8,128]{2,1,0:T(8,128)(2,1)S...) custom-call(bf16[512,128]{1,0:T(8,128)(2,1)S(1)} %get-tuple-element.57.refs_19_.refs_0_, ...), custom_call_target="tpu_custom_call" | custom-call | flops 11534336 | bytes 2883584 | tf_op jit(solution)/shard_map/early/pallas_call | solution.py:349
  47.0 0.0 collective-permute-done.11.refs_0_
  47.0 0.7 %collective-permute-start.10 = (bf16[16,4096]{1,0:T(8,128)(2,1)S(1)}, bf16[16,4096]{1,0:T(8,128)(2,1)S(1)}, u32[]{:S(2)}, u32[]{:S(2)}) collective-permute-start(bf16[16,4096]{1,0:T(8,128)(2,1)S(1)} %get-tuple-element.65), channel_id=1, source_target_pairs={{0,1},{1,0},{2,3},{3,2},{4,5},{5,4},{6,7},{7,6},{8,9},{9,8},{10,11... | collective-permute-start | bytes 393224 | tf_op jit(solution)/shard_map/ppermute | solution.py:210
  47.7 0.0 collective-permute-done.12.refs_1_
  47.7 0.0 collective-permute-done.13.refs_2_
  47.7 5.8 %collective-permute-done.14.refs_3_ = bf16[512,128]{1,0:T(8,128)(2,1)S(1)} collective-permute-done((bf16[512,128]{1,0:T(8,128)(2,1)S(1)}, bf16[512,128]{1,0:T(8,128)(2,1)S(1)}, u32[]{:S(2)}, u32[]{:S(2)}) %collective-permute-start.14) | collective-permute-done | bytes 131104 | tf_op jit(solution)/shard_map/ppermute | solution.py:320
  53.5 0.0 collective-permute-done.15.refs_4_
  53.5 2.0 %late.1 = (bf16[16,4096]{1,0:T(8,128)(2,1)S(1)}, bf16[16,256,128]{2,1,0:T(8,128)(2,1)}, bf16[16,256,128]{2,1,0:T(8,128)(2,1)}) custom-call(bf16[512,128]{1,0:T(8,128)(2,1)S(1)} %collective-permute-done.11.refs_0_, bf16[512,128]{1,0:T(8,128)(2,1)S(1)} %collective-permute-done.12.refs_1_, ...), custom_call_target="tpu_custom_call", output_to_operand_aliasing={{1}: (10, {}), {2}: (11, {})} | custom-call | flops 150994944 | bytes 10485760 | tf_op jit(solution)/shard_map/late/pallas_call | solution.py:375
  55.6 0.6 collective-permute-start.16
  56.1 0.0 collective-permute-done.10
  56.1 0.7 %add_convert_fusion.1 = bf16[16,4096]{1,0:T(8,128)(2,1)} fusion(bf16[16,4096]{1,0:T(8,128)(2,1)S(1)} %collective-permute-done.10, bf16[16,4096]{1,0:T(8,128)(2,1)S(1)} %get-tuple-element.65), kind=kLoop, calls=%fused_computation.1 | loop fusion | flops 262144 | bytes 393216 | tf_op jit(solution)/shard_map/convert_element_type | solution.py:211
  56.8 0.3 collective-permute-done.16
  57.1 0.7 %add_convert_fusion = bf16[16,4096]{1,0:T(8,128)(2,1)} fusion(bf16[16,4096]{1,0:T(8,128)(2,1)S(1)} %collective-permute-done.16, bf16[16,4096]{1,0:T(8,128)(2,1)S(1)} %get-tuple-element.77), kind=kLoop, calls=%fused_computation | loop fusion | flops 262144 | bytes 393216 | tf_op jit(solution)/shard_map/convert_element_type | solution.py:211
Async XLA Ops:
  2.3 15.1 %collective-permute-start = (bf16[512,128]{1,0:T(8,128)(2,1)S(1)}, bf16[512,128]{1,0:T(8,128)(2,1)S(1)}, u32[]{:S(2)}, u32[]{:S(2)}) collective-permute-start(bf16[512,128]{1,0:T(8,128)(2,1)S(1)} %get-tuple-element.42.refs_4_), channel_id=1, source_target_pairs={{0,16},{2,18},{4,20},{6,22},{8,24},{10,26},{12,28},{14,30},{16,0},... | collective-permute-start | bytes 393224 | tf_op jit(solution)/shard_map/ppermute | solution.py:320
  2.5 18.5 %collective-permute-start.1 = (bf16[512,128]{1,0:T(8,128)(2,1)S(1)}, bf16[512,128]{1,0:T(8,128)(2,1)S(1)}, u32[]{:S(2)}, u32[]{:S(2)}) collective-permute-start(bf16[512,128]{1,0:T(8,128)(2,1)S(1)} %get-tuple-element.43.refs_5_), channel_id=1, source_target_pairs={{0,14},{2,12},{4,10},{6,8},{8,22},{10,20},{12,18},{14,16},{16,30},... | collective-permute-start | bytes 393224 | tf_op jit(solution)/shard_map/ppermute | solution.py:320
  4.6 16.3 %collective-permute-start.2 = (bf16[512,128]{1,0:T(8,128)(2,1)S(1)}, bf16[512,128]{1,0:T(8,128)(2,1)S(1)}, u32[]{:S(2)}, u32[]{:S(2)}) collective-permute-start(bf16[512,128]{1,0:T(8,128)(2,1)S(1)} %get-tuple-element.44.refs_6_), channel_id=1, source_target_pairs={{0,22},{2,20},{4,18},{6,16},{8,30},{10,28},{12,26},{14,24},{16,6},... | collective-permute-start | bytes 393224 | tf_op jit(solution)/shard_map/ppermute | solution.py:320
  7.9 14.2 %collective-permute-start.3 = (bf16[512,128]{1,0:T(8,128)(2,1)S(1)}, bf16[512,128]{1,0:T(8,128)(2,1)S(1)}, u32[]{:S(2)}, u32[]{:S(2)}) collective-permute-start(bf16[512,128]{1,0:T(8,128)(2,1)S(1)} %get-tuple-element.45.refs_7_), channel_id=1, source_target_pairs={{0,30},{2,28},{4,26},{6,24},{8,6},{10,4},{12,2},{14,0},{16,14},{18... | collective-permute-start | bytes 393224 | tf_op jit(solution)/shard_map/ppermute | solution.py:320
  9.8 14.1 %collective-permute-start.4 = (bf16[512,128]{1,0:T(8,128)(2,1)S(1)}, bf16[512,128]{1,0:T(8,128)(2,1)S(1)}, u32[]{:S(2)}, u32[]{:S(2)}) collective-permute-start(bf16[512,128]{1,0:T(8,128)(2,1)S(1)} %get-tuple-element.46.refs_8_), channel_id=1, source_target_pairs={{0,6},{2,4},{4,2},{6,0},{8,14},{10,12},{12,10},{14,8},{16,22},{18,... | collective-permute-start | bytes 393224 | tf_op jit(solution)/shard_map/ppermute | solution.py:320
  17.5 8.8 %collective-permute-start.5 = (bf16[512,128]{1,0:T(8,128)(2,1)S(1)}, bf16[512,128]{1,0:T(8,128)(2,1)S(1)}, u32[]{:S(2)}, u32[]{:S(2)}) collective-permute-start(bf16[512,128]{1,0:T(8,128)(2,1)S(1)} %get-tuple-element.59.refs_9_), channel_id=1, source_target_pairs={{0,12},{2,14},{4,8},{6,10},{8,20},{10,22},{12,16},{14,18},{16,28},... | collective-permute-start | bytes 393224 | tf_op jit(solution)/shard_map/ppermute | solution.py:320
  21.0 7.4 %collective-permute-start.6 = (bf16[512,128]{1,0:T(8,128)(2,1)S(1)}, bf16[512,128]{1,0:T(8,128)(2,1)S(1)}, u32[]{:S(2)}, u32[]{:S(2)}) collective-permute-start(bf16[512,128]{1,0:T(8,128)(2,1)S(1)} %get-tuple-element.60.refs_10_), channel_id=1, source_target_pairs={{0,20},{2,22},{4,16},{6,18},{8,28},{10,30},{12,24},{14,26},{16,4},... | collective-permute-start | bytes 393224 | tf_op jit(solution)/shard_map/ppermute | solution.py:320
  21.0 15.5 %collective-permute-start.7 = (bf16[512,128]{1,0:T(8,128)(2,1)S(1)}, bf16[512,128]{1,0:T(8,128)(2,1)S(1)}, u32[]{:S(2)}, u32[]{:S(2)}) collective-permute-start(bf16[512,128]{1,0:T(8,128)(2,1)S(1)} %get-tuple-element.61.refs_11_), channel_id=1, source_target_pairs={{0,28},{2,30},{4,24},{6,26},{8,4},{10,6},{12,0},{14,2},{16,12},{18... | collective-permute-start | bytes 393224 | tf_op jit(solution)/shard_map/ppermute | solution.py:320
  22.1 15.3 %collective-permute-start.8 = (bf16[512,128]{1,0:T(8,128)(2,1)S(1)}, bf16[512,128]{1,0:T(8,128)(2,1)S(1)}, u32[]{:S(2)}, u32[]{:S(2)}) collective-permute-start(bf16[512,128]{1,0:T(8,128)(2,1)S(1)} %get-tuple-element.62.refs_12_), channel_id=1, source_target_pairs={{0,4},{2,6},{4,0},{6,2},{8,12},{10,14},{12,8},{14,10},{16,20},{18,... | collective-permute-start | bytes 393224 | tf_op jit(solution)/shard_map/ppermute | solution.py:320
  23.9 20.7 %collective-permute-start.9 = (bf16[512,128]{1,0:T(8,128)(2,1)S(1)}, bf16[512,128]{1,0:T(8,128)(2,1)S(1)}, u32[]{:S(2)}, u32[]{:S(2)}) collective-permute-start(bf16[512,128]{1,0:T(8,128)(2,1)S(1)} %get-tuple-element.63.refs_13_), channel_id=1, source_target_pairs={{0,10},{2,8},{4,14},{6,12},{8,18},{10,16},{12,22},{14,20},{16,26},... | collective-permute-start | bytes 393224 | tf_op jit(solution)/shard_map/ppermute | solution.py:320
  26.3 20.7 %collective-permute-start.11 = (bf16[512,128]{1,0:T(8,128)(2,1)S(1)}, bf16[512,128]{1,0:T(8,128)(2,1)S(1)}, u32[]{:S(2)}, u32[]{:S(2)}) collective-permute-start(bf16[512,128]{1,0:T(8,128)(2,1)S(1)} %get-tuple-element.66.refs_14_), channel_id=1, source_target_pairs={{0,18},{2,16},{4,22},{6,20},{8,26},{10,24},{12,30},{14,28},{16,2},... | collective-permute-start | bytes 393224 | tf_op jit(solution)/shard_map/ppermute | solution.py:320
  28.4 19.3 %collective-permute-start.12 = (bf16[512,128]{1,0:T(8,128)(2,1)S(1)}, bf16[512,128]{1,0:T(8,128)(2,1)S(1)}, u32[]{:S(2)}, u32[]{:S(2)}) collective-permute-start(bf16[512,128]{1,0:T(8,128)(2,1)S(1)} %get-tuple-element.67.refs_15_), channel_id=1, source_target_pairs={{0,26},{2,24},{4,30},{6,28},{8,2},{10,0},{12,6},{14,4},{16,10},{18... | collective-permute-start | bytes 393224 | tf_op jit(solution)/shard_map/ppermute | solution.py:320
  36.4 11.3 %collective-permute-start.13 = (bf16[512,128]{1,0:T(8,128)(2,1)S(1)}, bf16[512,128]{1,0:T(8,128)(2,1)S(1)}, u32[]{:S(2)}, u32[]{:S(2)}) collective-permute-start(bf16[512,128]{1,0:T(8,128)(2,1)S(1)} %get-tuple-element.68.refs_16_), channel_id=1, source_target_pairs={{0,2},{2,0},{4,6},{6,4},{8,10},{10,8},{12,14},{14,12},{16,18},{18,... | collective-permute-start | bytes 393224 | tf_op jit(solution)/shard_map/ppermute | solution.py:320
  37.4 16.2 %collective-permute-start.14 = (bf16[512,128]{1,0:T(8,128)(2,1)S(1)}, bf16[512,128]{1,0:T(8,128)(2,1)S(1)}, u32[]{:S(2)}, u32[]{:S(2)}) collective-permute-start(bf16[512,128]{1,0:T(8,128)(2,1)S(1)} %get-tuple-element.69.refs_17_), channel_id=1, source_target_pairs={{0,8},{2,10},{4,12},{6,14},{8,16},{10,18},{12,20},{14,22},{16,24},... | collective-permute-start | bytes 393224 | tf_op jit(solution)/shard_map/ppermute | solution.py:320
  44.7 8.9 %collective-permute-start.15 = (bf16[512,128]{1,0:T(8,128)(2,1)S(1)}, bf16[512,128]{1,0:T(8,128)(2,1)S(1)}, u32[]{:S(2)}, u32[]{:S(2)}) collective-permute-start(bf16[512,128]{1,0:T(8,128)(2,1)S(1)} %get-tuple-element.70.refs_18_), channel_id=1, source_target_pairs={{0,24},{2,26},{4,28},{6,30},{8,0},{10,2},{12,4},{14,6},{16,8},{18,... | collective-permute-start | bytes 393224 | tf_op jit(solution)/shard_map/ppermute | solution.py:320
  47.0 9.1 %collective-permute-start.10 = (bf16[16,4096]{1,0:T(8,128)(2,1)S(1)}, bf16[16,4096]{1,0:T(8,128)(2,1)S(1)}, u32[]{:S(2)}, u32[]{:S(2)}) collective-permute-start(bf16[16,4096]{1,0:T(8,128)(2,1)S(1)} %get-tuple-element.65), channel_id=1, source_target_pairs={{0,1},{1,0},{2,3},{3,2},{4,5},{5,4},{6,7},{7,6},{8,9},{9,8},{10,11... | collective-permute-start | bytes 393224 | tf_op jit(solution)/shard_map/ppermute | solution.py:210
  55.6 1.5 %collective-permute-start.16 = (bf16[16,4096]{1,0:T(8,128)(2,1)S(1)}, bf16[16,4096]{1,0:T(8,128)(2,1)S(1)}, u32[]{:S(2)}, u32[]{:S(2)}) collective-permute-start(bf16[16,4096]{1,0:T(8,128)(2,1)S(1)} %get-tuple-element.77), channel_id=1, source_target_pairs={{0,1},{1,0},{2,3},{3,2},{4,5},{5,4},{6,7},{7,6},{8,9},{9,8},{10,11... | collective-permute-start | bytes 393224 | tf_op jit(solution)/shard_map/ppermute | solution.py:210

commit v14 on v13

--- a/solution.py
+++ b/solution.py
@@ -221,11 +221,9 @@
 
 
 def step_order(n):
-    part = n // Z
-    order = [(2, 0)]
-    for b in range(part - 1, 0, -1):
-        order += [(1, b), (2, b), (3, b), (0, b)]
-    return order + [(1, 0), (3, 0)]
+    down = range(n // Z - 1, -1, -1)
+    turns = [(a, b) for b in down for a in (1, 3)]
+    return [(2, 0)] + turns + [(a, b) for b in down if b for a in (0, 2)]
 
 
 def target(at, step, n):

time: 58.1 us -> 58.3 us (level)
  the two profiles are of different devices: /device:TPU:21 before, /device:TPU:0 now
where the time goes in v14:
time: 58.3 us; the launch traced here: 58 us
  starting transfers between devices  31.5 us (54%)
  Pallas kernels  12.5 us (21%)
  waiting for transfers between devices  12 us (21%)
  other arithmetic  1.38 us (2%)
  between operations  0.73 us (1%)
    ppermute x15, starting transfers between devices, send(): lax.ppermute(block, 'inst', [(d, target(d, steps[i], n)) for d in range(n)])  31.4 us
    ppermute x15, waiting for transfers between devices, send(): lax.ppermute(block, 'inst', [(d, target(d, steps[i], n)) for d in range(n)])  11.3 us
    pallas_call x1, Pallas kernels, shards(): pl.pallas_call(functools.partial(first_kernel, steps, span), out_shape=[j...  4.67 us
    pallas_call x2, Pallas kernels, pack(): pl.pallas_call(functools.partial(pack_kernel, n, chosen, pages), out_shap...  3.48 us
    pallas_call x1, Pallas kernels, shards(): pl.pallas_call(functools.partial(early_kernel, some, span), out_shape=[ca...  2.31 us
    pallas_call x1, Pallas kernels, shards(): pl.pallas_call(functools.partial(late_kernel, LATE, span), out_shape=[jax...  2.01 us
    convert_element_type x2, other arithmetic, total(): (partial.astype(jnp.float32) + other.astype(jnp.float32)).astype(jnp.bflo...  1.38 us
  transfers between devices with their start and end apart: 17, of which 5 were waited for; matrix products, arithmetic and copies ran while one was open for 1% of the time, Pallas kernels for 19%

profile of v14, /device:TPU:0, one launch (start us, length us, event | category | flops | bytes accessed | tf_op | source)
XLA Modules:
  0.0 58.0 jit_solution(17780210968857646715)
XLA Ops:
  0.6 1.7 %pack.2 = (bf16[512,128]{1,0:T(8,128)(2,1)S(1)}, bf16[512,128]{1,0:T(8,128)(2,1)S(1)}, bf16[512,128]{1,0:T(8,128)(2,1)S(1)}, bf16[512,128]{1,0:T(8,128)(2,1)S(1)}, bf16[512,128]{1,0:T(8,128)(2,1)S(1)}) custom-call(s32[4,16]{1,0:T(4,128)} %bitcast.23, s32[16]{0:T(128)} %refs_0_.1, s32[16]{0:T(128)} %refs_1_.5, s32[16]{0:T(128)} %refs_3_.4, ...), custom_call_target="tpu_custom_call" | custom-call | bytes 1310720 | tf_op jit(solution)/shard_map/pack/pallas_call | solution.py:278
  2.3 4.1 %collective-permute-start = (bf16[512,128]{1,0:T(8,128)(2,1)S(1)}, bf16[512,128]{1,0:T(8,128)(2,1)S(1)}, u32[]{:S(2)}, u32[]{:S(2)}) collective-permute-start(bf16[512,128]{1,0:T(8,128)(2,1)S(1)} %get-tuple-element.42.refs_4_), channel_id=1, source_target_pairs={{0,16},{2,18},{4,20},{6,22},{8,24},{10,26},{12,28},{14,30},{16,0},... | collective-permute-start | bytes 393224 | tf_op jit(solution)/shard_map/ppermute | solution.py:318
  6.5 3.5 %collective-permute-start.1 = (bf16[512,128]{1,0:T(8,128)(2,1)S(1)}, bf16[512,128]{1,0:T(8,128)(2,1)S(1)}, u32[]{:S(2)}, u32[]{:S(2)}) collective-permute-start(bf16[512,128]{1,0:T(8,128)(2,1)S(1)} %get-tuple-element.43.refs_5_), channel_id=1, source_target_pairs={{0,14},{2,12},{4,10},{6,8},{8,22},{10,20},{12,18},{14,16},{16,30},... | collective-permute-start | bytes 393224 | tf_op jit(solution)/shard_map/ppermute | solution.py:318
  9.9 2.2 %collective-permute-start.2 = (bf16[512,128]{1,0:T(8,128)(2,1)S(1)}, bf16[512,128]{1,0:T(8,128)(2,1)S(1)}, u32[]{:S(2)}, u32[]{:S(2)}) collective-permute-start(bf16[512,128]{1,0:T(8,128)(2,1)S(1)} %get-tuple-element.44.refs_6_), channel_id=1, source_target_pairs={{0,30},{2,28},{4,26},{6,24},{8,6},{10,4},{12,2},{14,0},{16,14},{18... | collective-permute-start | bytes 393224 | tf_op jit(solution)/shard_map/ppermute | solution.py:318
  12.1 0.7 %collective-permute-start.3 = (bf16[512,128]{1,0:T(8,128)(2,1)S(1)}, bf16[512,128]{1,0:T(8,128)(2,1)S(1)}, u32[]{:S(2)}, u32[]{:S(2)}) collective-permute-start(bf16[512,128]{1,0:T(8,128)(2,1)S(1)} %get-tuple-element.45.refs_7_), channel_id=1, source_target_pairs={{0,12},{2,14},{4,8},{6,10},{8,20},{10,22},{12,16},{14,18},{16,28},... | collective-permute-start | bytes 393224 | tf_op jit(solution)/shard_map/ppermute | solution.py:318
  12.8 4.0 %collective-permute-start.4 = (bf16[512,128]{1,0:T(8,128)(2,1)S(1)}, bf16[512,128]{1,0:T(8,128)(2,1)S(1)}, u32[]{:S(2)}, u32[]{:S(2)}) collective-permute-start(bf16[512,128]{1,0:T(8,128)(2,1)S(1)} %get-tuple-element.46.refs_8_), channel_id=1, source_target_pairs={{0,28},{2,30},{4,24},{6,26},{8,4},{10,6},{12,0},{14,2},{16,12},{18... | collective-permute-start | bytes 393224 | tf_op jit(solution)/shard_map/ppermute | solution.py:318
  16.8 1.8 %pack.3 = (bf16[512,128]{1,0:T(8,128)(2,1)S(1)}, bf16[512,128]{1,0:T(8,128)(2,1)S(1)}, bf16[512,128]{1,0:T(8,128)(2,1)S(1)}, bf16[512,128]{1,0:T(8,128)(2,1)S(1)...) custom-call(s32[4,16]{1,0:T(4,128)} %bitcast.24, ...), custom_call_target="tpu_custom_call" | custom-call | bytes 2883584 | tf_op jit(solution)/shard_map/pack/pallas_call | solution.py:278
  18.6 4.7 %first.1 = (bf16[16,4096]{1,0:T(8,128)(2,1)S(1)}, bf16[1024,4096]{1,0:T(8,128)(2,1)S(1)}) custom-call(s32[16]{0:T(128)} %refs_0_.1, s32[16]{0:T(128)} %refs_1_.5, bf16[16,8,128]{2,1,0:T(8,128)(2,1)} %refs_2_.5, bf16[1024,4096]{1,0:T(8,128)(2,1)} %refs_3_.5, bf16[512,128]{1,0:T(8,128)(2,1)S(1)} %get-tuple-element.42.refs_4_, ...), custom_call_target="tpu_custom_call" | custom-call | flops 150994944 | bytes 10485760 | tf_op jit(solution)/shard_map/first/pallas_call | solution.py:321
  23.2 0.0 collective-permute-done.refs_1_
  23.3 0.1 collective-permute-start.5
  23.3 0.0 collective-permute-done.1.refs_2_
  23.3 4.7 %collective-permute-start.6 = (bf16[512,128]{1,0:T(8,128)(2,1)S(1)}, bf16[512,128]{1,0:T(8,128)(2,1)S(1)}, u32[]{:S(2)}, u32[]{:S(2)}) collective-permute-start(bf16[512,128]{1,0:T(8,128)(2,1)S(1)} %get-tuple-element.60.refs_10_), channel_id=1, source_target_pairs={{0,26},{2,24},{4,30},{6,28},{8,2},{10,0},{12,6},{14,4},{16,10},{18... | collective-permute-start | bytes 393224 | tf_op jit(solution)/shard_map/ppermute | solution.py:318
  28.0 0.0 collective-permute-done.2.refs_3_
  28.0 0.0 collective-permute-start.7
  28.0 0.0 collective-permute-done.3.refs_4_
  28.0 3.8 %collective-permute-start.8 = (bf16[512,128]{1,0:T(8,128)(2,1)S(1)}, bf16[512,128]{1,0:T(8,128)(2,1)S(1)}, u32[]{:S(2)}, u32[]{:S(2)}) collective-permute-start(bf16[512,128]{1,0:T(8,128)(2,1)S(1)} %get-tuple-element.62.refs_12_), channel_id=1, source_target_pairs={{0,24},{2,26},{4,28},{6,30},{8,0},{10,2},{12,4},{14,6},{16,8},{18,... | collective-permute-start | bytes 393224 | tf_op jit(solution)/shard_map/ppermute | solution.py:318
  31.9 0.0 collective-permute-done.4.refs_5_
  31.9 2.4 %collective-permute-start.9 = (bf16[512,128]{1,0:T(8,128)(2,1)S(1)}, bf16[512,128]{1,0:T(8,128)(2,1)S(1)}, u32[]{:S(2)}, u32[]{:S(2)}) collective-permute-start(bf16[512,128]{1,0:T(8,128)(2,1)S(1)} %get-tuple-element.63.refs_13_), channel_id=1, source_target_pairs={{0,6},{2,4},{4,2},{6,0},{8,14},{10,12},{12,10},{14,8},{16,22},{18,... | collective-permute-start | bytes 393224 | tf_op jit(solution)/shard_map/ppermute | solution.py:318
  34.3 0.0 collective-permute-done.5.refs_6_
  34.3 0.0 collective-permute-start.11
  34.3 0.0 collective-permute-done.6.refs_7_
  34.3 0.6 collective-permute-start.12
  34.9 3.4 %collective-permute-done.7.refs_8_ = bf16[512,128]{1,0:T(8,128)(2,1)S(1)} collective-permute-done((bf16[512,128]{1,0:T(8,128)(2,1)S(1)}, bf16[512,128]{1,0:T(8,128)(2,1)S(1)}, u32[]{:S(2)}, u32[]{:S(2)}) %collective-permute-start.7) | collective-permute-done | bytes 131104 | tf_op jit(solution)/shard_map/ppermute | solution.py:318
  38.3 0.6 %collective-permute-start.13 = (bf16[512,128]{1,0:T(8,128)(2,1)S(1)}, bf16[512,128]{1,0:T(8,128)(2,1)S(1)}, u32[]{:S(2)}, u32[]{:S(2)}) collective-permute-start(bf16[512,128]{1,0:T(8,128)(2,1)S(1)} %get-tuple-element.68.refs_16_), channel_id=1, source_target_pairs={{0,20},{2,22},{4,16},{6,18},{8,28},{10,30},{12,24},{14,26},{16,4},... | collective-permute-start | bytes 393224 | tf_op jit(solution)/shard_map/ppermute | solution.py:318
  38.9 0.0 collective-permute-done.8.refs_9_
  38.9 4.2 %collective-permute-start.14 = (bf16[512,128]{1,0:T(8,128)(2,1)S(1)}, bf16[512,128]{1,0:T(8,128)(2,1)S(1)}, u32[]{:S(2)}, u32[]{:S(2)}) collective-permute-start(bf16[512,128]{1,0:T(8,128)(2,1)S(1)} %get-tuple-element.69.refs_17_), channel_id=1, source_target_pairs={{0,2},{2,0},{4,6},{6,4},{8,10},{10,8},{12,14},{14,12},{16,18},{18,... | collective-permute-start | bytes 393224 | tf_op jit(solution)/shard_map/ppermute | solution.py:318
  43.1 0.0 collective-permute-done.9.refs_10_
  43.1 0.6 collective-permute-start.15
  43.6 2.3 %early.1 = (bf16[16,256,128]{2,1,0:T(8,128)(2,1)}, bf16[16,256,128]{2,1,0:T(8,128)(2,1)}, f32[16,8,128]{2,1,0:T(8,128)S(1)}, bf16[16,8,128]{2,1,0:T(8,128)(2,1)S...) custom-call(bf16[512,128]{1,0:T(8,128)(2,1)S(1)} %get-tuple-element.57.refs_19_.refs_0_, ...), custom_call_target="tpu_custom_call" | custom-call | flops 11534336 | bytes 2883584 | tf_op jit(solution)/shard_map/early/pallas_call | solution.py:347
  46.0 4.9 %collective-permute-done.11.refs_0_ = bf16[512,128]{1,0:T(8,128)(2,1)S(1)} collective-permute-done((bf16[512,128]{1,0:T(8,128)(2,1)S(1)}, bf16[512,128]{1,0:T(8,128)(2,1)S(1)}, u32[]{:S(2)}, u32[]{:S(2)}) %collective-permute-start.11) | collective-permute-done | bytes 131104 | tf_op jit(solution)/shard_map/ppermute | solution.py:318
  50.9 0.0 collective-permute-start.10
  50.9 0.0 collective-permute-done.12.refs_1_
  50.9 1.5 %collective-permute-done.13.refs_2_ = bf16[512,128]{1,0:T(8,128)(2,1)S(1)} collective-permute-done((bf16[512,128]{1,0:T(8,128)(2,1)S(1)}, bf16[512,128]{1,0:T(8,128)(2,1)S(1)}, u32[]{:S(2)}, u32[]{:S(2)}) %collective-permute-start.13) | collective-permute-done | bytes 131104 | tf_op jit(solution)/shard_map/ppermute | solution.py:318
  52.4 0.0 collective-permute-done.14.refs_3_
  52.4 1.5 %collective-permute-done.15.refs_4_ = bf16[512,128]{1,0:T(8,128)(2,1)S(1)} collective-permute-done((bf16[512,128]{1,0:T(8,128)(2,1)S(1)}, bf16[512,128]{1,0:T(8,128)(2,1)S(1)}, u32[]{:S(2)}, u32[]{:S(2)}) %collective-permute-start.15) | collective-permute-done | bytes 131104 | tf_op jit(solution)/shard_map/ppermute | solution.py:318
  53.9 2.0 %late.1 = (bf16[16,4096]{1,0:T(8,128)(2,1)S(1)}, bf16[16,256,128]{2,1,0:T(8,128)(2,1)}, bf16[16,256,128]{2,1,0:T(8,128)(2,1)}) custom-call(bf16[512,128]{1,0:T(8,128)(2,1)S(1)} %collective-permute-done.11.refs_0_, bf16[512,128]{1,0:T(8,128)(2,1)S(1)} %collective-permute-done.12.refs_1_, ...), custom_call_target="tpu_custom_call", output_to_operand_aliasing={{1}: (10, {}), {2}: (11, {})} | custom-call | flops 150994944 | bytes 10485760 | tf_op jit(solution)/shard_map/late/pallas_call | solution.py:373
  55.9 0.1 collective-permute-start.16
  56.0 0.0 collective-permute-done.10
  56.0 0.7 %add_convert_fusion.1 = bf16[16,4096]{1,0:T(8,128)(2,1)} fusion(bf16[16,4096]{1,0:T(8,128)(2,1)S(1)} %collective-permute-done.10, bf16[16,4096]{1,0:T(8,128)(2,1)S(1)} %get-tuple-element.65), kind=kLoop, calls=%fused_computation.1 | loop fusion | flops 262144 | bytes 393216 | tf_op jit(solution)/shard_map/convert_element_type | solution.py:211
  56.7 0.6 %collective-permute-done.16 = bf16[16,4096]{1,0:T(8,128)(2,1)S(1)} collective-permute-done((bf16[16,4096]{1,0:T(8,128)(2,1)S(1)}, bf16[16,4096]{1,0:T(8,128)(2,1)S(1)}, u32[]{:S(2)}, u32[]{:S(2)}) %collective-permute-start.16) | collective-permute-done | bytes 131104 | tf_op jit(solution)/shard_map/ppermute | solution.py:210
  57.4 0.7 %add_convert_fusion = bf16[16,4096]{1,0:T(8,128)(2,1)} fusion(bf16[16,4096]{1,0:T(8,128)(2,1)S(1)} %collective-permute-done.16, bf16[16,4096]{1,0:T(8,128)(2,1)S(1)} %get-tuple-element.77), kind=kLoop, calls=%fused_computation | loop fusion | flops 262144 | bytes 393216 | tf_op jit(solution)/shard_map/convert_element_type | solution.py:211
Async XLA Ops:
  2.3 20.9 %collective-permute-start = (bf16[512,128]{1,0:T(8,128)(2,1)S(1)}, bf16[512,128]{1,0:T(8,128)(2,1)S(1)}, u32[]{:S(2)}, u32[]{:S(2)}) collective-permute-start(bf16[512,128]{1,0:T(8,128)(2,1)S(1)} %get-tuple-element.42.refs_4_), channel_id=1, source_target_pairs={{0,16},{2,18},{4,20},{6,22},{8,24},{10,26},{12,28},{14,30},{16,0},... | collective-permute-start | bytes 393224 | tf_op jit(solution)/shard_map/ppermute | solution.py:318
  6.5 16.9 %collective-permute-start.1 = (bf16[512,128]{1,0:T(8,128)(2,1)S(1)}, bf16[512,128]{1,0:T(8,128)(2,1)S(1)}, u32[]{:S(2)}, u32[]{:S(2)}) collective-permute-start(bf16[512,128]{1,0:T(8,128)(2,1)S(1)} %get-tuple-element.43.refs_5_), channel_id=1, source_target_pairs={{0,14},{2,12},{4,10},{6,8},{8,22},{10,20},{12,18},{14,16},{16,30},... | collective-permute-start | bytes 393224 | tf_op jit(solution)/shard_map/ppermute | solution.py:318
  9.9 18.1 %collective-permute-start.2 = (bf16[512,128]{1,0:T(8,128)(2,1)S(1)}, bf16[512,128]{1,0:T(8,128)(2,1)S(1)}, u32[]{:S(2)}, u32[]{:S(2)}) collective-permute-start(bf16[512,128]{1,0:T(8,128)(2,1)S(1)} %get-tuple-element.44.refs_6_), channel_id=1, source_target_pairs={{0,30},{2,28},{4,26},{6,24},{8,6},{10,4},{12,2},{14,0},{16,14},{18... | collective-permute-start | bytes 393224 | tf_op jit(solution)/shard_map/ppermute | solution.py:318
  12.1 16.0 %collective-permute-start.3 = (bf16[512,128]{1,0:T(8,128)(2,1)S(1)}, bf16[512,128]{1,0:T(8,128)(2,1)S(1)}, u32[]{:S(2)}, u32[]{:S(2)}) collective-permute-start(bf16[512,128]{1,0:T(8,128)(2,1)S(1)} %get-tuple-element.45.refs_7_), channel_id=1, source_target_pairs={{0,12},{2,14},{4,8},{6,10},{8,20},{10,22},{12,16},{14,18},{16,28},... | collective-permute-start | bytes 393224 | tf_op jit(solution)/shard_map/ppermute | solution.py:318
  12.8 19.1 %collective-permute-start.4 = (bf16[512,128]{1,0:T(8,128)(2,1)S(1)}, bf16[512,128]{1,0:T(8,128)(2,1)S(1)}, u32[]{:S(2)}, u32[]{:S(2)}) collective-permute-start(bf16[512,128]{1,0:T(8,128)(2,1)S(1)} %get-tuple-element.46.refs_8_), channel_id=1, source_target_pairs={{0,28},{2,30},{4,24},{6,26},{8,4},{10,6},{12,0},{14,2},{16,12},{18... | collective-permute-start | bytes 393224 | tf_op jit(solution)/shard_map/ppermute | solution.py:318
  23.3 11.1 %collective-permute-start.5 = (bf16[512,128]{1,0:T(8,128)(2,1)S(1)}, bf16[512,128]{1,0:T(8,128)(2,1)S(1)}, u32[]{:S(2)}, u32[]{:S(2)}) collective-permute-start(bf16[512,128]{1,0:T(8,128)(2,1)S(1)} %get-tuple-element.59.refs_9_), channel_id=1, source_target_pairs={{0,10},{2,8},{4,14},{6,12},{8,18},{10,16},{12,22},{14,20},{16,26},... | collective-permute-start | bytes 393224 | tf_op jit(solution)/shard_map/ppermute | solution.py:318
  23.3 11.0 %collective-permute-start.6 = (bf16[512,128]{1,0:T(8,128)(2,1)S(1)}, bf16[512,128]{1,0:T(8,128)(2,1)S(1)}, u32[]{:S(2)}, u32[]{:S(2)}) collective-permute-start(bf16[512,128]{1,0:T(8,128)(2,1)S(1)} %get-tuple-element.60.refs_10_), channel_id=1, source_target_pairs={{0,26},{2,24},{4,30},{6,28},{8,2},{10,0},{12,6},{14,4},{16,10},{18... | collective-permute-start | bytes 393224 | tf_op jit(solution)/shard_map/ppermute | solution.py:318
  28.0 10.2 %collective-permute-start.7 = (bf16[512,128]{1,0:T(8,128)(2,1)S(1)}, bf16[512,128]{1,0:T(8,128)(2,1)S(1)}, u32[]{:S(2)}, u32[]{:S(2)}) collective-permute-start(bf16[512,128]{1,0:T(8,128)(2,1)S(1)} %get-tuple-element.61.refs_11_), channel_id=1, source_target_pairs={{0,8},{2,10},{4,12},{6,14},{8,16},{10,18},{12,20},{14,22},{16,24},... | collective-permute-start | bytes 393224 | tf_op jit(solution)/shard_map/ppermute | solution.py:318
  28.0 10.8 %collective-permute-start.8 = (bf16[512,128]{1,0:T(8,128)(2,1)S(1)}, bf16[512,128]{1,0:T(8,128)(2,1)S(1)}, u32[]{:S(2)}, u32[]{:S(2)}) collective-permute-start(bf16[512,128]{1,0:T(8,128)(2,1)S(1)} %get-tuple-element.62.refs_12_), channel_id=1, source_target_pairs={{0,24},{2,26},{4,28},{6,30},{8,0},{10,2},{12,4},{14,6},{16,8},{18,... | collective-permute-start | bytes 393224 | tf_op jit(solution)/shard_map/ppermute | solution.py:318
  31.9 11.2 %collective-permute-start.9 = (bf16[512,128]{1,0:T(8,128)(2,1)S(1)}, bf16[512,128]{1,0:T(8,128)(2,1)S(1)}, u32[]{:S(2)}, u32[]{:S(2)}) collective-permute-start(bf16[512,128]{1,0:T(8,128)(2,1)S(1)} %get-tuple-element.63.refs_13_), channel_id=1, source_target_pairs={{0,6},{2,4},{4,2},{6,0},{8,14},{10,12},{12,10},{14,8},{16,22},{18,... | collective-permute-start | bytes 393224 | tf_op jit(solution)/shard_map/ppermute | solution.py:318
  34.3 16.6 %collective-permute-start.11 = (bf16[512,128]{1,0:T(8,128)(2,1)S(1)}, bf16[512,128]{1,0:T(8,128)(2,1)S(1)}, u32[]{:S(2)}, u32[]{:S(2)}) collective-permute-start(bf16[512,128]{1,0:T(8,128)(2,1)S(1)} %get-tuple-element.66.refs_14_), channel_id=1, source_target_pairs={{0,22},{2,20},{4,18},{6,16},{8,30},{10,28},{12,26},{14,24},{16,6},... | collective-permute-start | bytes 393224 | tf_op jit(solution)/shard_map/ppermute | solution.py:318
  34.3 16.6 %collective-permute-start.12 = (bf16[512,128]{1,0:T(8,128)(2,1)S(1)}, bf16[512,128]{1,0:T(8,128)(2,1)S(1)}, u32[]{:S(2)}, u32[]{:S(2)}) collective-permute-start(bf16[512,128]{1,0:T(8,128)(2,1)S(1)} %get-tuple-element.67.refs_15_), channel_id=1, source_target_pairs={{0,4},{2,6},{4,0},{6,2},{8,12},{10,14},{12,8},{14,10},{16,20},{18,... | collective-permute-start | bytes 393224 | tf_op jit(solution)/shard_map/ppermute | solution.py:318
  38.3 14.2 %collective-permute-start.13 = (bf16[512,128]{1,0:T(8,128)(2,1)S(1)}, bf16[512,128]{1,0:T(8,128)(2,1)S(1)}, u32[]{:S(2)}, u32[]{:S(2)}) collective-permute-start(bf16[512,128]{1,0:T(8,128)(2,1)S(1)} %get-tuple-element.68.refs_16_), channel_id=1, source_target_pairs={{0,20},{2,22},{4,16},{6,18},{8,28},{10,30},{12,24},{14,26},{16,4},... | collective-permute-start | bytes 393224 | tf_op jit(solution)/shard_map/ppermute | solution.py:318
  38.9 13.5 %collective-permute-start.14 = (bf16[512,128]{1,0:T(8,128)(2,1)S(1)}, bf16[512,128]{1,0:T(8,128)(2,1)S(1)}, u32[]{:S(2)}, u32[]{:S(2)}) collective-permute-start(bf16[512,128]{1,0:T(8,128)(2,1)S(1)} %get-tuple-element.69.refs_17_), channel_id=1, source_target_pairs={{0,2},{2,0},{4,6},{6,4},{8,10},{10,8},{12,14},{14,12},{16,18},{18,... | collective-permute-start | bytes 393224 | tf_op jit(solution)/shard_map/ppermute | solution.py:318
  43.1 10.8 %collective-permute-start.15 = (bf16[512,128]{1,0:T(8,128)(2,1)S(1)}, bf16[512,128]{1,0:T(8,128)(2,1)S(1)}, u32[]{:S(2)}, u32[]{:S(2)}) collective-permute-start(bf16[512,128]{1,0:T(8,128)(2,1)S(1)} %get-tuple-element.70.refs_18_), channel_id=1, source_target_pairs={{0,18},{2,16},{4,22},{6,20},{8,26},{10,24},{12,30},{14,28},{16,2},... | collective-permute-start | bytes 393224 | tf_op jit(solution)/shard_map/ppermute | solution.py:318
  50.9 5.1 %collective-permute-start.10 = (bf16[16,4096]{1,0:T(8,128)(2,1)S(1)}, bf16[16,4096]{1,0:T(8,128)(2,1)S(1)}, u32[]{:S(2)}, u32[]{:S(2)}) collective-permute-start(bf16[16,4096]{1,0:T(8,128)(2,1)S(1)} %get-tuple-element.65), channel_id=1, source_target_pairs={{0,1},{1,0},{2,3},{3,2},{4,5},{5,4},{6,7},{7,6},{8,9},{9,8},{10,11... | collective-permute-start | bytes 393224 | tf_op jit(solution)/shard_map/ppermute | solution.py:210
  55.9 1.4 %collective-permute-start.16 = (bf16[16,4096]{1,0:T(8,128)(2,1)S(1)}, bf16[16,4096]{1,0:T(8,128)(2,1)S(1)}, u32[]{:S(2)}, u32[]{:S(2)}) collective-permute-start(bf16[16,4096]{1,0:T(8,128)(2,1)S(1)} %get-tuple-element.77), channel_id=1, source_target_pairs={{0,1},{1,0},{2,3},{3,2},{4,5},{5,4},{6,7},{7,6},{8,9},{9,8},{10,11... | collective-permute-start | bytes 393224 | tf_op jit(solution)/shard_map/ppermute | solution.py:210

commit v15 on v10

--- a/solution.py
+++ b/solution.py
@@ -220,8 +220,8 @@
 
 def step_order(n):
     half = n // 2
-    crossing = [half] + list(range(half + 1, n))[::-1]
-    staying = list(range(1, half))[::-1]
+    crossing = list(range(half, n))
+    staying = list(range(1, half))
     order = []
     for kind in "cncncncncncncnc":
         queue = crossing if kind == "c" else staying

time: 57.9 us -> 57.3 us (0.990)
  waiting for transfers between devices: 8.67 us -> 8.01 us
    ppermute x15, waiting for transfers between devices: 8.03 us -> 7.37 us  [send(): return lax.ppermute(block, 'inst', [(d, d ^ steps[i]) for d in range(n)])]
  transfers between devices with their start and end apart: 17 -> 17, of which waited for: 7 -> 6; matrix products, arithmetic and copies ran while one was open for 1% -> 1% of each run, Pallas kernels for 19% -> 19%
where the time goes in v15:
time: 57.3 us; the launch traced here: 57 us
  starting transfers between devices  34.4 us (60%)
  Pallas kernels  12.5 us (22%)
  waiting for transfers between devices  8.01 us (14%)
  other arithmetic  1.38 us (2%)
  between operations  0.73 us (1%)
    ppermute x15, starting transfers between devices, send(): return lax.ppermute(block, 'inst', [(d, d ^ steps[i]) for d in range(n)])  34.3 us
    ppermute x15, waiting for transfers between devices, send(): return lax.ppermute(block, 'inst', [(d, d ^ steps[i]) for d in range(n)])  7.37 us
    pallas_call x1, Pallas kernels, shards(): pl.pallas_call(functools.partial(first_kernel, steps, span), out_shape=[j...  4.66 us
    pallas_call x2, Pallas kernels, pack(): pl.pallas_call(functools.partial(pack_kernel, n, chosen, pages), out_shap...  3.48 us
    pallas_call x1, Pallas kernels, shards(): pl.pallas_call(functools.partial(early_kernel, some, span), out_shape=[ca...  2.31 us
    pallas_call x1, Pallas kernels, shards(): pl.pallas_call(functools.partial(late_kernel, LATE, span), out_shape=[jax...  2.01 us
    convert_element_type x2, other arithmetic, total(): (partial.astype(jnp.float32) + other.astype(jnp.float32)).astype(jnp.bflo...  1.38 us
  transfers between devices with their start and end apart: 17, of which 6 were waited for; matrix products, arithmetic and copies ran while one was open for 1% of the time, Pallas kernels for 19%

profile of v15, /device:TPU:0, one launch (start us, length us, event | category | flops | bytes accessed | tf_op | source)
XLA Modules:
  0.0 57.0 jit_solution(4352723100112496584)
XLA Ops:
  0.6 1.7 %pack.2 = (bf16[512,128]{1,0:T(8,128)(2,1)S(1)}, bf16[512,128]{1,0:T(8,128)(2,1)S(1)}, bf16[512,128]{1,0:T(8,128)(2,1)S(1)}, bf16[512,128]{1,0:T(8,128)(2,1)S(1)}, bf16[512,128]{1,0:T(8,128)(2,1)S(1)}) custom-call(s32[4,16]{1,0:T(4,128)} %bitcast.23, s32[16]{0:T(128)} %refs_0_.1, s32[16]{0:T(128)} %refs_1_.5, s32[16]{0:T(128)} %refs_3_.4, ...), custom_call_target="tpu_custom_call" | custom-call | bytes 1310720 | tf_op jit(solution)/shard_map/pack/pallas_call | solution.py:280
  2.3 4.1 %collective-permute-start = (bf16[512,128]{1,0:T(8,128)(2,1)S(1)}, bf16[512,128]{1,0:T(8,128)(2,1)S(1)}, u32[]{:S(2)}, u32[]{:S(2)}) collective-permute-start(bf16[512,128]{1,0:T(8,128)(2,1)S(1)} %get-tuple-element.42.refs_4_), channel_id=1, source_target_pairs={{0,16},{2,18},{4,20},{6,22},{8,24},{10,26},{12,28},{14,30},{16,0},... | collective-permute-start | bytes 393224 | tf_op jit(solution)/shard_map/ppermute | solution.py:320
  6.5 1.5 %collective-permute-start.1 = (bf16[512,128]{1,0:T(8,128)(2,1)S(1)}, bf16[512,128]{1,0:T(8,128)(2,1)S(1)}, u32[]{:S(2)}, u32[]{:S(2)}) collective-permute-start(bf16[512,128]{1,0:T(8,128)(2,1)S(1)} %get-tuple-element.43.refs_5_), channel_id=1, source_target_pairs={{0,2},{2,0},{4,6},{6,4},{8,10},{10,8},{12,14},{14,12},{16,18},{18,... | collective-permute-start | bytes 393224 | tf_op jit(solution)/shard_map/ppermute | solution.py:320
  7.9 0.0 collective-permute-start.2
  8.0 1.8 %collective-permute-start.3 = (bf16[512,128]{1,0:T(8,128)(2,1)S(1)}, bf16[512,128]{1,0:T(8,128)(2,1)S(1)}, u32[]{:S(2)}, u32[]{:S(2)}) collective-permute-start(bf16[512,128]{1,0:T(8,128)(2,1)S(1)} %get-tuple-element.45.refs_7_), channel_id=1, source_target_pairs={{0,4},{2,6},{4,0},{6,2},{8,12},{10,14},{12,8},{14,10},{16,20},{18,... | collective-permute-start | bytes 393224 | tf_op jit(solution)/shard_map/ppermute | solution.py:320
  9.8 2.5 %collective-permute-start.4 = (bf16[512,128]{1,0:T(8,128)(2,1)S(1)}, bf16[512,128]{1,0:T(8,128)(2,1)S(1)}, u32[]{:S(2)}, u32[]{:S(2)}) collective-permute-start(bf16[512,128]{1,0:T(8,128)(2,1)S(1)} %get-tuple-element.46.refs_8_), channel_id=1, source_target_pairs={{0,20},{2,22},{4,16},{6,18},{8,28},{10,30},{12,24},{14,26},{16,4},... | collective-permute-start | bytes 393224 | tf_op jit(solution)/shard_map/ppermute | solution.py:320
  12.3 1.8 %pack.3 = (bf16[512,128]{1,0:T(8,128)(2,1)S(1)}, bf16[512,128]{1,0:T(8,128)(2,1)S(1)}, bf16[512,128]{1,0:T(8,128)(2,1)S(1)}, bf16[512,128]{1,0:T(8,128)(2,1)S(1)...) custom-call(s32[4,16]{1,0:T(4,128)} %bitcast.24, ...), custom_call_target="tpu_custom_call" | custom-call | bytes 2883584 | tf_op jit(solution)/shard_map/pack/pallas_call | solution.py:280
  14.1 4.7 %first.1 = (bf16[16,4096]{1,0:T(8,128)(2,1)S(1)}, bf16[1024,4096]{1,0:T(8,128)(2,1)S(1)}) custom-call(s32[16]{0:T(128)} %refs_0_.1, s32[16]{0:T(128)} %refs_1_.5, bf16[16,8,128]{2,1,0:T(8,128)(2,1)} %refs_2_.5, bf16[1024,4096]{1,0:T(8,128)(2,1)} %refs_3_.5, bf16[512,128]{1,0:T(8,128)(2,1)S(1)} %get-tuple-element.42.refs_4_, ...), custom_call_target="tpu_custom_call" | custom-call | flops 150994944 | bytes 10485760 | tf_op jit(solution)/shard_map/first/pallas_call | solution.py:323
  18.7 0.5 collective-permute-done.refs_1_
  19.2 2.8 %collective-permute-start.5 = (bf16[512,128]{1,0:T(8,128)(2,1)S(1)}, bf16[512,128]{1,0:T(8,128)(2,1)S(1)}, u32[]{:S(2)}, u32[]{:S(2)}) collective-permute-start(bf16[512,128]{1,0:T(8,128)(2,1)S(1)} %get-tuple-element.59.refs_9_), channel_id=1, source_target_pairs={{0,6},{2,4},{4,2},{6,0},{8,14},{10,12},{12,10},{14,8},{16,22},{18,... | collective-permute-start | bytes 393224 | tf_op jit(solution)/shard_map/ppermute | solution.py:320
  22.0 0.0 collective-permute-done.1.refs_2_
  22.0 0.0 collective-permute-start.6
  22.0 1.3 %collective-permute-done.2.refs_3_ = bf16[512,128]{1,0:T(8,128)(2,1)S(1)} collective-permute-done((bf16[512,128]{1,0:T(8,128)(2,1)S(1)}, bf16[512,128]{1,0:T(8,128)(2,1)S(1)}, u32[]{:S(2)}, u32[]{:S(2)}) %collective-permute-start.2) | collective-permute-done | bytes 131104 | tf_op jit(solution)/shard_map/ppermute | solution.py:320
  23.3 1.7 %collective-permute-start.7 = (bf16[512,128]{1,0:T(8,128)(2,1)S(1)}, bf16[512,128]{1,0:T(8,128)(2,1)S(1)}, u32[]{:S(2)}, u32[]{:S(2)}) collective-permute-start(bf16[512,128]{1,0:T(8,128)(2,1)S(1)} %get-tuple-element.61.refs_11_), channel_id=1, source_target_pairs={{0,8},{2,10},{4,12},{6,14},{8,0},{10,2},{12,4},{14,6},{16,24},{18,... | collective-permute-start | bytes 393224 | tf_op jit(solution)/shard_map/ppermute | solution.py:320
  24.9 0.0 collective-permute-done.3.refs_4_
  24.9 2.2 %collective-permute-start.8 = (bf16[512,128]{1,0:T(8,128)(2,1)S(1)}, bf16[512,128]{1,0:T(8,128)(2,1)S(1)}, u32[]{:S(2)}, u32[]{:S(2)}) collective-permute-start(bf16[512,128]{1,0:T(8,128)(2,1)S(1)} %get-tuple-element.62.refs_12_), channel_id=1, source_target_pairs={{0,24},{2,26},{4,28},{6,30},{8,16},{10,18},{12,20},{14,22},{16,8},... | collective-permute-start | bytes 393224 | tf_op jit(solution)/shard_map/ppermute | solution.py:320
  27.2 0.5 collective-permute-done.4.refs_5_
  27.7 1.0 %collective-permute-start.9 = (bf16[512,128]{1,0:T(8,128)(2,1)S(1)}, bf16[512,128]{1,0:T(8,128)(2,1)S(1)}, u32[]{:S(2)}, u32[]{:S(2)}) collective-permute-start(bf16[512,128]{1,0:T(8,128)(2,1)S(1)} %get-tuple-element.63.refs_13_), channel_id=1, source_target_pairs={{0,10},{2,8},{4,14},{6,12},{8,2},{10,0},{12,6},{14,4},{16,26},{18,... | collective-permute-start | bytes 393224 | tf_op jit(solution)/shard_map/ppermute | solution.py:320
  28.7 0.0 collective-permute-done.5.refs_6_
  28.7 3.7 %collective-permute-start.11 = (bf16[512,128]{1,0:T(8,128)(2,1)S(1)}, bf16[512,128]{1,0:T(8,128)(2,1)S(1)}, u32[]{:S(2)}, u32[]{:S(2)}) collective-permute-start(bf16[512,128]{1,0:T(8,128)(2,1)S(1)} %get-tuple-element.66.refs_14_), channel_id=1, source_target_pairs={{0,26},{2,24},{4,30},{6,28},{8,18},{10,16},{12,22},{14,20},{16,10}... | collective-permute-start | bytes 393224 | tf_op jit(solution)/shard_map/ppermute | solution.py:320
  32.4 1.3 %collective-permute-done.6.refs_7_ = bf16[512,128]{1,0:T(8,128)(2,1)S(1)} collective-permute-done((bf16[512,128]{1,0:T(8,128)(2,1)S(1)}, bf16[512,128]{1,0:T(8,128)(2,1)S(1)}, u32[]{:S(2)}, u32[]{:S(2)}) %collective-permute-start.6) | collective-permute-done | bytes 131104 | tf_op jit(solution)/shard_map/ppermute | solution.py:320
  33.8 0.8 %collective-permute-start.12 = (bf16[512,128]{1,0:T(8,128)(2,1)S(1)}, bf16[512,128]{1,0:T(8,128)(2,1)S(1)}, u32[]{:S(2)}, u32[]{:S(2)}) collective-permute-start(bf16[512,128]{1,0:T(8,128)(2,1)S(1)} %get-tuple-element.67.refs_15_), channel_id=1, source_target_pairs={{0,12},{2,14},{4,8},{6,10},{8,4},{10,6},{12,0},{14,2},{16,28},{18,... | collective-permute-start | bytes 393224 | tf_op jit(solution)/shard_map/ppermute | solution.py:320
  34.6 0.0 collective-permute-done.7.refs_8_
  34.6 8.4 %collective-permute-start.13 = (bf16[512,128]{1,0:T(8,128)(2,1)S(1)}, bf16[512,128]{1,0:T(8,128)(2,1)S(1)}, u32[]{:S(2)}, u32[]{:S(2)}) collective-permute-start(bf16[512,128]{1,0:T(8,128)(2,1)S(1)} %get-tuple-element.68.refs_16_), channel_id=1, source_target_pairs={{0,28},{2,30},{4,24},{6,26},{8,20},{10,22},{12,16},{14,18},{16,12}... | collective-permute-start | bytes 393224 | tf_op jit(solution)/shard_map/ppermute | solution.py:320
  43.0 0.0 collective-permute-done.8.refs_9_
  43.0 0.0 collective-permute-start.14
  43.0 0.0 collective-permute-done.9.refs_10_
  43.0 3.7 %collective-permute-start.15 = (bf16[512,128]{1,0:T(8,128)(2,1)S(1)}, bf16[512,128]{1,0:T(8,128)(2,1)S(1)}, u32[]{:S(2)}, u32[]{:S(2)}) collective-permute-start(bf16[512,128]{1,0:T(8,128)(2,1)S(1)} %get-tuple-element.70.refs_18_), channel_id=1, source_target_pairs={{0,30},{2,28},{4,26},{6,24},{8,22},{10,20},{12,18},{14,16},{16,14}... | collective-permute-start | bytes 393224 | tf_op jit(solution)/shard_map/ppermute | solution.py:320
  46.7 2.3 %early.1 = (bf16[16,256,128]{2,1,0:T(8,128)(2,1)}, bf16[16,256,128]{2,1,0:T(8,128)(2,1)}, f32[16,8,128]{2,1,0:T(8,128)S(1)}, bf16[16,8,128]{2,1,0:T(8,128)(2,1)S...) custom-call(bf16[512,128]{1,0:T(8,128)(2,1)S(1)} %get-tuple-element.57.refs_19_.refs_0_, ...), custom_call_target="tpu_custom_call" | custom-call | flops 11534336 | bytes 2883584 | tf_op jit(solution)/shard_map/early/pallas_call | solution.py:349
  49.0 0.0 collective-permute-done.11.refs_0_
  49.0 0.1 collective-permute-start.10
  49.1 0.0 collective-permute-done.12.refs_1_
  49.1 0.0 collective-permute-done.13.refs_2_
  49.1 3.8 %collective-permute-done.14.refs_3_ = bf16[512,128]{1,0:T(8,128)(2,1)S(1)} collective-permute-done((bf16[512,128]{1,0:T(8,128)(2,1)S(1)}, bf16[512,128]{1,0:T(8,128)(2,1)S(1)}, u32[]{:S(2)}, u32[]{:S(2)}) %collective-permute-start.14) | collective-permute-done | bytes 131104 | tf_op jit(solution)/shard_map/ppermute | solution.py:320
  52.9 0.0 collective-permute-done.15.refs_4_
  52.9 2.0 %late.1 = (bf16[16,4096]{1,0:T(8,128)(2,1)S(1)}, bf16[16,256,128]{2,1,0:T(8,128)(2,1)}, bf16[16,256,128]{2,1,0:T(8,128)(2,1)}) custom-call(bf16[512,128]{1,0:T(8,128)(2,1)S(1)} %collective-permute-done.11.refs_0_, bf16[512,128]{1,0:T(8,128)(2,1)S(1)} %collective-permute-done.12.refs_1_, ...), custom_call_target="tpu_custom_call", output_to_operand_aliasing={{1}: (10, {}), {2}: (11, {})} | custom-call | flops 150994944 | bytes 10485760 | tf_op jit(solution)/shard_map/late/pallas_call | solution.py:375
  54.9 0.1 collective-permute-start.16
  55.0 0.0 collective-permute-done.10
  55.0 0.7 %add_convert_fusion.1 = bf16[16,4096]{1,0:T(8,128)(2,1)} fusion(bf16[16,4096]{1,0:T(8,128)(2,1)S(1)} %collective-permute-done.10, bf16[16,4096]{1,0:T(8,128)(2,1)S(1)} %get-tuple-element.65), kind=kLoop, calls=%fused_computation.1 | loop fusion | flops 262144 | bytes 393216 | tf_op jit(solution)/shard_map/convert_element_type | solution.py:209
  55.7 0.6 %collective-permute-done.16 = bf16[16,4096]{1,0:T(8,128)(2,1)S(1)} collective-permute-done((bf16[16,4096]{1,0:T(8,128)(2,1)S(1)}, bf16[16,4096]{1,0:T(8,128)(2,1)S(1)}, u32[]{:S(2)}, u32[]{:S(2)}) %collective-permute-start.16) | collective-permute-done | bytes 131104 | tf_op jit(solution)/shard_map/ppermute | solution.py:208
  56.3 0.7 %add_convert_fusion = bf16[16,4096]{1,0:T(8,128)(2,1)} fusion(bf16[16,4096]{1,0:T(8,128)(2,1)S(1)} %collective-permute-done.16, bf16[16,4096]{1,0:T(8,128)(2,1)S(1)} %get-tuple-element.77), kind=kLoop, calls=%fused_computation | loop fusion | flops 262144 | bytes 393216 | tf_op jit(solution)/shard_map/convert_element_type | solution.py:209
Async XLA Ops:
  2.3 16.9 %collective-permute-start = (bf16[512,128]{1,0:T(8,128)(2,1)S(1)}, bf16[512,128]{1,0:T(8,128)(2,1)S(1)}, u32[]{:S(2)}, u32[]{:S(2)}) collective-permute-start(bf16[512,128]{1,0:T(8,128)(2,1)S(1)} %get-tuple-element.42.refs_4_), channel_id=1, source_target_pairs={{0,16},{2,18},{4,20},{6,22},{8,24},{10,26},{12,28},{14,30},{16,0},... | collective-permute-start | bytes 393224 | tf_op jit(solution)/shard_map/ppermute | solution.py:320
  6.5 15.5 %collective-permute-start.1 = (bf16[512,128]{1,0:T(8,128)(2,1)S(1)}, bf16[512,128]{1,0:T(8,128)(2,1)S(1)}, u32[]{:S(2)}, u32[]{:S(2)}) collective-permute-start(bf16[512,128]{1,0:T(8,128)(2,1)S(1)} %get-tuple-element.43.refs_5_), channel_id=1, source_target_pairs={{0,2},{2,0},{4,6},{6,4},{8,10},{10,8},{12,14},{14,12},{16,18},{18,... | collective-permute-start | bytes 393224 | tf_op jit(solution)/shard_map/ppermute | solution.py:320
  7.9 15.3 %collective-permute-start.2 = (bf16[512,128]{1,0:T(8,128)(2,1)S(1)}, bf16[512,128]{1,0:T(8,128)(2,1)S(1)}, u32[]{:S(2)}, u32[]{:S(2)}) collective-permute-start(bf16[512,128]{1,0:T(8,128)(2,1)S(1)} %get-tuple-element.44.refs_6_), channel_id=1, source_target_pairs={{0,18},{2,16},{4,22},{6,20},{8,26},{10,24},{12,30},{14,28},{16,2},... | collective-permute-start | bytes 393224 | tf_op jit(solution)/shard_map/ppermute | solution.py:320
  8.0 16.9 %collective-permute-start.3 = (bf16[512,128]{1,0:T(8,128)(2,1)S(1)}, bf16[512,128]{1,0:T(8,128)(2,1)S(1)}, u32[]{:S(2)}, u32[]{:S(2)}) collective-permute-start(bf16[512,128]{1,0:T(8,128)(2,1)S(1)} %get-tuple-element.45.refs_7_), channel_id=1, source_target_pairs={{0,4},{2,6},{4,0},{6,2},{8,12},{10,14},{12,8},{14,10},{16,20},{18,... | collective-permute-start | bytes 393224 | tf_op jit(solution)/shard_map/ppermute | solution.py:320
  9.8 17.9 %collective-permute-start.4 = (bf16[512,128]{1,0:T(8,128)(2,1)S(1)}, bf16[512,128]{1,0:T(8,128)(2,1)S(1)}, u32[]{:S(2)}, u32[]{:S(2)}) collective-permute-start(bf16[512,128]{1,0:T(8,128)(2,1)S(1)} %get-tuple-element.46.refs_8_), channel_id=1, source_target_pairs={{0,20},{2,22},{4,16},{6,18},{8,28},{10,30},{12,24},{14,26},{16,4},... | collective-permute-start | bytes 393224 | tf_op jit(solution)/shard_map/ppermute | solution.py:320
  19.2 9.5 %collective-permute-start.5 = (bf16[512,128]{1,0:T(8,128)(2,1)S(1)}, bf16[512,128]{1,0:T(8,128)(2,1)S(1)}, u32[]{:S(2)}, u32[]{:S(2)}) collective-permute-start(bf16[512,128]{1,0:T(8,128)(2,1)S(1)} %get-tuple-element.59.refs_9_), channel_id=1, source_target_pairs={{0,6},{2,4},{4,2},{6,0},{8,14},{10,12},{12,10},{14,8},{16,22},{18,... | collective-permute-start | bytes 393224 | tf_op jit(solution)/shard_map/ppermute | solution.py:320
  22.0 11.8 %collective-permute-start.6 = (bf16[512,128]{1,0:T(8,128)(2,1)S(1)}, bf16[512,128]{1,0:T(8,128)(2,1)S(1)}, u32[]{:S(2)}, u32[]{:S(2)}) collective-permute-start(bf16[512,128]{1,0:T(8,128)(2,1)S(1)} %get-tuple-element.60.refs_10_), channel_id=1, source_target_pairs={{0,22},{2,20},{4,18},{6,16},{8,30},{10,28},{12,26},{14,24},{16,6},... | collective-permute-start | bytes 393224 | tf_op jit(solution)/shard_map/ppermute | solution.py:320
  23.3 11.3 %collective-permute-start.7 = (bf16[512,128]{1,0:T(8,128)(2,1)S(1)}, bf16[512,128]{1,0:T(8,128)(2,1)S(1)}, u32[]{:S(2)}, u32[]{:S(2)}) collective-permute-start(bf16[512,128]{1,0:T(8,128)(2,1)S(1)} %get-tuple-element.61.refs_11_), channel_id=1, source_target_pairs={{0,8},{2,10},{4,12},{6,14},{8,0},{10,2},{12,4},{14,6},{16,24},{18,... | collective-permute-start | bytes 393224 | tf_op jit(solution)/shard_map/ppermute | solution.py:320
  24.9 18.0 %collective-permute-start.8 = (bf16[512,128]{1,0:T(8,128)(2,1)S(1)}, bf16[512,128]{1,0:T(8,128)(2,1)S(1)}, u32[]{:S(2)}, u32[]{:S(2)}) collective-permute-start(bf16[512,128]{1,0:T(8,128)(2,1)S(1)} %get-tuple-element.62.refs_12_), channel_id=1, source_target_pairs={{0,24},{2,26},{4,28},{6,30},{8,16},{10,18},{12,20},{14,22},{16,8},... | collective-permute-start | bytes 393224 | tf_op jit(solution)/shard_map/ppermute | solution.py:320
  27.7 15.3 %collective-permute-start.9 = (bf16[512,128]{1,0:T(8,128)(2,1)S(1)}, bf16[512,128]{1,0:T(8,128)(2,1)S(1)}, u32[]{:S(2)}, u32[]{:S(2)}) collective-permute-start(bf16[512,128]{1,0:T(8,128)(2,1)S(1)} %get-tuple-element.63.refs_13_), channel_id=1, source_target_pairs={{0,10},{2,8},{4,14},{6,12},{8,2},{10,0},{12,6},{14,4},{16,26},{18,... | collective-permute-start | bytes 393224 | tf_op jit(solution)/shard_map/ppermute | solution.py:320
  28.7 20.3 %collective-permute-start.11 = (bf16[512,128]{1,0:T(8,128)(2,1)S(1)}, bf16[512,128]{1,0:T(8,128)(2,1)S(1)}, u32[]{:S(2)}, u32[]{:S(2)}) collective-permute-start(bf16[512,128]{1,0:T(8,128)(2,1)S(1)} %get-tuple-element.66.refs_14_), channel_id=1, source_target_pairs={{0,26},{2,24},{4,30},{6,28},{8,18},{10,16},{12,22},{14,20},{16,10}... | collective-permute-start | bytes 393224 | tf_op jit(solution)/shard_map/ppermute | solution.py:320
  33.8 15.3 %collective-permute-start.12 = (bf16[512,128]{1,0:T(8,128)(2,1)S(1)}, bf16[512,128]{1,0:T(8,128)(2,1)S(1)}, u32[]{:S(2)}, u32[]{:S(2)}) collective-permute-start(bf16[512,128]{1,0:T(8,128)(2,1)S(1)} %get-tuple-element.67.refs_15_), channel_id=1, source_target_pairs={{0,12},{2,14},{4,8},{6,10},{8,4},{10,6},{12,0},{14,2},{16,28},{18,... | collective-permute-start | bytes 393224 | tf_op jit(solution)/shard_map/ppermute | solution.py:320
  34.6 14.5 %collective-permute-start.13 = (bf16[512,128]{1,0:T(8,128)(2,1)S(1)}, bf16[512,128]{1,0:T(8,128)(2,1)S(1)}, u32[]{:S(2)}, u32[]{:S(2)}) collective-permute-start(bf16[512,128]{1,0:T(8,128)(2,1)S(1)} %get-tuple-element.68.refs_16_), channel_id=1, source_target_pairs={{0,28},{2,30},{4,24},{6,26},{8,20},{10,22},{12,16},{14,18},{16,12}... | collective-permute-start | bytes 393224 | tf_op jit(solution)/shard_map/ppermute | solution.py:320
  43.0 9.9 %collective-permute-start.14 = (bf16[512,128]{1,0:T(8,128)(2,1)S(1)}, bf16[512,128]{1,0:T(8,128)(2,1)S(1)}, u32[]{:S(2)}, u32[]{:S(2)}) collective-permute-start(bf16[512,128]{1,0:T(8,128)(2,1)S(1)} %get-tuple-element.69.refs_17_), channel_id=1, source_target_pairs={{0,14},{2,12},{4,10},{6,8},{8,6},{10,4},{12,2},{14,0},{16,30},{18,... | collective-permute-start | bytes 393224 | tf_op jit(solution)/shard_map/ppermute | solution.py:320
  43.0 9.9 %collective-permute-start.15 = (bf16[512,128]{1,0:T(8,128)(2,1)S(1)}, bf16[512,128]{1,0:T(8,128)(2,1)S(1)}, u32[]{:S(2)}, u32[]{:S(2)}) collective-permute-start(bf16[512,128]{1,0:T(8,128)(2,1)S(1)} %get-tuple-element.70.refs_18_), channel_id=1, source_target_pairs={{0,30},{2,28},{4,26},{6,24},{8,22},{10,20},{12,18},{14,16},{16,14}... | collective-permute-start | bytes 393224 | tf_op jit(solution)/shard_map/ppermute | solution.py:320
  49.0 6.0 %collective-permute-start.10 = (bf16[16,4096]{1,0:T(8,128)(2,1)S(1)}, bf16[16,4096]{1,0:T(8,128)(2,1)S(1)}, u32[]{:S(2)}, u32[]{:S(2)}) collective-permute-start(bf16[16,4096]{1,0:T(8,128)(2,1)S(1)} %get-tuple-element.65), channel_id=1, source_target_pairs={{0,1},{1,0},{2,3},{3,2},{4,5},{5,4},{6,7},{7,6},{8,9},{9,8},{10,11... | collective-permute-start | bytes 393224 | tf_op jit(solution)/shard_map/ppermute | solution.py:208
  54.9 1.4 %collective-permute-start.16 = (bf16[16,4096]{1,0:T(8,128)(2,1)S(1)}, bf16[16,4096]{1,0:T(8,128)(2,1)S(1)}, u32[]{:S(2)}, u32[]{:S(2)}) collective-permute-start(bf16[16,4096]{1,0:T(8,128)(2,1)S(1)} %get-tuple-element.77), channel_id=1, source_target_pairs={{0,1},{1,0},{2,3},{3,2},{4,5},{5,4},{6,7},{7,6},{8,9},{9,8},{10,11... | collective-permute-start | bytes 393224 | tf_op jit(solution)/shard_map/ppermute | solution.py:208

commit v16 on v15

--- a/solution.py
+++ b/solution.py
@@ -222,6 +222,8 @@
     half = n // 2
     crossing = list(range(half, n))
     staying = list(range(1, half))
+    for queue, at in ((crossing, half // 2), (staying, half // 4)):
+        queue[at], queue[-1] = queue[-1], queue[at]
     order = []
     for kind in "cncncncncncncnc":
         queue = crossing if kind == "c" else staying

time: 57.3 us -> 56.2 us (0.981)
  starting transfers between devices: 34.4 us -> 31.5 us
  waiting for transfers between devices: 8.01 us -> 9.87 us
    ppermute x15, starting transfers between devices: 34.3 us -> 31.4 us  [send(): return lax.ppermute(block, 'inst', [(d, d ^ steps[i]) for d in range(n)])]
    ppermute x15, waiting for transfers between devices: 7.37 us -> 9.24 us  [send(): return lax.ppermute(block, 'inst', [(d, d ^ steps[i]) for d in range(n)])]
where the time goes in v16:
time: 56.2 us; the launch traced here: 56 us
  starting transfers between devices  31.5 us (56%)
  Pallas kernels  12.5 us (22%)
  waiting for transfers between devices  9.87 us (18%)
  other arithmetic  1.38 us (2%)
  between operations  0.71 us (1%)
    ppermute x15, starting transfers between devices, send(): return lax.ppermute(block, 'inst', [(d, d ^ steps[i]) for d in range(n)])  31.4 us
    ppermute x15, waiting for transfers between devices, send(): return lax.ppermute(block, 'inst', [(d, d ^ steps[i]) for d in range(n)])  9.24 us
    pallas_call x1, Pallas kernels, shards(): pl.pallas_call(functools.partial(first_kernel, steps, span), out_shape=[j...  4.66 us
    pallas_call x2, Pallas kernels, pack(): pl.pallas_call(functools.partial(pack_kernel, n, chosen, pages), out_shap...  3.48 us
    pallas_call x1, Pallas kernels, shards(): pl.pallas_call(functools.partial(early_kernel, some, span), out_shape=[ca...  2.31 us
    pallas_call x1, Pallas kernels, shards(): pl.pallas_call(functools.partial(late_kernel, LATE, span), out_shape=[jax...  2.02 us
    convert_element_type x2, other arithmetic, total(): (partial.astype(jnp.float32) + other.astype(jnp.float32)).astype(jnp.bflo...  1.38 us
  transfers between devices with their start and end apart: 17, of which 6 were waited for; matrix products, arithmetic and copies ran while one was open for 1% of the time, Pallas kernels for 19%

profile of v16, /device:TPU:0, one launch (start us, length us, event | category | flops | bytes accessed | tf_op | source)
XLA Modules:
  0.0 56.0 jit_solution(17824203399129135395)
XLA Ops:
  0.6 1.7 %pack.2 = (bf16[512,128]{1,0:T(8,128)(2,1)S(1)}, bf16[512,128]{1,0:T(8,128)(2,1)S(1)}, bf16[512,128]{1,0:T(8,128)(2,1)S(1)}, bf16[512,128]{1,0:T(8,128)(2,1)S(1)}, bf16[512,128]{1,0:T(8,128)(2,1)S(1)}) custom-call(s32[4,16]{1,0:T(4,128)} %bitcast.23, s32[16]{0:T(128)} %refs_0_.1, s32[16]{0:T(128)} %refs_1_.5, s32[16]{0:T(128)} %refs_3_.4, ...), custom_call_target="tpu_custom_call" | custom-call | bytes 1310720 | tf_op jit(solution)/shard_map/pack/pallas_call | solution.py:282
  2.3 4.1 %collective-permute-start = (bf16[512,128]{1,0:T(8,128)(2,1)S(1)}, bf16[512,128]{1,0:T(8,128)(2,1)S(1)}, u32[]{:S(2)}, u32[]{:S(2)}) collective-permute-start(bf16[512,128]{1,0:T(8,128)(2,1)S(1)} %get-tuple-element.42.refs_4_), channel_id=1, source_target_pairs={{0,16},{2,18},{4,20},{6,22},{8,24},{10,26},{12,28},{14,30},{16,0},... | collective-permute-start | bytes 393224 | tf_op jit(solution)/shard_map/ppermute | solution.py:322
  6.5 1.5 %collective-permute-start.1 = (bf16[512,128]{1,0:T(8,128)(2,1)S(1)}, bf16[512,128]{1,0:T(8,128)(2,1)S(1)}, u32[]{:S(2)}, u32[]{:S(2)}) collective-permute-start(bf16[512,128]{1,0:T(8,128)(2,1)S(1)} %get-tuple-element.43.refs_5_), channel_id=1, source_target_pairs={{0,2},{2,0},{4,6},{6,4},{8,10},{10,8},{12,14},{14,12},{16,18},{18,... | collective-permute-start | bytes 393224 | tf_op jit(solution)/shard_map/ppermute | solution.py:322
  7.9 0.0 collective-permute-start.2
  8.0 1.8 %collective-permute-start.3 = (bf16[512,128]{1,0:T(8,128)(2,1)S(1)}, bf16[512,128]{1,0:T(8,128)(2,1)S(1)}, u32[]{:S(2)}, u32[]{:S(2)}) collective-permute-start(bf16[512,128]{1,0:T(8,128)(2,1)S(1)} %get-tuple-element.45.refs_7_), channel_id=1, source_target_pairs={{0,4},{2,6},{4,0},{6,2},{8,12},{10,14},{12,8},{14,10},{16,20},{18,... | collective-permute-start | bytes 393224 | tf_op jit(solution)/shard_map/ppermute | solution.py:322
  9.8 2.5 %collective-permute-start.4 = (bf16[512,128]{1,0:T(8,128)(2,1)S(1)}, bf16[512,128]{1,0:T(8,128)(2,1)S(1)}, u32[]{:S(2)}, u32[]{:S(2)}) collective-permute-start(bf16[512,128]{1,0:T(8,128)(2,1)S(1)} %get-tuple-element.46.refs_8_), channel_id=1, source_target_pairs={{0,20},{2,22},{4,16},{6,18},{8,28},{10,30},{12,24},{14,26},{16,4},... | collective-permute-start | bytes 393224 | tf_op jit(solution)/shard_map/ppermute | solution.py:322
  12.3 1.8 %pack.3 = (bf16[512,128]{1,0:T(8,128)(2,1)S(1)}, bf16[512,128]{1,0:T(8,128)(2,1)S(1)}, bf16[512,128]{1,0:T(8,128)(2,1)S(1)}, bf16[512,128]{1,0:T(8,128)(2,1)S(1)...) custom-call(s32[4,16]{1,0:T(4,128)} %bitcast.24, ...), custom_call_target="tpu_custom_call" | custom-call | bytes 2883584 | tf_op jit(solution)/shard_map/pack/pallas_call | solution.py:282
  14.1 4.7 %first.1 = (bf16[16,4096]{1,0:T(8,128)(2,1)S(1)}, bf16[1024,4096]{1,0:T(8,128)(2,1)S(1)}) custom-call(s32[16]{0:T(128)} %refs_0_.1, s32[16]{0:T(128)} %refs_1_.5, bf16[16,8,128]{2,1,0:T(8,128)(2,1)} %refs_2_.5, bf16[1024,4096]{1,0:T(8,128)(2,1)} %refs_3_.5, bf16[512,128]{1,0:T(8,128)(2,1)S(1)} %get-tuple-element.42.refs_4_, ...), custom_call_target="tpu_custom_call" | custom-call | flops 150994944 | bytes 10485760 | tf_op jit(solution)/shard_map/first/pallas_call | solution.py:325
  18.7 0.5 collective-permute-done.refs_1_
  19.2 3.1 %collective-permute-start.5 = (bf16[512,128]{1,0:T(8,128)(2,1)S(1)}, bf16[512,128]{1,0:T(8,128)(2,1)S(1)}, u32[]{:S(2)}, u32[]{:S(2)}) collective-permute-start(bf16[512,128]{1,0:T(8,128)(2,1)S(1)} %get-tuple-element.59.refs_9_), channel_id=1, source_target_pairs={{0,14},{2,12},{4,10},{6,8},{8,6},{10,4},{12,2},{14,0},{16,30},{18,... | collective-permute-start | bytes 393224 | tf_op jit(solution)/shard_map/ppermute | solution.py:322
  22.3 0.0 collective-permute-done.1.refs_2_
  22.3 2.1 %collective-permute-start.6 = (bf16[512,128]{1,0:T(8,128)(2,1)S(1)}, bf16[512,128]{1,0:T(8,128)(2,1)S(1)}, u32[]{:S(2)}, u32[]{:S(2)}) collective-permute-start(bf16[512,128]{1,0:T(8,128)(2,1)S(1)} %get-tuple-element.60.refs_10_), channel_id=1, source_target_pairs={{0,22},{2,20},{4,18},{6,16},{8,30},{10,28},{12,26},{14,24},{16,6},... | collective-permute-start | bytes 393224 | tf_op jit(solution)/shard_map/ppermute | solution.py:322
  24.4 0.0 collective-permute-done.2.refs_3_
  24.4 0.1 collective-permute-start.7
  24.5 0.0 collective-permute-done.3.refs_4_
  24.5 4.0 %collective-permute-start.8 = (bf16[512,128]{1,0:T(8,128)(2,1)S(1)}, bf16[512,128]{1,0:T(8,128)(2,1)S(1)}, u32[]{:S(2)}, u32[]{:S(2)}) collective-permute-start(bf16[512,128]{1,0:T(8,128)(2,1)S(1)} %get-tuple-element.62.refs_12_), channel_id=1, source_target_pairs={{0,30},{2,28},{4,26},{6,24},{8,22},{10,20},{12,18},{14,16},{16,14}... | collective-permute-start | bytes 393224 | tf_op jit(solution)/shard_map/ppermute | solution.py:322
  28.5 0.0 collective-permute-done.4.refs_5_
  28.5 0.3 collective-permute-start.9
  28.8 2.3 %collective-permute-done.5.refs_6_ = bf16[512,128]{1,0:T(8,128)(2,1)S(1)} collective-permute-done((bf16[512,128]{1,0:T(8,128)(2,1)S(1)}, bf16[512,128]{1,0:T(8,128)(2,1)S(1)}, u32[]{:S(2)}, u32[]{:S(2)}) %collective-permute-start.5) | collective-permute-done | bytes 131104 | tf_op jit(solution)/shard_map/ppermute | solution.py:322
  31.0 3.5 %collective-permute-start.11 = (bf16[512,128]{1,0:T(8,128)(2,1)S(1)}, bf16[512,128]{1,0:T(8,128)(2,1)S(1)}, u32[]{:S(2)}, u32[]{:S(2)}) collective-permute-start(bf16[512,128]{1,0:T(8,128)(2,1)S(1)} %get-tuple-element.66.refs_14_), channel_id=1, source_target_pairs={{0,26},{2,24},{4,30},{6,28},{8,18},{10,16},{12,22},{14,20},{16,10}... | collective-permute-start | bytes 393224 | tf_op jit(solution)/shard_map/ppermute | solution.py:322
  34.5 0.0 collective-permute-done.6.refs_7_
  34.5 0.0 collective-permute-start.12
  34.5 2.2 %collective-permute-done.7.refs_8_ = bf16[512,128]{1,0:T(8,128)(2,1)S(1)} collective-permute-done((bf16[512,128]{1,0:T(8,128)(2,1)S(1)}, bf16[512,128]{1,0:T(8,128)(2,1)S(1)}, u32[]{:S(2)}, u32[]{:S(2)}) %collective-permute-start.7) | collective-permute-done | bytes 131104 | tf_op jit(solution)/shard_map/ppermute | solution.py:322
  36.8 3.6 %collective-permute-start.13 = (bf16[512,128]{1,0:T(8,128)(2,1)S(1)}, bf16[512,128]{1,0:T(8,128)(2,1)S(1)}, u32[]{:S(2)}, u32[]{:S(2)}) collective-permute-start(bf16[512,128]{1,0:T(8,128)(2,1)S(1)} %get-tuple-element.68.refs_16_), channel_id=1, source_target_pairs={{0,28},{2,30},{4,24},{6,26},{8,20},{10,22},{12,16},{14,18},{16,12}... | collective-permute-start | bytes 393224 | tf_op jit(solution)/shard_map/ppermute | solution.py:322
  40.3 0.0 collective-permute-done.8.refs_9_
  40.3 1.1 %collective-permute-start.14 = (bf16[512,128]{1,0:T(8,128)(2,1)S(1)}, bf16[512,128]{1,0:T(8,128)(2,1)S(1)}, u32[]{:S(2)}, u32[]{:S(2)}) collective-permute-start(bf16[512,128]{1,0:T(8,128)(2,1)S(1)} %get-tuple-element.69.refs_17_), channel_id=1, source_target_pairs={{0,6},{2,4},{4,2},{6,0},{8,14},{10,12},{12,10},{14,8},{16,22},{18,... | collective-permute-start | bytes 393224 | tf_op jit(solution)/shard_map/ppermute | solution.py:322
  41.5 0.3 collective-permute-done.9.refs_10_
  41.8 3.7 %collective-permute-start.15 = (bf16[512,128]{1,0:T(8,128)(2,1)S(1)}, bf16[512,128]{1,0:T(8,128)(2,1)S(1)}, u32[]{:S(2)}, u32[]{:S(2)}) collective-permute-start(bf16[512,128]{1,0:T(8,128)(2,1)S(1)} %get-tuple-element.70.refs_18_), channel_id=1, source_target_pairs={{0,24},{2,26},{4,28},{6,30},{8,16},{10,18},{12,20},{14,22},{16,8},... | collective-permute-start | bytes 393224 | tf_op jit(solution)/shard_map/ppermute | solution.py:322
  45.4 2.3 %early.1 = (bf16[16,256,128]{2,1,0:T(8,128)(2,1)}, bf16[16,256,128]{2,1,0:T(8,128)(2,1)}, f32[16,8,128]{2,1,0:T(8,128)S(1)}, bf16[16,8,128]{2,1,0:T(8,128)(2,1)S...) custom-call(bf16[512,128]{1,0:T(8,128)(2,1)S(1)} %get-tuple-element.57.refs_19_.refs_0_, ...), custom_call_target="tpu_custom_call" | custom-call | flops 11534336 | bytes 2883584 | tf_op jit(solution)/shard_map/early/pallas_call | solution.py:351
  47.8 0.0 collective-permute-done.11.refs_0_
  47.8 0.1 collective-permute-start.10
  47.9 4.0 %collective-permute-done.12.refs_1_ = bf16[512,128]{1,0:T(8,128)(2,1)S(1)} collective-permute-done((bf16[512,128]{1,0:T(8,128)(2,1)S(1)}, bf16[512,128]{1,0:T(8,128)(2,1)S(1)}, u32[]{:S(2)}, u32[]{:S(2)}) %collective-permute-start.12) | collective-permute-done | bytes 131104 | tf_op jit(solution)/shard_map/ppermute | solution.py:322
  51.8 0.0 collective-permute-done.13.refs_2_
  51.8 0.0 collective-permute-done.14.refs_3_
  51.8 0.0 collective-permute-done.15.refs_4_
  51.8 2.0 %late.1 = (bf16[16,4096]{1,0:T(8,128)(2,1)S(1)}, bf16[16,256,128]{2,1,0:T(8,128)(2,1)}, bf16[16,256,128]{2,1,0:T(8,128)(2,1)}) custom-call(bf16[512,128]{1,0:T(8,128)(2,1)S(1)} %collective-permute-done.11.refs_0_, bf16[512,128]{1,0:T(8,128)(2,1)S(1)} %collective-permute-done.12.refs_1_, ...), custom_call_target="tpu_custom_call", output_to_operand_aliasing={{1}: (10, {}), {2}: (11, {})} | custom-call | flops 150994944 | bytes 10485760 | tf_op jit(solution)/shard_map/late/pallas_call | solution.py:377
  53.9 0.1 collective-permute-start.16
  53.9 0.0 collective-permute-done.10
  53.9 0.7 %add_convert_fusion.1 = bf16[16,4096]{1,0:T(8,128)(2,1)} fusion(bf16[16,4096]{1,0:T(8,128)(2,1)S(1)} %collective-permute-done.10, bf16[16,4096]{1,0:T(8,128)(2,1)S(1)} %get-tuple-element.65), kind=kLoop, calls=%fused_computation.1 | loop fusion | flops 262144 | bytes 393216 | tf_op jit(solution)/shard_map/convert_element_type | solution.py:209
  54.6 0.6 %collective-permute-done.16 = bf16[16,4096]{1,0:T(8,128)(2,1)S(1)} collective-permute-done((bf16[16,4096]{1,0:T(8,128)(2,1)S(1)}, bf16[16,4096]{1,0:T(8,128)(2,1)S(1)}, u32[]{:S(2)}, u32[]{:S(2)}) %collective-permute-start.16) | collective-permute-done | bytes 131104 | tf_op jit(solution)/shard_map/ppermute | solution.py:208
  55.3 0.7 %add_convert_fusion = bf16[16,4096]{1,0:T(8,128)(2,1)} fusion(bf16[16,4096]{1,0:T(8,128)(2,1)S(1)} %collective-permute-done.16, bf16[16,4096]{1,0:T(8,128)(2,1)S(1)} %get-tuple-element.77), kind=kLoop, calls=%fused_computation | loop fusion | flops 262144 | bytes 393216 | tf_op jit(solution)/shard_map/convert_element_type | solution.py:209
Async XLA Ops:
  2.3 16.9 %collective-permute-start = (bf16[512,128]{1,0:T(8,128)(2,1)S(1)}, bf16[512,128]{1,0:T(8,128)(2,1)S(1)}, u32[]{:S(2)}, u32[]{:S(2)}) collective-permute-start(bf16[512,128]{1,0:T(8,128)(2,1)S(1)} %get-tuple-element.42.refs_4_), channel_id=1, source_target_pairs={{0,16},{2,18},{4,20},{6,22},{8,24},{10,26},{12,28},{14,30},{16,0},... | collective-permute-start | bytes 393224 | tf_op jit(solution)/shard_map/ppermute | solution.py:322
  6.5 15.8 %collective-permute-start.1 = (bf16[512,128]{1,0:T(8,128)(2,1)S(1)}, bf16[512,128]{1,0:T(8,128)(2,1)S(1)}, u32[]{:S(2)}, u32[]{:S(2)}) collective-permute-start(bf16[512,128]{1,0:T(8,128)(2,1)S(1)} %get-tuple-element.43.refs_5_), channel_id=1, source_target_pairs={{0,2},{2,0},{4,6},{6,4},{8,10},{10,8},{12,14},{14,12},{16,18},{18,... | collective-permute-start | bytes 393224 | tf_op jit(solution)/shard_map/ppermute | solution.py:322
  7.9 16.4 %collective-permute-start.2 = (bf16[512,128]{1,0:T(8,128)(2,1)S(1)}, bf16[512,128]{1,0:T(8,128)(2,1)S(1)}, u32[]{:S(2)}, u32[]{:S(2)}) collective-permute-start(bf16[512,128]{1,0:T(8,128)(2,1)S(1)} %get-tuple-element.44.refs_6_), channel_id=1, source_target_pairs={{0,18},{2,16},{4,22},{6,20},{8,26},{10,24},{12,30},{14,28},{16,2},... | collective-permute-start | bytes 393224 | tf_op jit(solution)/shard_map/ppermute | solution.py:322
  8.0 16.5 %collective-permute-start.3 = (bf16[512,128]{1,0:T(8,128)(2,1)S(1)}, bf16[512,128]{1,0:T(8,128)(2,1)S(1)}, u32[]{:S(2)}, u32[]{:S(2)}) collective-permute-start(bf16[512,128]{1,0:T(8,128)(2,1)S(1)} %get-tuple-element.45.refs_7_), channel_id=1, source_target_pairs={{0,4},{2,6},{4,0},{6,2},{8,12},{10,14},{12,8},{14,10},{16,20},{18,... | collective-permute-start | bytes 393224 | tf_op jit(solution)/shard_map/ppermute | solution.py:322
  9.8 18.7 %collective-permute-start.4 = (bf16[512,128]{1,0:T(8,128)(2,1)S(1)}, bf16[512,128]{1,0:T(8,128)(2,1)S(1)}, u32[]{:S(2)}, u32[]{:S(2)}) collective-permute-start(bf16[512,128]{1,0:T(8,128)(2,1)S(1)} %get-tuple-element.46.refs_8_), channel_id=1, source_target_pairs={{0,20},{2,22},{4,16},{6,18},{8,28},{10,30},{12,24},{14,26},{16,4},... | collective-permute-start | bytes 393224 | tf_op jit(solution)/shard_map/ppermute | solution.py:322
  19.2 11.8 %collective-permute-start.5 = (bf16[512,128]{1,0:T(8,128)(2,1)S(1)}, bf16[512,128]{1,0:T(8,128)(2,1)S(1)}, u32[]{:S(2)}, u32[]{:S(2)}) collective-permute-start(bf16[512,128]{1,0:T(8,128)(2,1)S(1)} %get-tuple-element.59.refs_9_), channel_id=1, source_target_pairs={{0,14},{2,12},{4,10},{6,8},{8,6},{10,4},{12,2},{14,0},{16,30},{18,... | collective-permute-start | bytes 393224 | tf_op jit(solution)/shard_map/ppermute | solution.py:322
  22.3 12.2 %collective-permute-start.6 = (bf16[512,128]{1,0:T(8,128)(2,1)S(1)}, bf16[512,128]{1,0:T(8,128)(2,1)S(1)}, u32[]{:S(2)}, u32[]{:S(2)}) collective-permute-start(bf16[512,128]{1,0:T(8,128)(2,1)S(1)} %get-tuple-element.60.refs_10_), channel_id=1, source_target_pairs={{0,22},{2,20},{4,18},{6,16},{8,30},{10,28},{12,26},{14,24},{16,6},... | collective-permute-start | bytes 393224 | tf_op jit(solution)/shard_map/ppermute | solution.py:322
  24.4 12.4 %collective-permute-start.7 = (bf16[512,128]{1,0:T(8,128)(2,1)S(1)}, bf16[512,128]{1,0:T(8,128)(2,1)S(1)}, u32[]{:S(2)}, u32[]{:S(2)}) collective-permute-start(bf16[512,128]{1,0:T(8,128)(2,1)S(1)} %get-tuple-element.61.refs_11_), channel_id=1, source_target_pairs={{0,8},{2,10},{4,12},{6,14},{8,0},{10,2},{12,4},{14,6},{16,24},{18,... | collective-permute-start | bytes 393224 | tf_op jit(solution)/shard_map/ppermute | solution.py:322
  24.5 15.9 %collective-permute-start.8 = (bf16[512,128]{1,0:T(8,128)(2,1)S(1)}, bf16[512,128]{1,0:T(8,128)(2,1)S(1)}, u32[]{:S(2)}, u32[]{:S(2)}) collective-permute-start(bf16[512,128]{1,0:T(8,128)(2,1)S(1)} %get-tuple-element.62.refs_12_), channel_id=1, source_target_pairs={{0,30},{2,28},{4,26},{6,24},{8,22},{10,20},{12,18},{14,16},{16,14}... | collective-permute-start | bytes 393224 | tf_op jit(solution)/shard_map/ppermute | solution.py:322
  28.5 13.3 %collective-permute-start.9 = (bf16[512,128]{1,0:T(8,128)(2,1)S(1)}, bf16[512,128]{1,0:T(8,128)(2,1)S(1)}, u32[]{:S(2)}, u32[]{:S(2)}) collective-permute-start(bf16[512,128]{1,0:T(8,128)(2,1)S(1)} %get-tuple-element.63.refs_13_), channel_id=1, source_target_pairs={{0,10},{2,8},{4,14},{6,12},{8,2},{10,0},{12,6},{14,4},{16,26},{18,... | collective-permute-start | bytes 393224 | tf_op jit(solution)/shard_map/ppermute | solution.py:322
  31.0 16.7 %collective-permute-start.11 = (bf16[512,128]{1,0:T(8,128)(2,1)S(1)}, bf16[512,128]{1,0:T(8,128)(2,1)S(1)}, u32[]{:S(2)}, u32[]{:S(2)}) collective-permute-start(bf16[512,128]{1,0:T(8,128)(2,1)S(1)} %get-tuple-element.66.refs_14_), channel_id=1, source_target_pairs={{0,26},{2,24},{4,30},{6,28},{8,18},{10,16},{12,22},{14,20},{16,10}... | collective-permute-start | bytes 393224 | tf_op jit(solution)/shard_map/ppermute | solution.py:322
  34.5 17.3 %collective-permute-start.12 = (bf16[512,128]{1,0:T(8,128)(2,1)S(1)}, bf16[512,128]{1,0:T(8,128)(2,1)S(1)}, u32[]{:S(2)}, u32[]{:S(2)}) collective-permute-start(bf16[512,128]{1,0:T(8,128)(2,1)S(1)} %get-tuple-element.67.refs_15_), channel_id=1, source_target_pairs={{0,12},{2,14},{4,8},{6,10},{8,4},{10,6},{12,0},{14,2},{16,28},{18,... | collective-permute-start | bytes 393224 | tf_op jit(solution)/shard_map/ppermute | solution.py:322
  36.8 15.1 %collective-permute-start.13 = (bf16[512,128]{1,0:T(8,128)(2,1)S(1)}, bf16[512,128]{1,0:T(8,128)(2,1)S(1)}, u32[]{:S(2)}, u32[]{:S(2)}) collective-permute-start(bf16[512,128]{1,0:T(8,128)(2,1)S(1)} %get-tuple-element.68.refs_16_), channel_id=1, source_target_pairs={{0,28},{2,30},{4,24},{6,26},{8,20},{10,22},{12,16},{14,18},{16,12}... | collective-permute-start | bytes 393224 | tf_op jit(solution)/shard_map/ppermute | solution.py:322
  40.3 11.5 %collective-permute-start.14 = (bf16[512,128]{1,0:T(8,128)(2,1)S(1)}, bf16[512,128]{1,0:T(8,128)(2,1)S(1)}, u32[]{:S(2)}, u32[]{:S(2)}) collective-permute-start(bf16[512,128]{1,0:T(8,128)(2,1)S(1)} %get-tuple-element.69.refs_17_), channel_id=1, source_target_pairs={{0,6},{2,4},{4,2},{6,0},{8,14},{10,12},{12,10},{14,8},{16,22},{18,... | collective-permute-start | bytes 393224 | tf_op jit(solution)/shard_map/ppermute | solution.py:322
  41.8 10.1 %collective-permute-start.15 = (bf16[512,128]{1,0:T(8,128)(2,1)S(1)}, bf16[512,128]{1,0:T(8,128)(2,1)S(1)}, u32[]{:S(2)}, u32[]{:S(2)}) collective-permute-start(bf16[512,128]{1,0:T(8,128)(2,1)S(1)} %get-tuple-element.70.refs_18_), channel_id=1, source_target_pairs={{0,24},{2,26},{4,28},{6,30},{8,16},{10,18},{12,20},{14,22},{16,8},... | collective-permute-start | bytes 393224 | tf_op jit(solution)/shard_map/ppermute | solution.py:322
  47.8 6.2 %collective-permute-start.10 = (bf16[16,4096]{1,0:T(8,128)(2,1)S(1)}, bf16[16,4096]{1,0:T(8,128)(2,1)S(1)}, u32[]{:S(2)}, u32[]{:S(2)}) collective-permute-start(bf16[16,4096]{1,0:T(8,128)(2,1)S(1)} %get-tuple-element.65), channel_id=1, source_target_pairs={{0,1},{1,0},{2,3},{3,2},{4,5},{5,4},{6,7},{7,6},{8,9},{9,8},{10,11... | collective-permute-start | bytes 393224 | tf_op jit(solution)/shard_map/ppermute | solution.py:208
  53.9 1.4 %collective-permute-start.16 = (bf16[16,4096]{1,0:T(8,128)(2,1)S(1)}, bf16[16,4096]{1,0:T(8,128)(2,1)S(1)}, u32[]{:S(2)}, u32[]{:S(2)}) collective-permute-start(bf16[16,4096]{1,0:T(8,128)(2,1)S(1)} %get-tuple-element.77), channel_id=1, source_target_pairs={{0,1},{1,0},{2,3},{3,2},{4,5},{5,4},{6,7},{7,6},{8,9},{9,8},{10,11... | collective-permute-start | bytes 393224 | tf_op jit(solution)/shard_map/ppermute | solution.py:208

commit v17 on v16

--- a/solution.py
+++ b/solution.py
@@ -224,6 +224,8 @@
     staying = list(range(1, half))
     for queue, at in ((crossing, half // 2), (staying, half // 4)):
         queue[at], queue[-1] = queue[-1], queue[at]
+    for queue, at in ((crossing, half // 4), (staying, half // 4 - 1)):
+        queue[at], queue[-2] = queue[-2], queue[at]
     order = []
     for kind in "cncncncncncncnc":
         queue = crossing if kind == "c" else staying

time: 56.2 us -> 56 us (level)
  starting transfers between devices: 31.5 us -> 26.9 us
  waiting for transfers between devices: 9.87 us -> 14.2 us
    ppermute x15, starting transfers between devices: 31.4 us -> 26.8 us  [send(): return lax.ppermute(block, 'inst', [(d, d ^ steps[i]) for d in range(n)])]
    ppermute x15, waiting for transfers between devices: 9.24 us -> 13.6 us  [send(): return lax.ppermute(block, 'inst', [(d, d ^ steps[i]) for d in range(n)])]
where the time goes in v17:
time: 56 us; the launch traced here: 55.7 us
  starting transfers between devices  26.9 us (48%)
  waiting for transfers between devices  14.2 us (25%)
  Pallas kernels  12.5 us (22%)
  other arithmetic  1.38 us (2%)
  between operations  0.73 us (1%)
    ppermute x15, starting transfers between devices, send(): return lax.ppermute(block, 'inst', [(d, d ^ steps[i]) for d in range(n)])  26.8 us
    ppermute x15, waiting for transfers between devices, send(): return lax.ppermute(block, 'inst', [(d, d ^ steps[i]) for d in range(n)])  13.6 us
    pallas_call x1, Pallas kernels, shards(): pl.pallas_call(functools.partial(first_kernel, steps, span), out_shape=[j...  4.66 us
    pallas_call x2, Pallas kernels, pack(): pl.pallas_call(functools.partial(pack_kernel, n, chosen, pages), out_shap...  3.48 us
    pallas_call x1, Pallas kernels, shards(): pl.pallas_call(functools.partial(early_kernel, some, span), out_shape=[ca...  2.31 us
    pallas_call x1, Pallas kernels, shards(): pl.pallas_call(functools.partial(late_kernel, LATE, span), out_shape=[jax...  2.02 us
    convert_element_type x2, other arithmetic, total(): (partial.astype(jnp.float32) + other.astype(jnp.float32)).astype(jnp.bflo...  1.38 us
  transfers between devices with their start and end apart: 17, of which 6 were waited for; matrix products, arithmetic and copies ran while one was open for 1% of the time, Pallas kernels for 19%

profile of v17, /device:TPU:0, one launch (start us, length us, event | category | flops | bytes accessed | tf_op | source)
XLA Modules:
  0.0 55.7 jit_solution(9594121827289145126)
XLA Ops:
  0.6 1.7 %pack.2 = (bf16[512,128]{1,0:T(8,128)(2,1)S(1)}, bf16[512,128]{1,0:T(8,128)(2,1)S(1)}, bf16[512,128]{1,0:T(8,128)(2,1)S(1)}, bf16[512,128]{1,0:T(8,128)(2,1)S(1)}, bf16[512,128]{1,0:T(8,128)(2,1)S(1)}) custom-call(s32[4,16]{1,0:T(4,128)} %bitcast.23, s32[16]{0:T(128)} %refs_0_.1, s32[16]{0:T(128)} %refs_1_.5, s32[16]{0:T(128)} %refs_3_.4, ...), custom_call_target="tpu_custom_call" | custom-call | bytes 1310720 | tf_op jit(solution)/shard_map/pack/pallas_call | solution.py:284
  2.3 4.1 %collective-permute-start = (bf16[512,128]{1,0:T(8,128)(2,1)S(1)}, bf16[512,128]{1,0:T(8,128)(2,1)S(1)}, u32[]{:S(2)}, u32[]{:S(2)}) collective-permute-start(bf16[512,128]{1,0:T(8,128)(2,1)S(1)} %get-tuple-element.42.refs_4_), channel_id=1, source_target_pairs={{0,16},{2,18},{4,20},{6,22},{8,24},{10,26},{12,28},{14,30},{16,0},... | collective-permute-start | bytes 393224 | tf_op jit(solution)/shard_map/ppermute | solution.py:324
  6.5 1.5 %collective-permute-start.1 = (bf16[512,128]{1,0:T(8,128)(2,1)S(1)}, bf16[512,128]{1,0:T(8,128)(2,1)S(1)}, u32[]{:S(2)}, u32[]{:S(2)}) collective-permute-start(bf16[512,128]{1,0:T(8,128)(2,1)S(1)} %get-tuple-element.43.refs_5_), channel_id=1, source_target_pairs={{0,2},{2,0},{4,6},{6,4},{8,10},{10,8},{12,14},{14,12},{16,18},{18,... | collective-permute-start | bytes 393224 | tf_op jit(solution)/shard_map/ppermute | solution.py:324
  7.9 0.0 collective-permute-start.2
  8.0 2.8 %collective-permute-start.3 = (bf16[512,128]{1,0:T(8,128)(2,1)S(1)}, bf16[512,128]{1,0:T(8,128)(2,1)S(1)}, u32[]{:S(2)}, u32[]{:S(2)}) collective-permute-start(bf16[512,128]{1,0:T(8,128)(2,1)S(1)} %get-tuple-element.45.refs_7_), channel_id=1, source_target_pairs={{0,12},{2,14},{4,8},{6,10},{8,4},{10,6},{12,0},{14,2},{16,28},{18,... | collective-permute-start | bytes 393224 | tf_op jit(solution)/shard_map/ppermute | solution.py:324
  10.8 2.4 %collective-permute-start.4 = (bf16[512,128]{1,0:T(8,128)(2,1)S(1)}, bf16[512,128]{1,0:T(8,128)(2,1)S(1)}, u32[]{:S(2)}, u32[]{:S(2)}) collective-permute-start(bf16[512,128]{1,0:T(8,128)(2,1)S(1)} %get-tuple-element.46.refs_8_), channel_id=1, source_target_pairs={{0,28},{2,30},{4,24},{6,26},{8,20},{10,22},{12,16},{14,18},{16,12}... | collective-permute-start | bytes 393224 | tf_op jit(solution)/shard_map/ppermute | solution.py:324
  13.2 1.8 %pack.3 = (bf16[512,128]{1,0:T(8,128)(2,1)S(1)}, bf16[512,128]{1,0:T(8,128)(2,1)S(1)}, bf16[512,128]{1,0:T(8,128)(2,1)S(1)}, bf16[512,128]{1,0:T(8,128)(2,1)S(1)...) custom-call(s32[4,16]{1,0:T(4,128)} %bitcast.24, ...), custom_call_target="tpu_custom_call" | custom-call | bytes 2883584 | tf_op jit(solution)/shard_map/pack/pallas_call | solution.py:284
  15.0 4.7 %first.1 = (bf16[16,4096]{1,0:T(8,128)(2,1)S(1)}, bf16[1024,4096]{1,0:T(8,128)(2,1)S(1)}) custom-call(s32[16]{0:T(128)} %refs_0_.1, s32[16]{0:T(128)} %refs_1_.5, bf16[16,8,128]{2,1,0:T(8,128)(2,1)} %refs_2_.5, bf16[1024,4096]{1,0:T(8,128)(2,1)} %refs_3_.5, bf16[512,128]{1,0:T(8,128)(2,1)S(1)} %get-tuple-element.42.refs_4_, ...), custom_call_target="tpu_custom_call" | custom-call | flops 150994944 | bytes 10485760 | tf_op jit(solution)/shard_map/first/pallas_call | solution.py:327
  19.6 0.0 collective-permute-done.refs_1_
  19.7 2.6 %collective-permute-start.5 = (bf16[512,128]{1,0:T(8,128)(2,1)S(1)}, bf16[512,128]{1,0:T(8,128)(2,1)S(1)}, u32[]{:S(2)}, u32[]{:S(2)}) collective-permute-start(bf16[512,128]{1,0:T(8,128)(2,1)S(1)} %get-tuple-element.59.refs_9_), channel_id=1, source_target_pairs={{0,14},{2,12},{4,10},{6,8},{8,6},{10,4},{12,2},{14,0},{16,30},{18,... | collective-permute-start | bytes 393224 | tf_op jit(solution)/shard_map/ppermute | solution.py:324
  22.3 0.0 collective-permute-done.1.refs_2_
  22.3 2.2 %collective-permute-start.6 = (bf16[512,128]{1,0:T(8,128)(2,1)S(1)}, bf16[512,128]{1,0:T(8,128)(2,1)S(1)}, u32[]{:S(2)}, u32[]{:S(2)}) collective-permute-start(bf16[512,128]{1,0:T(8,128)(2,1)S(1)} %get-tuple-element.60.refs_10_), channel_id=1, source_target_pairs={{0,22},{2,20},{4,18},{6,16},{8,30},{10,28},{12,26},{14,24},{16,6},... | collective-permute-start | bytes 393224 | tf_op jit(solution)/shard_map/ppermute | solution.py:324
  24.5 0.0 collective-permute-done.2.refs_3_
  24.5 0.1 collective-permute-start.7
  24.6 0.0 collective-permute-done.3.refs_4_
  24.6 3.9 %collective-permute-start.8 = (bf16[512,128]{1,0:T(8,128)(2,1)S(1)}, bf16[512,128]{1,0:T(8,128)(2,1)S(1)}, u32[]{:S(2)}, u32[]{:S(2)}) collective-permute-start(bf16[512,128]{1,0:T(8,128)(2,1)S(1)} %get-tuple-element.62.refs_12_), channel_id=1, source_target_pairs={{0,30},{2,28},{4,26},{6,24},{8,22},{10,20},{12,18},{14,16},{16,14}... | collective-permute-start | bytes 393224 | tf_op jit(solution)/shard_map/ppermute | solution.py:324
  28.5 0.0 collective-permute-done.4.refs_5_
  28.5 0.4 collective-permute-start.9
  28.9 0.0 collective-permute-done.5.refs_6_
  28.9 3.3 %collective-permute-start.11 = (bf16[512,128]{1,0:T(8,128)(2,1)S(1)}, bf16[512,128]{1,0:T(8,128)(2,1)S(1)}, u32[]{:S(2)}, u32[]{:S(2)}) collective-permute-start(bf16[512,128]{1,0:T(8,128)(2,1)S(1)} %get-tuple-element.66.refs_14_), channel_id=1, source_target_pairs={{0,26},{2,24},{4,30},{6,28},{8,18},{10,16},{12,22},{14,20},{16,10}... | collective-permute-start | bytes 393224 | tf_op jit(solution)/shard_map/ppermute | solution.py:324
  32.2 2.1 %collective-permute-done.6.refs_7_ = bf16[512,128]{1,0:T(8,128)(2,1)S(1)} collective-permute-done((bf16[512,128]{1,0:T(8,128)(2,1)S(1)}, bf16[512,128]{1,0:T(8,128)(2,1)S(1)}, u32[]{:S(2)}, u32[]{:S(2)}) %collective-permute-start.6) | collective-permute-done | bytes 131104 | tf_op jit(solution)/shard_map/ppermute | solution.py:324
  34.3 0.4 collective-permute-start.12
  34.7 0.4 collective-permute-done.7.refs_8_
  35.1 0.0 collective-permute-start.13
  35.2 2.9 %collective-permute-done.8.refs_9_ = bf16[512,128]{1,0:T(8,128)(2,1)S(1)} collective-permute-done((bf16[512,128]{1,0:T(8,128)(2,1)S(1)}, bf16[512,128]{1,0:T(8,128)(2,1)S(1)}, u32[]{:S(2)}, u32[]{:S(2)}) %collective-permute-start.8) | collective-permute-done | bytes 131104 | tf_op jit(solution)/shard_map/ppermute | solution.py:324
  38.1 0.0 collective-permute-start.14
  38.1 1.0 %collective-permute-done.9.refs_10_ = bf16[512,128]{1,0:T(8,128)(2,1)S(1)} collective-permute-done((bf16[512,128]{1,0:T(8,128)(2,1)S(1)}, bf16[512,128]{1,0:T(8,128)(2,1)S(1)}, u32[]{:S(2)}, u32[]{:S(2)}) %collective-permute-start.9) | collective-permute-done | bytes 131104 | tf_op jit(solution)/shard_map/ppermute | solution.py:324
  39.1 2.9 %collective-permute-start.15 = (bf16[512,128]{1,0:T(8,128)(2,1)S(1)}, bf16[512,128]{1,0:T(8,128)(2,1)S(1)}, u32[]{:S(2)}, u32[]{:S(2)}) collective-permute-start(bf16[512,128]{1,0:T(8,128)(2,1)S(1)} %get-tuple-element.70.refs_18_), channel_id=1, source_target_pairs={{0,24},{2,26},{4,28},{6,30},{8,16},{10,18},{12,20},{14,22},{16,8},... | collective-permute-start | bytes 393224 | tf_op jit(solution)/shard_map/ppermute | solution.py:324
  42.0 2.3 %early.1 = (bf16[16,256,128]{2,1,0:T(8,128)(2,1)}, bf16[16,256,128]{2,1,0:T(8,128)(2,1)}, f32[16,8,128]{2,1,0:T(8,128)S(1)}, bf16[16,8,128]{2,1,0:T(8,128)(2,1)S...) custom-call(bf16[512,128]{1,0:T(8,128)(2,1)S(1)} %get-tuple-element.57.refs_19_.refs_0_, ...), custom_call_target="tpu_custom_call" | custom-call | flops 11534336 | bytes 2883584 | tf_op jit(solution)/shard_map/early/pallas_call | solution.py:353
  44.4 0.0 collective-permute-done.11.refs_0_
  44.4 0.1 collective-permute-start.10
  44.5 0.0 collective-permute-done.12.refs_1_
  44.5 7.1 %collective-permute-done.13.refs_2_ = bf16[512,128]{1,0:T(8,128)(2,1)S(1)} collective-permute-done((bf16[512,128]{1,0:T(8,128)(2,1)S(1)}, bf16[512,128]{1,0:T(8,128)(2,1)S(1)}, u32[]{:S(2)}, u32[]{:S(2)}) %collective-permute-start.13) | collective-permute-done | bytes 131104 | tf_op jit(solution)/shard_map/ppermute | solution.py:324
  51.6 0.0 collective-permute-done.14.refs_3_
  51.6 0.0 collective-permute-done.15.refs_4_
  51.6 2.0 %late.1 = (bf16[16,4096]{1,0:T(8,128)(2,1)S(1)}, bf16[16,256,128]{2,1,0:T(8,128)(2,1)}, bf16[16,256,128]{2,1,0:T(8,128)(2,1)}) custom-call(bf16[512,128]{1,0:T(8,128)(2,1)S(1)} %collective-permute-done.11.refs_0_, bf16[512,128]{1,0:T(8,128)(2,1)S(1)} %collective-permute-done.12.refs_1_, ...), custom_call_target="tpu_custom_call", output_to_operand_aliasing={{1}: (10, {}), {2}: (11, {})} | custom-call | flops 150994944 | bytes 10485760 | tf_op jit(solution)/shard_map/late/pallas_call | solution.py:379
  53.6 0.1 collective-permute-start.16
  53.7 0.0 collective-permute-done.10
  53.7 0.7 %add_convert_fusion.1 = bf16[16,4096]{1,0:T(8,128)(2,1)} fusion(bf16[16,4096]{1,0:T(8,128)(2,1)S(1)} %collective-permute-done.10, bf16[16,4096]{1,0:T(8,128)(2,1)S(1)} %get-tuple-element.65), kind=kLoop, calls=%fused_computation.1 | loop fusion | flops 262144 | bytes 393216 | tf_op jit(solution)/shard_map/convert_element_type | solution.py:209
  54.4 0.6 %collective-permute-done.16 = bf16[16,4096]{1,0:T(8,128)(2,1)S(1)} collective-permute-done((bf16[16,4096]{1,0:T(8,128)(2,1)S(1)}, bf16[16,4096]{1,0:T(8,128)(2,1)S(1)}, u32[]{:S(2)}, u32[]{:S(2)}) %collective-permute-start.16) | collective-permute-done | bytes 131104 | tf_op jit(solution)/shard_map/ppermute | solution.py:208
  55.0 0.7 %add_convert_fusion = bf16[16,4096]{1,0:T(8,128)(2,1)} fusion(bf16[16,4096]{1,0:T(8,128)(2,1)S(1)} %collective-permute-done.16, bf16[16,4096]{1,0:T(8,128)(2,1)S(1)} %get-tuple-element.77), kind=kLoop, calls=%fused_computation | loop fusion | flops 262144 | bytes 393216 | tf_op jit(solution)/shard_map/convert_element_type | solution.py:209
Async XLA Ops:
  2.3 17.3 %collective-permute-start = (bf16[512,128]{1,0:T(8,128)(2,1)S(1)}, bf16[512,128]{1,0:T(8,128)(2,1)S(1)}, u32[]{:S(2)}, u32[]{:S(2)}) collective-permute-start(bf16[512,128]{1,0:T(8,128)(2,1)S(1)} %get-tuple-element.42.refs_4_), channel_id=1, source_target_pairs={{0,16},{2,18},{4,20},{6,22},{8,24},{10,26},{12,28},{14,30},{16,0},... | collective-permute-start | bytes 393224 | tf_op jit(solution)/shard_map/ppermute | solution.py:324
  6.5 15.8 %collective-permute-start.1 = (bf16[512,128]{1,0:T(8,128)(2,1)S(1)}, bf16[512,128]{1,0:T(8,128)(2,1)S(1)}, u32[]{:S(2)}, u32[]{:S(2)}) collective-permute-start(bf16[512,128]{1,0:T(8,128)(2,1)S(1)} %get-tuple-element.43.refs_5_), channel_id=1, source_target_pairs={{0,2},{2,0},{4,6},{6,4},{8,10},{10,8},{12,14},{14,12},{16,18},{18,... | collective-permute-start | bytes 393224 | tf_op jit(solution)/shard_map/ppermute | solution.py:324
  7.9 16.5 %collective-permute-start.2 = (bf16[512,128]{1,0:T(8,128)(2,1)S(1)}, bf16[512,128]{1,0:T(8,128)(2,1)S(1)}, u32[]{:S(2)}, u32[]{:S(2)}) collective-permute-start(bf16[512,128]{1,0:T(8,128)(2,1)S(1)} %get-tuple-element.44.refs_6_), channel_id=1, source_target_pairs={{0,18},{2,16},{4,22},{6,20},{8,26},{10,24},{12,30},{14,28},{16,2},... | collective-permute-start | bytes 393224 | tf_op jit(solution)/shard_map/ppermute | solution.py:324
  8.0 16.6 %collective-permute-start.3 = (bf16[512,128]{1,0:T(8,128)(2,1)S(1)}, bf16[512,128]{1,0:T(8,128)(2,1)S(1)}, u32[]{:S(2)}, u32[]{:S(2)}) collective-permute-start(bf16[512,128]{1,0:T(8,128)(2,1)S(1)} %get-tuple-element.45.refs_7_), channel_id=1, source_target_pairs={{0,12},{2,14},{4,8},{6,10},{8,4},{10,6},{12,0},{14,2},{16,28},{18,... | collective-permute-start | bytes 393224 | tf_op jit(solution)/shard_map/ppermute | solution.py:324
  10.8 17.7 %collective-permute-start.4 = (bf16[512,128]{1,0:T(8,128)(2,1)S(1)}, bf16[512,128]{1,0:T(8,128)(2,1)S(1)}, u32[]{:S(2)}, u32[]{:S(2)}) collective-permute-start(bf16[512,128]{1,0:T(8,128)(2,1)S(1)} %get-tuple-element.46.refs_8_), channel_id=1, source_target_pairs={{0,28},{2,30},{4,24},{6,26},{8,20},{10,22},{12,16},{14,18},{16,12}... | collective-permute-start | bytes 393224 | tf_op jit(solution)/shard_map/ppermute | solution.py:324
  19.7 9.3 %collective-permute-start.5 = (bf16[512,128]{1,0:T(8,128)(2,1)S(1)}, bf16[512,128]{1,0:T(8,128)(2,1)S(1)}, u32[]{:S(2)}, u32[]{:S(2)}) collective-permute-start(bf16[512,128]{1,0:T(8,128)(2,1)S(1)} %get-tuple-element.59.refs_9_), channel_id=1, source_target_pairs={{0,14},{2,12},{4,10},{6,8},{8,6},{10,4},{12,2},{14,0},{16,30},{18,... | collective-permute-start | bytes 393224 | tf_op jit(solution)/shard_map/ppermute | solution.py:324
  22.3 12.1 %collective-permute-start.6 = (bf16[512,128]{1,0:T(8,128)(2,1)S(1)}, bf16[512,128]{1,0:T(8,128)(2,1)S(1)}, u32[]{:S(2)}, u32[]{:S(2)}) collective-permute-start(bf16[512,128]{1,0:T(8,128)(2,1)S(1)} %get-tuple-element.60.refs_10_), channel_id=1, source_target_pairs={{0,22},{2,20},{4,18},{6,16},{8,30},{10,28},{12,26},{14,24},{16,6},... | collective-permute-start | bytes 393224 | tf_op jit(solution)/shard_map/ppermute | solution.py:324
  24.5 10.7 %collective-permute-start.7 = (bf16[512,128]{1,0:T(8,128)(2,1)S(1)}, bf16[512,128]{1,0:T(8,128)(2,1)S(1)}, u32[]{:S(2)}, u32[]{:S(2)}) collective-permute-start(bf16[512,128]{1,0:T(8,128)(2,1)S(1)} %get-tuple-element.61.refs_11_), channel_id=1, source_target_pairs={{0,8},{2,10},{4,12},{6,14},{8,0},{10,2},{12,4},{14,6},{16,24},{18,... | collective-permute-start | bytes 393224 | tf_op jit(solution)/shard_map/ppermute | solution.py:324
  24.6 13.5 %collective-permute-start.8 = (bf16[512,128]{1,0:T(8,128)(2,1)S(1)}, bf16[512,128]{1,0:T(8,128)(2,1)S(1)}, u32[]{:S(2)}, u32[]{:S(2)}) collective-permute-start(bf16[512,128]{1,0:T(8,128)(2,1)S(1)} %get-tuple-element.62.refs_12_), channel_id=1, source_target_pairs={{0,30},{2,28},{4,26},{6,24},{8,22},{10,20},{12,18},{14,16},{16,14}... | collective-permute-start | bytes 393224 | tf_op jit(solution)/shard_map/ppermute | solution.py:324
  28.5 10.6 %collective-permute-start.9 = (bf16[512,128]{1,0:T(8,128)(2,1)S(1)}, bf16[512,128]{1,0:T(8,128)(2,1)S(1)}, u32[]{:S(2)}, u32[]{:S(2)}) collective-permute-start(bf16[512,128]{1,0:T(8,128)(2,1)S(1)} %get-tuple-element.63.refs_13_), channel_id=1, source_target_pairs={{0,10},{2,8},{4,14},{6,12},{8,2},{10,0},{12,6},{14,4},{16,26},{18,... | collective-permute-start | bytes 393224 | tf_op jit(solution)/shard_map/ppermute | solution.py:324
  28.9 15.5 %collective-permute-start.11 = (bf16[512,128]{1,0:T(8,128)(2,1)S(1)}, bf16[512,128]{1,0:T(8,128)(2,1)S(1)}, u32[]{:S(2)}, u32[]{:S(2)}) collective-permute-start(bf16[512,128]{1,0:T(8,128)(2,1)S(1)} %get-tuple-element.66.refs_14_), channel_id=1, source_target_pairs={{0,26},{2,24},{4,30},{6,28},{8,18},{10,16},{12,22},{14,20},{16,10}... | collective-permute-start | bytes 393224 | tf_op jit(solution)/shard_map/ppermute | solution.py:324
  34.3 10.1 %collective-permute-start.12 = (bf16[512,128]{1,0:T(8,128)(2,1)S(1)}, bf16[512,128]{1,0:T(8,128)(2,1)S(1)}, u32[]{:S(2)}, u32[]{:S(2)}) collective-permute-start(bf16[512,128]{1,0:T(8,128)(2,1)S(1)} %get-tuple-element.67.refs_15_), channel_id=1, source_target_pairs={{0,4},{2,6},{4,0},{6,2},{8,12},{10,14},{12,8},{14,10},{16,20},{18,... | collective-permute-start | bytes 393224 | tf_op jit(solution)/shard_map/ppermute | solution.py:324
  35.1 16.4 %collective-permute-start.13 = (bf16[512,128]{1,0:T(8,128)(2,1)S(1)}, bf16[512,128]{1,0:T(8,128)(2,1)S(1)}, u32[]{:S(2)}, u32[]{:S(2)}) collective-permute-start(bf16[512,128]{1,0:T(8,128)(2,1)S(1)} %get-tuple-element.68.refs_16_), channel_id=1, source_target_pairs={{0,20},{2,22},{4,16},{6,18},{8,28},{10,30},{12,24},{14,26},{16,4},... | collective-permute-start | bytes 393224 | tf_op jit(solution)/shard_map/ppermute | solution.py:324
  38.1 13.5 %collective-permute-start.14 = (bf16[512,128]{1,0:T(8,128)(2,1)S(1)}, bf16[512,128]{1,0:T(8,128)(2,1)S(1)}, u32[]{:S(2)}, u32[]{:S(2)}) collective-permute-start(bf16[512,128]{1,0:T(8,128)(2,1)S(1)} %get-tuple-element.69.refs_17_), channel_id=1, source_target_pairs={{0,6},{2,4},{4,2},{6,0},{8,14},{10,12},{12,10},{14,8},{16,22},{18,... | collective-permute-start | bytes 393224 | tf_op jit(solution)/shard_map/ppermute | solution.py:324
  39.1 12.5 %collective-permute-start.15 = (bf16[512,128]{1,0:T(8,128)(2,1)S(1)}, bf16[512,128]{1,0:T(8,128)(2,1)S(1)}, u32[]{:S(2)}, u32[]{:S(2)}) collective-permute-start(bf16[512,128]{1,0:T(8,128)(2,1)S(1)} %get-tuple-element.70.refs_18_), channel_id=1, source_target_pairs={{0,24},{2,26},{4,28},{6,30},{8,16},{10,18},{12,20},{14,22},{16,8},... | collective-permute-start | bytes 393224 | tf_op jit(solution)/shard_map/ppermute | solution.py:324
  44.4 9.3 %collective-permute-start.10 = (bf16[16,4096]{1,0:T(8,128)(2,1)S(1)}, bf16[16,4096]{1,0:T(8,128)(2,1)S(1)}, u32[]{:S(2)}, u32[]{:S(2)}) collective-permute-start(bf16[16,4096]{1,0:T(8,128)(2,1)S(1)} %get-tuple-element.65), channel_id=1, source_target_pairs={{0,1},{1,0},{2,3},{3,2},{4,5},{5,4},{6,7},{7,6},{8,9},{9,8},{10,11... | collective-permute-start | bytes 393224 | tf_op jit(solution)/shard_map/ppermute | solution.py:208
  53.6 1.4 %collective-permute-start.16 = (bf16[16,4096]{1,0:T(8,128)(2,1)S(1)}, bf16[16,4096]{1,0:T(8,128)(2,1)S(1)}, u32[]{:S(2)}, u32[]{:S(2)}) collective-permute-start(bf16[16,4096]{1,0:T(8,128)(2,1)S(1)} %get-tuple-element.77), channel_id=1, source_target_pairs={{0,1},{1,0},{2,3},{3,2},{4,5},{5,4},{6,7},{7,6},{8,9},{9,8},{10,11... | collective-permute-start | bytes 393224 | tf_op jit(solution)/shard_map/ppermute | solution.py:208

commit v18 on v17

--- a/solution.py
+++ b/solution.py
@@ -226,6 +226,7 @@
         queue[at], queue[-1] = queue[-1], queue[at]
     for queue, at in ((crossing, half // 4), (staying, half // 4 - 1)):
         queue[at], queue[-2] = queue[-2], queue[at]
+    crossing[1], crossing[-3] = crossing[-3], crossing[1]
     order = []
     for kind in "cncncncncncncnc":
         queue = crossing if kind == "c" else staying

time: 56 us -> 57.5 us (1.027)
  the two profiles are of different devices: /device:TPU:0 before, /device:TPU:19 now
where the time goes in v18:
time: 57.5 us; the launch traced here: 57.2 us
  waiting for transfers between devices  25.3 us (44%)
  starting transfers between devices  17.3 us (30%)
  Pallas kernels  12.5 us (22%)
  other arithmetic  1.38 us (2%)
  between operations  0.72 us (1%)
    ppermute x15, waiting for transfers between devices, send(): return lax.ppermute(block, 'inst', [(d, d ^ steps[i]) for d in range(n)])  25 us
    ppermute x15, starting transfers between devices, send(): return lax.ppermute(block, 'inst', [(d, d ^ steps[i]) for d in range(n)])  15.4 us
    pallas_call x1, Pallas kernels, shards(): pl.pallas_call(functools.partial(first_kernel, steps, span), out_shape=[j...  4.66 us
    pallas_call x2, Pallas kernels, pack(): pl.pallas_call(functools.partial(pack_kernel, n, chosen, pages), out_shap...  3.48 us
    pallas_call x1, Pallas kernels, shards(): pl.pallas_call(functools.partial(early_kernel, some, span), out_shape=[ca...  2.31 us
    pallas_call x1, Pallas kernels, shards(): pl.pallas_call(functools.partial(late_kernel, LATE, span), out_shape=[jax...  2.01 us
    ppermute x2, starting transfers between devices, total(): other = lax.ppermute(partial, 'tp', [(0, 1), (1, 0)])  1.86 us
    convert_element_type x2, other arithmetic, total(): (partial.astype(jnp.float32) + other.astype(jnp.float32)).astype(jnp.bflo...  1.38 us
  transfers between devices with their start and end apart: 17, of which 6 were waited for; matrix products, arithmetic and copies ran while one was open for 1% of the time, Pallas kernels for 19%

profile of v18, /device:TPU:19, one launch (start us, length us, event | category | flops | bytes accessed | tf_op | source)
XLA Modules:
  0.0 57.2 jit_solution(756112888116027425)
XLA Ops:
  0.6 1.7 %pack.2 = (bf16[512,128]{1,0:T(8,128)(2,1)S(1)}, bf16[512,128]{1,0:T(8,128)(2,1)S(1)}, bf16[512,128]{1,0:T(8,128)(2,1)S(1)}, bf16[512,128]{1,0:T(8,128)(2,1)S(1)}, bf16[512,128]{1,0:T(8,128)(2,1)S(1)}) custom-call(s32[4,16]{1,0:T(4,128)} %bitcast.23, s32[16]{0:T(128)} %refs_0_.1, s32[16]{0:T(128)} %refs_1_.5, s32[16]{0:T(128)} %refs_3_.4, ...), custom_call_target="tpu_custom_call" | custom-call | bytes 1310720 | tf_op jit(solution)/shard_map/pack/pallas_call | solution.py:285
  2.3 0.1 collective-permute-start
  2.5 0.3 collective-permute-start.1
  2.7 3.3 %collective-permute-start.2 = (bf16[512,128]{1,0:T(8,128)(2,1)S(1)}, bf16[512,128]{1,0:T(8,128)(2,1)S(1)}, u32[]{:S(2)}, u32[]{:S(2)}) collective-permute-start(bf16[512,128]{1,0:T(8,128)(2,1)S(1)} %get-tuple-element.44.refs_6_), channel_id=1, source_target_pairs={{0,26},{2,24},{4,30},{6,28},{8,18},{10,16},{12,22},{14,20},{16,10}... | collective-permute-start | bytes 393224 | tf_op jit(solution)/shard_map/ppermute | solution.py:325
  6.1 2.0 %collective-permute-start.3 = (bf16[512,128]{1,0:T(8,128)(2,1)S(1)}, bf16[512,128]{1,0:T(8,128)(2,1)S(1)}, u32[]{:S(2)}, u32[]{:S(2)}) collective-permute-start(bf16[512,128]{1,0:T(8,128)(2,1)S(1)} %get-tuple-element.45.refs_7_), channel_id=1, source_target_pairs={{0,12},{2,14},{4,8},{6,10},{8,4},{10,6},{12,0},{14,2},{16,28},{18,... | collective-permute-start | bytes 393224 | tf_op jit(solution)/shard_map/ppermute | solution.py:325
  8.1 0.1 collective-permute-start.4
  8.2 1.8 %pack.3 = (bf16[512,128]{1,0:T(8,128)(2,1)S(1)}, bf16[512,128]{1,0:T(8,128)(2,1)S(1)}, bf16[512,128]{1,0:T(8,128)(2,1)S(1)}, bf16[512,128]{1,0:T(8,128)(2,1)S(1)...) custom-call(s32[4,16]{1,0:T(4,128)} %bitcast.24, ...), custom_call_target="tpu_custom_call" | custom-call | bytes 2883584 | tf_op jit(solution)/shard_map/pack/pallas_call | solution.py:285
  10.0 4.7 %first.1 = (bf16[16,4096]{1,0:T(8,128)(2,1)S(1)}, bf16[1024,4096]{1,0:T(8,128)(2,1)S(1)}) custom-call(s32[16]{0:T(128)} %refs_0_.1, s32[16]{0:T(128)} %refs_1_.5, bf16[16,8,128]{2,1,0:T(8,128)(2,1)} %refs_2_.5, bf16[1024,4096]{1,0:T(8,128)(2,1)} %refs_3_.5, bf16[512,128]{1,0:T(8,128)(2,1)S(1)} %get-tuple-element.42.refs_4_, ...), custom_call_target="tpu_custom_call" | custom-call | flops 150994944 | bytes 10485760 | tf_op jit(solution)/shard_map/first/pallas_call | solution.py:328
  14.7 0.0 collective-permute-done.refs_1_
  14.7 2.9 %collective-permute-start.5 = (bf16[512,128]{1,0:T(8,128)(2,1)S(1)}, bf16[512,128]{1,0:T(8,128)(2,1)S(1)}, u32[]{:S(2)}, u32[]{:S(2)}) collective-permute-start(bf16[512,128]{1,0:T(8,128)(2,1)S(1)} %get-tuple-element.59.refs_9_), channel_id=1, source_target_pairs={{0,14},{2,12},{4,10},{6,8},{8,6},{10,4},{12,2},{14,0},{16,30},{18,... | collective-permute-start | bytes 393224 | tf_op jit(solution)/shard_map/ppermute | solution.py:325
  17.6 0.0 collective-permute-done.1.refs_2_
  17.6 1.5 %collective-permute-start.6 = (bf16[512,128]{1,0:T(8,128)(2,1)S(1)}, bf16[512,128]{1,0:T(8,128)(2,1)S(1)}, u32[]{:S(2)}, u32[]{:S(2)}) collective-permute-start(bf16[512,128]{1,0:T(8,128)(2,1)S(1)} %get-tuple-element.60.refs_10_), channel_id=1, source_target_pairs={{0,22},{2,20},{4,18},{6,16},{8,30},{10,28},{12,26},{14,24},{16,6},... | collective-permute-start | bytes 393224 | tf_op jit(solution)/shard_map/ppermute | solution.py:325
  19.0 1.3 %collective-permute-done.2.refs_3_ = bf16[512,128]{1,0:T(8,128)(2,1)S(1)} collective-permute-done((bf16[512,128]{1,0:T(8,128)(2,1)S(1)}, bf16[512,128]{1,0:T(8,128)(2,1)S(1)}, u32[]{:S(2)}, u32[]{:S(2)}) %collective-permute-start.2) | collective-permute-done | bytes 131104 | tf_op jit(solution)/shard_map/ppermute | solution.py:325
  20.3 0.0 collective-permute-start.7
  20.3 0.0 collective-permute-done.3.refs_4_
  20.4 1.7 %collective-permute-start.8 = (bf16[512,128]{1,0:T(8,128)(2,1)S(1)}, bf16[512,128]{1,0:T(8,128)(2,1)S(1)}, u32[]{:S(2)}, u32[]{:S(2)}) collective-permute-start(bf16[512,128]{1,0:T(8,128)(2,1)S(1)} %get-tuple-element.62.refs_12_), channel_id=1, source_target_pairs={{0,30},{2,28},{4,26},{6,24},{8,22},{10,20},{12,18},{14,16},{16,14}... | collective-permute-start | bytes 393224 | tf_op jit(solution)/shard_map/ppermute | solution.py:325
  22.0 6.3 %collective-permute-done.4.refs_5_ = bf16[512,128]{1,0:T(8,128)(2,1)S(1)} collective-permute-done((bf16[512,128]{1,0:T(8,128)(2,1)S(1)}, bf16[512,128]{1,0:T(8,128)(2,1)S(1)}, u32[]{:S(2)}, u32[]{:S(2)}) %collective-permute-start.4) | collective-permute-done | bytes 131104 | tf_op jit(solution)/shard_map/ppermute | solution.py:325
  28.3 0.0 collective-permute-start.9
  28.3 0.0 collective-permute-done.5.refs_6_
  28.3 0.0 collective-permute-start.11
  28.3 0.0 collective-permute-done.6.refs_7_
  28.3 0.2 collective-permute-start.12
  28.6 0.0 collective-permute-done.7.refs_8_
  28.6 2.1 %collective-permute-start.13 = (bf16[512,128]{1,0:T(8,128)(2,1)S(1)}, bf16[512,128]{1,0:T(8,128)(2,1)S(1)}, u32[]{:S(2)}, u32[]{:S(2)}) collective-permute-start(bf16[512,128]{1,0:T(8,128)(2,1)S(1)} %get-tuple-element.68.refs_16_), channel_id=1, source_target_pairs={{0,20},{2,22},{4,16},{6,18},{8,28},{10,30},{12,24},{14,26},{16,4},... | collective-permute-start | bytes 393224 | tf_op jit(solution)/shard_map/ppermute | solution.py:325
  30.7 14.7 %collective-permute-done.8.refs_9_ = bf16[512,128]{1,0:T(8,128)(2,1)S(1)} collective-permute-done((bf16[512,128]{1,0:T(8,128)(2,1)S(1)}, bf16[512,128]{1,0:T(8,128)(2,1)S(1)}, u32[]{:S(2)}, u32[]{:S(2)}) %collective-permute-start.8) | collective-permute-done | bytes 131104 | tf_op jit(solution)/shard_map/ppermute | solution.py:325
  45.4 1.2 %collective-permute-start.14 = (bf16[512,128]{1,0:T(8,128)(2,1)S(1)}, bf16[512,128]{1,0:T(8,128)(2,1)S(1)}, u32[]{:S(2)}, u32[]{:S(2)}) collective-permute-start(bf16[512,128]{1,0:T(8,128)(2,1)S(1)} %get-tuple-element.69.refs_17_), channel_id=1, source_target_pairs={{0,6},{2,4},{4,2},{6,0},{8,14},{10,12},{12,10},{14,8},{16,22},{18,... | collective-permute-start | bytes 393224 | tf_op jit(solution)/shard_map/ppermute | solution.py:325
  46.6 0.0 collective-permute-done.9.refs_10_
  46.6 0.0 collective-permute-start.15
  46.6 2.3 %early.1 = (bf16[16,256,128]{2,1,0:T(8,128)(2,1)}, bf16[16,256,128]{2,1,0:T(8,128)(2,1)}, f32[16,8,128]{2,1,0:T(8,128)S(1)}, bf16[16,8,128]{2,1,0:T(8,128)(2,1)S...) custom-call(bf16[512,128]{1,0:T(8,128)(2,1)S(1)} %get-tuple-element.57.refs_19_.refs_0_, ...), custom_call_target="tpu_custom_call" | custom-call | flops 11534336 | bytes 2883584 | tf_op jit(solution)/shard_map/early/pallas_call | solution.py:354
  48.9 0.0 collective-permute-done.11.refs_0_
  48.9 0.9 %collective-permute-start.10 = (bf16[16,4096]{1,0:T(8,128)(2,1)S(1)}, bf16[16,4096]{1,0:T(8,128)(2,1)S(1)}, u32[]{:S(2)}, u32[]{:S(2)}) collective-permute-start(bf16[16,4096]{1,0:T(8,128)(2,1)S(1)} %get-tuple-element.65), channel_id=1, source_target_pairs={{0,1},{1,0},{2,3},{3,2},{4,5},{5,4},{6,7},{7,6},{8,9},{9,8},{10,11... | collective-permute-start | bytes 393224 | tf_op jit(solution)/shard_map/ppermute | solution.py:208
  49.9 0.0 collective-permute-done.12.refs_1_
  49.9 0.0 collective-permute-done.13.refs_2_
  49.9 0.9 %collective-permute-done.14.refs_3_ = bf16[512,128]{1,0:T(8,128)(2,1)S(1)} collective-permute-done((bf16[512,128]{1,0:T(8,128)(2,1)S(1)}, bf16[512,128]{1,0:T(8,128)(2,1)S(1)}, u32[]{:S(2)}, u32[]{:S(2)}) %collective-permute-start.14) | collective-permute-done | bytes 131104 | tf_op jit(solution)/shard_map/ppermute | solution.py:325
  50.7 1.8 %collective-permute-done.15.refs_4_ = bf16[512,128]{1,0:T(8,128)(2,1)S(1)} collective-permute-done((bf16[512,128]{1,0:T(8,128)(2,1)S(1)}, bf16[512,128]{1,0:T(8,128)(2,1)S(1)}, u32[]{:S(2)}, u32[]{:S(2)}) %collective-permute-start.15) | collective-permute-done | bytes 131104 | tf_op jit(solution)/shard_map/ppermute | solution.py:325
  52.6 2.0 %late.1 = (bf16[16,4096]{1,0:T(8,128)(2,1)S(1)}, bf16[16,256,128]{2,1,0:T(8,128)(2,1)}, bf16[16,256,128]{2,1,0:T(8,128)(2,1)}) custom-call(bf16[512,128]{1,0:T(8,128)(2,1)S(1)} %collective-permute-done.11.refs_0_, bf16[512,128]{1,0:T(8,128)(2,1)S(1)} %collective-permute-done.12.refs_1_, ...), custom_call_target="tpu_custom_call", output_to_operand_aliasing={{1}: (10, {}), {2}: (11, {})} | custom-call | flops 150994944 | bytes 10485760 | tf_op jit(solution)/shard_map/late/pallas_call | solution.py:380
  54.6 0.9 %collective-permute-start.16 = (bf16[16,4096]{1,0:T(8,128)(2,1)S(1)}, bf16[16,4096]{1,0:T(8,128)(2,1)S(1)}, u32[]{:S(2)}, u32[]{:S(2)}) collective-permute-start(bf16[16,4096]{1,0:T(8,128)(2,1)S(1)} %get-tuple-element.77), channel_id=1, source_target_pairs={{0,1},{1,0},{2,3},{3,2},{4,5},{5,4},{6,7},{7,6},{8,9},{9,8},{10,11... | collective-permute-start | bytes 393224 | tf_op jit(solution)/shard_map/ppermute | solution.py:208
  55.5 0.0 collective-permute-done.10
  55.5 0.7 %add_convert_fusion.1 = bf16[16,4096]{1,0:T(8,128)(2,1)} fusion(bf16[16,4096]{1,0:T(8,128)(2,1)S(1)} %collective-permute-done.10, bf16[16,4096]{1,0:T(8,128)(2,1)S(1)} %get-tuple-element.65), kind=kLoop, calls=%fused_computation.1 | loop fusion | flops 262144 | bytes 393216 | tf_op jit(solution)/shard_map/convert_element_type | solution.py:209
  56.2 0.3 collective-permute-done.16
  56.5 0.7 %add_convert_fusion = bf16[16,4096]{1,0:T(8,128)(2,1)} fusion(bf16[16,4096]{1,0:T(8,128)(2,1)S(1)} %collective-permute-done.16, bf16[16,4096]{1,0:T(8,128)(2,1)S(1)} %get-tuple-element.77), kind=kLoop, calls=%fused_computation | loop fusion | flops 262144 | bytes 393216 | tf_op jit(solution)/shard_map/convert_element_type | solution.py:209
Async XLA Ops:
  2.3 12.3 %collective-permute-start = (bf16[512,128]{1,0:T(8,128)(2,1)S(1)}, bf16[512,128]{1,0:T(8,128)(2,1)S(1)}, u32[]{:S(2)}, u32[]{:S(2)}) collective-permute-start(bf16[512,128]{1,0:T(8,128)(2,1)S(1)} %get-tuple-element.42.refs_4_), channel_id=1, source_target_pairs={{0,16},{2,18},{4,20},{6,22},{8,24},{10,26},{12,28},{14,30},{16,0},... | collective-permute-start | bytes 393224 | tf_op jit(solution)/shard_map/ppermute | solution.py:325
  2.5 15.1 %collective-permute-start.1 = (bf16[512,128]{1,0:T(8,128)(2,1)S(1)}, bf16[512,128]{1,0:T(8,128)(2,1)S(1)}, u32[]{:S(2)}, u32[]{:S(2)}) collective-permute-start(bf16[512,128]{1,0:T(8,128)(2,1)S(1)} %get-tuple-element.43.refs_5_), channel_id=1, source_target_pairs={{0,2},{2,0},{4,6},{6,4},{8,10},{10,8},{12,14},{14,12},{16,18},{18,... | collective-permute-start | bytes 393224 | tf_op jit(solution)/shard_map/ppermute | solution.py:325
  2.7 17.6 %collective-permute-start.2 = (bf16[512,128]{1,0:T(8,128)(2,1)S(1)}, bf16[512,128]{1,0:T(8,128)(2,1)S(1)}, u32[]{:S(2)}, u32[]{:S(2)}) collective-permute-start(bf16[512,128]{1,0:T(8,128)(2,1)S(1)} %get-tuple-element.44.refs_6_), channel_id=1, source_target_pairs={{0,26},{2,24},{4,30},{6,28},{8,18},{10,16},{12,22},{14,20},{16,10}... | collective-permute-start | bytes 393224 | tf_op jit(solution)/shard_map/ppermute | solution.py:325
  6.1 14.3 %collective-permute-start.3 = (bf16[512,128]{1,0:T(8,128)(2,1)S(1)}, bf16[512,128]{1,0:T(8,128)(2,1)S(1)}, u32[]{:S(2)}, u32[]{:S(2)}) collective-permute-start(bf16[512,128]{1,0:T(8,128)(2,1)S(1)} %get-tuple-element.45.refs_7_), channel_id=1, source_target_pairs={{0,12},{2,14},{4,8},{6,10},{8,4},{10,6},{12,0},{14,2},{16,28},{18,... | collective-permute-start | bytes 393224 | tf_op jit(solution)/shard_map/ppermute | solution.py:325
  8.1 20.2 %collective-permute-start.4 = (bf16[512,128]{1,0:T(8,128)(2,1)S(1)}, bf16[512,128]{1,0:T(8,128)(2,1)S(1)}, u32[]{:S(2)}, u32[]{:S(2)}) collective-permute-start(bf16[512,128]{1,0:T(8,128)(2,1)S(1)} %get-tuple-element.46.refs_8_), channel_id=1, source_target_pairs={{0,28},{2,30},{4,24},{6,26},{8,20},{10,22},{12,16},{14,18},{16,12}... | collective-permute-start | bytes 393224 | tf_op jit(solution)/shard_map/ppermute | solution.py:325
  14.7 13.6 %collective-permute-start.5 = (bf16[512,128]{1,0:T(8,128)(2,1)S(1)}, bf16[512,128]{1,0:T(8,128)(2,1)S(1)}, u32[]{:S(2)}, u32[]{:S(2)}) collective-permute-start(bf16[512,128]{1,0:T(8,128)(2,1)S(1)} %get-tuple-element.59.refs_9_), channel_id=1, source_target_pairs={{0,14},{2,12},{4,10},{6,8},{8,6},{10,4},{12,2},{14,0},{16,30},{18,... | collective-permute-start | bytes 393224 | tf_op jit(solution)/shard_map/ppermute | solution.py:325
  17.6 10.8 %collective-permute-start.6 = (bf16[512,128]{1,0:T(8,128)(2,1)S(1)}, bf16[512,128]{1,0:T(8,128)(2,1)S(1)}, u32[]{:S(2)}, u32[]{:S(2)}) collective-permute-start(bf16[512,128]{1,0:T(8,128)(2,1)S(1)} %get-tuple-element.60.refs_10_), channel_id=1, source_target_pairs={{0,22},{2,20},{4,18},{6,16},{8,30},{10,28},{12,26},{14,24},{16,6},... | collective-permute-start | bytes 393224 | tf_op jit(solution)/shard_map/ppermute | solution.py:325
  20.3 8.2 %collective-permute-start.7 = (bf16[512,128]{1,0:T(8,128)(2,1)S(1)}, bf16[512,128]{1,0:T(8,128)(2,1)S(1)}, u32[]{:S(2)}, u32[]{:S(2)}) collective-permute-start(bf16[512,128]{1,0:T(8,128)(2,1)S(1)} %get-tuple-element.61.refs_11_), channel_id=1, source_target_pairs={{0,8},{2,10},{4,12},{6,14},{8,0},{10,2},{12,4},{14,6},{16,24},{18,... | collective-permute-start | bytes 393224 | tf_op jit(solution)/shard_map/ppermute | solution.py:325
  20.4 25.0 %collective-permute-start.8 = (bf16[512,128]{1,0:T(8,128)(2,1)S(1)}, bf16[512,128]{1,0:T(8,128)(2,1)S(1)}, u32[]{:S(2)}, u32[]{:S(2)}) collective-permute-start(bf16[512,128]{1,0:T(8,128)(2,1)S(1)} %get-tuple-element.62.refs_12_), channel_id=1, source_target_pairs={{0,30},{2,28},{4,26},{6,24},{8,22},{10,20},{12,18},{14,16},{16,14}... | collective-permute-start | bytes 393224 | tf_op jit(solution)/shard_map/ppermute | solution.py:325
  28.3 18.3 %collective-permute-start.9 = (bf16[512,128]{1,0:T(8,128)(2,1)S(1)}, bf16[512,128]{1,0:T(8,128)(2,1)S(1)}, u32[]{:S(2)}, u32[]{:S(2)}) collective-permute-start(bf16[512,128]{1,0:T(8,128)(2,1)S(1)} %get-tuple-element.63.refs_13_), channel_id=1, source_target_pairs={{0,10},{2,8},{4,14},{6,12},{8,2},{10,0},{12,6},{14,4},{16,26},{18,... | collective-permute-start | bytes 393224 | tf_op jit(solution)/shard_map/ppermute | solution.py:325
  28.3 20.6 %collective-permute-start.11 = (bf16[512,128]{1,0:T(8,128)(2,1)S(1)}, bf16[512,128]{1,0:T(8,128)(2,1)S(1)}, u32[]{:S(2)}, u32[]{:S(2)}) collective-permute-start(bf16[512,128]{1,0:T(8,128)(2,1)S(1)} %get-tuple-element.66.refs_14_), channel_id=1, source_target_pairs={{0,18},{2,16},{4,22},{6,20},{8,26},{10,24},{12,30},{14,28},{16,2},... | collective-permute-start | bytes 393224 | tf_op jit(solution)/shard_map/ppermute | solution.py:325
  28.3 21.5 %collective-permute-start.12 = (bf16[512,128]{1,0:T(8,128)(2,1)S(1)}, bf16[512,128]{1,0:T(8,128)(2,1)S(1)}, u32[]{:S(2)}, u32[]{:S(2)}) collective-permute-start(bf16[512,128]{1,0:T(8,128)(2,1)S(1)} %get-tuple-element.67.refs_15_), channel_id=1, source_target_pairs={{0,4},{2,6},{4,0},{6,2},{8,12},{10,14},{12,8},{14,10},{16,20},{18,... | collective-permute-start | bytes 393224 | tf_op jit(solution)/shard_map/ppermute | solution.py:325
  28.6 21.3 %collective-permute-start.13 = (bf16[512,128]{1,0:T(8,128)(2,1)S(1)}, bf16[512,128]{1,0:T(8,128)(2,1)S(1)}, u32[]{:S(2)}, u32[]{:S(2)}) collective-permute-start(bf16[512,128]{1,0:T(8,128)(2,1)S(1)} %get-tuple-element.68.refs_16_), channel_id=1, source_target_pairs={{0,20},{2,22},{4,16},{6,18},{8,28},{10,30},{12,24},{14,26},{16,4},... | collective-permute-start | bytes 393224 | tf_op jit(solution)/shard_map/ppermute | solution.py:325
  45.4 5.4 %collective-permute-start.14 = (bf16[512,128]{1,0:T(8,128)(2,1)S(1)}, bf16[512,128]{1,0:T(8,128)(2,1)S(1)}, u32[]{:S(2)}, u32[]{:S(2)}) collective-permute-start(bf16[512,128]{1,0:T(8,128)(2,1)S(1)} %get-tuple-element.69.refs_17_), channel_id=1, source_target_pairs={{0,6},{2,4},{4,2},{6,0},{8,14},{10,12},{12,10},{14,8},{16,22},{18,... | collective-permute-start | bytes 393224 | tf_op jit(solution)/shard_map/ppermute | solution.py:325
  46.6 6.0 %collective-permute-start.15 = (bf16[512,128]{1,0:T(8,128)(2,1)S(1)}, bf16[512,128]{1,0:T(8,128)(2,1)S(1)}, u32[]{:S(2)}, u32[]{:S(2)}) collective-permute-start(bf16[512,128]{1,0:T(8,128)(2,1)S(1)} %get-tuple-element.70.refs_18_), channel_id=1, source_target_pairs={{0,24},{2,26},{4,28},{6,30},{8,16},{10,18},{12,20},{14,22},{16,8},... | collective-permute-start | bytes 393224 | tf_op jit(solution)/shard_map/ppermute | solution.py:325
  48.9 6.6 %collective-permute-start.10 = (bf16[16,4096]{1,0:T(8,128)(2,1)S(1)}, bf16[16,4096]{1,0:T(8,128)(2,1)S(1)}, u32[]{:S(2)}, u32[]{:S(2)}) collective-permute-start(bf16[16,4096]{1,0:T(8,128)(2,1)S(1)} %get-tuple-element.65), channel_id=1, source_target_pairs={{0,1},{1,0},{2,3},{3,2},{4,5},{5,4},{6,7},{7,6},{8,9},{9,8},{10,11... | collective-permute-start | bytes 393224 | tf_op jit(solution)/shard_map/ppermute | solution.py:208
  54.6 1.9 %collective-permute-start.16 = (bf16[16,4096]{1,0:T(8,128)(2,1)S(1)}, bf16[16,4096]{1,0:T(8,128)(2,1)S(1)}, u32[]{:S(2)}, u32[]{:S(2)}) collective-permute-start(bf16[16,4096]{1,0:T(8,128)(2,1)S(1)} %get-tuple-element.77), channel_id=1, source_target_pairs={{0,1},{1,0},{2,3},{3,2},{4,5},{5,4},{6,7},{7,6},{8,9},{9,8},{10,11... | collective-permute-start | bytes 393224 | tf_op jit(solution)/shard_map/ppermute | solution.py:208
